TPU v7x, 32 devices: a whole 2x2x4 slice. The times are simulated.
32 devices in a mesh: row: 8 (over z, y), col: 4 (over x, core).
Axes of the slice: x: 2, y: 2, z: 4, core: 2. Of those that a mesh axis runs over, the one named last changes fastest.
Arguments:
- hidden: bfloat16 [4096, 1152], P('row', 'col'), may hold values from -60 to 60
- noisy_latent: bfloat16 [512, 128], P('row'), may hold values from -6 to 6
- tile_latent: int32 [32], replicated, may hold values from 0 to 14, as said below
- timesteps: int32 [32], replicated, may hold values from 0 to 49
- step_embedding: bfloat16 [50, 1152], replicated, may hold values from -6 to 6
- alpha_now: float32 [50], replicated, may hold values from 0.25 to 0.95
- alpha_next: float32 [50], replicated, may hold values from 0.3 to 0.99
- modulation: bfloat16 [1152, 8, 1152], P('row', None, 'col'), may hold values from -0.1875 to 0.1875
- attention_in: bfloat16 [1152, 3, 1152], P(None, None, 'col'), may hold values from -6 to 6
- attention_out: bfloat16 [1152, 1152], P('col'), may hold values from -0.1875 to 0.1875
- expand_weight: bfloat16 [1152, 2304], P('row', 'col'), may hold values from -0.1875 to 0.1875
- reduce_weight: bfloat16 [2304, 1152], P('col', 'row'), may hold values from -0.125 to 0.125
- noise_head: bfloat16 [1152, 16], P('col'), may hold values from -0.1875 to 0.1875
- preview_kernel: float32 [3, 3, 4, 4], replicated, may hold values from -1 to 1
Outputs:
- stepped: bfloat16 [512, 128], P('row')
- preview: bfloat16 [512, 128], P('row')
Inputs may be any that keep to these rules, and one draw needn't show every extreme that they name: `tile_latent`: latent ids start at 0 on the first tile and rise by 0 or 1 from one tile to the next; the first 4 tiles form latent 0, and every later aligned group of 4 tiles holds exactly two latents of 1 to 3 consecutive tiles each.
All inputs are finite; a program needn't handle non-finite values.
Results may differ from a plain program's by a relative error of at most 0.015.
Values may be sent and summed in bfloat16 or wider, within the bound.
No kernel may reach another device: no remote copies, remote signals or barrier semaphores. Data moves between devices by JAX's collectives and lax.ppermute only.
A program may use at most 64 MiB of HBM per device.

v0:
```python
import jax
import jax.numpy as jnp
from jax import lax
from jax.sharding import PartitionSpec as P

D = 1152
HEAD_DIM = 72
PATCH = 2
CHANNELS = 4
GRIDW = 16
TILE_ROWS = 8
STEPS = 50
TILE = 128


EPS_NORM = 1e-06


def normalize_scaled(values, shift_term, scale_term):
    summed = jnp.sum(values, axis=-1)
    squares = jnp.sum(values * values, axis=-1)
    summed, squares = lax.psum((summed, squares), "col")
    mean_value = summed / D
    spread = squares / D - mean_value * mean_value
    normed = (values - mean_value[..., None]) * lax.rsqrt(spread[..., None] + EPS_NORM)
    return normed * (1.0 + scale_term[:, None, :]) + shift_term[:, None, :]


def gather_features(normed):
    return lax.all_gather(normed, "col", axis=1, tiled=True)


def combine_columns(partial_value):
    return lax.psum_scatter(
        partial_value.astype(jnp.bfloat16), "col", scatter_dimension=1, tiled=True
    ).astype(jnp.float32)


def conv_bands(kernel):
    pixels = GRIDW * PATCH
    in_pixel = jnp.arange(pixels)[:, None]
    out_pixel = jnp.arange(pixels)[None, :]
    band_list = []
    for row_off in range(3):
        summed = jnp.zeros((pixels, CHANNELS, pixels, CHANNELS), jnp.float32)
        for col_off in range(3):
            shifted = (in_pixel == out_pixel + col_off - 1).astype(jnp.float32)
            summed = summed + shifted[:, None, :, None] * kernel[row_off, col_off][None, :, None, :]
        band_list.append(summed.reshape(pixels * CHANNELS, pixels * CHANNELS))
    return band_list


def shards(
    hidden,
    noisy_latent,
    tile_latent,
    timesteps,
    step_embedding,
    alpha_now,
    alpha_next,
    modulation,
    attention_in,
    attention_out,
    expand_weight,
    reduce_weight,
    noise_head,
    preview_kernel,
):
    token_count = hidden.shape[0]
    cols_here = hidden.shape[1]
    tiles_here = token_count // TILE
    heads_here = cols_here // HEAD_DIM
    row_index = lax.axis_index("row")
    first_tile = row_index * tiles_here
    my_latent = lax.dynamic_slice_in_dim(tile_latent, first_tile, tiles_here)
    latent_range = jnp.arange(timesteps.shape[0], dtype=jnp.int32)
    step_range = jnp.arange(STEPS, dtype=jnp.int32)
    latent_pick = my_latent[:, None] == latent_range[None, :]
    my_steps = jnp.sum(jnp.where(latent_pick, timesteps[None, :], 0), axis=1)
    step_match = my_steps[:, None] == step_range[None, :]
    step_pick = step_match.astype(jnp.float32)
    embedded = jnp.dot(
        step_pick.astype(jnp.bfloat16), step_embedding, preferred_element_type=jnp.float32
    )
    conditioning = jax.nn.silu(embedded).astype(jnp.bfloat16)
    columns = conditioning
    adaptive = jnp.einsum(
        "td,dkc->tkc",
        columns,
        lax.all_gather(modulation, "row", axis=0, tiled=True),
        preferred_element_type=jnp.float32,
    )
    tokens_tiled = hidden.astype(jnp.float32).reshape(tiles_here, TILE, cols_here)
    normed_in = normalize_scaled(tokens_tiled, adaptive[:, 0], adaptive[:, 1]).astype(jnp.bfloat16)
    features = gather_features(normed_in.reshape(token_count, cols_here))
    triple = jnp.einsum("td,dsc->tsc", features, attention_in, preferred_element_type=jnp.float32)
    triple = triple.astype(jnp.bfloat16)
    queries = triple[:, 0]
    key_pairs = triple[:, 1:]
    allowed = my_latent[:, None] == my_latent[None, :]
    token_allowed = jnp.repeat(jnp.repeat(allowed, TILE, axis=0), TILE, axis=1)
    scale_factor = HEAD_DIM ** (-0.5)
    head_outputs = []
    for head_index in range(heads_here):
        lower = head_index * HEAD_DIM
        query_head = queries[:, lower : lower + HEAD_DIM]
        key_head = key_pairs[:, 0, lower : lower + HEAD_DIM]
        value_head = key_pairs[:, 1, lower : lower + HEAD_DIM]
        scores = (
            jnp.einsum("qd,kd->qk", query_head, key_head, preferred_element_type=jnp.float32)
            * scale_factor
        )
        scores = jnp.where(token_allowed, scores, -1e30)
        row_peak = jnp.max(scores, axis=1, keepdims=True)
        raised = jnp.exp(scores - row_peak)
        weights = (raised / jnp.sum(raised, axis=1, keepdims=True)).astype(jnp.bfloat16)
        mixed = jnp.dot(weights, value_head, preferred_element_type=jnp.float32)
        head_outputs.append(mixed.astype(jnp.bfloat16))
    attended = jnp.concatenate(head_outputs, axis=1)
    attn_partial = jnp.dot(attended, attention_out, preferred_element_type=jnp.float32)
    attn_partial = attn_partial.astype(jnp.bfloat16).astype(jnp.float32)
    attn_sum = combine_columns(attn_partial).reshape(tiles_here, TILE, cols_here)
    residual = (tokens_tiled + adaptive[:, 2][:, None, :] * attn_sum).astype(jnp.bfloat16)
    residual_wide = residual.astype(jnp.float32)
    normed_mid = normalize_scaled(residual_wide, adaptive[:, 3], adaptive[:, 4]).astype(
        jnp.bfloat16
    )
    features_mid = gather_features(normed_mid.reshape(token_count, cols_here))
    columns = features_mid
    expanded = jnp.dot(
        columns,
        lax.all_gather(expand_weight, "row", axis=0, tiled=True),
        preferred_element_type=jnp.float32,
    )
    activated = jax.nn.gelu(expanded, approximate=True).astype(jnp.bfloat16)
    mlp_partial = jnp.dot(
        activated,
        lax.all_gather(reduce_weight, "row", axis=1, tiled=True),
        preferred_element_type=jnp.float32,
    )
    mlp_sum = combine_columns(mlp_partial).reshape(tiles_here, TILE, cols_here)
    second = (residual_wide + adaptive[:, 5][:, None, :] * mlp_sum).astype(jnp.bfloat16)
    normed_out = normalize_scaled(
        second.astype(jnp.float32), adaptive[:, 6], adaptive[:, 7]
    ).astype(jnp.bfloat16)
    noise_partial = jnp.dot(
        normed_out.reshape(token_count, cols_here), noise_head, preferred_element_type=jnp.float32
    )
    noise_pred = lax.psum(noise_partial.astype(jnp.bfloat16), "col").astype(jnp.float32)
    latent_width = GRIDW * PATCH * CHANNELS
    rows_per_tile = TILE_ROWS * PATCH
    noise_img = noise_pred.reshape(tiles_here, TILE_ROWS, GRIDW, PATCH, PATCH, CHANNELS)
    noise_img = noise_img.transpose(0, 1, 3, 2, 4, 5).reshape(
        tiles_here * rows_per_tile, latent_width
    )
    tile_now = jnp.sum(jnp.where(step_match, alpha_now[None, :], 0.0), axis=1)
    tile_next = jnp.sum(jnp.where(step_match, alpha_next[None, :], 0.0), axis=1)
    signal_now = jnp.repeat(tile_now, rows_per_tile)[:, None]
    signal_next = jnp.repeat(tile_next, rows_per_tile)[:, None]
    noisy_rows = noisy_latent.astype(jnp.float32)
    clean_rows = (noisy_rows - jnp.sqrt(1.0 - signal_now) * noise_img) / jnp.sqrt(signal_now)
    stepped = (jnp.sqrt(signal_next) * clean_rows + jnp.sqrt(1.0 - signal_next) * noise_img).astype(
        jnp.bfloat16
    )
    framed = jnp.pad(clean_rows, ((1, 1), (0, 0)))
    edge_pad = jnp.full((1,), -1, jnp.int32)
    row_latent = jnp.repeat(my_latent, rows_per_tile)
    above_ok = (jnp.concatenate([edge_pad, row_latent[:-1]]) == row_latent)[:, None]
    below_ok = (jnp.concatenate([row_latent[1:], edge_pad]) == row_latent)[:, None]
    band_list = conv_bands(preview_kernel)
    highest = lax.Precision.HIGHEST
    preview = (
        jnp.where(above_ok, jnp.dot(framed[:-2], band_list[0], precision=highest), 0.0)
        + jnp.dot(clean_rows, band_list[1], precision=highest)
        + jnp.where(below_ok, jnp.dot(framed[2:], band_list[2], precision=highest), 0.0)
    )
    return (stepped, preview.astype(jnp.bfloat16))


def solution(mesh):
    return jax.shard_map(
        shards,
        mesh=mesh,
        in_specs=(
            P("row", "col"),
            P("row", None),
            P(),
            P(),
            P(),
            P(),
            P(),
            P("row", None, "col"),
            P(None, None, "col"),
            P("col", None),
            P("row", "col"),
            P("col", "row"),
            P("col", None),
            P(),
        ),
        out_specs=(P("row", None), P("row", None)),
        check_vma=False,
    )
```

profile of v0, /device:TPU:0, one launch (start us, length us, event | category | flops | bytes accessed | tf_op | source)
XLA Modules:
  0.0 346.0 jit_solution(12952949491425328383)
XLA Ops:
  7.3 2.3 copy.36
  9.9 8.3 %all-reduce.3 = (f32[4,128]{1,0:T(4,128)S(1)}, f32[4,128]{1,0:T(4,128)S(1)}) all-reduce(f32[4,128]{1,0:T(4,128)S(1)} %bitcast.190, f32[4,128]{1,0:T(4,128)S(1)} %bitcast.189), channel_id=1, replica_groups=mesh['row'=8,'col'=4] {'col'}, use_global_device_ids=true, to_apply=%region_6.7 | all-reduce | flops 1024 | bytes 8192 | tf_op jit(solution)/shard_map/psum | solution.py:22
  18.2 0.2 select_reduce_fusion.2
  18.4 103.4 %all-gather.6.cloned.1.call-done = bf16[1152,8,288]{2,0,1:T(8,128)(2,1)} async-done(((bf16[144,8,288]{2,0,1:T(8,128)(2,1)}), bf16[1152,8,288]{2,0,1:T(8,128)(2,1)}) %all-gather.6.cloned.1.call-update) | async-done | bytes 5308432 | tf_op jit(solution)/shard_map/all_gather | solution.py:90
  121.8 4.2 %fusion.57 = f32[4,8,288]{2,0,1:T(4,128)S(1)} fusion(bf16[1152,8,288]{2,0,1:T(8,128)(2,1)} %all-gather.6.cloned.1.call-done, bf16[50,1152]{1,0:T(8,128)(2,1)S(1)} %copy-done.2, s32[4]{0:T(128)S(1)} %select_reduce_fusion.2), kind=kOutput, calls=%fused_computation.116 | convolution fusion | flops 21718104 | bytes 5460496 | tf_op jit(solution)/shard_map/td,dkc->tkc/dot_general | solution.py:87
  126.0 0.1 copy.38
  126.1 0.1 copy.39
  126.3 0.4 mul.356
  126.6 0.4 add.193
  127.0 0.9 fusion.23
  128.1 15.6 %all-gather.8.cloned.1.call-done = bf16[512,1152]{0,1:T(8,128)(2,1)} async-done(((bf16[512,288]{0,1:T(8,128)(2,1)}), bf16[512,1152]{0,1:T(8,128)(2,1)}) %all-gather.8.cloned.1.call-update) | async-done | bytes 1179664 | tf_op jit(solution)/shard_map/all_gather | solution.py:30
  143.7 2.6 convolution_convert_fusion.2
  146.3 0.4 fusion.82
  146.7 0.4 fusion.81
  147.1 0.4 fusion.80
  147.4 0.4 fusion.79
  147.8 0.2 fusion.11
  148.0 0.3 convolution_convert_fusion.6
  148.3 0.2 fusion.12
  148.5 0.3 convolution_convert_fusion.5
  148.8 0.2 fusion.13
  149.0 0.3 convolution_convert_fusion.4
  149.3 0.2 fusion.14
  149.5 0.3 convolution_convert_fusion.3
  149.8 0.8 copy-done.8
  150.6 1.8 convolution_convert_fusion.1
  152.5 0.5 all-gather.12.cloned.1.call-update
  153.1 0.5 all-gather.14.cloned.1.call-update
  153.7 0.1 copy.37
  153.8 0.1 copy.41
  154.0 0.1 copy.42
  154.1 24.2 %reduce-scatter.3.cloned.1.call-done = bf16[512,288]{0,1:T(8,128)(2,1)} async-done(((bf16[512,1152]{0,1:T(8,128)(2,1)}), bf16[512,288]{0,1:T(8,128)(2,1)}) %reduce-scatter.3.cloned.1.call-update) | async-done | bytes 294928 | tf_op jit(solution)/shard_map/reduce_scatter | solution.py:34
  178.3 0.4 mul.348
  178.7 1.1 convert_reduce_fusion
  179.8 5.8 %all-reduce.2 = (f32[4,128]{1,0:T(4,128)S(1)}, f32[4,128]{1,0:T(4,128)S(1)}) all-reduce(f32[4,128]{1,0:T(4,128)S(1)} %bitcast.188, f32[4,128]{1,0:T(4,128)S(1)} %bitcast.187), channel_id=1, replica_groups=mesh['row'=8,'col'=4] {'col'}, use_global_device_ids=true, to_apply=%region_19.20 | all-reduce | flops 1024 | bytes 8192 | tf_op jit(solution)/shard_map/psum | solution.py:22
  185.6 0.4 mul.373
  186.0 0.4 add.200
  186.3 0.9 fusion.29
  187.3 0.2 reduce-scatter.5.cloned.1.call-start
  187.5 36.7 %all-gather.12.cloned.1.call-done = bf16[1152,576]{1,0:T(8,128)(2,1)} async-done(((bf16[144,576]{1,0:T(8,128)(2,1)}), bf16[1152,576]{1,0:T(8,128)(2,1)}) %all-gather.12.cloned.1.call-update) | async-done | bytes 1327120 | tf_op jit(solution)/shard_map/all_gather | solution.py:132
  224.2 44.1 %all-gather.14.cloned.1.call-done = bf16[576,1152]{0,1:T(8,128)(2,1)} async-done(((bf16[576,144]{0,1:T(8,128)(2,1)}), bf16[576,1152]{0,1:T(8,128)(2,1)}) %all-gather.14.cloned.1.call-update) | async-done | bytes 1327120 | tf_op jit(solution)/shard_map/all_gather | solution.py:138
  268.3 17.3 %all-gather.10.cloned.1.call-done = bf16[512,1152]{0,1:T(8,128)(2,1)} async-done(((bf16[512,288]{0,1:T(8,128)(2,1)}), bf16[512,1152]{0,1:T(8,128)(2,1)}) %all-gather.10.cloned.1.call-update) | async-done | bytes 1179664 | tf_op jit(solution)/shard_map/all_gather | solution.py:30
  285.6 5.3 %convolution_convert_fusion = bf16[512,1152]{0,1:T(8,128)(2,1)} fusion(bf16[576,1152]{0,1:T(8,128)(2,1)} %all-gather.14.cloned.1.call-done, bf16[512,1152]{0,1:T(8,128)(2,1)} %all-gather.10.cloned.1.call-done, bf16[1152,576]{1,0:T(8,128)(2,1)} %all-gather.12.cloned.1.call-done), kind=kOutput, calls=%fused_computation | convolution fusion | flops 1362198528 | bytes 5013504 | tf_op jit(solution)/shard_map/dot_general | solution.py:136
  291.0 0.2 select_reduce_fusion
  291.9 3.4 multiply_add_fusion
  295.2 3.4 add.216
  298.8 3.3 add.219
  302.0 3.2 add.223
  305.7 0.1 copy.44
  305.9 10.9 %reduce-scatter.5.cloned.1.call-done = bf16[512,288]{0,1:T(8,128)(2,1)} async-done(((bf16[512,1152]{0,1:T(8,128)(2,1)}), bf16[512,288]{0,1:T(8,128)(2,1)}) %reduce-scatter.5.cloned.1.call-update) | async-done | bytes 294928 | tf_op jit(solution)/shard_map/reduce_scatter | solution.py:34
  316.8 0.4 mul.365
  317.2 1.1 convert_reduce_fusion.2
  318.3 5.8 %all-reduce.1 = (f32[4,128]{1,0:T(4,128)S(1)}, f32[4,128]{1,0:T(4,128)S(1)}) all-reduce(f32[4,128]{1,0:T(4,128)S(1)} %bitcast.186, f32[4,128]{1,0:T(4,128)S(1)} %bitcast.185), channel_id=1, replica_groups=mesh['row'=8,'col'=4] {'col'}, use_global_device_ids=true, to_apply=%region_24.25 | all-reduce | flops 1024 | bytes 8192 | tf_op jit(solution)/shard_map/psum | solution.py:22
  324.1 0.4 mul.390
  324.5 0.4 add.210
  324.8 0.2 convolution_convert_fusion.7
  325.1 0.2 reshape.285
  325.2 1.0 copy.45
  326.2 0.8 reshape.286
  327.1 10.1 %psum.55 = bf16[64,128]{1,0:T(8,128)(2,1)S(1)} all-reduce(bf16[64,128]{1,0:T(8,128)(2,1)S(1)} %reshape.286), channel_id=1, replica_groups=mesh['row'=8,'col'=4] {'col'}, use_global_device_ids=true, to_apply=%region_25.26 | all-reduce | flops 8192 | bytes 32768 | tf_op jit(solution)/shard_map/psum | solution.py:149
  337.2 0.7 fusion.50
  337.9 0.2 convolution_select_fusion.1
  338.1 0.2 convolution_add_fusion
  338.3 0.8 fusion.10
  (62 shorter events, 2.0 us)
Async XLA Ops:
  7.2 136.6 %copy-start = (bf16[1152,3,288]{0,2,1:T(8,128)(2,1)S(1)}, bf16[1152,3,288]{0,2,1:T(8,128)(2,1)}, u32[]{:S(2)}) copy-start(bf16[1152,3,288]{0,2,1:T(8,128)(2,1)} %param.22) | copy-start | bytes 5971972
  7.2 2.5 copy-start.9
  7.2 2.6 copy-start.1
  7.2 11.0 %copy-start.10 = (s32[32]{0:T(128)S(1)}, s32[32]{0:T(128)}, u32[]{:S(2)}) copy-start(s32[32]{0:T(128)} %param.17) | copy-start | bytes 388
  7.2 114.6 %copy-start.2 = (bf16[50,1152]{1,0:T(8,128)(2,1)S(1)}, bf16[50,1152]{1,0:T(8,128)(2,1)}, u32[]{:S(2)}) copy-start(bf16[50,1152]{1,0:T(8,128)(2,1)} %param.18) | copy-start | bytes 345604
  7.2 114.5 %all-gather.6.cloned.1.call-start = ((), (), s32[]{:S(2)}) async-start(), calls=%async_computation.2 | async-start | bytes 7962624 | tf_op jit(solution)/shard_map/all_gather | solution.py:90
  9.6 134.1 %all-gather.8.cloned.1.call-start = ((), (), s32[]{:S(2)}) async-start(), calls=%async_computation.3 | async-start | bytes 1474560 | tf_op jit(solution)/shard_map/all_gather | solution.py:30
  127.9 50.4 %reduce-scatter.3.cloned.1.call-start = ((), (), s32[]{:S(2)}) async-start(), calls=%async_computation.4 | async-start | bytes 1474560 | tf_op jit(solution)/shard_map/reduce_scatter | solution.py:34
  149.5 1.1 copy-start.8
  152.5 71.8 %all-gather.12.cloned.1.call-start = ((), (), s32[]{:S(2)}) async-start(), calls=%async_computation.6 | async-start | bytes 1658880 | tf_op jit(solution)/shard_map/all_gather | solution.py:132
  153.0 115.3 %all-gather.14.cloned.1.call-start = ((), (), s32[]{:S(2)}) async-start(), calls=%async_computation.7 | async-start | bytes 1658880 | tf_op jit(solution)/shard_map/all_gather | solution.py:138
  153.6 132.0 %all-gather.10.cloned.1.call-start = ((), (), s32[]{:S(2)}) async-start(), calls=%async_computation.5 | async-start | bytes 1474560 | tf_op jit(solution)/shard_map/all_gather | solution.py:30
  187.2 103.7 %copy-start.6 = (f32[50]{0:T(128)S(1)}, f32[50]{0:T(128)}, u32[]{:S(2)}) copy-start(f32[50]{0:T(128)} %param.19) | copy-start | bytes 604
  187.3 103.7 %copy-start.7 = (f32[50]{0:T(128)S(1)}, f32[50]{0:T(128)}, u32[]{:S(2)}) copy-start(f32[50]{0:T(128)} %param.20) | copy-start | bytes 604
  187.3 104.5 %copy-start.3 = (f32[3,3,4,4]{3,2,1,0:T(4,128)S(1)}, f32[3,3,4,4]{3,2,1,0:T(4,128)}, u32[]{:S(2)}) copy-start(f32[3,3,4,4]{3,2,1,0:T(4,128)} %param.27) | copy-start | bytes 1732
  187.3 129.5 %reduce-scatter.5.cloned.1.call-start = ((), (), s32[]{:S(2)}) async-start(), calls=%async_computation.8 | async-start | bytes 1474560 | tf_op jit(solution)/shard_map/reduce_scatter | solution.py:34
  305.6 19.3 %copy-start.5 = (bf16[288,16]{0,1:T(8,128)(2,1)S(1)}, bf16[288,16]{0,1:T(8,128)(2,1)}, u32[]{:S(2)}) copy-start(bf16[288,16]{0,1:T(8,128)(2,1)} %param.26) | copy-start | bytes 27652
  324.5 12.7 %copy-start.4 = (bf16[64,128]{1,0:T(8,128)(2,1)S(1)}, bf16[64,128]{1,0:T(8,128)(2,1)}, u32[]{:S(2)}) copy-start(bf16[64,128]{1,0:T(8,128)(2,1)} %param.15) | copy-start | bytes 49156
Sparse Core Ops, SparseCore 0:
  10.2 111.5 all-gather.5
  128.1 15.6 all-gather.7
  152.6 25.7 reduce-scatter.2
  180.6 43.5 all-gather.11
  226.5 41.7 all-gather.13
  269.8 15.7 all-gather.9
  291.1 25.7 reduce-scatter.4
where the time goes:
time: 346 us
  waiting for transfers between devices  253 us (73%)
  blocking collectives  30 us (9%)
  local copies, waits for them, and re-layouts  20.1 us (6%)
  matrix products  18 us (5%)
  between operations  14.5 us (4%)
  other arithmetic  9.63 us (3%)
    all_gather x1, waiting for transfers between devices, shards(): lax.all_gather(modulation, 'row', axis=0, tiled=True)  103 us
    all_gather x1, waiting for transfers between devices, shards(): lax.all_gather(reduce_weight, 'row', axis=1, tiled=True)  44.1 us
    all_gather x1, waiting for transfers between devices, shards(): lax.all_gather(expand_weight, 'row', axis=0, tiled=True)  36.7 us
    reduce_scatter x2, waiting for transfers between devices, combine_columns(): lax.psum_scatter(partial_value.astype(jnp.bfloat16), 'col', scatter_dimen...  35.2 us
    all_gather x2, waiting for transfers between devices, gather_features(): return lax.all_gather(normed, 'col', axis=1, tiled=True)  32.9 us
    psum x3, blocking collectives, normalize_scaled(): summed, squares = lax.psum((summed, squares), 'col')  19.9 us
    psum x1, blocking collectives, shards(): lax.psum(noise_partial.astype(jnp.bfloat16), 'col').astype(jnp.float32)  10.1 us
    add x3, local copies, waits for them, and re-layouts, conv_bands(): summed + shifted[:, None, :, None] * kernel[row_off, col_off][None, :, No...  9.86 us
  transfers between devices with their start and end apart: 7, of which 7 were waited for; matrix products, arithmetic and copies ran while one was open for 5% of the time, Pallas kernels for 0%

commit v1 on v0

v1 whole, which is shorter than its diff:
```python
import jax
import jax.numpy as jnp
from jax import lax
from jax.sharding import PartitionSpec as P

D = 1152
HEAD_DIM = 72
PATCH = 2
CHANNELS = 4
GRIDW = 16
TILE_ROWS = 8
STEPS = 50
TILE = 128
EPS_NORM = 1e-06


def exchange(value, axis, offset):
    size = lax.axis_size(axis)
    return lax.ppermute(value, axis, [(i, i ^ offset) for i in range(size)])


def gather_blocks(value):
    across = exchange(value, "col", 2)
    beside = exchange(value, "col", 1)
    diagonal = exchange(across, "col", 1)
    return value, beside, across, diagonal


def natural_order(blocks, axis):
    own, beside, across, diagonal = blocks
    col_index = lax.axis_index("col")
    odd = col_index % 2 == 1
    upper = col_index // 2 == 1
    near = jnp.where(odd, jnp.concatenate([beside, own], axis), jnp.concatenate([own, beside], axis))
    far = jnp.where(
        odd, jnp.concatenate([diagonal, across], axis), jnp.concatenate([across, diagonal], axis)
    )
    return jnp.where(upper, jnp.concatenate([far, near], axis), jnp.concatenate([near, far], axis))


def gather_rows(block):
    rows = lax.axis_size("row")
    if rows != 8:
        return lax.all_gather(block, "row", axis=0)
    pieces = {0: block}
    pieces[4] = exchange(block, "row", 4)
    pieces[2] = exchange(block, "row", 2)
    pieces[1] = exchange(block, "row", 1)
    pieces[3] = exchange(pieces[2], "row", 1)
    pieces[6] = exchange(pieces[4], "row", 2)
    pieces[5] = exchange(pieces[4], "row", 1)
    pieces[7] = exchange(pieces[6], "row", 1)
    here = lax.axis_index("row")
    whole = jnp.zeros((rows,) + block.shape, block.dtype)
    for offset in range(rows):
        whole = lax.dynamic_update_index_in_dim(whole, pieces[offset], here ^ offset, 0)
    return whole


def normalize(values, shift_term, scale_term):
    mean_value = jnp.sum(values, axis=-1, keepdims=True) / D
    spread = jnp.sum(values * values, axis=-1, keepdims=True) / D - mean_value * mean_value
    normed = (values - mean_value) * lax.rsqrt(spread + EPS_NORM)
    return normed * (1.0 + scale_term) + shift_term


def conv_bands(kernel):
    pixels = GRIDW * PATCH
    in_pixel = jnp.arange(pixels)[:, None]
    out_pixel = jnp.arange(pixels)[None, :]
    band_list = []
    for row_off in range(3):
        summed = jnp.zeros((pixels, CHANNELS, pixels, CHANNELS), jnp.float32)
        for col_off in range(3):
            shifted = (in_pixel == out_pixel + col_off - 1).astype(jnp.float32)
            summed = summed + shifted[:, None, :, None] * kernel[row_off, col_off][None, :, None, :]
        band_list.append(summed.reshape(pixels * CHANNELS, pixels * CHANNELS))
    return band_list


def shards(
    hidden,
    noisy_latent,
    tile_latent,
    timesteps,
    step_embedding,
    alpha_now,
    alpha_next,
    modulation,
    attention_in,
    attention_out,
    expand_weight,
    reduce_weight,
    noise_head,
    preview_kernel,
):
    wide = jnp.float32
    narrow = jnp.bfloat16
    rows = lax.axis_size("row")
    token_count, cols_here = hidden.shape
    tiles_here = token_count // TILE
    heads_here = cols_here // HEAD_DIM
    row_index = lax.axis_index("row")
    col_index = lax.axis_index("col")

    hidden_blocks = gather_blocks(hidden)

    ends = tile_latent.reshape(rows, tiles_here)[:, jnp.array([0, tiles_here - 1])].reshape(-1)
    latent_range = jnp.arange(timesteps.shape[0], dtype=jnp.int32)
    end_steps = jnp.sum(jnp.where(ends[:, None] == latent_range[None, :], timesteps[None, :], 0), axis=1)
    step_range = jnp.arange(STEPS, dtype=jnp.int32)
    depth = modulation.shape[0]
    embedding_here = lax.dynamic_slice_in_dim(step_embedding, row_index * depth, depth, 1)
    embedded = jnp.dot(
        (end_steps[:, None] == step_range[None, :]).astype(narrow),
        embedding_here,
        preferred_element_type=wide,
    )
    conditioning = jax.nn.silu(embedded).astype(narrow)
    partial = jnp.einsum("td,dkc->tkc", conditioning, modulation, preferred_element_type=wide)
    partial = partial.reshape(rows, 2, 8 * cols_here)
    adaptive = jnp.sum(lax.all_to_all(partial, "row", 0, 0, tiled=True), axis=0)
    adaptive = lax.all_gather(adaptive, "col", axis=0).reshape(-1, 2, 8, cols_here)
    adaptive = adaptive.transpose(1, 2, 0, 3).reshape(2, 8, D)

    weights_here = jnp.concatenate([expand_weight, reduce_weight.T], axis=0)
    out_weight = lax.all_gather(attention_out, "col", axis=0, tiled=True)
    gathered = gather_rows(weights_here)
    expand_all = gathered[:, :depth].reshape(D, -1)
    reduce_all = gathered[:, depth:].reshape(D, -1)

    my_latent = lax.dynamic_slice_in_dim(tile_latent, row_index * tiles_here, tiles_here)
    second_latent = my_latent != my_latent[0]
    per_tile = jnp.where(second_latent[:, None, None], adaptive[1][None], adaptive[0][None])
    term = lambda index: per_tile[:, index][:, None, :]

    tokens = natural_order(hidden_blocks, 1).astype(wide).reshape(tiles_here, TILE, D)
    normed_in = normalize(tokens, term(0), term(1)).astype(narrow).reshape(token_count, D)
    triple = jnp.einsum("td,dsc->tsc", normed_in, attention_in, preferred_element_type=wide)
    triple = triple.astype(narrow)
    queries = triple[:, 0]
    key_pairs = triple[:, 1:]
    allowed = my_latent[:, None] == my_latent[None, :]
    token_allowed = jnp.repeat(jnp.repeat(allowed, TILE, axis=0), TILE, axis=1)
    scale_factor = HEAD_DIM ** (-0.5)
    head_outputs = []
    for head_index in range(heads_here):
        lower = head_index * HEAD_DIM
        query_head = queries[:, lower : lower + HEAD_DIM]
        key_head = key_pairs[:, 0, lower : lower + HEAD_DIM]
        value_head = key_pairs[:, 1, lower : lower + HEAD_DIM]
        scores = (
            jnp.einsum("qd,kd->qk", query_head, key_head, preferred_element_type=wide)
            * scale_factor
        )
        scores = jnp.where(token_allowed, scores, -1e30)
        row_peak = jnp.max(scores, axis=1, keepdims=True)
        raised = jnp.exp(scores - row_peak)
        weights = (raised / jnp.sum(raised, axis=1, keepdims=True)).astype(narrow)
        mixed = jnp.dot(weights, value_head, preferred_element_type=wide)
        head_outputs.append(mixed.astype(narrow))
    attended_here = jnp.concatenate(head_outputs, axis=1)
    attended = natural_order(gather_blocks(attended_here), 1)
    attn_sum = jnp.dot(attended, out_weight, preferred_element_type=wide)
    residual = tokens + term(2) * attn_sum.reshape(tiles_here, TILE, D)
    residual = residual.astype(narrow)
    normed_mid = normalize(residual.astype(wide), term(3), term(4)).astype(narrow)

    def mlp_tiles(tile_list):
        rows_in = jnp.concatenate(
            [lax.dynamic_index_in_dim(normed_mid, index, 0, keepdims=False) for index in tile_list]
        )
        expanded = jnp.dot(rows_in, expand_all, preferred_element_type=wide)
        activated = jax.nn.gelu(expanded, approximate=True).astype(narrow)
        summed = lax.dot_general(
            activated, reduce_all, (((1,), (1,)), ((), ())), preferred_element_type=wide
        )
        return summed.reshape(len(tile_list), TILE, D)

    far = mlp_tiles([col_index ^ 2, col_index ^ 3])
    far_sum = far[0] + exchange(far[1].astype(narrow), "col", 1).astype(wide)
    crossed = exchange(far_sum.astype(narrow), "col", 2)
    near = mlp_tiles([col_index, col_index ^ 1])
    near_sum = near[0] + exchange(near[1].astype(narrow), "col", 1).astype(wide)
    mlp_sum = near_sum + crossed.astype(wide)
    own_tile = lambda array: lax.dynamic_index_in_dim(array, col_index, 0, keepdims=False)
    own_terms = own_tile(per_tile)
    second = own_tile(residual).astype(wide) + own_terms[5][None] * mlp_sum
    second = second.astype(narrow).astype(wide)
    normed_out = normalize(second, own_terms[6][None], own_terms[7][None]).astype(narrow)
    noise_weight = lax.all_gather(noise_head, "col", axis=0, tiled=True)
    noise_tile = jnp.dot(normed_out, noise_weight, preferred_element_type=wide)
    noise_tile = noise_tile.reshape(TILE_ROWS, GRIDW, PATCH, PATCH * CHANNELS)
    noise_tile = noise_tile.transpose(0, 2, 1, 3).reshape(TILE_ROWS * PATCH, -1)
    noise_img = lax.all_gather(noise_tile, "col", axis=0, tiled=True)

    rows_per_tile = TILE_ROWS * PATCH
    my_steps = jnp.sum(jnp.where(my_latent[:, None] == latent_range[None, :], timesteps[None, :], 0), axis=1)
    step_match = my_steps[:, None] == step_range[None, :]
    tile_now = jnp.sum(jnp.where(step_match, alpha_now[None, :], 0.0), axis=1)
    tile_next = jnp.sum(jnp.where(step_match, alpha_next[None, :], 0.0), axis=1)
    signal_now = jnp.repeat(tile_now, rows_per_tile)[:, None]
    signal_next = jnp.repeat(tile_next, rows_per_tile)[:, None]
    noisy_rows = noisy_latent.astype(wide)
    clean_rows = (noisy_rows - jnp.sqrt(1.0 - signal_now) * noise_img) / jnp.sqrt(signal_now)
    stepped = (jnp.sqrt(signal_next) * clean_rows + jnp.sqrt(1.0 - signal_next) * noise_img).astype(
        narrow
    )
    framed = jnp.pad(clean_rows, ((1, 1), (0, 0)))
    edge_pad = jnp.full((1,), -1, jnp.int32)
    row_latent = jnp.repeat(my_latent, rows_per_tile)
    above_ok = (jnp.concatenate([edge_pad, row_latent[:-1]]) == row_latent)[:, None]
    below_ok = (jnp.concatenate([row_latent[1:], edge_pad]) == row_latent)[:, None]
    band_list = conv_bands(preview_kernel)
    highest = lax.Precision.HIGHEST
    preview = (
        jnp.where(above_ok, jnp.dot(framed[:-2], band_list[0], precision=highest), 0.0)
        + jnp.dot(clean_rows, band_list[1], precision=highest)
        + jnp.where(below_ok, jnp.dot(framed[2:], band_list[2], precision=highest), 0.0)
    )
    return (stepped, preview.astype(narrow))


def solution(mesh):
    return jax.shard_map(
        shards,
        mesh=mesh,
        in_specs=(
            P("row", "col"),
            P("row", None),
            P(),
            P(),
            P(),
            P(),
            P(),
            P("row", None, "col"),
            P(None, None, "col"),
            P("col", None),
            P("row", "col"),
            P("col", "row"),
            P("col", None),
            P(),
        ),
        out_specs=(P("row", None), P("row", None)),
        check_vma=False,
    )
```

time: 346 us -> 168 us (0.49)
  waiting for transfers between devices: 253 us -> 11 us
  local copies, waits for them, and re-layouts: 20.1 us -> 50.8 us
  other arithmetic: 9.63 us -> 28.5 us
  starting transfers between devices: 0.46 us -> 18.2 us
  blocking collectives: 30 us -> 19 us
  matrix products: 18 us -> 24.5 us
    all_gather x5 -> x1, waiting for transfers between devices: 217 us -> 0.01 us  [shards(): out_weight = lax.all_gather(attention_out, 'col', axis=0, tiled=True)]
    reduce_scatter x2 -> x0, waiting for transfers between devices: 35.2 us -> none  [combine_columns(): lax.psum_scatter(partial_value.astype(jnp.bfloat16), 'col', scatter_dimen...]
    psum x4 -> x0, blocking collectives: 30 us -> none  [the longest x3 19.9 us: normalize_scaled(): summed, squares = lax.psum((summed, squares), 'col')]
    all_gather x0 -> x3, blocking collectives: none -> 19 us  [the longest x1 8.15 us: shards(): noise_weight = lax.all_gather(noise_head, 'col', axis=0, tiled=True)]
    ppermute x0 -> x16, starting transfers between devices: none -> 14.8 us  [exchange(): return lax.ppermute(value, axis, [(i, i ^ offset) for i in range(size)])]
    dynamic_update_slice x0 -> x7, local copies, waits for them, and re-layouts: none -> 7.72 us  [gather_rows(): lax.dynamic_update_index_in_dim(whole, pieces[offset], here ^ offset, 0)]
    select_n x0 -> x7, other arithmetic: none -> 6.24 us  [the longest x3 4.18 us: natural_order(): jnp.where(odd, jnp.concatenate([diagonal, across], axis), jnp.concatenate...]
    slice x0 -> x6, local copies, waits for them, and re-layouts: none -> 5.55 us  [the longest x1 1.9 us: shards(): expand_all = gathered[:, :depth].reshape(D, -1)]
  transfers between devices with their start and end apart: 7 -> 18, of which waited for: 7 -> 3; matrix products, arithmetic and copies ran while one was open for 5% -> 43% of each run, Pallas kernels for 0% -> 0%
where the time goes in v1:
time: 168 us; the launch traced here: 167 us
  local copies, waits for them, and re-layouts  50.8 us (30%)
  other arithmetic  28.5 us (17%)
  matrix products  24.5 us (15%)
  blocking collectives  19 us (11%)
  starting transfers between devices  18.2 us (11%)
  between operations  14.6 us (9%)
  waiting for transfers between devices  11 us (7%)
    ppermute x16, starting transfers between devices, exchange(): return lax.ppermute(value, axis, [(i, i ^ offset) for i in range(size)])  14.8 us
    add x3, local copies, waits for them, and re-layouts, conv_bands(): summed + shifted[:, None, :, None] * kernel[row_off, col_off][None, :, No...  11 us
    dot_general x2, matrix products, mlp_tiles(): lax.dot_general(activated, reduce_all, (((1,), (1,)), ((), ())), preferre...  9.11 us
    all_gather x1, blocking collectives, shards(): noise_weight = lax.all_gather(noise_head, 'col', axis=0, tiled=True)  8.15 us
    dynamic_update_slice x7, local copies, waits for them, and re-layouts, gather_rows(): lax.dynamic_update_index_in_dim(whole, pieces[offset], here ^ offset, 0)  7.72 us
    reduce_sum x3, other arithmetic, normalize(): mean_value = jnp.sum(values, axis=-1, keepdims=True) / D  6.55 us
    dot_general x1, matrix products, shards(): attn_sum = jnp.dot(attended, out_weight, preferred_element_type=wide)  5.77 us
    all_gather x1, blocking collectives, shards(): lax.all_gather(adaptive, 'col', axis=0).reshape(-1, 2, 8, cols_here)  5.63 us
  transfers between devices with their start and end apart: 18, of which 3 were waited for; matrix products, arithmetic and copies ran while one was open for 43% of the time, Pallas kernels for 0%

profile of v1, /device:TPU:0, one launch (start us, length us, event | category | flops | bytes accessed | tf_op | source)
XLA Modules:
  0.0 166.7 jit_solution(8142886516127124288)
XLA Ops:
  7.2 3.0 %collective-permute-start = (bf16[512,288]{0,1:T(8,128)(2,1)}, bf16[512,288]{0,1:T(8,128)(2,1)S(1)}, u32[]{:S(2)}, u32[]{:S(2)}) collective-permute-start(bf16[512,288]{0,1:T(8,128)(2,1)} %param.15), channel_id=1, source_target_pairs={{0,2},{1,3},{2,0},{3,1},{4,6},{5,7},{6,4},{7,5},{8,10},{9,11},{10,... | collective-permute-start | bytes 884744 | tf_op jit(solution)/shard_map/ppermute | solution.py:19
  10.2 1.8 %pad_maximum_fusion = bf16[288,576]{1,0:T(8,128)(2,1)} fusion(bf16[144,576]{1,0:T(8,128)(2,1)} %bitcast.204, bf16[144,576]{1,0:T(8,128)(2,1)} %param.25), kind=kLoop, calls=%fused_computation.116 | loop fusion | flops 663552 | bytes 663552 | tf_op jit(solution)/shard_map/concatenate | solution.py:126
  12.0 1.5 collective-permute-start.6
  13.5 1.6 collective-permute-start.7
  15.1 2.6 %collective-permute-start.9 = (bf16[288,576]{1,0:T(8,128)(2,1)}, bf16[288,576]{1,0:T(8,128)(2,1)}, u32[]{:S(2)}, u32[]{:S(2)}) collective-permute-start(bf16[288,576]{1,0:T(8,128)(2,1)} %pad_maximum_fusion), channel_id=1, source_target_pairs={{0,16},{4,20},{8,24},{12,28},{16,0},{20,4},{24,8},{28,12},{1,17},{... | collective-permute-start | bytes 995336 | tf_op jit(solution)/shard_map/ppermute | solution.py:19
  19.3 0.8 select_reduce_fusion
  20.1 1.6 fusion.25
  21.8 0.9 reshape.402
  22.7 3.4 %all-to-all-start = ((f32[8,2,2304]{2,1,0:T(2,128)}), f32[8,2,2304]{2,1,0:T(2,128)S(1)}, u32[]{:S(2)}, u32[]{:S(2)}) async-start(f32[8,2,2304]{2,1,0:T(2,128)} %reshape.402), calls=%async_computation | async-start | bytes 294912 | tf_op jit(solution)/shard_map/all_to_all | solution.py:122
  27.9 3.4 %multiply_add_fusion = (f32[32,4,32,4]{3,2,1,0:T(8,128)}, f32[32,4,32,4]{3,2,1,0:T(8,128)}, f32[32,4,32,4]{3,2,1,0:T(8,128)}) fusion(f32[4,4]{1,0:T(4,128)S(1)} %get-tuple-element.43, f32[4,4]{1,0:T(4,128)S(1)} %get-tuple-element.44, f32[4,4]{1,0:T(4,128)S(1)} %get-tuple-element.36, f32[32,32]{1,0:T(8,128)S(1)} %fusion.102, ...), kind=kLoop, calls=%fused_computation.21 | loop fusion | flops 245760 | bytes 209472 | tf_op jit(solution)/shard_map/add | solution.py:76
  31.3 0.9 copy.95
  32.5 5.3 %all-to-all-done = f32[8,2,2304]{2,1,0:T(2,128)S(1)} async-done(((f32[8,2,2304]{2,1,0:T(2,128)}), f32[8,2,2304]{2,1,0:T(2,128)S(1)}, u32[]{:S(2)}, u32[]{:S(2)}) %all-to-all-start) | async-done | bytes 147488 | tf_op jit(solution)/shard_map/all_to_all | solution.py:122
  37.8 5.6 %all-gather.1 = f32[4,2,2304]{2,1,0:T(2,128)S(1)} all-gather(f32[1,2,2304]{2,1,0:T(2,128)S(1)} %bitcast.208), channel_id=2, replica_groups=mesh['row'=8,'col'=4] {'col'}, dimensions={0}, use_global_device_ids=true | all-gather | bytes 92160 | tf_op jit(solution)/shard_map/all_gather | solution.py:123
  44.6 1.1 copy.104
  45.7 1.1 copy.105
  46.7 1.6 mul.345
  48.4 3.1 %copy.113 = f32[512,1152]{0,1:T(8,128)} copy(f32[512,1152]{1,0:T(8,128)} %bitcast.192) | data formatting | bytes 4718592 | tf_op jit(solution)/shard_map/mul | solution.py:165
  51.8 1.0 copy.115
  52.8 1.0 copy.116
  53.7 1.1 maximum_select_fusion.7
  54.8 1.2 collective-permute-start.10
  56.0 1.0 collective-permute-start.8
  57.0 1.8 %bitcast_dynamic-update-slice_fusion.6 = bf16[8,288,576]{2,1,0:T(8,128)(2,1)} fusion(bf16[8,288,576]{2,1,0:T(8,128)(2,1)} %copy-done.1, s32[]{:T(128)S(6)} %select_n.181, bf16[288,576]{1,0:T(8,128)(2,1)} %collective-permute-done.6), kind=kLoop, calls=%fused_computation.123 | loop fusion | bytes 737284 | tf_op jit(solution)/shard_map/jit(dynamic_update_index_in_dim)/dynamic_update_slice | solution.py:56
  58.7 1.8 %bitcast_dynamic-update-slice_fusion.5 = bf16[8,288,576]{2,1,0:T(8,128)(2,1)} fusion(bf16[8,288,576]{2,1,0:T(8,128)(2,1)} %bitcast_dynamic-update-slice_fusion.6, s32[]{:T(128)S(6)} %select_n.182, bf16[288,576]{1,0:T(8,128)(2,1)} %collective-permute-done.7), kind=kLoop, calls=%fused_computation.122 | loop fusion | bytes 737284 | tf_op jit(solution)/shard_map/jit(dynamic_update_index_in_dim)/dynamic_update_slice | solution.py:56
  60.5 1.0 copy.114
  61.5 2.9 %maximum_select_fusion.4 = (bf16[4,128,576]{2,1,0:T(8,128)(2,1)S(1)}, bf16[4,128,576]{2,1,0:T(8,128)(2,1)S(1)}) fusion(bf16[4,128,288]{2,1,0:T(8,128)(2,1)} %bitcast.197, bf16[4,128,288]{2,1,0:T(8,128)(2,1)} %bitcast.199, pred[]{:T(512)S(6)} %eq.228, bf16[4,128,288]{2,1,0:T(8,128)(2,1)} %bitcast.198, bf16[4,128,288]{2,1,0:T(8,128)(2,1)} %bitcast.196), kind=kLoop, calls=%fused_computation.70 | loop fusion | flops 5308416 | bytes 2359297 | tf_op jit(solution)/shard_map/jit(_where)/select_n | solution.py:35
  64.4 1.3 convert_reduce_fusion
  66.0 1.4 mul.351
  67.4 1.4 add.258
  68.9 1.5 convolution_convert_fusion
  74.5 1.0 collective-permute-start.12
  75.6 1.0 bitcast_dynamic-update-slice_fusion.4
  76.6 1.0 bitcast_dynamic-update-slice_fusion.3
  77.7 1.0 bitcast_dynamic-update-slice_fusion.2
  78.7 1.0 bitcast_dynamic-update-slice_fusion.1
  79.7 2.6 %collective-permute-done.3 = bf16[512,288]{0,1:T(8,128)(2,1)S(1)} collective-permute-done((bf16[512,288]{0,1:T(8,128)(2,1)S(1)}, bf16[512,288]{0,1:T(8,128)(2,1)S(1)}, u32[]{:S(2)}, u32[]{:S(2)}) %collective-permute-start.3) | collective-permute-done | bytes 294944 | tf_op jit(solution)/shard_map/ppermute | solution.py:19
  82.5 0.9 broadcast_select_fusion
  83.4 2.3 %collective-permute-done.12 = bf16[288,576]{1,0:T(8,128)(2,1)S(1)} collective-permute-done((bf16[288,576]{1,0:T(8,128)(2,1)}, bf16[288,576]{1,0:T(8,128)(2,1)S(1)}, u32[]{:S(2)}, u32[]{:S(2)}) %collective-permute-start.12) | collective-permute-done | bytes 331808 | tf_op jit(solution)/shard_map/ppermute | solution.py:19
  85.8 1.9 %fusion.132 = (bf16[8,144,576]{2,1,0:T(8,128)(2,1)}, bf16[8,144,576]{2,1,0:T(8,128)(2,1)}) fusion(bf16[8,288,576]{2,1,0:T(8,128)(2,1)S(1)} %bitcast_dynamic-update-slice_fusion), kind=kLoop, calls=%fused_computation.245 | loop fusion | bytes 5308416 | tf_op jit(solution)/shard_map/slice | solution.py:129
  87.7 1.0 maximum_select_fusion.8
  88.7 5.8 %fusion.10 = f32[512,1152]{1,0:T(8,128)} fusion(bf16[1152,1152]{1,0:T(8,128)(2,1)} %all-gather.5.cloned.1.call-done, bf16[512,576]{0,1:T(8,128)(2,1)} %broadcast_select_fusion, bf16[512,576]{0,1:T(8,128)(2,1)} %maximum_select_fusion.8, pred[]{:T(512)S(6)} %eq.227), kind=kOutput, calls=%fused_computation.33 | convolution fusion | flops 1364262912 | bytes 6193153 | tf_op jit(solution)/shard_map/dot_general | solution.py:164
  94.5 3.1 %copy.108 = f32[512,1152]{0,1:T(8,128)} copy(f32[512,1152]{1,0:T(8,128)} %fusion.10) | data formatting | bytes 4718592 | tf_op jit(solution)/shard_map/dot_general | solution.py:164
  97.6 3.9 %convert_reduce_fusion.1 = (f32[512]{0:T(512)S(1)}, f32[512]{0:T(512)S(1)}) fusion(f32[512,1152]{0,1:T(8,128)} %copy.113, f32[512,1152]{0,1:T(8,128)} %copy.108, bf16[512,576]{0,1:T(8,128)(2,1)} %copy-done.5, bf16[512,576]{0,1:T(8,128)(2,1)} %maximum_select_fusion.7, pred[]{:T(512)S(6)} %eq.227), kind=kLoop, calls=%fused_computation.5 | loop fusion | flops 10025984 | bytes 5902337 | tf_op jit(solution)/shard_map/reduce_sum | solution.py:61
  101.5 2.8 %add_convert_fusion = (bf16[4,128,1152]{2,1,0:T(8,128)(2,1)S(1)}, bf16[4,128,1152]{2,1,0:T(8,128)(2,1)}) fusion(f32[4,1152]{1,0:T(4,128)S(1)} %get-tuple-element.27, f32[4,1152]{1,0:T(4,128)S(1)} %get-tuple-element.28, f32[4,128]{1,0:T(4,128)S(1)} %fusion.110, f32[4,128]{1,0:T(4,128)S(1)} %multiply_bitcast_fusion, f32[4,128,1152]{2,1,0:T(8,128)S(1)} %bitcast.193, ...), kind=kLoop, calls=%fused_computation.20 | loop fusion | flops 11206656 | bytes 5957633 | tf_op jit(solution)/shard_map/convert_element_type | solution.py:167
  104.3 1.0 dynamic-slice_bitcast_fusion.3
  106.1 4.5 %fusion.69 = f32[256,1152]{1,0:T(8,128)} fusion(bf16[1152,576]{1,0:T(8,128)(2,1)} %bitcast.202, bf16[1152,576]{1,0:T(8,128)(2,1)S(1)} %bitcast.200, bf16[128,1152]{1,0:T(8,128)(2,1)} %get-tuple-element.21, bf16[128,1152]{1,0:T(8,128)(2,1)} %get-tuple-element.22), kind=kOutput, calls=%fused_computation.112 | convolution fusion | flops 681984000 | bytes 4423680 | tf_op jit(solution)/shard_map/dot_general | solution.py:175
  110.7 1.8 %slice.281 = bf16[128,1152]{1,0:T(8,128)(2,1)} slice(f32[256,1152]{1,0:T(8,128)} %fusion.69), slice={[128:256], [0:1152]} | slice | bytes 589824 | tf_op jit(solution)/shard_map/slice | solution.py:181
  112.5 4.6 %fusion.58 = f32[256,1152]{1,0:T(8,128)} fusion(bf16[1152,576]{1,0:T(8,128)(2,1)} %bitcast.203, bf16[1152,576]{1,0:T(8,128)(2,1)S(1)} %bitcast.201, bf16[128,1152]{1,0:T(8,128)(2,1)} %get-tuple-element.23, bf16[128,1152]{1,0:T(8,128)(2,1)} %get-tuple-element.20), kind=kOutput, calls=%fused_computation.107 | convolution fusion | flops 681984000 | bytes 4423680 | tf_op jit(solution)/shard_map/dot_general | solution.py:175
  117.0 1.8 %slice.282 = bf16[128,1152]{1,0:T(8,128)(2,1)} slice(f32[256,1152]{1,0:T(8,128)} %fusion.58), slice={[128:256], [0:1152]} | slice | bytes 589824 | tf_op jit(solution)/shard_map/slice | solution.py:184
  119.3 1.9 %fusion.48 = bf16[128,1152]{1,0:T(8,128)(2,1)} fusion(f32[256,1152]{1,0:T(8,128)} %fusion.69, bf16[128,1152]{1,0:T(8,128)(2,1)} %collective-permute-done.14), kind=kLoop, calls=%fused_computation.95 | loop fusion | flops 442368 | bytes 1179648 | tf_op jit(solution)/shard_map/convert_element_type | solution.py:182
  121.3 1.5 collective-permute-start.15
  123.3 8.2 %all-gather.2 = bf16[4,288,16]{1,2,0:T(8,128)(2,1)S(1)} all-gather(bf16[1,288,16]{1,2,0:T(8,128)(2,1)S(1)} %bitcast.214), channel_id=1, replica_groups=mesh['row'=8,'col'=4] {'col'}, dimensions={0}, use_global_device_ids=true | all-gather | bytes 46080 | tf_op jit(solution)/shard_map/all_gather | solution.py:191
  134.5 3.8 %add.299 = f32[128,128]{1,0:T(8,128)} reshape(f32[32,4,32,4]{3,2,1,0:T(8,128)} %get-tuple-element.35) | data formatting | bytes 131072 | tf_op jit(solution)/shard_map/add | solution.py:76
  138.3 3.9 %add.302 = f32[128,128]{1,0:T(8,128)} reshape(f32[32,4,32,4]{3,2,1,0:T(8,128)} %get-tuple-element.34) | data formatting | bytes 131072 | tf_op jit(solution)/shard_map/add | solution.py:76
  142.2 3.2 %add.306 = f32[128,128]{1,0:T(8,128)S(1)} reshape(f32[32,4,32,4]{3,2,1,0:T(8,128)} %get-tuple-element.33) | data formatting | bytes 131072 | tf_op jit(solution)/shard_map/add | solution.py:76
  145.4 1.3 add_compare_fusion.1
  146.8 0.8 fusion.104
  147.6 1.3 convert_reduce_fusion.2
  149.0 1.0 fusion.83
  150.3 5.2 %all_gather.19 = f32[64,128]{1,0:T(8,128)S(1)} all-gather(f32[16,128]{1,0:T(8,128)S(1)} %reshape.410), channel_id=1, replica_groups=mesh['row'=8,'col'=4] {'col'}, dimensions={0}, use_global_device_ids=true | all-gather | bytes 40960 | tf_op jit(solution)/shard_map/all_gather | solution.py:195
  155.5 1.4 add_convert_fusion.1
  156.9 1.0 convolution_select_fusion.1
  158.0 1.0 convolution_add_fusion
  159.0 0.8 fusion.20
  (151 shorter events, 14.8 us)
Async XLA Ops:
  7.2 61.7 %copy-start = (bf16[1152,3,288]{0,2,1:T(8,128)(2,1)S(1)}, bf16[1152,3,288]{0,2,1:T(8,128)(2,1)}, u32[]{:S(2)}) copy-start(bf16[1152,3,288]{0,2,1:T(8,128)(2,1)} %param.23) | copy-start | bytes 5971972
  7.2 19.7 %copy-start.22 = (s32[32]{0:T(128)S(1)}, s32[32]{0:T(128)}, u32[]{:S(2)}) copy-start(s32[32]{0:T(128)} %param.17) | copy-start | bytes 388
  7.2 19.8 %copy-start.25 = (s32[32]{0:T(128)S(1)}, s32[32]{0:T(128)}, u32[]{:S(2)}) copy-start(s32[32]{0:T(128)} %param.18) | copy-start | bytes 388
  7.2 20.1 %copy-start.18 = (f32[3,3,4,4]{3,2,1,0:T(4,128)S(1)}, f32[3,3,4,4]{3,2,1,0:T(4,128)}, u32[]{:S(2)}) copy-start(f32[3,3,4,4]{3,2,1,0:T(4,128)} %param.28) | copy-start | bytes 1732
  7.2 44.3 %collective-permute-start = (bf16[512,288]{0,1:T(8,128)(2,1)}, bf16[512,288]{0,1:T(8,128)(2,1)S(1)}, u32[]{:S(2)}, u32[]{:S(2)}) collective-permute-start(bf16[512,288]{0,1:T(8,128)(2,1)} %param.15), channel_id=1, source_target_pairs={{0,2},{1,3},{2,0},{3,1},{4,6},{5,7},{6,4},{7,5},{8,10},{9,11},{10,... | collective-permute-start | bytes 884744 | tf_op jit(solution)/shard_map/ppermute | solution.py:19
  10.2 42.6 %collective-permute-start.2 = (bf16[512,288]{0,1:T(8,128)(2,1)}, bf16[512,288]{0,1:T(8,128)(2,1)S(1)}, u32[]{:S(2)}, u32[]{:S(2)}) collective-permute-start(bf16[512,288]{0,1:T(8,128)(2,1)} %param.15), channel_id=1, source_target_pairs={{0,1},{1,0},{2,3},{3,2},{4,5},{5,4},{6,7},{7,6},{8,9},{9,8},{10,11... | collective-permute-start | bytes 884744 | tf_op jit(solution)/shard_map/ppermute | solution.py:19
  12.0 44.9 %collective-permute-start.6 = (bf16[288,576]{1,0:T(8,128)(2,1)}, bf16[288,576]{1,0:T(8,128)(2,1)}, u32[]{:S(2)}, u32[]{:S(2)}) collective-permute-start(bf16[288,576]{1,0:T(8,128)(2,1)} %pad_maximum_fusion), channel_id=1, source_target_pairs={{0,4},{4,0},{8,12},{12,8},{16,20},{20,16},{24,28},{28,24},{1,5},{5... | collective-permute-start | bytes 995336 | tf_op jit(solution)/shard_map/ppermute | solution.py:19
  13.5 42.4 %collective-permute-start.7 = (bf16[288,576]{1,0:T(8,128)(2,1)}, bf16[288,576]{1,0:T(8,128)(2,1)}, u32[]{:S(2)}, u32[]{:S(2)}) collective-permute-start(bf16[288,576]{1,0:T(8,128)(2,1)} %pad_maximum_fusion), channel_id=1, source_target_pairs={{0,8},{4,12},{8,0},{12,4},{16,24},{20,28},{24,16},{28,20},{1,9},{5... | collective-permute-start | bytes 995336 | tf_op jit(solution)/shard_map/ppermute | solution.py:19
  15.1 39.7 %collective-permute-start.9 = (bf16[288,576]{1,0:T(8,128)(2,1)}, bf16[288,576]{1,0:T(8,128)(2,1)}, u32[]{:S(2)}, u32[]{:S(2)}) collective-permute-start(bf16[288,576]{1,0:T(8,128)(2,1)} %pad_maximum_fusion), channel_id=1, source_target_pairs={{0,16},{4,20},{8,24},{12,28},{16,0},{20,4},{24,8},{28,12},{1,17},{... | collective-permute-start | bytes 995336 | tf_op jit(solution)/shard_map/ppermute | solution.py:19
  21.8 5.8 %copy-start.14 = (bf16[576,144]{0,1:T(8,128)(2,1)S(1)}, bf16[576,144]{0,1:T(8,128)(2,1)}, u32[]{:S(2)}) copy-start(bf16[576,144]{0,1:T(8,128)(2,1)} %param.26) | copy-start | bytes 497668
  21.8 5.8 %copy-start.15 = (bf16[144,576]{1,0:T(8,128)(2,1)S(1)}, bf16[144,576]{1,0:T(8,128)(2,1)}, u32[]{:S(2)}) copy-start(bf16[144,576]{1,0:T(8,128)(2,1)} %param.25) | copy-start | bytes 497668
  22.7 15.1 %all-to-all-start = ((f32[8,2,2304]{2,1,0:T(2,128)}), f32[8,2,2304]{2,1,0:T(2,128)S(1)}, u32[]{:S(2)}, u32[]{:S(2)}) async-start(f32[8,2,2304]{2,1,0:T(2,128)} %reshape.402), calls=%async_computation | async-start | bytes 294912 | tf_op jit(solution)/shard_map/all_to_all | solution.py:122
  26.1 1.6 copy-start.23
  26.1 1.6 copy-start.24
  26.1 62.6 %all-gather.5.cloned.1.call-start = ((), (), s32[]{:S(2)}) async-start(), calls=%async_computation.1 | async-start | bytes 3317760 | tf_op jit(solution)/shard_map/all_gather | solution.py:127
  27.7 3.6 %copy-start.1 = (bf16[8,288,576]{2,1,0:T(8,128)(2,1)}, bf16[8,288,576]{2,1,0:T(8,128)(2,1)S(1)}, u32[]{:S(2)}) copy-start(bf16[8,288,576]{2,1,0:T(8,128)(2,1)S(1)} %bitcast_dynamic-update-slice_fusion.7) | copy-start | bytes 7962628
  27.9 3.5 %copy-start.9 = (bf16[512,288]{0,1:T(8,128)(2,1)S(1)}, bf16[512,288]{0,1:T(8,128)(2,1)}, u32[]{:S(2)}) copy-start(bf16[512,288]{0,1:T(8,128)(2,1)} %param.15) | copy-start | bytes 884740
  44.0 0.7 copy-start.17
  51.5 10.0 %copy-start.10 = (bf16[512,288]{0,1:T(8,128)(2,1)}, bf16[512,288]{0,1:T(8,128)(2,1)S(1)}, u32[]{:S(2)}) copy-start(bf16[512,288]{0,1:T(8,128)(2,1)S(1)} %collective-permute-done) | copy-start | bytes 884740
  51.5 9.0 %collective-permute-start.1 = (bf16[512,288]{0,1:T(8,128)(2,1)S(1)}, bf16[512,288]{0,1:T(8,128)(2,1)S(1)}, u32[]{:S(2)}, u32[]{:S(2)}) collective-permute-start(bf16[512,288]{0,1:T(8,128)(2,1)S(1)} %collective-permute-done), channel_id=1, source_target_pairs={{0,1},{1,0},{2,3},{3,2},{4,5},{5,4},{6,7},{7,6},{8,9},{9,8},{10,11... | collective-permute-start | bytes 884744 | tf_op jit(solution)/shard_map/ppermute | solution.py:19
  54.8 22.8 %collective-permute-start.10 = (bf16[288,576]{1,0:T(8,128)(2,1)}, bf16[288,576]{1,0:T(8,128)(2,1)}, u32[]{:S(2)}, u32[]{:S(2)}) collective-permute-start(bf16[288,576]{1,0:T(8,128)(2,1)} %collective-permute-done.9), channel_id=1, source_target_pairs={{0,4},{4,0},{8,12},{12,8},{16,20},{20,16},{24,28},{28,24},{1,5},{5... | collective-permute-start | bytes 995336 | tf_op jit(solution)/shard_map/ppermute | solution.py:19
  56.0 18.5 %collective-permute-start.11 = (bf16[288,576]{1,0:T(8,128)(2,1)}, bf16[288,576]{1,0:T(8,128)(2,1)}, u32[]{:S(2)}, u32[]{:S(2)}) collective-permute-start(bf16[288,576]{1,0:T(8,128)(2,1)} %collective-permute-done.9), channel_id=1, source_target_pairs={{0,8},{4,12},{8,0},{12,4},{16,24},{20,28},{24,16},{28,20},{1,9},{5... | collective-permute-start | bytes 995336 | tf_op jit(solution)/shard_map/ppermute | solution.py:19
  56.0 19.6 %collective-permute-start.8 = (bf16[288,576]{1,0:T(8,128)(2,1)}, bf16[288,576]{1,0:T(8,128)(2,1)}, u32[]{:S(2)}, u32[]{:S(2)}) collective-permute-start(bf16[288,576]{1,0:T(8,128)(2,1)} %collective-permute-done.7), channel_id=1, source_target_pairs={{0,4},{4,0},{8,12},{12,8},{16,20},{20,16},{24,28},{28,24},{1,5},{5... | collective-permute-start | bytes 995336 | tf_op jit(solution)/shard_map/ppermute | solution.py:19
  60.5 1.0 copy-start.12
  61.5 4.2 %copy-start.11 = (bf16[512,288]{0,1:T(8,128)(2,1)S(1)}, bf16[512,288]{0,1:T(8,128)(2,1)}, u32[]{:S(2)}) copy-start(bf16[512,288]{0,1:T(8,128)(2,1)} %copy-done.10) | copy-start | bytes 884740
  61.5 4.2 %copy-start.13 = (bf16[512,288]{0,1:T(8,128)(2,1)S(1)}, bf16[512,288]{0,1:T(8,128)(2,1)}, u32[]{:S(2)}) copy-start(bf16[512,288]{0,1:T(8,128)(2,1)} %copy-done.12) | copy-start | bytes 884740
  61.5 4.5 %copy-start.6 = (f32[4,1152]{0,1:T(8,128)S(1)}, f32[4,1152]{0,1:T(8,128)}, u32[]{:S(2)}) copy-start(f32[4,1152]{0,1:T(8,128)} %copy.104) | copy-start | bytes 55300
  65.7 1.8 %copy-start.7 = (f32[4,1152]{0,1:T(8,128)S(1)}, f32[4,1152]{0,1:T(8,128)}, u32[]{:S(2)}) copy-start(f32[4,1152]{0,1:T(8,128)} %copy.105) | copy-start | bytes 55300
  66.0 2.9 %copy-start.5 = (bf16[512,576]{0,1:T(8,128)(2,1)}, bf16[512,576]{0,1:T(8,128)(2,1)S(1)}, u32[]{:S(2)}) copy-start(bf16[512,576]{0,1:T(8,128)(2,1)S(1)} %maximum_select_fusion.6) | copy-start | bytes 1769476
  67.4 1.5 copy-start.4
  73.6 2.0 %copy-start.2 = (bf16[8,288,576]{2,1,0:T(8,128)(2,1)S(1)}, bf16[8,288,576]{2,1,0:T(8,128)(2,1)}, u32[]{:S(2)}) copy-start(bf16[8,288,576]{2,1,0:T(8,128)(2,1)} %bitcast_dynamic-update-slice_fusion.5) | copy-start | bytes 7962628
  73.9 8.5 %collective-permute-start.3 = (bf16[512,288]{0,1:T(8,128)(2,1)S(1)}, bf16[512,288]{0,1:T(8,128)(2,1)S(1)}, u32[]{:S(2)}, u32[]{:S(2)}) collective-permute-start(bf16[512,288]{0,1:T(8,128)(2,1)S(1)} %pad_maximum_fusion.1), channel_id=1, source_target_pairs={{0,2},{1,3},{2,0},{3,1},{4,6},{5,7},{6,4},{7,5},{8,10},{9,11},{10,... | collective-permute-start | bytes 884744 | tf_op jit(solution)/shard_map/ppermute | solution.py:19
  74.5 7.9 %collective-permute-start.5 = (bf16[512,288]{0,1:T(8,128)(2,1)S(1)}, bf16[512,288]{0,1:T(8,128)(2,1)S(1)}, u32[]{:S(2)}, u32[]{:S(2)}) collective-permute-start(bf16[512,288]{0,1:T(8,128)(2,1)S(1)} %pad_maximum_fusion.1), channel_id=1, source_target_pairs={{0,1},{1,0},{2,3},{3,2},{4,5},{5,4},{6,7},{7,6},{8,9},{9,8},{10,11... | collective-permute-start | bytes 884744 | tf_op jit(solution)/shard_map/ppermute | solution.py:19
  74.5 11.2 %collective-permute-start.12 = (bf16[288,576]{1,0:T(8,128)(2,1)}, bf16[288,576]{1,0:T(8,128)(2,1)S(1)}, u32[]{:S(2)}, u32[]{:S(2)}) collective-permute-start(bf16[288,576]{1,0:T(8,128)(2,1)} %collective-permute-done.11), channel_id=1, source_target_pairs={{0,4},{4,0},{8,12},{12,8},{16,20},{20,16},{24,28},{28,24},{1,5},{5... | collective-permute-start | bytes 995336 | tf_op jit(solution)/shard_map/ppermute | solution.py:19
  82.4 5.3 %collective-permute-start.4 = (bf16[512,288]{0,1:T(8,128)(2,1)S(1)}, bf16[512,288]{0,1:T(8,128)(2,1)S(1)}, u32[]{:S(2)}, u32[]{:S(2)}) collective-permute-start(bf16[512,288]{0,1:T(8,128)(2,1)S(1)} %collective-permute-done.3), channel_id=1, source_target_pairs={{0,1},{1,0},{2,3},{3,2},{4,5},{5,4},{6,7},{7,6},{8,9},{9,8},{10,11... | collective-permute-start | bytes 884744 | tf_op jit(solution)/shard_map/ppermute | solution.py:19
  97.6 3.9 %copy-start.3 = (f32[512,1152]{1,0:T(8,128)S(1)}, f32[512,1152]{1,0:T(8,128)}, u32[]{:S(2)}) copy-start(f32[512,1152]{1,0:T(8,128)} %fusion.10) | copy-start | bytes 7077892
  104.3 1.8 %copy-start.8 = (bf16[8,144,576]{2,1,0:T(8,128)(2,1)S(1)}, bf16[8,144,576]{2,1,0:T(8,128)(2,1)}, u32[]{:S(2)}) copy-start(bf16[8,144,576]{2,1,0:T(8,128)(2,1)} %get-tuple-element.18) | copy-start | bytes 3981316
  112.5 6.9 %collective-permute-start.14 = (bf16[128,1152]{1,0:T(8,128)(2,1)}, bf16[128,1152]{1,0:T(8,128)(2,1)}, u32[]{:S(2)}, u32[]{:S(2)}) collective-permute-start(bf16[128,1152]{1,0:T(8,128)(2,1)} %slice.281), channel_id=1, source_target_pairs={{0,1},{1,0},{2,3},{3,2},{4,5},{5,4},{6,7},{7,6},{8,9},{9,8},{10,11... | collective-permute-start | bytes 884744 | tf_op jit(solution)/shard_map/ppermute | solution.py:19
  112.5 10.9 %copy-start.20 = (bf16[288,16]{0,1:T(8,128)(2,1)S(1)}, bf16[288,16]{0,1:T(8,128)(2,1)}, u32[]{:S(2)}) copy-start(bf16[288,16]{0,1:T(8,128)(2,1)} %param.27) | copy-start | bytes 27652
  118.8 28.7 %collective-permute-start.13 = (bf16[128,1152]{1,0:T(8,128)(2,1)}, bf16[128,1152]{1,0:T(8,128)(2,1)S(1)}, u32[]{:S(2)}, u32[]{:S(2)}) collective-permute-start(bf16[128,1152]{1,0:T(8,128)(2,1)} %slice.282), channel_id=1, source_target_pairs={{0,1},{1,0},{2,3},{3,2},{4,5},{5,4},{6,7},{7,6},{8,9},{9,8},{10,11... | collective-permute-start | bytes 884744 | tf_op jit(solution)/shard_map/ppermute | solution.py:19
  121.3 26.3 %collective-permute-start.15 = (bf16[128,1152]{1,0:T(8,128)(2,1)}, bf16[128,1152]{1,0:T(8,128)(2,1)}, u32[]{:S(2)}, u32[]{:S(2)}) collective-permute-start(bf16[128,1152]{1,0:T(8,128)(2,1)} %fusion.48), channel_id=1, source_target_pairs={{0,2},{1,3},{2,0},{3,1},{4,6},{5,7},{6,4},{7,5},{8,10},{9,11},{10,... | collective-permute-start | bytes 884744 | tf_op jit(solution)/shard_map/ppermute | solution.py:19
  138.3 9.3 %copy-start.16 = (f32[256,1152]{1,0:T(8,128)S(1)}, f32[256,1152]{1,0:T(8,128)}, u32[]{:S(2)}) copy-start(f32[256,1152]{1,0:T(8,128)} %fusion.58) | copy-start | bytes 3538948
  145.4 10.1 %copy-start.19 = (bf16[64,128]{1,0:T(8,128)(2,1)S(1)}, bf16[64,128]{1,0:T(8,128)(2,1)}, u32[]{:S(2)}) copy-start(bf16[64,128]{1,0:T(8,128)(2,1)} %param.16) | copy-start | bytes 49156
  146.8 12.2 %copy-start.21 = (pred[64]{0:T(512)(128)(4,1)S(1)}, pred[64]{0:T(512)(128)(4,1)}, u32[]{:S(2)}) copy-start(pred[64]{0:T(512)(128)(4,1)} %get-tuple-element.45) | copy-start | bytes 196
Sparse Core Ops, SparseCore 0:
  28.5 26.5 all-gather.4

commit v2 on v1

v2 whole, which is shorter than its diff:
```python
import functools

import jax
import jax.numpy as jnp
from jax import lax
from jax.experimental import pallas as pl
from jax.experimental.pallas import tpu as pltpu
from jax.sharding import PartitionSpec as P

D = 1152
HEAD_DIM = 72
PATCH = 2
CHANNELS = 4
GRIDW = 16
TILE_ROWS = 8
STEPS = 50
TILE = 128
EPS_NORM = 1e-06
IMG_ROWS = TILE_ROWS * PATCH
IMG_WIDTH = GRIDW * PATCH * CHANNELS
WIDE = jnp.float32
NARROW = jnp.bfloat16
NT = (((1,), (1,)), ((), ()))
VMEM = pl.BlockSpec(memory_space=pltpu.VMEM)
SMEM = pl.BlockSpec(memory_space=pltpu.SMEM)
ANYWHERE = pl.BlockSpec(memory_space=pl.ANY)
VMEM_LIMIT = 40 * 1024 * 1024


def call(kernel, outs, in_specs, scratch=(), flops=0, nbytes=0, trans=0):
    return pl.pallas_call(
        kernel,
        out_shape=outs,
        in_specs=in_specs,
        out_specs=jax.tree.map(lambda _: VMEM, outs),
        scratch_shapes=list(scratch),
        compiler_params=pltpu.CompilerParams(vmem_limit_bytes=VMEM_LIMIT),
        cost_estimate=pl.CostEstimate(flops=flops, bytes_accessed=nbytes, transcendentals=trans),
    )


def exchange(value, axis, offset):
    size = lax.axis_size(axis)
    return lax.ppermute(value, axis, [(i, i ^ offset) for i in range(size)])


def gather_blocks(value):
    across = exchange(value, "col", 2)
    beside = exchange(value, "col", 1)
    diagonal = exchange(across, "col", 1)
    return value, beside, across, diagonal


def gather_rows(block):
    rows = lax.axis_size("row")
    if rows != 8:
        half = block.shape[0] // 2
        whole = lax.all_gather(block, "row", axis=0)
        return [jnp.concatenate([whole[:, :half], whole[:, half:]]).reshape(-1, block.shape[1])]
    pieces = {0: block}
    pieces[4] = exchange(block, "row", 4)
    pieces[2] = exchange(block, "row", 2)
    pieces[1] = exchange(block, "row", 1)
    pieces[3] = exchange(pieces[2], "row", 1)
    pieces[6] = exchange(pieces[4], "row", 2)
    pieces[5] = exchange(pieces[4], "row", 1)
    pieces[7] = exchange(pieces[6], "row", 1)
    return [pieces[offset] for offset in range(rows)]


def normalize(values, shift_term, scale_term):
    mean_value = jnp.sum(values, axis=-1, keepdims=True) * (1.0 / D)
    spread = jnp.sum(values * values, axis=-1, keepdims=True) * (1.0 / D) - mean_value * mean_value
    normed = (values - mean_value) * lax.rsqrt(spread + EPS_NORM)
    return normed * (1.0 + scale_term) + shift_term


def condition_kernel(tiles_here, latent_ref, steps_ref, embedding_ref, out_ref, onehot):
    count, depth = out_ref.shape

    def pick(index, carry):
        tile = (index // 2) * tiles_here + (index % 2) * (tiles_here - 1)
        step = steps_ref[latent_ref[tile]]
        lanes = lax.broadcasted_iota(jnp.int32, (1, STEPS), 1)
        onehot[pl.ds(index, 1), :] = jnp.where(lanes == step, 1.0, 0.0)
        return carry

    lax.fori_loop(0, count, pick, 0)
    embedded = jnp.dot(onehot[...].astype(NARROW), embedding_ref[...], preferred_element_type=WIDE)
    conditioning = (embedded / (1.0 + jnp.exp(-embedded))).astype(NARROW)
    first = lax.axis_index("row") * depth
    source = lax.broadcasted_iota(jnp.int32, (D, depth), 0)
    target = lax.broadcasted_iota(jnp.int32, (D, depth), 1) + first
    chosen = jnp.where(source == target, 1.0, 0.0).astype(NARROW)
    out_ref[...] = jnp.dot(conditioning, chosen, preferred_element_type=WIDE).astype(NARROW)


def tile_term(latent_ref, terms_ref, index, tile):
    first = lax.axis_index("row") * (lax.axis_size("col"))
    later = latent_ref[first + tile] != latent_ref[first]
    return jnp.where(later, terms_ref[8 + index : 9 + index, :], terms_ref[index : index + 1, :])


def attention_kernel(
    latent_ref, own, beside, across, diagonal, gathered_ref, weight_ref,
    tokens_ref, terms_ref, attended_ref, normed, triple,
):
    col = lax.axis_index("col")
    row = lax.axis_index("row")
    width = own.shape[1]
    tiles = own.shape[0] // TILE
    for place in range(4):
        terms_ref[:, place * width : (place + 1) * width] = gathered_ref[place]

        @pl.when(col == place)
        def _():
            for offset, block in enumerate((own, beside, across, diagonal)):
                lower = (place ^ offset) * width
                tokens_ref[:, lower : lower + width] = block[...]

    for tile in range(tiles):
        here = slice(tile * TILE, (tile + 1) * TILE)
        shift = tile_term(latent_ref, terms_ref, 0, tile)
        scale = tile_term(latent_ref, terms_ref, 1, tile)
        normed[here, :] = normalize(tokens_ref[here, :].astype(WIDE), shift, scale).astype(NARROW)
    triple[...] = jnp.dot(normed[...], weight_ref[...], preferred_element_type=WIDE).astype(NARROW)
    key_tile = lax.broadcasted_iota(jnp.int32, (1, tiles * TILE), 1) // TILE
    key_latent = jnp.zeros((1, tiles * TILE), jnp.int32)
    for tile in range(tiles):
        key_latent = jnp.where(key_tile == tile, latent_ref[row * tiles + tile], key_latent)
    factor = HEAD_DIM ** (-0.5) * 1.4426950408889634
    for head in range(width // HEAD_DIM):
        lower = head * HEAD_DIM
        keys = triple[:, width + lower : width + lower + HEAD_DIM]
        mixed_values = triple[:, 2 * width + lower : 2 * width + lower + HEAD_DIM]
        for tile in range(tiles):
            here = slice(tile * TILE, (tile + 1) * TILE)
            barred = jnp.where(key_latent == latent_ref[row * tiles + tile], 0.0, -1e30)
            scores = lax.dot_general(
                triple[here, lower : lower + HEAD_DIM], keys, NT, preferred_element_type=WIDE
            )
            scores = scores + barred
            peak = jnp.max(scores, axis=1, keepdims=True)
            raised = jnp.exp2((scores - peak) * factor)
            total = jnp.sum(raised, axis=1, keepdims=True)
            mixed = jnp.dot(raised.astype(NARROW), mixed_values, preferred_element_type=WIDE)
            attended_ref[here, lower : lower + HEAD_DIM] = (mixed / total).astype(NARROW)


def mlp_kernel(near, depth, latent_ref, att_own, att_beside, att_across, att_diagonal, tokens_ref, terms_ref, *refs):
    out_blocks, refs = refs[:4], refs[4:]
    count = len(refs) - (3 if near else 2) - 7
    pieces, refs = refs[:count], refs[count:]
    outs, scratch = refs[:-7], refs[-7:]
    out_weight, expand, reduce, attended, mid, out_sems, piece_sems = scratch
    col = lax.axis_index("col")
    row = lax.axis_index("row")
    width = att_own.shape[1]
    out_copies = []
    for offset, block in enumerate(out_blocks):
        start = pl.multiple_of((col ^ offset) * width, 16)
        out_copies.append(
            pltpu.make_async_copy(block, out_weight.at[pl.ds(start, width), :], out_sems.at[offset])
        )
    piece_copies = []
    for offset, piece in enumerate(pieces):
        start = pl.multiple_of((row ^ offset) * depth, 16) if count > 1 else 0
        for half, target in enumerate((expand, reduce)):
            piece_copies.append(
                pltpu.make_async_copy(
                    piece.at[pl.ds(half * depth, depth), :],
                    target.at[pl.ds(start, depth), :],
                    piece_sems.at[2 * offset + half],
                )
            )
    for copy in out_copies + piece_copies:
        copy.start()
    tile_offsets = (0, 1) if near else (2, 3)
    for place in range(4):

        @pl.when(col == place)
        def _():
            for offset, block in enumerate((att_own, att_beside, att_across, att_diagonal)):
                lower = (place ^ offset) * width
                for slot, tile_offset in enumerate(tile_offsets):
                    first = (place ^ tile_offset) * TILE
                    attended[slot * TILE : (slot + 1) * TILE, lower : lower + width] = block[
                        first : first + TILE, :
                    ]

    for copy in out_copies:
        copy.wait()
    attn_sum = jnp.dot(attended[...], out_weight[...], preferred_element_type=WIDE)
    for slot, tile_offset in enumerate(tile_offsets):
        tile = col ^ tile_offset
        term = functools.partial(tile_term, latent_ref, terms_ref, tile=tile)
        here = slice(slot * TILE, (slot + 1) * TILE)
        before = tokens_ref[pl.ds(pl.multiple_of(tile * TILE, TILE), TILE), :].astype(WIDE)
        residual = (before + term(2) * attn_sum[here]).astype(NARROW)
        if near and slot == 0:
            outs[2][...] = residual
        mid[here, :] = normalize(residual.astype(WIDE), term(3), term(4)).astype(NARROW)
    for copy in piece_copies:
        copy.wait()
    units = jnp.dot(mid[...], expand[...], preferred_element_type=WIDE)
    inner = 0.7978845608028654 * (units + 0.044715 * (units * units * units))
    activated = (0.5 * units * (1.0 + jnp.tanh(inner))).astype(NARROW)
    summed = lax.dot_general(activated, reduce[...], NT, preferred_element_type=WIDE)
    outs[0][...] = summed[:TILE]
    outs[1][...] = summed[TILE:].astype(NARROW)


def head_kernel(latent_ref, kept_ref, beside_ref, crossed_ref, residual_ref, terms_ref, out_ref):
    col = lax.axis_index("col")
    term = functools.partial(tile_term, latent_ref, terms_ref, tile=col)
    mlp_sum = kept_ref[...] + beside_ref[...].astype(WIDE) + crossed_ref[...].astype(WIDE)
    second = (residual_ref[...].astype(WIDE) + term(5) * mlp_sum).astype(NARROW).astype(WIDE)
    normed = normalize(second, term(6), term(7)).astype(NARROW)
    group = PATCH * CHANNELS
    token_place = lax.broadcasted_iota(jnp.int32, (TILE, IMG_WIDTH), 0) % GRIDW
    lane_place = lax.broadcasted_iota(jnp.int32, (TILE, IMG_WIDTH), 1) // group
    for dy in range(PATCH):
        rows = terms_ref[16 + dy * group : 16 + (dy + 1) * group, :].astype(NARROW)
        spread_rows = jnp.concatenate([rows.astype(WIDE)] * GRIDW, axis=0).astype(NARROW)
        noise = lax.dot_general(normed, spread_rows, NT, preferred_element_type=WIDE)
        noise = jnp.where(token_place == lane_place, noise, 0.0)
        folded = jnp.sum(noise.reshape(TILE_ROWS, GRIDW, IMG_WIDTH), axis=1)
        out_ref[:, dy * IMG_WIDTH : (dy + 1) * IMG_WIDTH] = folded


def bands_kernel(kernel_ref, out_ref):
    shape = (IMG_WIDTH, IMG_WIDTH)
    source = lax.broadcasted_iota(jnp.int32, shape, 0)
    target = lax.broadcasted_iota(jnp.int32, shape, 1)
    reach = 3 * CHANNELS
    apart = target - (source // CHANNELS) * CHANNELS + CHANNELS
    code = jnp.where((apart >= 0) & (apart < reach), (source % CHANNELS) * reach + apart, -1)
    bands = [jnp.zeros(shape, WIDE) for _ in range(3)]
    for channel in range(CHANNELS):
        for lane in range(reach):
            here = code == channel * reach + lane
            column, out_channel = 2 - lane // CHANNELS, lane % CHANNELS
            for line in range(3):
                place = ((line * 3 + column) * CHANNELS + channel) * CHANNELS + out_channel
                bands[line] = jnp.where(here, kernel_ref[place], bands[line])
    for line in range(3):
        out_ref[:, line * IMG_WIDTH : (line + 1) * IMG_WIDTH] = bands[line]


def step_kernel(
    latent_ref, steps_ref, now_ref, next_ref, noise_ref, noisy_ref, bands_ref,
    stepped_ref, preview_ref, image, clean, above, below,
):
    tiles = noise_ref.shape[0]
    row = lax.axis_index("row")
    for tile in range(tiles):
        for dy in range(PATCH):
            image[pl.ds(tile * IMG_ROWS + dy, TILE_ROWS, PATCH), :] = noise_ref[
                tile, :, dy * IMG_WIDTH : (dy + 1) * IMG_WIDTH
            ]
    for tile in range(tiles):
        here = slice(tile * IMG_ROWS, (tile + 1) * IMG_ROWS)
        step = steps_ref[latent_ref[row * tiles + tile]]
        signal_now = jnp.full((1, IMG_WIDTH), now_ref[step], WIDE)
        signal_next = jnp.full((1, IMG_WIDTH), next_ref[step], WIDE)
        noise = image[here, :]
        rows = (noisy_ref[here, :].astype(WIDE) - jnp.sqrt(1.0 - signal_now) * noise) / jnp.sqrt(signal_now)
        clean[here, :] = rows
        stepped = jnp.sqrt(signal_next) * rows + jnp.sqrt(1.0 - signal_next) * noise
        stepped_ref[here, :] = stepped.astype(NARROW)
    parts = jnp.dot(
        clean[...], bands_ref[...], precision=lax.Precision.HIGHEST, preferred_element_type=WIDE
    )
    count = tiles * IMG_ROWS
    above[8 : 8 + count, :] = parts[:, :IMG_WIDTH]
    below[8 : 8 + count, :] = parts[:, 2 * IMG_WIDTH :]
    for tile in range(tiles):
        here = slice(tile * IMG_ROWS, (tile + 1) * IMG_ROWS)
        start = 8 + tile * IMG_ROWS
        line = lax.broadcasted_iota(jnp.int32, (IMG_ROWS, IMG_WIDTH), 0)
        from_above = above[start - 1 : start - 1 + IMG_ROWS, :]
        from_below = below[start + 1 : start + 1 + IMG_ROWS, :]
        mine = latent_ref[row * tiles + tile]
        if tile == 0:
            above_ok = line > 0
        else:
            above_ok = (line > 0) | (latent_ref[row * tiles + tile - 1] == mine)
        if tile == tiles - 1:
            below_ok = line < IMG_ROWS - 1
        else:
            below_ok = (line < IMG_ROWS - 1) | (latent_ref[row * tiles + tile + 1] == mine)
        total = parts[here, IMG_WIDTH : 2 * IMG_WIDTH]
        total = total + jnp.where(above_ok, from_above, 0.0) + jnp.where(below_ok, from_below, 0.0)
        preview_ref[here, :] = total.astype(NARROW)


def shards(
    hidden,
    noisy_latent,
    tile_latent,
    timesteps,
    step_embedding,
    alpha_now,
    alpha_next,
    modulation,
    attention_in,
    attention_out,
    expand_weight,
    reduce_weight,
    noise_head,
    preview_kernel,
):
    rows = lax.axis_size("row")
    tokens_here, width = hidden.shape
    tiles = tokens_here // TILE
    depth = modulation.shape[0]
    units = expand_weight.shape[1]
    shape = jax.ShapeDtypeStruct

    hidden_blocks = gather_blocks(hidden)
    weights_here = jnp.concatenate([expand_weight, reduce_weight.T], axis=0)

    conditioning = call(
        functools.partial(condition_kernel, tiles),
        shape((2 * rows, depth), NARROW),
        [SMEM, SMEM, VMEM],
        [pltpu.VMEM((2 * rows, STEPS), WIDE)],
        flops=2 * 2 * rows * D * (STEPS + depth), nbytes=2 * STEPS * D,
    )(tile_latent, timesteps, step_embedding)
    partial = jnp.einsum("td,dkc->tkc", conditioning, modulation, preferred_element_type=WIDE)
    partial = partial.reshape(rows, 2, 8, width)
    adaptive = jnp.sum(lax.all_to_all(partial, "row", 0, 0, tiled=True), axis=0)
    shared = jnp.concatenate([adaptive.reshape(16, width), noise_head.T.astype(WIDE)])
    shared = lax.all_gather(shared, "col", axis=0)

    out_source, _ = lax.optimization_barrier((attention_out, hidden_blocks[2]))
    out_blocks = gather_blocks(out_source)
    pieces = gather_rows(weights_here)

    bands = call(
        bands_kernel, shape((IMG_WIDTH, 3 * IMG_WIDTH), WIDE), [SMEM], flops=10**8, nbytes=3 * 2**16
    )(preview_kernel.reshape(-1))

    tokens, terms, attended = call(
        attention_kernel,
        [shape((tokens_here, D), NARROW), shape((32, D), WIDE), shape((tokens_here, width), NARROW)],
        [SMEM] + [VMEM] * 6,
        [pltpu.VMEM((tokens_here, D), NARROW), pltpu.VMEM((tokens_here, 3 * width), NARROW)],
        flops=2 * tokens_here * (D * 3 * width + 2 * tokens_here * width), nbytes=5 * 2**20,
        trans=4 * tokens_here**2,
    )(tile_latent, *hidden_blocks, shared, attention_in.reshape(D, 3 * width))
    attended_blocks = gather_blocks(attended)

    def mlp(near):
        outs = [shape((TILE, D), WIDE), shape((TILE, D), NARROW)]
        if near:
            outs.append(shape((TILE, D), NARROW))
        piece_depth = pieces[0].shape[0] // 2
        return call(
            functools.partial(mlp_kernel, near, piece_depth),
            outs,
            [SMEM] + [VMEM] * 6 + [ANYWHERE] * (4 + len(pieces)),
            [
                pltpu.VMEM((D, D), NARROW),
                pltpu.VMEM((D, units), NARROW),
                pltpu.VMEM((D, units), NARROW),
                pltpu.VMEM((2 * TILE, D), NARROW),
                pltpu.VMEM((2 * TILE, D), NARROW),
                pltpu.SemaphoreType.DMA((4,)),
                pltpu.SemaphoreType.DMA((2 * len(pieces),)),
            ],
            flops=4 * TILE * D * (D + 2 * units), nbytes=8 * 2**20, trans=2 * TILE * units,
        )(tile_latent, *attended_blocks, tokens, terms, *out_blocks, *pieces)

    far_kept, far_sent = mlp(False)
    far_sum = (far_kept + exchange(far_sent, "col", 1).astype(WIDE)).astype(NARROW)
    crossed = exchange(far_sum, "col", 2)
    near_kept, near_sent, residual = mlp(True)
    beside = exchange(near_sent, "col", 1)
    noise = call(
        head_kernel,
        shape((TILE_ROWS, PATCH * IMG_WIDTH), WIDE),
        [SMEM] + [VMEM] * 5,
        flops=4 * TILE * D * IMG_WIDTH, nbytes=2**21,
    )(tile_latent, near_kept, beside, crossed, residual, terms)
    noise = lax.all_gather(noise, "col", axis=0)

    img_rows = tiles * IMG_ROWS
    stepped, preview = call(
        step_kernel,
        [shape((img_rows, IMG_WIDTH), NARROW)] * 2,
        [SMEM] * 4 + [VMEM] * 3,
        [pltpu.VMEM((img_rows, IMG_WIDTH), WIDE)] * 2
        + [pltpu.VMEM((img_rows + 16, IMG_WIDTH), WIDE)] * 2,
        flops=12 * img_rows * IMG_WIDTH**2, nbytes=2**19,
    )(tile_latent, timesteps, alpha_now, alpha_next, noise, noisy_latent, bands)
    return (stepped, preview)


def solution(mesh):
    return jax.shard_map(
        shards,
        mesh=mesh,
        in_specs=(
            P("row", "col"),
            P("row", None),
            P(),
            P(),
            P(),
            P(),
            P(),
            P("row", None, "col"),
            P(None, None, "col"),
            P("col", None),
            P("row", "col"),
            P("col", "row"),
            P("col", None),
            P(),
        ),
        out_specs=(P("row", None), P("row", None)),
        check_vma=False,
    )
```

time: 168 us -> 103 us (0.61)
  local copies, waits for them, and re-layouts: 50.8 us -> 14.2 us
  Pallas kernels: 0 us -> 29.9 us
  other arithmetic: 28.5 us -> 2.53 us
  matrix products: 24.5 us -> 0.24 us
  between operations: 14.6 us -> 0.81 us
  waiting for transfers between devices: 11 us -> 21.3 us
  blocking collectives: 19 us -> 10.8 us
  starting transfers between devices: 18.2 us -> 22.8 us
    pallas_call x0 -> x7, Pallas kernels: none -> 29.9 us  [the longest x2 16.2 us: mlp(): call(functools.partial(mlp_kernel, near, piece_depth), outs, [SMEM] + [VM...]
    dot_general x16 -> x0, matrix products: 22.8 us -> none  [the longest x2 9.11 us: mlp_tiles(): lax.dot_general(activated, reduce_all, (((1,), (1,)), ((), ())), preferre...]
    ppermute x16 -> x19, waiting for transfers between devices: 5.01 us -> 21.1 us  [exchange(): return lax.ppermute(value, axis, [(i, i ^ offset) for i in range(size)])]
    add x5 -> x0, local copies, waits for them, and re-layouts: 13.5 us -> none  [the longest x3 11 us: conv_bands(): summed + shifted[:, None, :, None] * kernel[row_off, col_off][None, :, No...]
    reduce_sum x10 -> x0, other arithmetic: 8.53 us -> none  [the longest x3 6.55 us: normalize(): mean_value = jnp.sum(values, axis=-1, keepdims=True) / D]
    all_gather x3 -> x2, blocking collectives: 19 us -> 10.8 us  [the longest x1 5.59 us: shards(): shared = lax.all_gather(shared, 'col', axis=0)]
    dynamic_update_slice x7 -> x0, local copies, waits for them, and re-layouts: 7.72 us -> none  [gather_rows(): lax.dynamic_update_index_in_dim(whole, pieces[offset], here ^ offset, 0)]
    mul x5 -> x0, local copies, waits for them, and re-layouts: 7.23 us -> none  [the longest x2 4.73 us: shards(): residual = tokens + term(2) * attn_sum.reshape(tiles_here, TILE, D)]
  transfers between devices with their start and end apart: 18 -> 20, of which waited for: 3 -> 7; matrix products, arithmetic and copies ran while one was open for 43% -> 8% of each run, Pallas kernels for 0% -> 19%
where the time goes in v2:
time: 103 us
  Pallas kernels  29.9 us (29%)
  starting transfers between devices  22.8 us (22%)
  waiting for transfers between devices  21.3 us (21%)
  local copies, waits for them, and re-layouts  14.2 us (14%)
  blocking collectives  10.8 us (10%)
  other arithmetic  2.53 us (2%)
    ppermute x19, waiting for transfers between devices, exchange(): return lax.ppermute(value, axis, [(i, i ^ offset) for i in range(size)])  21.1 us
    ppermute x19, starting transfers between devices, exchange(): return lax.ppermute(value, axis, [(i, i ^ offset) for i in range(size)])  17 us
    pallas_call x2, Pallas kernels, mlp(): call(functools.partial(mlp_kernel, near, piece_depth), outs, [SMEM] + [VM...  16.2 us
    unnamed x39, local copies, waits for them, and re-layouts  9.12 us
    pallas_call x1, Pallas kernels, shards(): call(attention_kernel, [shape((tokens_here, D), NARROW), shape((32, D), W...  8.82 us
    all_to_all x1, starting transfers between devices, shards(): adaptive = jnp.sum(lax.all_to_all(partial, 'row', 0, 0, tiled=True), axis=0)  5.83 us
    all_gather x1, blocking collectives, shards(): shared = lax.all_gather(shared, 'col', axis=0)  5.59 us
    all_gather x1, blocking collectives, shards(): noise = lax.all_gather(noise, 'col', axis=0)  5.19 us
  transfers between devices with their start and end apart: 20, of which 7 were waited for; matrix products, arithmetic and copies ran while one was open for 8% of the time, Pallas kernels for 19%

profile of v2, /device:TPU:0, one launch (start us, length us, event | category | flops | bytes accessed | tf_op | source)
XLA Modules:
  0.0 102.6 jit_solution(4264828156989889844)
XLA Ops:
  0.6 0.0 copy-start
  0.7 1.2 %copy.39.own = bf16[512,288]{1,0:T(8,128)(2,1)S(1)} copy(bf16[512,288]{0,1:T(8,128)(2,1)} %param.14) | data formatting | bytes 589824 | tf_op args[0]
  1.9 3.0 %collective-permute-start.1 = (bf16[512,288]{1,0:T(8,128)(2,1)S(1)}, bf16[512,288]{1,0:T(8,128)(2,1)}, u32[]{:S(2)}, u32[]{:S(2)}) collective-permute-start(bf16[512,288]{1,0:T(8,128)(2,1)S(1)} %copy.39.own), channel_id=1, source_target_pairs={{0,2},{1,3},{2,0},{3,1},{4,6},{5,7},{6,4},{7,5},{8,10},{9,11},{10,... | collective-permute-start | bytes 884744 | tf_op jit(solution)/shard_map/ppermute | solution.py:44
  4.9 1.0 %pad_maximum_fusion.refs_4_ = bf16[288,576]{1,0:T(8,128)(2,1)S(1)} fusion(bf16[144,576]{1,0:T(8,128)(2,1)} %bitcast.17, bf16[144,576]{1,0:T(8,128)(2,1)} %param.24), kind=kLoop, calls=%fused_computation.3 | loop fusion | flops 663552 | bytes 663552 | tf_op jit(solution)/shard_map/concatenate | solution.py:321
  6.0 2.7 %collective-permute-start.12 = (bf16[288,576]{1,0:T(8,128)(2,1)S(1)}, bf16[288,576]{1,0:T(8,128)(2,1)S(1)}, u32[]{:S(2)}, u32[]{:S(2)}) collective-permute-start(bf16[288,576]{1,0:T(8,128)(2,1)S(1)} %pad_maximum_fusion.refs_4_), channel_id=1, source_target_pairs={{0,16},{4,20},{8,24},{12,28},{16,0},{20,4},{24,8},{28,12},{1,17},{... | collective-permute-start | bytes 995336 | tf_op jit(solution)/shard_map/ppermute | solution.py:44
  8.6 0.0 collective-permute-start
  8.6 0.9 copy-done.9
  9.5 0.7 copy-done.11
  10.2 0.7 copy-done.13
  10.8 1.1 %shard_map.149 = bf16[16,144]{1,0:T(8,128)(2,1)S(1)} custom-call(s32[32]{0:T(128)S(1)} %copy-done.11, s32[32]{0:T(128)S(1)} %copy-done.13, bf16[50,1152]{1,0:T(8,128)(2,1)S(1)} %copy-done.9), custom_call_target="tpu_custom_call" | custom-call | flops 7151616 | bytes 115200 | tf_op jit(solution)/shard_map/pallas_call | solution.py:323
  11.9 2.2 %collective-permute-done.1.across = bf16[512,288]{1,0:T(8,128)(2,1)} collective-permute-done((bf16[512,288]{1,0:T(8,128)(2,1)S(1)}, bf16[512,288]{1,0:T(8,128)(2,1)}, u32[]{:S(2)}, u32[]{:S(2)}) %collective-permute-start.1) | collective-permute-done | bytes 294944 | tf_op jit(solution)/shard_map/ppermute | solution.py:44
  14.1 1.7 %collective-permute-start.7 = (bf16[288,1152]{1,0:T(8,128)(2,1)}, bf16[288,1152]{1,0:T(8,128)(2,1)S(1)}, u32[]{:S(2)}, u32[]{:S(2)}) collective-permute-start(bf16[288,1152]{1,0:T(8,128)(2,1)} %refs_0_.1), channel_id=1, source_target_pairs={{0,2},{1,3},{2,0},{3,1},{4,6},{5,7},{6,4},{7,5},{8,10},{9,11},{10,... | collective-permute-start | bytes 1990664 | tf_op jit(solution)/shard_map/ppermute | solution.py:44
  15.9 0.2 fusion
  16.1 0.1 reshape.16
  16.2 0.7 copy.36
  17.0 5.8 %all-to-all-start = ((f32[8,2,8,288]{3,1,2,0:T(2,128)}), f32[8,2,8,288]{3,1,2,0:T(2,128)S(1)}, u32[]{:S(2)}, u32[]{:S(2)}) async-start(f32[8,2,8,288]{3,1,2,0:T(2,128)} %copy.36), calls=%async_computation | async-start | bytes 393216 | tf_op jit(solution)/shard_map/all_to_all | solution.py:332
  22.8 2.0 %collective-permute-start.10 = (bf16[288,576]{1,0:T(8,128)(2,1)S(1)}, bf16[288,576]{1,0:T(8,128)(2,1)S(1)}, u32[]{:S(2)}, u32[]{:S(2)}) collective-permute-start(bf16[288,576]{1,0:T(8,128)(2,1)S(1)} %pad_maximum_fusion.refs_4_), channel_id=1, source_target_pairs={{0,8},{4,12},{8,0},{12,4},{16,24},{20,28},{24,16},{28,20},{1,9},{5... | collective-permute-start | bytes 995336 | tf_op jit(solution)/shard_map/ppermute | solution.py:44
  24.8 1.5 %collective-permute-start.9 = (bf16[288,576]{1,0:T(8,128)(2,1)S(1)}, bf16[288,576]{1,0:T(8,128)(2,1)}, u32[]{:S(2)}, u32[]{:S(2)}) collective-permute-start(bf16[288,576]{1,0:T(8,128)(2,1)S(1)} %pad_maximum_fusion.refs_4_), channel_id=1, source_target_pairs={{0,4},{4,0},{8,12},{12,8},{16,20},{20,16},{24,28},{28,24},{1,5},{5... | collective-permute-start | bytes 995336 | tf_op jit(solution)/shard_map/ppermute | solution.py:44
  26.3 0.0 collective-permute-start.2
  26.3 0.0 collective-permute-done.12.refs_8_
  26.3 0.7 collective-permute-start.14
  27.0 0.6 convert_bitcast_fusion
  27.6 4.1 %copy.40.weight_ref = bf16[1152,864]{1,0:T(8,128)(2,1)} copy(bf16[1152,864]{0,1:T(8,128)(2,1)} %bitcast.16) | data formatting | bytes 3981312 | tf_op jit(solution)/shard_map/reshape | solution.py:351
  31.8 0.2 all-to-all-done
  32.0 0.1 reduce_sum.9
  32.1 0.7 pad_maximum_fusion.1
  32.8 5.6 %all-gather = f32[128,288]{1,0:T(8,128)S(1)} all-gather(f32[32,288]{1,0:T(8,128)S(1)} %pad_maximum_fusion.1), channel_id=2, replica_groups=mesh['row'=8,'col'=4] {'col'}, dimensions={0}, use_global_device_ids=true | all-gather | bytes 184320 | tf_op jit(solution)/shard_map/all_gather | solution.py:334
  38.4 0.4 collective-permute-start.6
  38.8 1.2 %collective-permute-start.13 = (bf16[288,576]{1,0:T(8,128)(2,1)S(1)}, bf16[288,576]{1,0:T(8,128)(2,1)S(1)}, u32[]{:S(2)}, u32[]{:S(2)}) collective-permute-start(bf16[288,576]{1,0:T(8,128)(2,1)S(1)} %collective-permute-done.12.refs_8_), channel_id=1, source_target_pairs={{0,4},{4,0},{8,12},{12,8},{16,20},{20,16},{24,28},{28,24},{1,5},{5... | collective-permute-start | bytes 995336 | tf_op jit(solution)/shard_map/ppermute | solution.py:44
  40.0 0.0 collective-permute-done.2.diagonal
  40.0 0.8 collective-permute-start.11
  40.8 0.0 collective-permute-done.7.refs_2_
  40.8 0.0 collective-permute-start.8
  40.8 1.6 %copy-done.2 = bf16[1152,864]{1,0:T(8,128)(2,1)S(1)} copy-done((bf16[1152,864]{1,0:T(8,128)(2,1)S(1)}, bf16[1152,864]{1,0:T(8,128)(2,1)}, u32[]{:S(2)}) %copy-start.2) | copy-done | bytes 1990680
  42.4 1.0 copy-done.6
  43.4 8.8 %shard_map.150 = (bf16[512,1152]{1,0:T(8,128)(2,1)S(1)}, f32[32,1152]{1,0:T(8,128)S(1)}, bf16[512,288]{1,0:T(8,128)(2,1)S(1)}) custom-call(s32[32]{0:T(128)S(1)} %copy-done.12, bf16[512,288]{1,0:T(8,128)(2,1)S(1)} %copy-done.6, bf16[512,288]{1,0:T(8,128)(2,1)} %collective-permute-done.beside, bf16[512,288]{1,0:T(8,128)(2,1)} %collective-permute-done.1.across, ...), custom_call_target="tpu_custom_call" | custom-call | flops 1321205760 | bytes 5242880 | tf_op jit(solution)/shard_map/pallas_call | solution.py:344
  52.2 0.0 collective-permute-done.14.refs_10_
  52.2 0.6 collective-permute-start.4
  52.8 0.0 collective-permute-done.13.refs_9_
  52.8 1.2 %collective-permute-start.15 = (bf16[288,576]{1,0:T(8,128)(2,1)}, bf16[288,576]{1,0:T(8,128)(2,1)S(1)}, u32[]{:S(2)}, u32[]{:S(2)}) collective-permute-start(bf16[288,576]{1,0:T(8,128)(2,1)} %collective-permute-done.14.refs_10_), channel_id=1, source_target_pairs={{0,4},{4,0},{8,12},{12,8},{16,20},{20,16},{24,28},{28,24},{1,5},{5... | collective-permute-start | bytes 995336 | tf_op jit(solution)/shard_map/ppermute | solution.py:44
  54.0 4.1 %collective-permute-done.11.refs_7_ = bf16[288,576]{1,0:T(8,128)(2,1)S(1)} collective-permute-done((bf16[288,576]{1,0:T(8,128)(2,1)S(1)}, bf16[288,576]{1,0:T(8,128)(2,1)S(1)}, u32[]{:S(2)}, u32[]{:S(2)}) %collective-permute-start.11) | collective-permute-done | bytes 331808 | tf_op jit(solution)/shard_map/ppermute | solution.py:44
  58.1 5.7 %collective-permute-done.4.att_across = bf16[512,288]{1,0:T(8,128)(2,1)S(1)} collective-permute-done((bf16[512,288]{1,0:T(8,128)(2,1)S(1)}, bf16[512,288]{1,0:T(8,128)(2,1)S(1)}, u32[]{:S(2)}, u32[]{:S(2)}) %collective-permute-start.4) | collective-permute-done | bytes 294944 | tf_op jit(solution)/shard_map/ppermute | solution.py:44
  63.8 1.4 %collective-permute-done.15.refs_11_ = bf16[288,576]{1,0:T(8,128)(2,1)S(1)} collective-permute-done((bf16[288,576]{1,0:T(8,128)(2,1)}, bf16[288,576]{1,0:T(8,128)(2,1)S(1)}, u32[]{:S(2)}, u32[]{:S(2)}) %collective-permute-start.15) | collective-permute-done | bytes 331808 | tf_op jit(solution)/shard_map/ppermute | solution.py:44
  65.2 0.3 collective-permute-done.5.att_diagonal
  65.5 0.0 collective-permute-done.8.refs_3_
  65.5 7.8 %shard_map.152 = (f32[128,1152]{1,0:T(8,128)S(1)}, bf16[128,1152]{1,0:T(8,128)(2,1)S(1)}) custom-call(s32[32]{0:T(128)S(1)} %copy-done.12, bf16[512,288]{1,0:T(8,128)(2,1)S(1)} %get-tuple-element.11.att_own, bf16[512,288]{1,0:T(8,128)(2,1)S(1)} %collective-permute-done.3.att_beside, bf16[512,288]{1,0:T(8,128)(2,1)S(1)} %collective-permute-done.4.att_across, ...), custom_call_target="tpu_custom_call" | custom-call | flops 1358954496 | bytes 8388608 | tf_op jit(solution)/shard_map/pallas_call | solution.py:359
  73.3 0.0 copy-start.17
  73.3 0.2 collective-permute-start.17
  73.5 8.4 %shard_map.151 = (f32[128,1152]{1,0:T(8,128)S(1)}, bf16[128,1152]{1,0:T(8,128)(2,1)}, bf16[128,1152]{1,0:T(8,128)(2,1)S(1)}) custom-call(s32[32]{0:T(128)S(1)} %copy-done.12, bf16[512,288]{1,0:T(8,128)(2,1)S(1)} %get-tuple-element.11.att_own, bf16[512,288]{1,0:T(8,128)(2,1)S(1)} %collective-permute-done.3.att_beside, ...), custom_call_target="tpu_custom_call" | custom-call | flops 1358954496 | bytes 8388608 | tf_op jit(solution)/shard_map/pallas_call | solution.py:359
  81.9 0.8 copy-done.3
  82.7 0.0 copy-start.16
  82.8 0.4 collective-permute-start.16
  83.2 0.0 collective-permute-done.17
  83.2 0.1 add_convert_fusion
  83.3 0.2 copy-done.7
  83.4 0.6 collective-permute-start.18
  84.0 0.1 reshape.19.kernel_ref
  84.1 1.2 %shard_map.154.bands_ref = f32[128,384]{1,0:T(8,128)S(1)} custom-call(f32[144]{0:T(256)S(1)} %reshape.19.kernel_ref), custom_call_target="tpu_custom_call" | custom-call | flops 100000000 | bytes 196608 | tf_op jit(solution)/shard_map/pallas_call | solution.py:340
  85.3 7.4 %collective-permute-done.18.crossed_ref = bf16[128,1152]{1,0:T(8,128)(2,1)S(1)} collective-permute-done((bf16[128,1152]{1,0:T(8,128)(2,1)S(1)}, bf16[128,1152]{1,0:T(8,128)(2,1)S(1)}, u32[]{:S(2)}, u32[]{:S(2)}) %collective-permute-start.18) | collective-permute-done | bytes 294944 | tf_op jit(solution)/shard_map/ppermute | solution.py:44
  92.7 1.1 %copy-done.4 = f32[128,1152]{1,0:T(8,128)S(1)} copy-done((f32[128,1152]{1,0:T(8,128)S(1)}, f32[128,1152]{1,0:T(8,128)}, u32[]{:S(2)}) %copy-start.4) | copy-done | bytes 589848
  93.8 1.0 copy-done.8
  94.8 1.1 %shard_map.153 = f32[8,256]{1,0:T(8,128)S(1)} custom-call(s32[32]{0:T(128)S(1)} %copy-done.12, f32[128,1152]{1,0:T(8,128)S(1)} %copy-done.4, bf16[128,1152]{1,0:T(8,128)(2,1)S(1)} %collective-permute-done.16.beside_ref, bf16[128,1152]{1,0:T(8,128)(2,1)S(1)} %collective-permute-done.18.crossed_ref, bf16[128,1152]{1,0:T(8,128)(2,1)S(1)} %copy-done.8, ...), custom_call_target="tpu_custom_call" | custom-call | flops 75497472 | bytes 2097152 | tf_op jit(solution)/shard_map/pallas_call | solution.py:380
  95.9 5.2 %all-gather.1 = f32[32,256]{1,0:T(8,128)S(1)} all-gather(f32[8,256]{1,0:T(8,128)S(1)} %shard_map.153), channel_id=3, replica_groups=mesh['row'=8,'col'=4] {'col'}, dimensions={0}, use_global_device_ids=true | all-gather | bytes 40960 | tf_op jit(solution)/shard_map/all_gather | solution.py:386
  101.1 1.5 %shard_map.155 = (bf16[64,128]{1,0:T(8,128)(2,1)}, bf16[64,128]{1,0:T(8,128)(2,1)}) custom-call(s32[32]{0:T(128)S(1)} %copy-done.12, s32[32]{0:T(128)S(1)} %copy-done.14, f32[50]{0:T(128)S(1)} %copy-done.15, f32[50]{0:T(128)S(1)} %copy-done.16, f32[4,8,256]{2,1,0:T(8,128)S(1)} %bitcast.15, bf16[64,128]{1,0:T(8,128)(2,1)S(1)} %copy-done.10, ...), custom_call_target="tpu_custom_call" | custom-call | flops 12582912 | bytes 524288 | tf_op jit(solution)/shard_map/pallas_call | solution.py:389
  (35 shorter events, 0.1 us)
Async XLA Ops:
  0.6 15.3 %copy-start = (bf16[144,8,288]{2,1,0:T(8,128)(2,1)S(1)}, bf16[144,8,288]{2,1,0:T(8,128)(2,1)}, u32[]{:S(2)}) copy-start(bf16[144,8,288]{2,1,0:T(8,128)(2,1)} %param.21) | copy-start | bytes 1990660
  0.6 26.4 %copy-start.18 = (bf16[288,16]{0,1:T(8,128)(2,1)S(1)}, bf16[288,16]{0,1:T(8,128)(2,1)}, u32[]{:S(2)}) copy-start(bf16[288,16]{0,1:T(8,128)(2,1)} %param.26) | copy-start | bytes 27652
  1.9 25.7 %copy-start.5 = (bf16[512,288]{1,0:T(8,128)(2,1)}, bf16[512,288]{1,0:T(8,128)(2,1)S(1)}, u32[]{:S(2)}) copy-start(bf16[512,288]{1,0:T(8,128)(2,1)S(1)} %copy.39.own) | copy-start | bytes 884740
  1.9 12.2 %collective-permute-start.1 = (bf16[512,288]{1,0:T(8,128)(2,1)S(1)}, bf16[512,288]{1,0:T(8,128)(2,1)}, u32[]{:S(2)}, u32[]{:S(2)}) collective-permute-start(bf16[512,288]{1,0:T(8,128)(2,1)S(1)} %copy.39.own), channel_id=1, source_target_pairs={{0,2},{1,3},{2,0},{3,1},{4,6},{5,7},{6,4},{7,5},{8,10},{9,11},{10,... | collective-permute-start | bytes 884744 | tf_op jit(solution)/shard_map/ppermute | solution.py:44
  6.0 20.3 %collective-permute-start.12 = (bf16[288,576]{1,0:T(8,128)(2,1)S(1)}, bf16[288,576]{1,0:T(8,128)(2,1)S(1)}, u32[]{:S(2)}, u32[]{:S(2)}) collective-permute-start(bf16[288,576]{1,0:T(8,128)(2,1)S(1)} %pad_maximum_fusion.refs_4_), channel_id=1, source_target_pairs={{0,16},{4,20},{8,24},{12,28},{16,0},{20,4},{24,8},{28,12},{1,17},{... | collective-permute-start | bytes 995336 | tf_op jit(solution)/shard_map/ppermute | solution.py:44
  8.6 17.7 %collective-permute-start = (bf16[512,288]{1,0:T(8,128)(2,1)S(1)}, bf16[512,288]{1,0:T(8,128)(2,1)}, u32[]{:S(2)}, u32[]{:S(2)}) collective-permute-start(bf16[512,288]{1,0:T(8,128)(2,1)S(1)} %copy.39.own), channel_id=1, source_target_pairs={{0,1},{1,0},{2,3},{3,2},{4,5},{5,4},{6,7},{7,6},{8,9},{9,8},{10,11... | collective-permute-start | bytes 884744 | tf_op jit(solution)/shard_map/ppermute | solution.py:44
  8.6 0.9 copy-start.9
  9.5 0.7 copy-start.11
  10.2 0.7 copy-start.13
  14.1 26.7 %collective-permute-start.7 = (bf16[288,1152]{1,0:T(8,128)(2,1)}, bf16[288,1152]{1,0:T(8,128)(2,1)S(1)}, u32[]{:S(2)}, u32[]{:S(2)}) collective-permute-start(bf16[288,1152]{1,0:T(8,128)(2,1)} %refs_0_.1), channel_id=1, source_target_pairs={{0,2},{1,3},{2,0},{3,1},{4,6},{5,7},{6,4},{7,5},{8,10},{9,11},{10,... | collective-permute-start | bytes 1990664 | tf_op jit(solution)/shard_map/ppermute | solution.py:44
  17.0 15.0 %all-to-all-start = ((f32[8,2,8,288]{3,1,2,0:T(2,128)}), f32[8,2,8,288]{3,1,2,0:T(2,128)S(1)}, u32[]{:S(2)}, u32[]{:S(2)}) async-start(f32[8,2,8,288]{3,1,2,0:T(2,128)} %copy.36), calls=%async_computation | async-start | bytes 393216 | tf_op jit(solution)/shard_map/all_to_all | solution.py:332
  22.8 15.6 %collective-permute-start.10 = (bf16[288,576]{1,0:T(8,128)(2,1)S(1)}, bf16[288,576]{1,0:T(8,128)(2,1)S(1)}, u32[]{:S(2)}, u32[]{:S(2)}) collective-permute-start(bf16[288,576]{1,0:T(8,128)(2,1)S(1)} %pad_maximum_fusion.refs_4_), channel_id=1, source_target_pairs={{0,8},{4,12},{8,0},{12,4},{16,24},{20,28},{24,16},{28,20},{1,9},{5... | collective-permute-start | bytes 995336 | tf_op jit(solution)/shard_map/ppermute | solution.py:44
  24.8 14.0 %collective-permute-start.9 = (bf16[288,576]{1,0:T(8,128)(2,1)S(1)}, bf16[288,576]{1,0:T(8,128)(2,1)}, u32[]{:S(2)}, u32[]{:S(2)}) collective-permute-start(bf16[288,576]{1,0:T(8,128)(2,1)S(1)} %pad_maximum_fusion.refs_4_), channel_id=1, source_target_pairs={{0,4},{4,0},{8,12},{12,8},{16,20},{20,16},{24,28},{28,24},{1,5},{5... | collective-permute-start | bytes 995336 | tf_op jit(solution)/shard_map/ppermute | solution.py:44
  26.3 13.7 %collective-permute-start.2 = (bf16[512,288]{1,0:T(8,128)(2,1)}, bf16[512,288]{1,0:T(8,128)(2,1)}, u32[]{:S(2)}, u32[]{:S(2)}) collective-permute-start(bf16[512,288]{1,0:T(8,128)(2,1)} %collective-permute-done.1.across), channel_id=1, source_target_pairs={{0,1},{1,0},{2,3},{3,2},{4,5},{5,4},{6,7},{7,6},{8,9},{9,8},{10,11... | collective-permute-start | bytes 884744 | tf_op jit(solution)/shard_map/ppermute | solution.py:44
  26.3 25.9 %collective-permute-start.14 = (bf16[288,576]{1,0:T(8,128)(2,1)S(1)}, bf16[288,576]{1,0:T(8,128)(2,1)}, u32[]{:S(2)}, u32[]{:S(2)}) collective-permute-start(bf16[288,576]{1,0:T(8,128)(2,1)S(1)} %collective-permute-done.12.refs_8_), channel_id=1, source_target_pairs={{0,8},{4,12},{8,0},{12,4},{16,24},{20,28},{24,16},{28,20},{1,9},{5... | collective-permute-start | bytes 995336 | tf_op jit(solution)/shard_map/ppermute | solution.py:44
  27.6 10.8 %copy-start.1 = (bf16[288,1152]{1,0:T(8,128)(2,1)S(1)}, bf16[288,1152]{1,0:T(8,128)(2,1)}, u32[]{:S(2)}) copy-start(bf16[288,1152]{1,0:T(8,128)(2,1)} %refs_0_.1) | copy-start | bytes 1990660
  27.6 13.2 %copy-start.12 = (s32[32]{0:T(128)S(1)}, s32[32]{0:T(128)}, u32[]{:S(2)}) copy-start(s32[32]{0:T(128)} %latent_ref.11) | copy-start | bytes 388
  38.4 25.4 %collective-permute-start.6 = (bf16[288,1152]{1,0:T(8,128)(2,1)S(1)}, bf16[288,1152]{1,0:T(8,128)(2,1)S(1)}, u32[]{:S(2)}, u32[]{:S(2)}) collective-permute-start(bf16[288,1152]{1,0:T(8,128)(2,1)S(1)} %copy-done.1), channel_id=1, source_target_pairs={{0,1},{1,0},{2,3},{3,2},{4,5},{5,4},{6,7},{7,6},{8,9},{9,8},{10,11... | collective-permute-start | bytes 1990664 | tf_op jit(solution)/shard_map/ppermute | solution.py:44
  38.8 14.0 %collective-permute-start.13 = (bf16[288,576]{1,0:T(8,128)(2,1)S(1)}, bf16[288,576]{1,0:T(8,128)(2,1)S(1)}, u32[]{:S(2)}, u32[]{:S(2)}) collective-permute-start(bf16[288,576]{1,0:T(8,128)(2,1)S(1)} %collective-permute-done.12.refs_8_), channel_id=1, source_target_pairs={{0,4},{4,0},{8,12},{12,8},{16,20},{20,16},{24,28},{28,24},{1,5},{5... | collective-permute-start | bytes 995336 | tf_op jit(solution)/shard_map/ppermute | solution.py:44
  40.0 18.1 %collective-permute-start.11 = (bf16[288,576]{1,0:T(8,128)(2,1)S(1)}, bf16[288,576]{1,0:T(8,128)(2,1)S(1)}, u32[]{:S(2)}, u32[]{:S(2)}) collective-permute-start(bf16[288,576]{1,0:T(8,128)(2,1)S(1)} %collective-permute-done.10.refs_6_), channel_id=1, source_target_pairs={{0,4},{4,0},{8,12},{12,8},{16,20},{20,16},{24,28},{28,24},{1,5},{5... | collective-permute-start | bytes 995336 | tf_op jit(solution)/shard_map/ppermute | solution.py:44
  40.8 24.7 %collective-permute-start.8 = (bf16[288,1152]{1,0:T(8,128)(2,1)S(1)}, bf16[288,1152]{1,0:T(8,128)(2,1)S(1)}, u32[]{:S(2)}, u32[]{:S(2)}) collective-permute-start(bf16[288,1152]{1,0:T(8,128)(2,1)S(1)} %collective-permute-done.7.refs_2_), channel_id=1, source_target_pairs={{0,1},{1,0},{2,3},{3,2},{4,5},{5,4},{6,7},{7,6},{8,9},{9,8},{10,11... | collective-permute-start | bytes 1990664 | tf_op jit(solution)/shard_map/ppermute | solution.py:44
  40.8 1.6 %copy-start.2 = (bf16[1152,864]{1,0:T(8,128)(2,1)S(1)}, bf16[1152,864]{1,0:T(8,128)(2,1)}, u32[]{:S(2)}) copy-start(bf16[1152,864]{1,0:T(8,128)(2,1)} %copy.40.weight_ref) | copy-start | bytes 5971972
  42.4 1.0 copy-start.6
  52.2 11.6 %collective-permute-start.4 = (bf16[512,288]{1,0:T(8,128)(2,1)S(1)}, bf16[512,288]{1,0:T(8,128)(2,1)S(1)}, u32[]{:S(2)}, u32[]{:S(2)}) collective-permute-start(bf16[512,288]{1,0:T(8,128)(2,1)S(1)} %get-tuple-element.11.att_own), channel_id=1, source_target_pairs={{0,2},{1,3},{2,0},{3,1},{4,6},{5,7},{6,4},{7,5},{8,10},{9,11},{10,... | collective-permute-start | bytes 884744 | tf_op jit(solution)/shard_map/ppermute | solution.py:44
  52.8 12.4 %collective-permute-start.15 = (bf16[288,576]{1,0:T(8,128)(2,1)}, bf16[288,576]{1,0:T(8,128)(2,1)S(1)}, u32[]{:S(2)}, u32[]{:S(2)}) collective-permute-start(bf16[288,576]{1,0:T(8,128)(2,1)} %collective-permute-done.14.refs_10_), channel_id=1, source_target_pairs={{0,4},{4,0},{8,12},{12,8},{16,20},{20,16},{24,28},{28,24},{1,5},{5... | collective-permute-start | bytes 995336 | tf_op jit(solution)/shard_map/ppermute | solution.py:44
  58.1 5.7 %collective-permute-start.3 = (bf16[512,288]{1,0:T(8,128)(2,1)S(1)}, bf16[512,288]{1,0:T(8,128)(2,1)S(1)}, u32[]{:S(2)}, u32[]{:S(2)}) collective-permute-start(bf16[512,288]{1,0:T(8,128)(2,1)S(1)} %get-tuple-element.11.att_own), channel_id=1, source_target_pairs={{0,1},{1,0},{2,3},{3,2},{4,5},{5,4},{6,7},{7,6},{8,9},{9,8},{10,11... | collective-permute-start | bytes 884744 | tf_op jit(solution)/shard_map/ppermute | solution.py:44
  63.8 1.7 %collective-permute-start.5 = (bf16[512,288]{1,0:T(8,128)(2,1)S(1)}, bf16[512,288]{1,0:T(8,128)(2,1)S(1)}, u32[]{:S(2)}, u32[]{:S(2)}) collective-permute-start(bf16[512,288]{1,0:T(8,128)(2,1)S(1)} %collective-permute-done.4.att_across), channel_id=1, source_target_pairs={{0,1},{1,0},{2,3},{3,2},{4,5},{5,4},{6,7},{7,6},{8,9},{9,8},{10,11... | collective-permute-start | bytes 884744 | tf_op jit(solution)/shard_map/ppermute | solution.py:44
  73.3 10.7 %copy-start.17 = (f32[3,3,4,4]{3,2,1,0:T(4,128)S(1)}, f32[3,3,4,4]{3,2,1,0:T(4,128)}, u32[]{:S(2)}) copy-start(f32[3,3,4,4]{3,2,1,0:T(4,128)} %param.27) | copy-start | bytes 1732
  73.3 9.9 %collective-permute-start.17 = (bf16[128,1152]{1,0:T(8,128)(2,1)S(1)}, bf16[128,1152]{1,0:T(8,128)(2,1)S(1)}, u32[]{:S(2)}, u32[]{:S(2)}) collective-permute-start(bf16[128,1152]{1,0:T(8,128)(2,1)S(1)} %get-tuple-element.18), channel_id=1, source_target_pairs={{0,1},{1,0},{2,3},{3,2},{4,5},{5,4},{6,7},{7,6},{8,9},{9,8},{10,11... | collective-permute-start | bytes 884744 | tf_op jit(solution)/shard_map/ppermute | solution.py:44
  81.9 0.8 copy-start.3
  82.7 0.7 copy-start.7
  82.7 18.4 %copy-start.10 = (bf16[64,128]{1,0:T(8,128)(2,1)S(1)}, bf16[64,128]{1,0:T(8,128)(2,1)}, u32[]{:S(2)}) copy-start(bf16[64,128]{1,0:T(8,128)(2,1)} %noisy_ref.1) | copy-start | bytes 49156
  82.7 18.4 %copy-start.14 = (s32[32]{0:T(128)S(1)}, s32[32]{0:T(128)}, u32[]{:S(2)}) copy-start(s32[32]{0:T(128)} %steps_ref.3) | copy-start | bytes 388
  82.7 18.4 %copy-start.15 = (f32[50]{0:T(128)S(1)}, f32[50]{0:T(128)}, u32[]{:S(2)}) copy-start(f32[50]{0:T(128)} %now_ref.1) | copy-start | bytes 604
  82.7 18.4 %copy-start.16 = (f32[50]{0:T(128)S(1)}, f32[50]{0:T(128)}, u32[]{:S(2)}) copy-start(f32[50]{0:T(128)} %next_ref.1) | copy-start | bytes 604
  82.8 2.6 %collective-permute-start.16 = (bf16[128,1152]{1,0:T(8,128)(2,1)}, bf16[128,1152]{1,0:T(8,128)(2,1)S(1)}, u32[]{:S(2)}, u32[]{:S(2)}) collective-permute-start(bf16[128,1152]{1,0:T(8,128)(2,1)} %get-tuple-element.16), channel_id=1, source_target_pairs={{0,1},{1,0},{2,3},{3,2},{4,5},{5,4},{6,7},{7,6},{8,9},{9,8},{10,11... | collective-permute-start | bytes 884744 | tf_op jit(solution)/shard_map/ppermute | solution.py:44
  83.4 9.3 %collective-permute-start.18 = (bf16[128,1152]{1,0:T(8,128)(2,1)S(1)}, bf16[128,1152]{1,0:T(8,128)(2,1)S(1)}, u32[]{:S(2)}, u32[]{:S(2)}) collective-permute-start(bf16[128,1152]{1,0:T(8,128)(2,1)S(1)} %add_convert_fusion), channel_id=1, source_target_pairs={{0,2},{1,3},{2,0},{3,1},{4,6},{5,7},{6,4},{7,5},{8,10},{9,11},{10,... | collective-permute-start | bytes 884744 | tf_op jit(solution)/shard_map/ppermute | solution.py:44
  92.7 1.1 %copy-start.4 = (f32[128,1152]{1,0:T(8,128)S(1)}, f32[128,1152]{1,0:T(8,128)}, u32[]{:S(2)}) copy-start(f32[128,1152]{1,0:T(8,128)} %copy-done.3) | copy-start | bytes 1769476
  93.8 1.0 copy-start.8

commit v3 on v2

v3 whole, which is shorter than its diff:
```python
import functools

import jax
import jax.numpy as jnp
from jax import lax
from jax.experimental import pallas as pl
from jax.experimental.pallas import tpu as pltpu
from jax.sharding import PartitionSpec as P

D = 1152
HEAD_DIM = 72
PATCH = 2
CHANNELS = 4
GRIDW = 16
TILE_ROWS = 8
STEPS = 50
TILE = 128
EPS_NORM = 1e-06
IMG_ROWS = TILE_ROWS * PATCH
IMG_WIDTH = GRIDW * PATCH * CHANNELS
WIDE = jnp.float32
NARROW = jnp.bfloat16
NT = (((1,), (1,)), ((), ()))
VMEM = pl.BlockSpec(memory_space=pltpu.VMEM)
SMEM = pl.BlockSpec(memory_space=pltpu.SMEM)
ANYWHERE = pl.BlockSpec(memory_space=pl.ANY)
MIB = 1024 * 1024


def call(kernel, outs, in_specs, scratch=(), flops=0, nbytes=0, trans=0, limit=4):
    return pl.pallas_call(
        kernel,
        out_shape=outs,
        in_specs=in_specs,
        out_specs=jax.tree.map(lambda _: VMEM, outs),
        scratch_shapes=list(scratch),
        compiler_params=pltpu.CompilerParams(vmem_limit_bytes=limit * MIB),
        cost_estimate=pl.CostEstimate(flops=flops, bytes_accessed=nbytes, transcendentals=trans),
    )


def exchange(value, axis, offset):
    size = lax.axis_size(axis)
    return lax.ppermute(value, axis, [(i, i ^ offset) for i in range(size)])


def gather_blocks(value):
    across = exchange(value, "col", 2)
    beside = exchange(value, "col", 1)
    diagonal = exchange(across, "col", 1)
    return value, beside, across, diagonal


def gather_late(value, late):
    across = exchange(value, "col", 2)
    value, across = after((value, across), late)
    return value, exchange(value, "col", 1), across, exchange(across, "col", 1)


def after(value, *others):
    return lax.optimization_barrier((value, *others))[0]


def gather_rows(expand, reduce):
    if lax.axis_size("row") != 8:
        return [[lax.all_gather(part, "row", axis=0, tiled=True) for part in (expand, reduce)]]
    pieces = {0: jnp.concatenate([expand, reduce], axis=0)}
    for offset, source, step in ((4, 0, 4), (2, 0, 2), (1, 0, 1), (6, 4, 2), (3, 2, 1), (5, 4, 1), (7, 6, 1)):
        pieces[offset] = exchange(pieces[source], "row", step)
    return [[pieces[offset]] for offset in range(8)]


def normalize(values, shift_term, scale_term):
    mean_value = jnp.sum(values, axis=-1, keepdims=True) * (1.0 / D)
    spread = jnp.sum(values * values, axis=-1, keepdims=True) * (1.0 / D) - mean_value * mean_value
    normed = (values - mean_value) * lax.rsqrt(spread + EPS_NORM)
    return normed * (1.0 + scale_term) + shift_term


def condition_kernel(tiles_here, latent_ref, steps_ref, embedding_ref, out_ref, onehot):
    count, depth = out_ref.shape

    def pick(index, carry):
        tile = (index // 2) * tiles_here + (index % 2) * (tiles_here - 1)
        step = steps_ref[latent_ref[tile]]
        lanes = lax.broadcasted_iota(jnp.int32, (1, STEPS), 1)
        onehot[pl.ds(index, 1), :] = jnp.where(lanes == step, 1.0, 0.0)
        return carry

    lax.fori_loop(0, count, pick, 0)
    embedded = jnp.dot(onehot[...].astype(NARROW), embedding_ref[...], preferred_element_type=WIDE)
    conditioning = (embedded / (1.0 + jnp.exp(-embedded))).astype(NARROW)
    first = lax.axis_index("row") * depth
    source = lax.broadcasted_iota(jnp.int32, (D, depth), 0)
    target = lax.broadcasted_iota(jnp.int32, (D, depth), 1) + first
    chosen = jnp.where(source == target, 1.0, 0.0).astype(NARROW)
    out_ref[...] = jnp.dot(conditioning, chosen, preferred_element_type=WIDE).astype(NARROW)


def tile_term(latent_ref, terms_ref, index, tile):
    first = lax.axis_index("row") * (lax.axis_size("col"))
    later = latent_ref[first + tile] != latent_ref[first]
    return jnp.where(later, terms_ref[8 + index : 9 + index, :], terms_ref[index : index + 1, :])


def tokens_kernel(own, beside, across, diagonal, kernel_ref, tokens_ref, bands_ref):
    col = lax.axis_index("col")
    width = own.shape[0]
    for place in range(4):

        @pl.when(col == place)
        def _():
            for offset, block in enumerate((own, beside, across, diagonal)):
                lower = (place ^ offset) * width
                tokens_ref[:, lower : lower + width] = block[...].T

    fill_bands(kernel_ref, bands_ref)


def attention_kernel(
    latent_ref, tokens_ref, terms_own, terms_beside, terms_across, terms_diagonal, weight_ref,
    terms_ref, attended_ref, weight, weight_sem, normed, triple, mixed,
):
    fetch = pltpu.make_async_copy(weight_ref, weight, weight_sem)
    fetch.start()
    col = lax.axis_index("col")
    row = lax.axis_index("row")
    width = terms_own.shape[1]
    tiles = tokens_ref.shape[0] // TILE
    for place in range(4):

        @pl.when(col == place)
        def _():
            for offset, block in enumerate((terms_own, terms_beside, terms_across, terms_diagonal)):
                lower = (place ^ offset) * width
                terms_ref[:, lower : lower + width] = block[...]

    for tile in range(tiles):
        here = slice(tile * TILE, (tile + 1) * TILE)
        shift = tile_term(latent_ref, terms_ref, 0, tile)
        scale = tile_term(latent_ref, terms_ref, 1, tile)
        normed[here, :] = normalize(tokens_ref[here, :].astype(WIDE), shift, scale).astype(NARROW)
    fetch.wait()
    triple[...] = lax.dot_general(weight[...], normed[...], NT, preferred_element_type=WIDE)
    latents = [latent_ref[row * tiles + tile] for tile in range(tiles)]
    factor = HEAD_DIM ** (-0.5) * 1.4426950408889634
    pair = 2
    for head in range(width // HEAD_DIM):
        lower = head * HEAD_DIM
        queries = triple[lower : lower + HEAD_DIM, :].astype(NARROW)
        keys = triple[width + lower : width + lower + HEAD_DIM, :].T.astype(NARROW)
        values = triple[2 * width + lower : 2 * width + lower + HEAD_DIM, :]
        values = jnp.concatenate([values, jnp.ones((8, values.shape[1]), WIDE)]).astype(NARROW)
        for first in range(0, tiles, pair):
            here = slice(first * TILE, (first + pair) * TILE)
            scores = jnp.dot(keys, queries[:, here], preferred_element_type=WIDE)
            columns = []
            for tile in range(first, first + pair):
                lanes = slice((tile - first) * TILE, (tile - first + 1) * TILE)
                blocks = [
                    scores[other * TILE : (other + 1) * TILE, lanes]
                    + jnp.where(latents[other] == latents[tile], 0.0, -1e30)
                    for other in range(tiles)
                ]
                peak = functools.reduce(jnp.maximum, blocks)
                peak = jnp.max(peak, axis=0, keepdims=True)
                raised = [jnp.exp2((block - peak) * factor).astype(NARROW) for block in blocks]
                columns.append(jnp.concatenate(raised, axis=0))
            summed = jnp.dot(values, jnp.concatenate(columns, axis=1), preferred_element_type=WIDE)
            mixed[lower : lower + HEAD_DIM, here] = summed[:HEAD_DIM] / summed[HEAD_DIM : HEAD_DIM + 1]
    attended_ref[...] = mixed[...].T.astype(NARROW)


def stack_kernel(*refs):
    width = refs[0].shape[0]
    for offset, block in enumerate(refs[:-1]):
        refs[-1][offset * width : (offset + 1) * width, :] = block[...]


def weights_kernel(counts, depth, *refs):
    pieces, (expand, reduce) = list(refs[:-2]), refs[-2:]
    row = lax.axis_index("row")
    for offset, count in enumerate(counts):
        start = pl.multiple_of((row ^ offset) * depth, 16) if len(counts) > 1 else 0
        here = pl.ds(start, depth)
        if count == 1:
            both = pieces.pop(0)
            expand[here, :] = both[:depth, :]
            reduce[here, :] = both[depth:, :]
        else:
            expand[here, :] = pieces.pop(0)[...]
            reduce[here, :] = pieces.pop(0)[...]


def shared_kernel(parts_ref, head_ref, out_ref):
    count = parts_ref.shape[1]
    out_ref[:count, :] = jnp.sum(parts_ref[...], axis=0)
    out_ref[count:, :] = head_ref[...].astype(WIDE)


def mlp_kernel(
    near, latent_ref, att_own, att_beside, att_across, att_diagonal, tokens_ref, terms_ref, out_weight, expand, reduce, *refs
):
    outs, (attended, mid) = refs[:-2], refs[-2:]
    col = lax.axis_index("col")
    width = att_own.shape[1]
    tile_list = [col ^ offset for offset in ((0, 1) if near else (2, 3))]
    starts = [pl.multiple_of(tile * TILE, TILE) for tile in tile_list]
    for offset, block in enumerate((att_own, att_beside, att_across, att_diagonal)):
        for slot, start in enumerate(starts):
            here = slice(slot * TILE, (slot + 1) * TILE)
            attended[here, offset * width : (offset + 1) * width] = block[pl.ds(start, TILE), :]
    attn_sum = jnp.dot(attended[...], out_weight[...], preferred_element_type=WIDE)
    for slot, tile in enumerate(tile_list):
        term = functools.partial(tile_term, latent_ref, terms_ref, tile=tile)
        here = slice(slot * TILE, (slot + 1) * TILE)
        before = tokens_ref[pl.ds(starts[slot], TILE), :].astype(WIDE)
        residual = (before + term(2) * attn_sum[here]).astype(NARROW)
        if near and slot == 0:
            outs[2][...] = residual
        mid[here, :] = normalize(residual.astype(WIDE), term(3), term(4)).astype(NARROW)
    units = jnp.dot(mid[...], expand[...], preferred_element_type=WIDE)
    inner = 0.7978845608028654 * (units + 0.044715 * (units * units * units))
    activated = (0.5 * units * (1.0 + jnp.tanh(inner))).astype(NARROW)
    summed = lax.dot_general(activated, reduce[...], NT, preferred_element_type=WIDE)
    outs[0][...] = summed[:TILE]
    outs[1][...] = summed[TILE:].astype(NARROW)


def head_kernel(latent_ref, kept_ref, beside_ref, crossed_ref, residual_ref, terms_ref, out_ref):
    col = lax.axis_index("col")
    term = functools.partial(tile_term, latent_ref, terms_ref, tile=col)
    mlp_sum = kept_ref[...] + beside_ref[...].astype(WIDE) + crossed_ref[...].astype(WIDE)
    second = (residual_ref[...].astype(WIDE) + term(5) * mlp_sum).astype(NARROW).astype(WIDE)
    normed = normalize(second, term(6), term(7)).astype(NARROW)
    group = PATCH * CHANNELS
    token_place = lax.broadcasted_iota(jnp.int32, (TILE, IMG_WIDTH), 0) % GRIDW
    lane_place = lax.broadcasted_iota(jnp.int32, (TILE, IMG_WIDTH), 1) // group
    for dy in range(PATCH):
        rows = terms_ref[16 + dy * group : 16 + (dy + 1) * group, :].astype(NARROW)
        spread_rows = jnp.concatenate([rows.astype(WIDE)] * GRIDW, axis=0).astype(NARROW)
        noise = lax.dot_general(normed, spread_rows, NT, preferred_element_type=WIDE)
        noise = jnp.where(token_place == lane_place, noise, 0.0)
        folded = jnp.sum(noise.reshape(TILE_ROWS, GRIDW, IMG_WIDTH), axis=1)
        out_ref[:, dy * IMG_WIDTH : (dy + 1) * IMG_WIDTH] = folded


def fill_bands(kernel_ref, out_ref):
    shape = (IMG_WIDTH, IMG_WIDTH)
    source = lax.broadcasted_iota(jnp.int32, shape, 0)
    target = lax.broadcasted_iota(jnp.int32, shape, 1)
    reach = 3 * CHANNELS
    apart = target - (source // CHANNELS) * CHANNELS + CHANNELS
    code = jnp.where((apart >= 0) & (apart < reach), (source % CHANNELS) * reach + apart, -1)
    bands = [jnp.zeros(shape, WIDE) for _ in range(3)]
    for channel in range(CHANNELS):
        for lane in range(reach):
            here = code == channel * reach + lane
            column, out_channel = 2 - lane // CHANNELS, lane % CHANNELS
            for line in range(3):
                place = ((line * 3 + column) * CHANNELS + channel) * CHANNELS + out_channel
                bands[line] = jnp.where(here, kernel_ref[place], bands[line])
    for line in range(3):
        out_ref[:, line * IMG_WIDTH : (line + 1) * IMG_WIDTH] = bands[line]


def step_kernel(
    latent_ref, steps_ref, now_ref, next_ref, own, beside, across, diagonal, noisy_ref, bands_ref,
    stepped_ref, preview_ref, image, clean, above, below,
):
    tiles = noisy_ref.shape[0] // IMG_ROWS
    row = lax.axis_index("row")
    col = lax.axis_index("col")
    for place in range(4):

        @pl.when(col == place)
        def _():
            for offset, block in enumerate((own, beside, across, diagonal)):
                for dy in range(PATCH):
                    start = (place ^ offset) * IMG_ROWS + dy
                    image[pl.ds(start, TILE_ROWS, PATCH), :] = block[:, dy * IMG_WIDTH : (dy + 1) * IMG_WIDTH]

    for tile in range(tiles):
        here = slice(tile * IMG_ROWS, (tile + 1) * IMG_ROWS)
        step = steps_ref[latent_ref[row * tiles + tile]]
        signal_now = jnp.full((1, IMG_WIDTH), now_ref[step], WIDE)
        signal_next = jnp.full((1, IMG_WIDTH), next_ref[step], WIDE)
        noise = image[here, :]
        rows = (noisy_ref[here, :].astype(WIDE) - jnp.sqrt(1.0 - signal_now) * noise) / jnp.sqrt(signal_now)
        clean[here, :] = rows
        stepped = jnp.sqrt(signal_next) * rows + jnp.sqrt(1.0 - signal_next) * noise
        stepped_ref[here, :] = stepped.astype(NARROW)
    parts = jnp.dot(
        clean[...], bands_ref[...], precision=lax.Precision.HIGHEST, preferred_element_type=WIDE
    )
    count = tiles * IMG_ROWS
    above[8 : 8 + count, :] = parts[:, :IMG_WIDTH]
    below[8 : 8 + count, :] = parts[:, 2 * IMG_WIDTH :]
    for tile in range(tiles):
        here = slice(tile * IMG_ROWS, (tile + 1) * IMG_ROWS)
        start = 8 + tile * IMG_ROWS
        line = lax.broadcasted_iota(jnp.int32, (IMG_ROWS, IMG_WIDTH), 0)
        from_above = above[start - 1 : start - 1 + IMG_ROWS, :]
        from_below = below[start + 1 : start + 1 + IMG_ROWS, :]
        mine = latent_ref[row * tiles + tile]
        if tile == 0:
            above_ok = line > 0
        else:
            above_ok = (line > 0) | (latent_ref[row * tiles + tile - 1] == mine)
        if tile == tiles - 1:
            below_ok = line < IMG_ROWS - 1
        else:
            below_ok = (line < IMG_ROWS - 1) | (latent_ref[row * tiles + tile + 1] == mine)
        total = parts[here, IMG_WIDTH : 2 * IMG_WIDTH]
        total = total + jnp.where(above_ok, from_above, 0.0) + jnp.where(below_ok, from_below, 0.0)
        preview_ref[here, :] = total.astype(NARROW)


def shards(
    hidden,
    noisy_latent,
    tile_latent,
    timesteps,
    step_embedding,
    alpha_now,
    alpha_next,
    modulation,
    attention_in,
    attention_out,
    expand_weight,
    reduce_weight,
    noise_head,
    preview_kernel,
):
    rows = lax.axis_size("row")
    tokens_here, width = hidden.shape
    tiles = tokens_here // TILE
    depth = modulation.shape[0]
    units = expand_weight.shape[1]
    shape = jax.ShapeDtypeStruct

    conditioning = call(
        functools.partial(condition_kernel, tiles),
        shape((2 * rows, depth), NARROW),
        [SMEM, SMEM, VMEM],
        [pltpu.VMEM((2 * rows, STEPS), WIDE)],
        flops=2 * 2 * rows * D * (STEPS + depth), nbytes=2 * STEPS * D,
    )(tile_latent, timesteps, step_embedding)
    partial = jnp.einsum("td,dkc->tkc", conditioning, modulation, preferred_element_type=WIDE)
    partial = partial.reshape(rows, 16, width)
    received = lax.all_to_all(partial, "row", 0, 0, tiled=True)
    hidden_blocks = gather_blocks(hidden.T)
    out_rows = after(attention_out, hidden_blocks[2])
    pieces = gather_rows(expand_weight, reduce_weight.T)
    hidden_blocks = after(hidden_blocks, [piece for piece in pieces[:5] if piece is not pieces[3 % len(pieces)]])
    tokens, bands = call(
        tokens_kernel,
        [shape((tokens_here, D), NARROW), shape((IMG_WIDTH, 3 * IMG_WIDTH), WIDE)],
        [VMEM] * 4 + [SMEM],
        nbytes=4 * tokens_here * D, limit=8,
    )(*hidden_blocks, preview_kernel.reshape(-1))
    shared = call(shared_kernel, shape((32, width), WIDE), [VMEM] * 2, nbytes=2**18)(after(received, tokens), noise_head.T)
    shared_blocks = gather_blocks(shared)
    attention_weight = attention_in.transpose(1, 2, 0).reshape(3 * width, D)
    terms, attended = call(
        attention_kernel,
        [shape((32, D), WIDE), shape((tokens_here, width), NARROW)],
        [SMEM] + [VMEM] * 5 + [ANYWHERE],
        [
            pltpu.VMEM((3 * width, D), NARROW),
            pltpu.SemaphoreType.DMA,
            pltpu.VMEM((tokens_here, D), NARROW),
            pltpu.VMEM((3 * width, tokens_here), WIDE),
            pltpu.VMEM((width, tokens_here), WIDE),
        ],
        flops=2 * tokens_here * (D * 3 * width + 2 * tokens_here * width), nbytes=5 * 2**20,
        trans=4 * tokens_here**2, limit=24,
    )(tile_latent, tokens, *shared_blocks, attention_weight)
    out_blocks = gather_late(out_rows, attended)
    attended_blocks = gather_blocks(attended)

    out_weight = call(
        stack_kernel, shape((D, D), NARROW), [VMEM] * 4, nbytes=4 * D * D, limit=8
    )(*out_blocks)
    expand_all, reduce_all = call(
        functools.partial(weights_kernel, [len(piece) for piece in pieces], D // len(pieces)),
        [shape((D, units), NARROW)] * 2, [VMEM] * sum(map(len, pieces)), nbytes=8 * D * units, limit=8,
    )(*sum(pieces, []))
    def mlp(near, inputs):
        outs = [shape((TILE, D), WIDE), shape((TILE, D), NARROW)]
        if near:
            outs.append(shape((TILE, D), NARROW))
        return call(
            functools.partial(mlp_kernel, near),
            outs,
            [SMEM] + [VMEM] * 9,
            [pltpu.VMEM((2 * TILE, D), NARROW)] * 2,
            flops=4 * TILE * D * (D + 2 * units), nbytes=8 * 2**20, trans=2 * TILE * units, limit=20,
        )(tile_latent, *inputs, out_weight, expand_all, reduce_all)

    inputs = (*attended_blocks, tokens, terms)
    far_kept, far_sent = mlp(False, inputs)
    far_sum = (far_kept + exchange(far_sent, "col", 1).astype(WIDE)).astype(NARROW)
    far_sum, inputs = lax.optimization_barrier((far_sum, inputs))
    crossed = exchange(far_sum, "col", 2)
    near_kept, near_sent, residual = mlp(True, inputs)
    near_sent, crossed, bands = lax.optimization_barrier((near_sent, crossed, bands))
    beside = exchange(near_sent, "col", 1)
    noise = call(
        head_kernel,
        shape((TILE_ROWS, PATCH * IMG_WIDTH), WIDE),
        [SMEM] + [VMEM] * 5,
        flops=4 * TILE * D * IMG_WIDTH, nbytes=2**21, limit=8,
    )(tile_latent, near_kept, beside, crossed, residual, terms)

    img_rows = tiles * IMG_ROWS
    stepped, preview = call(
        step_kernel,
        [shape((img_rows, IMG_WIDTH), NARROW)] * 2,
        [SMEM] * 4 + [VMEM] * 6,
        [pltpu.VMEM((img_rows, IMG_WIDTH), WIDE)] * 2
        + [pltpu.VMEM((img_rows + 16, IMG_WIDTH), WIDE)] * 2,
        flops=12 * img_rows * IMG_WIDTH**2, nbytes=2**19,
    )(tile_latent, timesteps, alpha_now, alpha_next, *gather_blocks(noise), noisy_latent, bands)
    return (stepped, preview)


def solution(mesh):
    return jax.shard_map(
        shards,
        mesh=mesh,
        in_specs=(
            P("row", "col"),
            P("row", None),
            P(),
            P(),
            P(),
            P(),
            P(),
            P("row", None, "col"),
            P(None, None, "col"),
            P("col", None),
            P("row", "col"),
            P("col", "row"),
            P("col", None),
            P(),
        ),
        out_specs=(P("row", None), P("row", None)),
        check_vma=False,
    )
```

time: 103 us -> 90.7 us (0.88)
  waiting for transfers between devices: 21.3 us -> 37.6 us
  blocking collectives: 10.8 us -> 0 us
  Pallas kernels: 29.9 us -> 20.3 us
  local copies, waits for them, and re-layouts: 14.2 us -> 9.75 us
  starting transfers between devices: 22.8 us -> 20.2 us
  other arithmetic: 2.53 us -> 1.11 us
    ppermute x19 -> x25, waiting for transfers between devices: 21.1 us -> 37.6 us  [exchange(): return lax.ppermute(value, axis, [(i, i ^ offset) for i in range(size)])]
    all_gather x2 -> x0, blocking collectives: 10.8 us -> none  [the longest x1 5.59 us: shards(): shared = lax.all_gather(shared, 'col', axis=0)]
    pallas_call x4 -> x7, Pallas kernels: 26.2 us -> 16.6 us  [the longest x1 6.52 us: shards(): call(attention_kernel, [shape((32, D), WIDE), shape((tokens_here, width),...]
    reshape x3 -> x0, local copies, waits for them, and re-layouts: 4.99 us -> none  [the longest x1 4.14 us: shards(): attention_in.reshape(D, 3 * width)]
    all_to_all x1, starting transfers between devices: 5.83 us -> 4.02 us  [shards(): received = lax.all_to_all(partial, 'row', 0, 0, tiled=True)]
    ppermute x19 -> x25, starting transfers between devices: 17 us -> 16.2 us  [exchange(): return lax.ppermute(value, axis, [(i, i ^ offset) for i in range(size)])]
    unnamed x39 -> x44, local copies, waits for them, and re-layouts: 9.12 us -> 8.9 us
  transfers between devices with their start and end apart: 20 -> 26, of which waited for: 7 -> 10; matrix products, arithmetic and copies ran while one was open for 8% -> 2% of each run, Pallas kernels for 19% -> 16%
where the time goes in v3:
time: 90.7 us; the launch traced here: 90.2 us
  waiting for transfers between devices  37.6 us (41%)
  Pallas kernels  20.3 us (22%)
  starting transfers between devices  20.2 us (22%)
  local copies, waits for them, and re-layouts  9.75 us (11%)
  other arithmetic  1.11 us (1%)
  between operations  0.93 us (1%)
    ppermute x25, waiting for transfers between devices, exchange(): return lax.ppermute(value, axis, [(i, i ^ offset) for i in range(size)])  37.6 us
    ppermute x25, starting transfers between devices, exchange(): return lax.ppermute(value, axis, [(i, i ^ offset) for i in range(size)])  16.2 us
    unnamed x44, local copies, waits for them, and re-layouts  8.9 us
    pallas_call x1, Pallas kernels, shards(): call(attention_kernel, [shape((32, D), WIDE), shape((tokens_here, width),...  6.52 us
    pallas_call x2, Pallas kernels, mlp(): call(functools.partial(mlp_kernel, near), outs, [SMEM] + [VMEM] * 9, [plt...  5.99 us
    all_to_all x1, starting transfers between devices, shards(): received = lax.all_to_all(partial, 'row', 0, 0, tiled=True)  4.02 us
    pallas_call x1, Pallas kernels, shards(): call(tokens_kernel, [shape((tokens_here, D), NARROW), shape((IMG_WIDTH, 3...  2.52 us
  transfers between devices with their start and end apart: 26, of which 10 were waited for; matrix products, arithmetic and copies ran while one was open for 2% of the time, Pallas kernels for 16%

profile of v3, /device:TPU:0, one launch (start us, length us, event | category | flops | bytes accessed | tf_op | source)
XLA Modules:
  0.0 90.2 jit_solution(17656774107239870931)
XLA Ops:
  0.6 0.0 copy-start
  0.7 3.0 %collective-permute-start.1 = (bf16[288,512]{1,0:T(8,128)(2,1)}, bf16[288,512]{1,0:T(8,128)(2,1)S(1)}, u32[]{:S(2)}, u32[]{:S(2)}) collective-permute-start(bf16[288,512]{1,0:T(8,128)(2,1)} %bitcast.10), channel_id=1, source_target_pairs={{0,2},{1,3},{2,0},{3,1},{4,6},{5,7},{6,4},{7,5},{8,10},{9,11},{10,... | collective-permute-start | bytes 884744 | tf_op jit(solution)/shard_map/ppermute | solution.py:44
  3.7 0.0 collective-permute-start
  3.7 1.0 %pad_maximum_fusion.refs_0_ = bf16[288,576]{1,0:T(8,128)(2,1)S(1)} fusion(bf16[144,576]{1,0:T(8,128)(2,1)} %bitcast.15, bf16[144,576]{1,0:T(8,128)(2,1)} %param.24), kind=kLoop, calls=%fused_computation.3 | loop fusion | flops 663552 | bytes 663552 | tf_op jit(solution)/shard_map/concatenate | solution.py:67
  4.7 2.7 %collective-permute-start.5 = (bf16[288,576]{1,0:T(8,128)(2,1)S(1)}, bf16[288,576]{1,0:T(8,128)(2,1)}, u32[]{:S(2)}, u32[]{:S(2)}) collective-permute-start(bf16[288,576]{1,0:T(8,128)(2,1)S(1)} %pad_maximum_fusion.refs_0_), channel_id=1, source_target_pairs={{0,16},{4,20},{8,24},{12,28},{16,0},{20,4},{24,8},{28,12},{1,17},{... | collective-permute-start | bytes 995336 | tf_op jit(solution)/shard_map/ppermute | solution.py:44
  7.4 1.6 %collective-permute-start.4 = (bf16[288,576]{1,0:T(8,128)(2,1)S(1)}, bf16[288,576]{1,0:T(8,128)(2,1)S(1)}, u32[]{:S(2)}, u32[]{:S(2)}) collective-permute-start(bf16[288,576]{1,0:T(8,128)(2,1)S(1)} %pad_maximum_fusion.refs_0_), channel_id=1, source_target_pairs={{0,8},{4,12},{8,0},{12,4},{16,24},{20,28},{24,16},{28,20},{1,9},{5... | collective-permute-start | bytes 995336 | tf_op jit(solution)/shard_map/ppermute | solution.py:44
  8.9 1.5 %collective-permute-start.3 = (bf16[288,576]{1,0:T(8,128)(2,1)S(1)}, bf16[288,576]{1,0:T(8,128)(2,1)S(1)}, u32[]{:S(2)}, u32[]{:S(2)}) collective-permute-start(bf16[288,576]{1,0:T(8,128)(2,1)S(1)} %pad_maximum_fusion.refs_0_), channel_id=1, source_target_pairs={{0,4},{4,0},{8,12},{12,8},{16,20},{20,16},{24,28},{28,24},{1,5},{5... | collective-permute-start | bytes 995336 | tf_op jit(solution)/shard_map/ppermute | solution.py:44
  10.5 0.9 copy-done.11
  11.4 0.7 copy-done.13
  12.0 0.7 copy-done.16
  12.7 1.1 %shard_map.150 = bf16[16,144]{1,0:T(8,128)(2,1)S(1)} custom-call(s32[32]{0:T(128)S(1)} %copy-done.13, s32[32]{0:T(128)S(1)} %copy-done.16, bf16[50,1152]{1,0:T(8,128)(2,1)S(1)} %copy-done.11), custom_call_target="tpu_custom_call" | custom-call | flops 7151616 | bytes 115200 | tf_op jit(solution)/shard_map/pallas_call | solution.py:342
  13.8 0.0 copy-start.14
  13.8 0.0 collective-permute-done.1.across
  13.8 0.6 collective-permute-start.12
  14.4 0.0 collective-permute-done.beside
  14.4 0.7 copy-done.9
  15.1 0.0 collective-permute-start.2
  15.1 0.2 fusion
  15.4 0.7 copy.17
  16.1 4.0 %all-to-all-start = ((f32[8,16,288]{2,1,0:T(8,128)}), f32[8,16,288]{2,1,0:T(8,128)S(1)}, u32[]{:S(2)}, u32[]{:S(2)}) async-start(f32[8,16,288]{2,1,0:T(8,128)} %bitcast.3), calls=%async_computation | async-start | bytes 393216 | tf_op jit(solution)/shard_map/all_to_all | solution.py:351
  20.2 5.0 %collective-permute-done.5.refs_4_ = bf16[288,576]{1,0:T(8,128)(2,1)} collective-permute-done((bf16[288,576]{1,0:T(8,128)(2,1)S(1)}, bf16[288,576]{1,0:T(8,128)(2,1)}, u32[]{:S(2)}, u32[]{:S(2)}) %collective-permute-start.5) | collective-permute-done | bytes 331808 | tf_op jit(solution)/shard_map/ppermute | solution.py:44
  25.1 0.4 collective-permute-start.17
  25.5 0.1 reshape.13.kernel_ref
  25.6 0.0 collective-permute-done.4.refs_2_
  25.7 0.0 collective-permute-done.3.refs_1_
  25.7 0.7 copy-done.2
  26.4 0.8 copy-done.4
  27.2 1.0 %copy-done.6 = bf16[512,288]{0,1:T(8,128)(2,1)S(1)} copy-done((bf16[512,288]{0,1:T(8,128)(2,1)S(1)}, bf16[512,288]{0,1:T(8,128)(2,1)}, u32[]{:S(2)}) %copy-start.6) | copy-done | bytes 294936
  28.1 1.0 %copy-done.8 = bf16[288,512]{1,0:T(8,128)(2,1)S(1)} copy-done((bf16[288,512]{1,0:T(8,128)(2,1)S(1)}, bf16[288,512]{1,0:T(8,128)(2,1)}, u32[]{:S(2)}) %copy-start.8) | copy-done | bytes 294936
  29.1 1.0 %copy-done.10 = bf16[288,512]{1,0:T(8,128)(2,1)S(1)} copy-done((bf16[288,512]{1,0:T(8,128)(2,1)S(1)}, bf16[288,512]{1,0:T(8,128)(2,1)}, u32[]{:S(2)}) %copy-start.10) | copy-done | bytes 294936
  30.1 2.5 %shard_map.149 = (bf16[512,1152]{1,0:T(8,128)(2,1)S(1)}, f32[128,384]{1,0:T(8,128)S(1)}) custom-call(bf16[288,512]{1,0:T(8,128)(2,1)S(1)} %bitcast.12, bf16[288,512]{1,0:T(8,128)(2,1)S(1)} %copy-done.10, bf16[288,512]{1,0:T(8,128)(2,1)S(1)} %copy-done.8, bf16[288,512]{1,0:T(8,128)(2,1)} %collective-permute-done.2.diagonal, f32[144]{0:T(256)S(1)} %reshape.13.kernel_ref), custom_call_target="tpu_custom_call" | custom-call | bytes 2359296 | tf_op jit(solution)/shard_map/pallas_call | solution.py:356
  32.6 0.6 collective-permute-start.7
  33.2 3.6 %collective-permute-done.7.terms_across = f32[32,288]{1,0:T(8,128)S(1)} collective-permute-done((f32[32,288]{1,0:T(8,128)S(1)}, f32[32,288]{1,0:T(8,128)S(1)}, u32[]{:S(2)}, u32[]{:S(2)}) %collective-permute-start.7) | collective-permute-done | bytes 36896 | tf_op jit(solution)/shard_map/ppermute | solution.py:44
  36.8 1.5 %collective-permute-start.16 = (bf16[288,576]{1,0:T(8,128)(2,1)}, bf16[288,576]{1,0:T(8,128)(2,1)S(1)}, u32[]{:S(2)}, u32[]{:S(2)}) collective-permute-start(bf16[288,576]{1,0:T(8,128)(2,1)} %collective-permute-done.5.refs_4_), channel_id=1, source_target_pairs={{0,4},{4,0},{8,12},{12,8},{16,20},{20,16},{24,28},{28,24},{1,5},{5... | collective-permute-start | bytes 995336 | tf_op jit(solution)/shard_map/ppermute | solution.py:44
  38.3 0.0 copy-start.20
  38.3 1.5 %copy-done.20 = bf16[1152,3,288]{0,2,1:T(8,128)(2,1)S(1)} copy-done((bf16[1152,3,288]{0,2,1:T(8,128)(2,1)S(1)}, bf16[1152,3,288]{0,2,1:T(8,128)(2,1)}, u32[]{:S(2)}) %copy-start.20) | copy-done | bytes 1990680
  39.9 6.5 %shard_map.152 = (f32[32,1152]{1,0:T(8,128)S(1)}, bf16[512,288]{1,0:T(8,128)(2,1)S(1)}) custom-call(s32[32]{0:T(128)S(1)} %copy-done.14, bf16[512,1152]{1,0:T(8,128)(2,1)S(1)} %get-tuple-element.50.tokens_ref, f32[32,288]{1,0:T(8,128)S(1)} %shard_map.151.terms_own, f32[32,288]{1,0:T(8,128)S(1)} %collective-permute-done.6.terms_beside, ...), custom_call_target="tpu_custom_call" | custom-call | flops 1321205760 | bytes 5242880 | tf_op jit(solution)/shard_map/pallas_call | solution.py:365
  46.4 0.3 collective-permute-start.13
  46.7 0.3 collective-permute-start.14
  47.0 1.2 %collective-permute-start.15 = (bf16[288,576]{1,0:T(8,128)(2,1)S(1)}, bf16[288,576]{1,0:T(8,128)(2,1)S(1)}, u32[]{:S(2)}, u32[]{:S(2)}) collective-permute-start(bf16[288,576]{1,0:T(8,128)(2,1)S(1)} %copy-done.3), channel_id=1, source_target_pairs={{0,4},{4,0},{8,12},{12,8},{16,20},{20,16},{24,28},{28,24},{1,5},{5... | collective-permute-start | bytes 995336 | tf_op jit(solution)/shard_map/ppermute | solution.py:44
  48.2 0.5 collective-permute-start.10
  48.7 0.8 collective-permute-start.18
  49.5 8.9 %collective-permute-done.15.refs_3_ = bf16[288,576]{1,0:T(8,128)(2,1)S(1)} collective-permute-done((bf16[288,576]{1,0:T(8,128)(2,1)S(1)}, bf16[288,576]{1,0:T(8,128)(2,1)S(1)}, u32[]{:S(2)}, u32[]{:S(2)}) %collective-permute-start.15) | collective-permute-done | bytes 331808 | tf_op jit(solution)/shard_map/ppermute | solution.py:44
  58.5 0.7 collective-permute-done.10.att_across
  59.1 6.5 %collective-permute-done.18.refs_7_ = bf16[288,576]{1,0:T(8,128)(2,1)S(1)} collective-permute-done((bf16[288,576]{1,0:T(8,128)(2,1)}, bf16[288,576]{1,0:T(8,128)(2,1)S(1)}, u32[]{:S(2)}, u32[]{:S(2)}) %collective-permute-start.18) | collective-permute-done | bytes 331808 | tf_op jit(solution)/shard_map/ppermute | solution.py:44
  65.6 1.3 %shard_map.154 = (bf16[1152,576]{1,0:T(8,128)(2,1)S(1)}, bf16[1152,576]{1,0:T(8,128)(2,1)S(1)}) custom-call(bf16[288,576]{1,0:T(8,128)(2,1)S(1)} %pad_maximum_fusion.refs_0_, bf16[288,576]{1,0:T(8,128)(2,1)S(1)} %copy-done.5, bf16[288,576]{1,0:T(8,128)(2,1)S(1)} %copy-done.3, bf16[288,576]{1,0:T(8,128)(2,1)S(1)} %collective-permute-done.15.refs_3_, ...), custom_call_target="tpu_custom_call" | custom-call | bytes 5308416 | tf_op jit(solution)/shard_map/pallas_call | solution.py:385
  67.0 0.2 shard_map.153.out_weight
  67.2 3.0 %shard_map.155 = (f32[128,1152]{1,0:T(8,128)S(1)}, bf16[128,1152]{1,0:T(8,128)(2,1)S(1)}) custom-call(s32[32]{0:T(128)S(1)} %copy-done.14, bf16[512,288]{1,0:T(8,128)(2,1)S(1)} %get-tuple-element.46.att_own, bf16[512,288]{1,0:T(8,128)(2,1)S(1)} %collective-permute-done.9.att_beside, bf16[512,288]{1,0:T(8,128)(2,1)S(1)} %collective-permute-done.10.att_across, ...), custom_call_target="tpu_custom_call" | custom-call | flops 1358954496 | bytes 8388608 | tf_op jit(solution)/shard_map/pallas_call | solution.py:393
  70.2 0.1 collective-permute-start.19
  70.3 1.6 %collective-permute-done.19 = bf16[128,1152]{1,0:T(8,128)(2,1)S(1)} collective-permute-done((bf16[128,1152]{1,0:T(8,128)(2,1)S(1)}, bf16[128,1152]{1,0:T(8,128)(2,1)S(1)}, u32[]{:S(2)}, u32[]{:S(2)}) %collective-permute-start.19) | collective-permute-done | bytes 294944 | tf_op jit(solution)/shard_map/ppermute | solution.py:44
  71.9 0.1 add_convert_fusion
  71.9 0.6 collective-permute-start.20
  72.5 3.0 %shard_map.156 = (f32[128,1152]{1,0:T(8,128)S(1)}, bf16[128,1152]{1,0:T(8,128)(2,1)S(1)}, bf16[128,1152]{1,0:T(8,128)(2,1)S(1)}) custom-call(s32[32]{0:T(128)S(1)} %copy-done.14, bf16[512,288]{1,0:T(8,128)(2,1)S(1)} %get-tuple-element.46.att_own, bf16[512,288]{1,0:T(8,128)(2,1)S(1)} %collective-permute-done.9.att_beside, ...), custom_call_target="tpu_custom_call" | custom-call | flops 1358954496 | bytes 8388608 | tf_op jit(solution)/shard_map/pallas_call | solution.py:393
  75.5 0.0 copy-start.12
  75.5 0.0 copy-start.17
  75.5 0.0 copy-start.18
  75.5 0.0 copy-start.19
  75.6 5.5 %collective-permute-done.20.crossed_ref = bf16[128,1152]{1,0:T(8,128)(2,1)S(1)} collective-permute-done((bf16[128,1152]{1,0:T(8,128)(2,1)S(1)}, bf16[128,1152]{1,0:T(8,128)(2,1)S(1)}, u32[]{:S(2)}, u32[]{:S(2)}) %collective-permute-start.20) | collective-permute-done | bytes 294944 | tf_op jit(solution)/shard_map/ppermute | solution.py:44
  81.1 1.6 %collective-permute-done.21.beside_ref = bf16[128,1152]{1,0:T(8,128)(2,1)S(1)} collective-permute-done((bf16[128,1152]{1,0:T(8,128)(2,1)S(1)}, bf16[128,1152]{1,0:T(8,128)(2,1)S(1)}, u32[]{:S(2)}, u32[]{:S(2)}) %collective-permute-start.21) | collective-permute-done | bytes 294944 | tf_op jit(solution)/shard_map/ppermute | solution.py:44
  82.6 1.2 %shard_map.157.own = f32[8,256]{1,0:T(8,128)S(1)} custom-call(s32[32]{0:T(128)S(1)} %copy-done.14, f32[128,1152]{1,0:T(8,128)S(1)} %get-tuple-element.52.kept_ref, bf16[128,1152]{1,0:T(8,128)(2,1)S(1)} %collective-permute-done.21.beside_ref, bf16[128,1152]{1,0:T(8,128)(2,1)S(1)} %collective-permute-done.20.crossed_ref, ...), custom_call_target="tpu_custom_call" | custom-call | flops 75497472 | bytes 2097152 | tf_op jit(solution)/shard_map/pallas_call | solution.py:409
  83.8 0.6 collective-permute-start.23
  84.4 3.2 %collective-permute-done.23.across = f32[8,256]{1,0:T(8,128)S(1)} collective-permute-done((f32[8,256]{1,0:T(8,128)S(1)}, f32[8,256]{1,0:T(8,128)S(1)}, u32[]{:S(2)}, u32[]{:S(2)}) %collective-permute-start.23) | collective-permute-done | bytes 8224 | tf_op jit(solution)/shard_map/ppermute | solution.py:44
  87.5 1.2 %collective-permute-done.24.diagonal = f32[8,256]{1,0:T(8,128)S(1)} collective-permute-done((f32[8,256]{1,0:T(8,128)S(1)}, f32[8,256]{1,0:T(8,128)S(1)}, u32[]{:S(2)}, u32[]{:S(2)}) %collective-permute-start.24) | collective-permute-done | bytes 8224 | tf_op jit(solution)/shard_map/ppermute | solution.py:44
  88.7 1.5 %shard_map.158 = (bf16[64,128]{1,0:T(8,128)(2,1)}, bf16[64,128]{1,0:T(8,128)(2,1)}) custom-call(s32[32]{0:T(128)S(1)} %copy-done.14, s32[32]{0:T(128)S(1)} %copy-done.17, f32[50]{0:T(128)S(1)} %copy-done.18, f32[50]{0:T(128)S(1)} %copy-done.19, f32[8,256]{1,0:T(8,128)S(1)} %shard_map.157.own, f32[8,256]{1,0:T(8,128)S(1)} %collective-permute-done.22.beside, ...), custom_call_target="tpu_custom_call" | custom-call | flops 12582912 | bytes 524288 | tf_op jit(solution)/shard_map/pallas_call | solution.py:417
  (47 shorter events, 0.1 us)
Async XLA Ops:
  0.6 14.5 %copy-start = (bf16[144,8,288]{2,1,0:T(8,128)(2,1)S(1)}, bf16[144,8,288]{2,1,0:T(8,128)(2,1)}, u32[]{:S(2)}) copy-start(bf16[144,8,288]{2,1,0:T(8,128)(2,1)} %param.21) | copy-start | bytes 1990660
  0.6 24.9 %copy-start.21 = (f32[3,3,4,4]{3,2,1,0:T(4,128)S(1)}, f32[3,3,4,4]{3,2,1,0:T(4,128)}, u32[]{:S(2)}) copy-start(f32[3,3,4,4]{3,2,1,0:T(4,128)} %param.27) | copy-start | bytes 1732
  0.7 13.2 %collective-permute-start.1 = (bf16[288,512]{1,0:T(8,128)(2,1)}, bf16[288,512]{1,0:T(8,128)(2,1)S(1)}, u32[]{:S(2)}, u32[]{:S(2)}) collective-permute-start(bf16[288,512]{1,0:T(8,128)(2,1)} %bitcast.10), channel_id=1, source_target_pairs={{0,2},{1,3},{2,0},{3,1},{4,6},{5,7},{6,4},{7,5},{8,10},{9,11},{10,... | collective-permute-start | bytes 884744 | tf_op jit(solution)/shard_map/ppermute | solution.py:44
  3.7 10.8 %collective-permute-start = (bf16[288,512]{1,0:T(8,128)(2,1)}, bf16[288,512]{1,0:T(8,128)(2,1)S(1)}, u32[]{:S(2)}, u32[]{:S(2)}) collective-permute-start(bf16[288,512]{1,0:T(8,128)(2,1)} %bitcast.11), channel_id=1, source_target_pairs={{0,1},{1,0},{2,3},{3,2},{4,5},{5,4},{6,7},{7,6},{8,9},{9,8},{10,11... | collective-permute-start | bytes 884744 | tf_op jit(solution)/shard_map/ppermute | solution.py:44
  4.7 20.4 %collective-permute-start.5 = (bf16[288,576]{1,0:T(8,128)(2,1)S(1)}, bf16[288,576]{1,0:T(8,128)(2,1)}, u32[]{:S(2)}, u32[]{:S(2)}) collective-permute-start(bf16[288,576]{1,0:T(8,128)(2,1)S(1)} %pad_maximum_fusion.refs_0_), channel_id=1, source_target_pairs={{0,16},{4,20},{8,24},{12,28},{16,0},{20,4},{24,8},{28,12},{1,17},{... | collective-permute-start | bytes 995336 | tf_op jit(solution)/shard_map/ppermute | solution.py:44
  7.4 18.3 %collective-permute-start.4 = (bf16[288,576]{1,0:T(8,128)(2,1)S(1)}, bf16[288,576]{1,0:T(8,128)(2,1)S(1)}, u32[]{:S(2)}, u32[]{:S(2)}) collective-permute-start(bf16[288,576]{1,0:T(8,128)(2,1)S(1)} %pad_maximum_fusion.refs_0_), channel_id=1, source_target_pairs={{0,8},{4,12},{8,0},{12,4},{16,24},{20,28},{24,16},{28,20},{1,9},{5... | collective-permute-start | bytes 995336 | tf_op jit(solution)/shard_map/ppermute | solution.py:44
  8.9 16.7 %collective-permute-start.3 = (bf16[288,576]{1,0:T(8,128)(2,1)S(1)}, bf16[288,576]{1,0:T(8,128)(2,1)S(1)}, u32[]{:S(2)}, u32[]{:S(2)}) collective-permute-start(bf16[288,576]{1,0:T(8,128)(2,1)S(1)} %pad_maximum_fusion.refs_0_), channel_id=1, source_target_pairs={{0,4},{4,0},{8,12},{12,8},{16,20},{20,16},{24,28},{28,24},{1,5},{5... | collective-permute-start | bytes 995336 | tf_op jit(solution)/shard_map/ppermute | solution.py:44
  10.5 0.9 %copy-start.11 = (bf16[50,1152]{1,0:T(8,128)(2,1)S(1)}, bf16[50,1152]{1,0:T(8,128)(2,1)}, u32[]{:S(2)}) copy-start(bf16[50,1152]{1,0:T(8,128)(2,1)} %embedding_ref.1) | copy-start | bytes 345604
  11.4 0.7 copy-start.13
  12.0 0.7 copy-start.16
  13.8 18.8 %copy-start.15 = (bf16[288,16]{0,1:T(8,128)(2,1)S(1)}, bf16[288,16]{0,1:T(8,128)(2,1)}, u32[]{:S(2)}) copy-start(bf16[288,16]{0,1:T(8,128)(2,1)} %param.26) | copy-start | bytes 27652
  13.8 24.6 %copy-start.14 = (s32[32]{0:T(128)S(1)}, s32[32]{0:T(128)}, u32[]{:S(2)}) copy-start(s32[32]{0:T(128)} %latent_ref.11) | copy-start | bytes 388
  13.8 11.9 %copy-start.7 = (bf16[288,512]{1,0:T(8,128)(2,1)}, bf16[288,512]{1,0:T(8,128)(2,1)S(1)}, u32[]{:S(2)}) copy-start(bf16[288,512]{1,0:T(8,128)(2,1)S(1)} %collective-permute-done.1.across) | copy-start | bytes 884740
  13.8 32.6 %collective-permute-start.12 = (bf16[288,1152]{1,0:T(8,128)(2,1)}, bf16[288,1152]{1,0:T(8,128)(2,1)S(1)}, u32[]{:S(2)}, u32[]{:S(2)}) collective-permute-start(bf16[288,1152]{1,0:T(8,128)(2,1)} %refs_0_), channel_id=1, source_target_pairs={{0,2},{1,3},{2,0},{3,1},{4,6},{5,7},{6,4},{7,5},{8,10},{9,11},{10,... | collective-permute-start | bytes 1990664 | tf_op jit(solution)/shard_map/ppermute | solution.py:44
  14.4 0.7 copy-start.9
  15.1 12.0 %collective-permute-start.2 = (bf16[288,512]{1,0:T(8,128)(2,1)S(1)}, bf16[288,512]{1,0:T(8,128)(2,1)}, u32[]{:S(2)}, u32[]{:S(2)}) collective-permute-start(bf16[288,512]{1,0:T(8,128)(2,1)S(1)} %collective-permute-done.1.across), channel_id=1, source_target_pairs={{0,1},{1,0},{2,3},{3,2},{4,5},{5,4},{6,7},{7,6},{8,9},{9,8},{10,11... | collective-permute-start | bytes 884744 | tf_op jit(solution)/shard_map/ppermute | solution.py:44
  16.1 16.5 %all-to-all-start = ((f32[8,16,288]{2,1,0:T(8,128)}), f32[8,16,288]{2,1,0:T(8,128)S(1)}, u32[]{:S(2)}, u32[]{:S(2)}) async-start(f32[8,16,288]{2,1,0:T(8,128)} %bitcast.3), calls=%async_computation | async-start | bytes 393216 | tf_op jit(solution)/shard_map/all_to_all | solution.py:351
  25.1 23.1 %collective-permute-start.17 = (bf16[288,576]{1,0:T(8,128)(2,1)}, bf16[288,576]{1,0:T(8,128)(2,1)}, u32[]{:S(2)}, u32[]{:S(2)}) collective-permute-start(bf16[288,576]{1,0:T(8,128)(2,1)} %collective-permute-done.5.refs_4_), channel_id=1, source_target_pairs={{0,8},{4,12},{8,0},{12,4},{16,24},{20,28},{24,16},{28,20},{1,9},{5... | collective-permute-start | bytes 995336 | tf_op jit(solution)/shard_map/ppermute | solution.py:44
  25.7 0.8 copy-start.2
  26.4 0.8 copy-start.4
  27.2 1.0 %copy-start.6 = (bf16[512,288]{0,1:T(8,128)(2,1)S(1)}, bf16[512,288]{0,1:T(8,128)(2,1)}, u32[]{:S(2)}) copy-start(bf16[512,288]{0,1:T(8,128)(2,1)} %param.14) | copy-start | bytes 884740
  28.1 1.0 %copy-start.8 = (bf16[288,512]{1,0:T(8,128)(2,1)S(1)}, bf16[288,512]{1,0:T(8,128)(2,1)}, u32[]{:S(2)}) copy-start(bf16[288,512]{1,0:T(8,128)(2,1)} %copy-done.7) | copy-start | bytes 884740
  29.1 1.0 %copy-start.10 = (bf16[288,512]{1,0:T(8,128)(2,1)S(1)}, bf16[288,512]{1,0:T(8,128)(2,1)}, u32[]{:S(2)}) copy-start(bf16[288,512]{1,0:T(8,128)(2,1)} %copy-done.9) | copy-start | bytes 884740
  32.6 4.2 %collective-permute-start.7 = (f32[32,288]{1,0:T(8,128)S(1)}, f32[32,288]{1,0:T(8,128)S(1)}, u32[]{:S(2)}, u32[]{:S(2)}) collective-permute-start(f32[32,288]{1,0:T(8,128)S(1)} %shard_map.151.terms_own), channel_id=1, source_target_pairs={{0,2},{1,3},{2,0},{3,1},{4,6},{5,7},{6,4},{7,5},{8,10},{9,11},{10,... | collective-permute-start | bytes 110600 | tf_op jit(solution)/shard_map/ppermute | solution.py:44
  33.2 5.1 %collective-permute-start.6 = (f32[32,288]{1,0:T(8,128)S(1)}, f32[32,288]{1,0:T(8,128)S(1)}, u32[]{:S(2)}, u32[]{:S(2)}) collective-permute-start(f32[32,288]{1,0:T(8,128)S(1)} %shard_map.151.terms_own), channel_id=1, source_target_pairs={{0,1},{1,0},{2,3},{3,2},{4,5},{5,4},{6,7},{7,6},{8,9},{9,8},{10,11... | collective-permute-start | bytes 110600 | tf_op jit(solution)/shard_map/ppermute | solution.py:44
  36.8 1.5 %collective-permute-start.8 = (f32[32,288]{1,0:T(8,128)S(1)}, f32[32,288]{1,0:T(8,128)S(1)}, u32[]{:S(2)}, u32[]{:S(2)}) collective-permute-start(f32[32,288]{1,0:T(8,128)S(1)} %collective-permute-done.7.terms_across), channel_id=1, source_target_pairs={{0,1},{1,0},{2,3},{3,2},{4,5},{5,4},{6,7},{7,6},{8,9},{9,8},{10,11... | collective-permute-start | bytes 110600 | tf_op jit(solution)/shard_map/ppermute | solution.py:44
  36.8 11.9 %collective-permute-start.16 = (bf16[288,576]{1,0:T(8,128)(2,1)}, bf16[288,576]{1,0:T(8,128)(2,1)S(1)}, u32[]{:S(2)}, u32[]{:S(2)}) collective-permute-start(bf16[288,576]{1,0:T(8,128)(2,1)} %collective-permute-done.5.refs_4_), channel_id=1, source_target_pairs={{0,4},{4,0},{8,12},{12,8},{16,20},{20,16},{24,28},{28,24},{1,5},{5... | collective-permute-start | bytes 995336 | tf_op jit(solution)/shard_map/ppermute | solution.py:44
  38.3 1.6 %copy-start.20 = (bf16[1152,3,288]{0,2,1:T(8,128)(2,1)S(1)}, bf16[1152,3,288]{0,2,1:T(8,128)(2,1)}, u32[]{:S(2)}) copy-start(bf16[1152,3,288]{0,2,1:T(8,128)(2,1)} %param.22) | copy-start | bytes 5971972
  39.9 6.5 %copy-start.1 = (bf16[288,1152]{1,0:T(8,128)(2,1)S(1)}, bf16[288,1152]{1,0:T(8,128)(2,1)}, u32[]{:S(2)}) copy-start(bf16[288,1152]{1,0:T(8,128)(2,1)} %refs_0_) | copy-start | bytes 1990660
  39.9 7.1 %copy-start.3 = (bf16[288,576]{1,0:T(8,128)(2,1)S(1)}, bf16[288,576]{1,0:T(8,128)(2,1)}, u32[]{:S(2)}) copy-start(bf16[288,576]{1,0:T(8,128)(2,1)} %copy-done.2) | copy-start | bytes 995332
  39.9 25.8 %copy-start.5 = (bf16[288,576]{1,0:T(8,128)(2,1)S(1)}, bf16[288,576]{1,0:T(8,128)(2,1)}, u32[]{:S(2)}) copy-start(bf16[288,576]{1,0:T(8,128)(2,1)} %copy-done.4) | copy-start | bytes 995332
  46.4 20.5 %collective-permute-start.13 = (bf16[288,1152]{1,0:T(8,128)(2,1)S(1)}, bf16[288,1152]{1,0:T(8,128)(2,1)S(1)}, u32[]{:S(2)}, u32[]{:S(2)}) collective-permute-start(bf16[288,1152]{1,0:T(8,128)(2,1)S(1)} %copy-done.1), channel_id=1, source_target_pairs={{0,1},{1,0},{2,3},{3,2},{4,5},{5,4},{6,7},{7,6},{8,9},{9,8},{10,11... | collective-permute-start | bytes 1990664 | tf_op jit(solution)/shard_map/ppermute | solution.py:44
  46.7 20.3 %collective-permute-start.14 = (bf16[288,1152]{1,0:T(8,128)(2,1)S(1)}, bf16[288,1152]{1,0:T(8,128)(2,1)S(1)}, u32[]{:S(2)}, u32[]{:S(2)}) collective-permute-start(bf16[288,1152]{1,0:T(8,128)(2,1)S(1)} %collective-permute-done.12.refs_2_), channel_id=1, source_target_pairs={{0,1},{1,0},{2,3},{3,2},{4,5},{5,4},{6,7},{7,6},{8,9},{9,8},{10,11... | collective-permute-start | bytes 1990664 | tf_op jit(solution)/shard_map/ppermute | solution.py:44
  47.0 11.4 %collective-permute-start.15 = (bf16[288,576]{1,0:T(8,128)(2,1)S(1)}, bf16[288,576]{1,0:T(8,128)(2,1)S(1)}, u32[]{:S(2)}, u32[]{:S(2)}) collective-permute-start(bf16[288,576]{1,0:T(8,128)(2,1)S(1)} %copy-done.3), channel_id=1, source_target_pairs={{0,4},{4,0},{8,12},{12,8},{16,20},{20,16},{24,28},{28,24},{1,5},{5... | collective-permute-start | bytes 995336 | tf_op jit(solution)/shard_map/ppermute | solution.py:44
  48.2 10.9 %collective-permute-start.10 = (bf16[512,288]{1,0:T(8,128)(2,1)S(1)}, bf16[512,288]{1,0:T(8,128)(2,1)S(1)}, u32[]{:S(2)}, u32[]{:S(2)}) collective-permute-start(bf16[512,288]{1,0:T(8,128)(2,1)S(1)} %get-tuple-element.46.att_own), channel_id=1, source_target_pairs={{0,2},{1,3},{2,0},{3,1},{4,6},{5,7},{6,4},{7,5},{8,10},{9,11},{10,... | collective-permute-start | bytes 884744 | tf_op jit(solution)/shard_map/ppermute | solution.py:44
  48.7 16.9 %collective-permute-start.18 = (bf16[288,576]{1,0:T(8,128)(2,1)}, bf16[288,576]{1,0:T(8,128)(2,1)S(1)}, u32[]{:S(2)}, u32[]{:S(2)}) collective-permute-start(bf16[288,576]{1,0:T(8,128)(2,1)} %collective-permute-done.17.refs_6_), channel_id=1, source_target_pairs={{0,4},{4,0},{8,12},{12,8},{16,20},{20,16},{24,28},{28,24},{1,5},{5... | collective-permute-start | bytes 995336 | tf_op jit(solution)/shard_map/ppermute | solution.py:44
  58.4 8.8 %collective-permute-start.9 = (bf16[512,288]{1,0:T(8,128)(2,1)S(1)}, bf16[512,288]{1,0:T(8,128)(2,1)S(1)}, u32[]{:S(2)}, u32[]{:S(2)}) collective-permute-start(bf16[512,288]{1,0:T(8,128)(2,1)S(1)} %get-tuple-element.46.att_own), channel_id=1, source_target_pairs={{0,1},{1,0},{2,3},{3,2},{4,5},{5,4},{6,7},{7,6},{8,9},{9,8},{10,11... | collective-permute-start | bytes 884744 | tf_op jit(solution)/shard_map/ppermute | solution.py:44
  59.1 8.1 %collective-permute-start.11 = (bf16[512,288]{1,0:T(8,128)(2,1)S(1)}, bf16[512,288]{1,0:T(8,128)(2,1)S(1)}, u32[]{:S(2)}, u32[]{:S(2)}) collective-permute-start(bf16[512,288]{1,0:T(8,128)(2,1)S(1)} %collective-permute-done.10.att_across), channel_id=1, source_target_pairs={{0,1},{1,0},{2,3},{3,2},{4,5},{5,4},{6,7},{7,6},{8,9},{9,8},{10,11... | collective-permute-start | bytes 884744 | tf_op jit(solution)/shard_map/ppermute | solution.py:44
  70.2 1.6 %collective-permute-start.19 = (bf16[128,1152]{1,0:T(8,128)(2,1)S(1)}, bf16[128,1152]{1,0:T(8,128)(2,1)S(1)}, u32[]{:S(2)}, u32[]{:S(2)}) collective-permute-start(bf16[128,1152]{1,0:T(8,128)(2,1)S(1)} %get-tuple-element.45), channel_id=1, source_target_pairs={{0,1},{1,0},{2,3},{3,2},{4,5},{5,4},{6,7},{7,6},{8,9},{9,8},{10,11... | collective-permute-start | bytes 884744 | tf_op jit(solution)/shard_map/ppermute | solution.py:44
  71.9 9.1 %collective-permute-start.20 = (bf16[128,1152]{1,0:T(8,128)(2,1)S(1)}, bf16[128,1152]{1,0:T(8,128)(2,1)S(1)}, u32[]{:S(2)}, u32[]{:S(2)}) collective-permute-start(bf16[128,1152]{1,0:T(8,128)(2,1)S(1)} %add_convert_fusion), channel_id=1, source_target_pairs={{0,2},{1,3},{2,0},{3,1},{4,6},{5,7},{6,4},{7,5},{8,10},{9,11},{10,... | collective-permute-start | bytes 884744 | tf_op jit(solution)/shard_map/ppermute | solution.py:44
  75.5 13.2 %copy-start.12 = (bf16[64,128]{1,0:T(8,128)(2,1)S(1)}, bf16[64,128]{1,0:T(8,128)(2,1)}, u32[]{:S(2)}) copy-start(bf16[64,128]{1,0:T(8,128)(2,1)} %noisy_ref.1) | copy-start | bytes 49156
  75.5 13.2 %copy-start.17 = (s32[32]{0:T(128)S(1)}, s32[32]{0:T(128)}, u32[]{:S(2)}) copy-start(s32[32]{0:T(128)} %steps_ref.3) | copy-start | bytes 388
  75.5 13.2 %copy-start.18 = (f32[50]{0:T(128)S(1)}, f32[50]{0:T(128)}, u32[]{:S(2)}) copy-start(f32[50]{0:T(128)} %now_ref.1) | copy-start | bytes 604
  75.5 13.2 %copy-start.19 = (f32[50]{0:T(128)S(1)}, f32[50]{0:T(128)}, u32[]{:S(2)}) copy-start(f32[50]{0:T(128)} %next_ref.1) | copy-start | bytes 604
  81.1 1.6 %collective-permute-start.21 = (bf16[128,1152]{1,0:T(8,128)(2,1)S(1)}, bf16[128,1152]{1,0:T(8,128)(2,1)S(1)}, u32[]{:S(2)}, u32[]{:S(2)}) collective-permute-start(bf16[128,1152]{1,0:T(8,128)(2,1)S(1)} %get-tuple-element.56), channel_id=1, source_target_pairs={{0,1},{1,0},{2,3},{3,2},{4,5},{5,4},{6,7},{7,6},{8,9},{9,8},{10,11... | collective-permute-start | bytes 884744 | tf_op jit(solution)/shard_map/ppermute | solution.py:44
  83.8 3.7 %collective-permute-start.23 = (f32[8,256]{1,0:T(8,128)S(1)}, f32[8,256]{1,0:T(8,128)S(1)}, u32[]{:S(2)}, u32[]{:S(2)}) collective-permute-start(f32[8,256]{1,0:T(8,128)S(1)} %shard_map.157.own), channel_id=1, source_target_pairs={{0,2},{1,3},{2,0},{3,1},{4,6},{5,7},{6,4},{7,5},{8,10},{9,11},{10,... | collective-permute-start | bytes 24584 | tf_op jit(solution)/shard_map/ppermute | solution.py:44
  84.4 3.2 %collective-permute-start.22 = (f32[8,256]{1,0:T(8,128)S(1)}, f32[8,256]{1,0:T(8,128)S(1)}, u32[]{:S(2)}, u32[]{:S(2)}) collective-permute-start(f32[8,256]{1,0:T(8,128)S(1)} %shard_map.157.own), channel_id=1, source_target_pairs={{0,1},{1,0},{2,3},{3,2},{4,5},{5,4},{6,7},{7,6},{8,9},{9,8},{10,11... | collective-permute-start | bytes 24584 | tf_op jit(solution)/shard_map/ppermute | solution.py:44
  87.5 1.2 %collective-permute-start.24 = (f32[8,256]{1,0:T(8,128)S(1)}, f32[8,256]{1,0:T(8,128)S(1)}, u32[]{:S(2)}, u32[]{:S(2)}) collective-permute-start(f32[8,256]{1,0:T(8,128)S(1)} %collective-permute-done.23.across), channel_id=1, source_target_pairs={{0,1},{1,0},{2,3},{3,2},{4,5},{5,4},{6,7},{7,6},{8,9},{9,8},{10,11... | collective-permute-start | bytes 24584 | tf_op jit(solution)/shard_map/ppermute | solution.py:44

commit v4 on v3

v4 whole, which is shorter than its diff:
```python
import functools

import jax
import jax.numpy as jnp
from jax import lax
from jax.experimental import pallas as pl
from jax.experimental.pallas import tpu as pltpu
from jax.sharding import PartitionSpec as P

D = 1152
HEAD_DIM = 72
PATCH = 2
CHANNELS = 4
GRIDW = 16
TILE_ROWS = 8
STEPS = 50
TILE = 128
EPS_NORM = 1e-06
IMG_ROWS = TILE_ROWS * PATCH
IMG_WIDTH = GRIDW * PATCH * CHANNELS
WIDE = jnp.float32
NARROW = jnp.bfloat16
NT = (((1,), (1,)), ((), ()))
VMEM = pl.BlockSpec(memory_space=pltpu.VMEM)
SMEM = pl.BlockSpec(memory_space=pltpu.SMEM)
ANYWHERE = pl.BlockSpec(memory_space=pl.ANY)
MIB = 1024 * 1024


def call(kernel, outs, in_specs, scratch=(), flops=0, nbytes=0, trans=0, limit=4):
    return pl.pallas_call(
        kernel,
        out_shape=outs,
        in_specs=in_specs,
        out_specs=jax.tree.map(lambda _: VMEM, outs),
        scratch_shapes=list(scratch),
        compiler_params=pltpu.CompilerParams(vmem_limit_bytes=limit * MIB),
        cost_estimate=pl.CostEstimate(flops=flops, bytes_accessed=nbytes, transcendentals=trans),
    )


def exchange(value, axis, offset):
    size = lax.axis_size(axis)
    return lax.ppermute(value, axis, [(i, i ^ offset) for i in range(size)])


def gather_blocks(value):
    across = exchange(value, "col", 2)
    beside = exchange(value, "col", 1)
    diagonal = exchange(across, "col", 1)
    return value, beside, across, diagonal


def pack(first, second, *before):
    out = jax.ShapeDtypeStruct((2 * first.shape[0], first.shape[1]), first.dtype)
    return call(pair_kernel, out, [VMEM] * 2 + [ANYWHERE] * len(before), limit=8)(first, second, *before)


def normalize(values, shift_term, scale_term):
    mean_value = jnp.sum(values, axis=-1, keepdims=True) * (1.0 / D)
    spread = jnp.sum(values * values, axis=-1, keepdims=True) * (1.0 / D) - mean_value * mean_value
    normed = (values - mean_value) * lax.rsqrt(spread + EPS_NORM)
    return normed * (1.0 + scale_term) + shift_term


def condition_kernel(tiles_here, table_ref, embedding_ref, out_ref, mark_ref, onehot):
    count, depth = out_ref.shape
    tile_count = count // 2 * tiles_here
    mark_ref[...] = jnp.zeros(mark_ref.shape, WIDE)

    def pick(index, carry):
        tile = (index // 2) * tiles_here + (index % 2) * (tiles_here - 1)
        step = table_ref[tile_count + table_ref[tile]]
        lanes = lax.broadcasted_iota(jnp.int32, (1, STEPS), 1)
        onehot[pl.ds(index, 1), :] = jnp.where(lanes == step, 1.0, 0.0)
        return carry

    lax.fori_loop(0, count, pick, 0)
    embedded = jnp.dot(onehot[...].astype(NARROW), embedding_ref[...], preferred_element_type=WIDE)
    conditioning = (embedded / (1.0 + jnp.exp(-embedded))).astype(NARROW)
    first = lax.axis_index("row") * depth
    source = lax.broadcasted_iota(jnp.int32, (D, depth), 0)
    target = lax.broadcasted_iota(jnp.int32, (D, depth), 1) + first
    chosen = jnp.where(source == target, 1.0, 0.0).astype(NARROW)
    out_ref[...] = jnp.dot(conditioning, chosen, preferred_element_type=WIDE).astype(NARROW)


def tile_term(latent_ref, terms_ref, index, tile):
    first = lax.axis_index("row") * (lax.axis_size("col"))
    later = latent_ref[first + tile] != latent_ref[first]
    return jnp.where(later, terms_ref[8 + index : 9 + index, :], terms_ref[index : index + 1, :])


def pass_kernel(*refs):
    refs[-1][...] = refs[0][...]


def triple_kernel(
    latent_ref, own, beside, across, diagonal, terms_near, terms_far, weight_ref, *refs
):
    tokens_ref, terms_ref, triple_ref, weight, weight_sem, normed = refs[-6:]
    fetch = pltpu.make_async_copy(weight_ref, weight, weight_sem)
    fetch.start()
    col = lax.axis_index("col")
    width = terms_near.shape[1]
    tiles = tokens_ref.shape[0] // TILE
    for place in range(4):

        @pl.when(col == place)
        def _():
            for offset, block in enumerate((own, beside, across, diagonal)):
                lower = (place ^ offset) * width
                tokens_ref[:, lower : lower + width] = block[...].T
            for offset in range(4):
                block = (terms_near, terms_far)[offset // 2]
                lower = (place ^ offset) * width
                count = terms_ref.shape[0]
                terms_ref[:, lower : lower + width] = block[offset % 2 * count : (offset % 2 + 1) * count, :]

    for tile in range(tiles):
        here = slice(tile * TILE, (tile + 1) * TILE)
        shift = tile_term(latent_ref, terms_ref, 0, tile)
        scale = tile_term(latent_ref, terms_ref, 1, tile)
        normed[here, :] = normalize(tokens_ref[here, :].astype(WIDE), shift, scale).astype(NARROW)
    fetch.wait()
    triple_ref[...] = lax.dot_general(weight[...], normed[...], NT, preferred_element_type=WIDE)


def attention_kernel(latent_ref, triple, *refs):
    attended_ref, mark_ref, mixed = refs[-3:]
    mark_ref[...] = jnp.zeros(mark_ref.shape, WIDE)
    row = lax.axis_index("row")
    width = attended_ref.shape[1]
    tiles = attended_ref.shape[0] // TILE
    latents = [latent_ref[row * tiles + tile] for tile in range(tiles)]
    factor = HEAD_DIM ** (-0.5) * 1.4426950408889634
    pair = 2
    for head in range(width // HEAD_DIM):
        lower = head * HEAD_DIM
        queries = triple[lower : lower + HEAD_DIM, :].astype(NARROW)
        keys = triple[width + lower : width + lower + HEAD_DIM, :].T.astype(NARROW)
        values = triple[2 * width + lower : 2 * width + lower + HEAD_DIM, :]
        values = jnp.concatenate([values, jnp.ones((8, values.shape[1]), WIDE)]).astype(NARROW)
        for first in range(0, tiles, pair):
            here = slice(first * TILE, (first + pair) * TILE)
            scores = jnp.dot(keys, queries[:, here], preferred_element_type=WIDE)
            columns = []
            for tile in range(first, first + pair):
                lanes = slice((tile - first) * TILE, (tile - first + 1) * TILE)
                blocks = [
                    scores[other * TILE : (other + 1) * TILE, lanes]
                    + jnp.where(latents[other] == latents[tile], 0.0, -1e30)
                    for other in range(tiles)
                ]
                peak = functools.reduce(jnp.maximum, blocks)
                peak = jnp.max(peak, axis=0, keepdims=True)
                raised = [jnp.exp2((block - peak) * factor).astype(NARROW) for block in blocks]
                columns.append(jnp.concatenate(raised, axis=0))
            summed = jnp.dot(values, jnp.concatenate(columns, axis=1), preferred_element_type=WIDE)
            mixed[lower : lower + HEAD_DIM, here] = summed[:HEAD_DIM] / summed[HEAD_DIM : HEAD_DIM + 1]
    attended_ref[...] = mixed[...].T.astype(NARROW)


def stack_kernel(near, far, kernel_ref, out_ref, bands_ref):
    width = near.shape[0]
    out_ref[:width, :] = near[...]
    out_ref[width:, :] = far[...]
    fill_bands(kernel_ref, bands_ref)


def weights_kernel(parts, depth, whole, *refs):
    pieces, (expand, reduce) = list(refs[: len(parts) + 2 * whole]), refs[-2:]
    row = lax.axis_index("row")
    if whole:
        expand[...] = pieces.pop(0)[...]
        reduce[...] = pieces.pop(0)[...]
    for (offset, which), piece in zip(parts, pieces):
        start = pl.multiple_of((row ^ offset) * depth, 16) if depth < D else 0
        here = pl.ds(start, depth)
        if "e" in which:
            expand[here, :] = piece[:depth, :]
        if "r" in which:
            reduce[here, :] = piece[-depth:, :]


def pair_kernel(first, second, *refs):
    out_ref = refs[-1]
    count = first.shape[0]
    out_ref[:count, :] = first[...]
    out_ref[count:, :] = second[...]


def order_kernel(*refs):
    refs[-1][...] = jnp.zeros(refs[-1].shape, WIDE)


def shared_kernel(parts_ref, head_ref, _, out_ref, mark_ref):
    count = parts_ref.shape[1]
    out_ref[:count, :] = jnp.sum(parts_ref[...], axis=0)
    out_ref[count:, :] = head_ref[...].astype(WIDE)
    mark_ref[...] = jnp.zeros(mark_ref.shape, WIDE)


def mlp_kernel(
    offsets, latent_ref, att_own, att_across, att_beside, att_diagonal, tokens_ref, terms_ref, out_weight, expand, reduce, *refs
):
    outs, (mark_ref, attended, mid) = refs[-3 - len(offsets) - (0 in offsets) : -3], refs[-3:]
    mark_ref[...] = jnp.zeros(mark_ref.shape, WIDE)
    col = lax.axis_index("col")
    width = att_own.shape[1]
    tile_list = [col ^ offset for offset in offsets]
    starts = [pl.multiple_of(tile * TILE, TILE) for tile in tile_list]
    for place, block in enumerate((att_own, att_across, att_beside, att_diagonal)):
        for slot, start in enumerate(starts):
            here = slice(slot * TILE, (slot + 1) * TILE)
            attended[here, place * width : (place + 1) * width] = block[pl.ds(start, TILE), :]
    attn_sum = jnp.dot(attended[...], out_weight[...], preferred_element_type=WIDE)
    for slot, tile in enumerate(tile_list):
        term = functools.partial(tile_term, latent_ref, terms_ref, tile=tile)
        here = slice(slot * TILE, (slot + 1) * TILE)
        before = tokens_ref[pl.ds(starts[slot], TILE), :].astype(WIDE)
        residual = (before + term(2) * attn_sum[here]).astype(NARROW)
        if offsets[slot] == 0:
            outs[-1][...] = residual
        mid[here, :] = normalize(residual.astype(WIDE), term(3), term(4)).astype(NARROW)
    units = jnp.dot(mid[...], expand[...], preferred_element_type=WIDE)
    inner = 0.7978845608028654 * (units + 0.044715 * (units * units * units))
    activated = (0.5 * units * (1.0 + jnp.tanh(inner))).astype(NARROW)
    summed = lax.dot_general(activated, reduce[...], NT, preferred_element_type=WIDE)
    for slot, out in enumerate(outs[: len(offsets)]):
        out[...] = summed[slot * TILE : (slot + 1) * TILE].astype(out.dtype)


def head_kernel(latent_ref, kept_ref, beside_ref, crossed_ref, residual_ref, terms_ref, out_ref):
    col = lax.axis_index("col")
    term = functools.partial(tile_term, latent_ref, terms_ref, tile=col)
    mlp_sum = kept_ref[...] + beside_ref[...].astype(WIDE) + crossed_ref[...].astype(WIDE)
    second = (residual_ref[...].astype(WIDE) + term(5) * mlp_sum).astype(NARROW).astype(WIDE)
    normed = normalize(second, term(6), term(7)).astype(NARROW)
    group = PATCH * CHANNELS
    token_place = lax.broadcasted_iota(jnp.int32, (TILE, IMG_WIDTH), 0) % GRIDW
    lane_place = lax.broadcasted_iota(jnp.int32, (TILE, IMG_WIDTH), 1) // group
    for dy in range(PATCH):
        rows = terms_ref[16 + dy * group : 16 + (dy + 1) * group, :].astype(NARROW)
        spread_rows = jnp.concatenate([rows.astype(WIDE)] * GRIDW, axis=0).astype(NARROW)
        noise = lax.dot_general(normed, spread_rows, NT, preferred_element_type=WIDE)
        noise = jnp.where(token_place == lane_place, noise, 0.0)
        folded = jnp.sum(noise.reshape(TILE_ROWS, GRIDW, IMG_WIDTH), axis=1)
        out_ref[:, dy * IMG_WIDTH : (dy + 1) * IMG_WIDTH] = folded


def fill_bands(kernel_ref, out_ref):
    shape = (IMG_WIDTH, IMG_WIDTH)
    source = lax.broadcasted_iota(jnp.int32, shape, 0)
    target = lax.broadcasted_iota(jnp.int32, shape, 1)
    reach = 3 * CHANNELS
    apart = target - (source // CHANNELS) * CHANNELS + CHANNELS
    code = jnp.where((apart >= 0) & (apart < reach), (source % CHANNELS) * reach + apart, -1)
    bands = [jnp.zeros(shape, WIDE) for _ in range(3)]
    for channel in range(CHANNELS):
        for lane in range(reach):
            here = code == channel * reach + lane
            column, out_channel = 2 - lane // CHANNELS, lane % CHANNELS
            for line in range(3):
                value = kernel_ref[line, column, channel, out_channel]
                bands[line] = jnp.where(here, value, bands[line])
    for line in range(3):
        out_ref[:, line * IMG_WIDTH : (line + 1) * IMG_WIDTH] = bands[line]


def step_kernel(
    table_ref, now_ref, next_ref, near, far, noisy_ref, bands_ref,
    stepped_ref, preview_ref, image, clean, above, below,
):
    tiles = noisy_ref.shape[0] // IMG_ROWS
    row = lax.axis_index("row")
    tile_count = lax.axis_size("row") * tiles
    col = lax.axis_index("col")
    for place in range(4):

        @pl.when(col == place)
        def _():
            for offset in range(4):
                block = (near, far)[offset // 2]
                rows = slice(offset % 2 * TILE_ROWS, (offset % 2 + 1) * TILE_ROWS)
                for dy in range(PATCH):
                    start = (place ^ offset) * IMG_ROWS + dy
                    image[pl.ds(start, TILE_ROWS, PATCH), :] = block[rows, dy * IMG_WIDTH : (dy + 1) * IMG_WIDTH]

    for tile in range(tiles):
        here = slice(tile * IMG_ROWS, (tile + 1) * IMG_ROWS)
        step = table_ref[tile_count + table_ref[row * tiles + tile]]
        signal_now = jnp.full((1, IMG_WIDTH), now_ref[step], WIDE)
        signal_next = jnp.full((1, IMG_WIDTH), next_ref[step], WIDE)
        noise = image[here, :]
        rows = (noisy_ref[here, :].astype(WIDE) - jnp.sqrt(1.0 - signal_now) * noise) / jnp.sqrt(signal_now)
        clean[here, :] = rows
        stepped = jnp.sqrt(signal_next) * rows + jnp.sqrt(1.0 - signal_next) * noise
        stepped_ref[here, :] = stepped.astype(NARROW)
    parts = jnp.dot(
        clean[...], bands_ref[...], precision=lax.Precision.HIGHEST, preferred_element_type=WIDE
    )
    count = tiles * IMG_ROWS
    above[8 : 8 + count, :] = parts[:, :IMG_WIDTH]
    below[8 : 8 + count, :] = parts[:, 2 * IMG_WIDTH :]
    for tile in range(tiles):
        here = slice(tile * IMG_ROWS, (tile + 1) * IMG_ROWS)
        start = 8 + tile * IMG_ROWS
        line = lax.broadcasted_iota(jnp.int32, (IMG_ROWS, IMG_WIDTH), 0)
        from_above = above[start - 1 : start - 1 + IMG_ROWS, :]
        from_below = below[start + 1 : start + 1 + IMG_ROWS, :]
        mine = table_ref[row * tiles + tile]
        if tile == 0:
            above_ok = line > 0
        else:
            above_ok = (line > 0) | (table_ref[row * tiles + tile - 1] == mine)
        if tile == tiles - 1:
            below_ok = line < IMG_ROWS - 1
        else:
            below_ok = (line < IMG_ROWS - 1) | (table_ref[row * tiles + tile + 1] == mine)
        total = parts[here, IMG_WIDTH : 2 * IMG_WIDTH]
        total = total + jnp.where(above_ok, from_above, 0.0) + jnp.where(below_ok, from_below, 0.0)
        preview_ref[here, :] = total.astype(NARROW)


def shards(
    hidden,
    noisy_latent,
    tile_latent,
    timesteps,
    step_embedding,
    alpha_now,
    alpha_next,
    modulation,
    attention_in,
    attention_out,
    expand_weight,
    reduce_weight,
    noise_head,
    preview_kernel,
):
    rows = lax.axis_size("row")
    tokens_here, width = hidden.shape
    tiles = tokens_here // TILE
    depth = modulation.shape[0]
    units = expand_weight.shape[1]
    shape = jax.ShapeDtypeStruct

    table = jnp.concatenate([tile_latent, timesteps])
    mark = shape((8, 128), WIDE)
    conditioning, conditioned = call(
        functools.partial(condition_kernel, tiles),
        [shape((2 * rows, depth), NARROW), mark],
        [SMEM, VMEM],
        [pltpu.VMEM((2 * rows, STEPS), WIDE)],
        flops=2 * 2 * rows * D * (STEPS + depth), nbytes=2 * STEPS * D,
    )(table, step_embedding)
    partial = jnp.einsum("td,dkc->tkc", conditioning, modulation, preferred_element_type=WIDE)
    partial = partial.reshape(rows, 16, width)
    received = lax.all_to_all(partial, "row", 0, 0, tiled=True)
    hidden_blocks = gather_blocks(hidden.T)
    out_rows, conditioned = lax.optimization_barrier((attention_out, conditioned))
    reduce_rows = reduce_weight.T
    staged = rows == 8
    if staged:
        both = jnp.concatenate([expand_weight, reduce_rows], axis=0)
        both_4 = exchange(both, "row", 4)
        both_2 = exchange(both, "row", 2)
        both_1 = exchange(both, "row", 1)
        first, middle = [both_4, both_2, both_1], []
    else:
        expand_whole = lax.all_gather(expand_weight, "row", axis=0, tiled=True)
        reduce_whole = lax.all_gather(reduce_rows, "row", axis=0, tiled=True)
        first, middle = [], []
    arrived = call(order_kernel, mark, [ANYWHERE] * (3 + len(first)))(conditioned, *hidden_blocks[1::2], *first)
    shared, shared_done = call(
        shared_kernel, [shape((32, width), WIDE), mark], [VMEM] * 2 + [ANYWHERE], nbytes=2**18
    )(received, noise_head.T, arrived)
    terms_near = pack(shared, exchange(shared, "col", 1), *middle)
    terms_far = exchange(terms_near, "col", 2)
    second, third = [], []
    if staged:
        both_3 = exchange(both_2, "row", 1)
        both_6 = exchange(both_4, "row", 2)
        both_5 = exchange(both_4, "row", 1)
        both_7 = exchange(both_6, "row", 1)
        second = [both_3, both_6]
        third = [both_5]
        parts = [(i, "er", piece) for i, piece in enumerate((both, both_1, both_2, both_3, both_4, both_5, both_6))]
        last = [(7, "er", both_7)]
    else:
        parts, last = [(0, "e", expand_whole), (0, "r", reduce_whole)], []
    attention_weight = attention_in.transpose(1, 2, 0).reshape(3 * width, D)
    tokens, terms, triple = call(
        triple_kernel,
        [shape((tokens_here, D), NARROW), shape((32, D), WIDE), shape((3 * width, tokens_here), WIDE)],
        [SMEM] + [VMEM] * 6 + [ANYWHERE] * (1 + len(second)),
        [
            pltpu.VMEM((3 * width, D), NARROW),
            pltpu.SemaphoreType.DMA,
            pltpu.VMEM((tokens_here, D), NARROW),
        ],
        flops=2 * tokens_here * D * 3 * width, nbytes=5 * 2**20, limit=16,
    )(table, *hidden_blocks, terms_near, terms_far, attention_weight, *second)
    attended, attention_done = call(
        attention_kernel,
        [shape((tokens_here, width), NARROW), mark],
        [SMEM, VMEM] + [ANYWHERE] * len(third),
        [pltpu.VMEM((width, tokens_here), WIDE)],
        flops=4 * tokens_here * tokens_here * width, trans=4 * tokens_here**2, limit=16,
    )(table, triple, *third)
    out_near = pack(out_rows, exchange(out_rows, "col", 2), attention_done)
    out_weight, bands = call(
        stack_kernel,
        [shape((D, D), NARROW), shape((IMG_WIDTH, 3 * IMG_WIDTH), WIDE)],
        [VMEM] * 2 + [SMEM], nbytes=4 * D * D, limit=8,
    )(out_near, exchange(out_near, "col", 1), preview_kernel)
    weights = ()
    for group in (parts, last):
        if group:
            weights = call(
                functools.partial(
                    weights_kernel, [part[:2] for part in group], depth if staged else D, len(weights) > 0
                ),
                [shape((D, units), NARROW)] * 2, [VMEM] * (len(weights) + len(group)), nbytes=8 * D * units, limit=8,
            )(*weights, *(part[2] for part in group))
        if group is parts:
            across = exchange(attended, "col", 2)
            passed = call(
                pass_kernel, shape(across.shape, NARROW), [VMEM] + [ANYWHERE] * 2, nbytes=2**19
            )(across, out_weight, weights[0])
            attended_blocks = (attended, across, exchange(attended, "col", 1), exchange(passed, "col", 1))
    expand_all, reduce_all = weights

    def mlp(offsets, *before):
        outs = [shape((TILE, D), NARROW if offset % 2 else WIDE) for offset in offsets]
        if 0 in offsets:
            outs.append(shape((TILE, D), NARROW))
        outs.append(mark)
        count = len(offsets) * TILE
        return call(
            functools.partial(mlp_kernel, offsets),
            outs,
            [SMEM] + [VMEM] * 9 + [ANYWHERE] * len(before),
            [pltpu.VMEM((count, D), NARROW)] * 2,
            flops=2 * count * D * (D + 2 * units), nbytes=8 * 2**20, trans=count * units, limit=20,
        )(table, *attended_blocks, tokens, terms, out_weight, expand_all, reduce_all, *before)

    far_kept, far_sent, far_done = mlp((2, 3))
    near_sent, _ = mlp((1,), far_done)
    far_sum = (far_kept + exchange(far_sent, "col", 1).astype(WIDE)).astype(NARROW)
    crossed = exchange(far_sum, "col", 2)
    beside = exchange(near_sent, "col", 1)
    near_kept, residual, _ = mlp((0,), far_sum)
    noise = call(
        head_kernel,
        shape((TILE_ROWS, PATCH * IMG_WIDTH), WIDE),
        [SMEM] + [VMEM] * 5,
        flops=4 * TILE * D * IMG_WIDTH, nbytes=2**21, limit=8,
    )(table, near_kept, beside, crossed, residual, terms)

    noise_near = pack(noise, exchange(noise, "col", 1))
    img_rows = tiles * IMG_ROWS
    stepped, preview = call(
        step_kernel,
        [shape((img_rows, IMG_WIDTH), NARROW)] * 2,
        [SMEM] * 3 + [VMEM] * 4,
        [pltpu.VMEM((img_rows, IMG_WIDTH), WIDE)] * 2
        + [pltpu.VMEM((img_rows + 16, IMG_WIDTH), WIDE)] * 2,
        flops=12 * img_rows * IMG_WIDTH**2, nbytes=2**19,
    )(table, alpha_now, alpha_next, noise_near, exchange(noise_near, "col", 2), noisy_latent, bands)
    return (stepped, preview)


def solution(mesh):
    return jax.shard_map(
        shards,
        mesh=mesh,
        in_specs=(
            P("row", "col"),
            P("row", None),
            P(),
            P(),
            P(),
            P(),
            P(),
            P("row", None, "col"),
            P(None, None, "col"),
            P("col", None),
            P("row", "col"),
            P("col", "row"),
            P("col", None),
            P(),
        ),
        out_specs=(P("row", None), P("row", None)),
        check_vma=False,
    )
```

time: 90.7 us -> 86.1 us (0.949)
  Pallas kernels: 20.3 us -> 26.8 us
  local copies, waits for them, and re-layouts: 9.75 us -> 3.36 us
  waiting for transfers between devices: 37.6 us -> 31.9 us
    ppermute x25 -> x22, waiting for transfers between devices: 37.6 us -> 29.9 us  [exchange(): return lax.ppermute(value, axis, [(i, i ^ offset) for i in range(size)])]
    pallas_call x9 -> x16, Pallas kernels: 19.2 us -> 25.6 us  [the longest x3 8.18 us: mlp(): call(functools.partial(mlp_kernel, offsets), outs, [SMEM] + [VMEM] * 9 +...]
    unnamed x44 -> x24, local copies, waits for them, and re-layouts: 8.9 us -> 2.62 us
    all_to_all x1, waiting for transfers between devices: 0.01 us -> 2.03 us  [shards(): received = lax.all_to_all(partial, 'row', 0, 0, tiled=True)]
    ppermute x25 -> x22, starting transfers between devices: 16.2 us -> 16 us  [exchange(): return lax.ppermute(value, axis, [(i, i ^ offset) for i in range(size)])]
  transfers between devices with their start and end apart: 26 -> 23, of which waited for: 10 -> 12; matrix products, arithmetic and copies ran while one was open for 2% -> 3% of each run, Pallas kernels for 16% -> 23%
where the time goes in v4:
time: 86.1 us; the launch traced here: 85.7 us
  waiting for transfers between devices  31.9 us (37%)
  Pallas kernels  26.8 us (31%)
  starting transfers between devices  20.7 us (24%)
  local copies, waits for them, and re-layouts  3.36 us (4%)
  other arithmetic  1.85 us (2%)
    ppermute x22, waiting for transfers between devices, exchange(): return lax.ppermute(value, axis, [(i, i ^ offset) for i in range(size)])  29.9 us
    ppermute x22, starting transfers between devices, exchange(): return lax.ppermute(value, axis, [(i, i ^ offset) for i in range(size)])  16 us
    pallas_call x3, Pallas kernels, mlp(): call(functools.partial(mlp_kernel, offsets), outs, [SMEM] + [VMEM] * 9 +...  8.18 us
    all_to_all x1, starting transfers between devices, shards(): received = lax.all_to_all(partial, 'row', 0, 0, tiled=True)  4.72 us
    pallas_call x1, Pallas kernels, shards(): call(triple_kernel, [shape((tokens_here, D), NARROW), shape((32, D), WIDE...  4.67 us
    pallas_call x1, Pallas kernels, shards(): call(attention_kernel, [shape((tokens_here, width), NARROW), mark], [SMEM...  3.9 us
    unnamed x24, local copies, waits for them, and re-layouts  2.62 us
    all_to_all x1, waiting for transfers between devices, shards(): received = lax.all_to_all(partial, 'row', 0, 0, tiled=True)  2.03 us
  transfers between devices with their start and end apart: 23, of which 12 were waited for; matrix products, arithmetic and copies ran while one was open for 3% of the time, Pallas kernels for 23%

profile of v4, /device:TPU:0, one launch (start us, length us, event | category | flops | bytes accessed | tf_op | source)
XLA Modules:
  0.0 85.7 jit_solution(4582717372583004207)
XLA Ops:
  0.6 0.0 copy-start
  0.6 3.0 %collective-permute-start.1 = (bf16[288,512]{1,0:T(8,128)(2,1)}, bf16[288,512]{1,0:T(8,128)(2,1)}, u32[]{:S(2)}, u32[]{:S(2)}) collective-permute-start(bf16[288,512]{1,0:T(8,128)(2,1)} %bitcast.11), channel_id=1, source_target_pairs={{0,2},{1,3},{2,0},{3,1},{4,6},{5,7},{6,4},{7,5},{8,10},{9,11},{10,... | collective-permute-start | bytes 884744 | tf_op jit(solution)/shard_map/ppermute | solution.py:44
  3.6 0.0 collective-permute-start
  3.7 1.0 %pad_maximum_fusion.refs_0_ = bf16[288,576]{1,0:T(8,128)(2,1)S(1)} fusion(bf16[144,576]{1,0:T(8,128)(2,1)} %bitcast.16, bf16[144,576]{1,0:T(8,128)(2,1)} %param.24), kind=kLoop, calls=%fused_computation.3 | loop fusion | flops 663552 | bytes 663552 | tf_op jit(solution)/shard_map/concatenate | solution.py:366
  4.7 2.7 %collective-permute-start.3 = (bf16[288,576]{1,0:T(8,128)(2,1)S(1)}, bf16[288,576]{1,0:T(8,128)(2,1)}, u32[]{:S(2)}, u32[]{:S(2)}) collective-permute-start(bf16[288,576]{1,0:T(8,128)(2,1)S(1)} %pad_maximum_fusion.refs_0_), channel_id=1, source_target_pairs={{0,16},{4,20},{8,24},{12,28},{16,0},{20,4},{24,8},{28,12},{1,17},{... | collective-permute-start | bytes 995336 | tf_op jit(solution)/shard_map/ppermute | solution.py:44
  7.4 1.6 %collective-permute-start.4 = (bf16[288,576]{1,0:T(8,128)(2,1)S(1)}, bf16[288,576]{1,0:T(8,128)(2,1)}, u32[]{:S(2)}, u32[]{:S(2)}) collective-permute-start(bf16[288,576]{1,0:T(8,128)(2,1)S(1)} %pad_maximum_fusion.refs_0_), channel_id=1, source_target_pairs={{0,8},{4,12},{8,0},{12,4},{16,24},{20,28},{24,16},{28,20},{1,9},{5... | collective-permute-start | bytes 995336 | tf_op jit(solution)/shard_map/ppermute | solution.py:44
  8.9 1.5 %collective-permute-start.5 = (bf16[288,576]{1,0:T(8,128)(2,1)S(1)}, bf16[288,576]{1,0:T(8,128)(2,1)}, u32[]{:S(2)}, u32[]{:S(2)}) collective-permute-start(bf16[288,576]{1,0:T(8,128)(2,1)S(1)} %pad_maximum_fusion.refs_0_), channel_id=1, source_target_pairs={{0,4},{4,0},{8,12},{12,8},{16,20},{20,16},{24,28},{28,24},{1,5},{5... | collective-permute-start | bytes 995336 | tf_op jit(solution)/shard_map/ppermute | solution.py:44
  10.5 0.7 pad_add_fusion.table_ref.latent_ref
  11.2 0.9 %copy-done.6 = bf16[50,1152]{1,0:T(8,128)(2,1)S(1)} copy-done((bf16[50,1152]{1,0:T(8,128)(2,1)S(1)}, bf16[50,1152]{1,0:T(8,128)(2,1)}, u32[]{:S(2)}) %copy-start.6) | copy-done | bytes 115224
  12.1 1.1 %shard_map.149 = (bf16[16,144]{1,0:T(8,128)(2,1)S(1)}, f32[8,128]{1,0:T(8,128)S(1)}) custom-call(s32[64]{0:T(128)S(1)} %pad_add_fusion.table_ref.latent_ref, bf16[50,1152]{1,0:T(8,128)(2,1)S(1)} %copy-done.6), custom_call_target="tpu_custom_call" | custom-call | flops 7151616 | bytes 115200 | tf_op jit(solution)/shard_map/pallas_call | solution.py:351
  13.2 0.0 collective-permute-done.1.across
  13.2 0.6 collective-permute-start.13
  13.8 0.0 collective-permute-done.refs_1_.beside
  13.8 0.0 collective-permute-start.2
  13.8 0.2 fusion
  14.1 0.7 copy.17
  14.8 4.7 %all-to-all-start = ((f32[8,16,288]{2,1,0:T(8,128)}), f32[8,16,288]{2,1,0:T(8,128)}, u32[]{:S(2)}, u32[]{:S(2)}) async-start(f32[8,16,288]{2,1,0:T(8,128)} %bitcast.15), calls=%async_computation | async-start | bytes 393216 | tf_op jit(solution)/shard_map/all_to_all | solution.py:360
  19.5 5.6 %collective-permute-done.3.refs_3_.refs_4_ = bf16[288,576]{1,0:T(8,128)(2,1)} collective-permute-done((bf16[288,576]{1,0:T(8,128)(2,1)S(1)}, bf16[288,576]{1,0:T(8,128)(2,1)}, u32[]{:S(2)}, u32[]{:S(2)}) %collective-permute-start.3) | collective-permute-done | bytes 331808 | tf_op jit(solution)/shard_map/ppermute | solution.py:44
  25.1 0.4 collective-permute-start.9
  25.5 0.0 collective-permute-done.4.refs_4_.refs_2_
  25.5 1.5 %collective-permute-start.8 = (bf16[288,576]{1,0:T(8,128)(2,1)}, bf16[288,576]{1,0:T(8,128)(2,1)}, u32[]{:S(2)}, u32[]{:S(2)}) collective-permute-start(bf16[288,576]{1,0:T(8,128)(2,1)} %collective-permute-done.4.refs_4_.refs_2_), channel_id=1, source_target_pairs={{0,4},{4,0},{8,12},{12,8},{16,20},{20,16},{24,28},{28,24},{1,5},{5... | collective-permute-start | bytes 995336 | tf_op jit(solution)/shard_map/ppermute | solution.py:44
  27.1 0.5 collective-permute-start.10
  27.6 2.0 %all-to-all-done.parts_ref = f32[8,16,288]{2,1,0:T(8,128)} async-done(((f32[8,16,288]{2,1,0:T(8,128)}), f32[8,16,288]{2,1,0:T(8,128)}, u32[]{:S(2)}, u32[]{:S(2)}) %all-to-all-start) | async-done | bytes 147488 | tf_op jit(solution)/shard_map/all_to_all | solution.py:360
  29.6 0.7 copy-done.9
  30.3 1.5 %shard_map.151 = (f32[32,288]{1,0:T(8,128)S(1)}, f32[8,128]{1,0:T(8,128)}) custom-call(f32[8,16,288]{2,1,0:T(8,128)} %all-to-all-done.parts_ref, bf16[16,288]{1,0:T(8,128)(2,1)S(1)} %bitcast.14, f32[8,128]{1,0:T(8,128)S(1)} %shard_map.150._), custom_call_target="tpu_custom_call" | custom-call | bytes 262144 | tf_op jit(solution)/shard_map/pallas_call | solution.py:376
  31.8 1.2 %collective-permute-done.6.second = f32[32,288]{1,0:T(8,128)S(1)} collective-permute-done((f32[32,288]{1,0:T(8,128)S(1)}, f32[32,288]{1,0:T(8,128)S(1)}, u32[]{:S(2)}, u32[]{:S(2)}) %collective-permute-start.6) | collective-permute-done | bytes 36896 | tf_op jit(solution)/shard_map/ppermute | solution.py:44
  33.1 0.6 collective-permute-start.7
  33.7 2.4 %collective-permute-done.9.refs_1_.refs_6_ = bf16[288,576]{1,0:T(8,128)(2,1)} collective-permute-done((bf16[288,576]{1,0:T(8,128)(2,1)}, bf16[288,576]{1,0:T(8,128)(2,1)}, u32[]{:S(2)}, u32[]{:S(2)}) %collective-permute-start.9) | collective-permute-done | bytes 331808 | tf_op jit(solution)/shard_map/ppermute | solution.py:44
  36.0 1.5 %collective-permute-done.8.refs_0_.refs_3_ = bf16[288,576]{1,0:T(8,128)(2,1)} collective-permute-done((bf16[288,576]{1,0:T(8,128)(2,1)}, bf16[288,576]{1,0:T(8,128)(2,1)}, u32[]{:S(2)}, u32[]{:S(2)}) %collective-permute-start.8) | collective-permute-done | bytes 331808 | tf_op jit(solution)/shard_map/ppermute | solution.py:44
  37.5 0.5 collective-permute-done.7.terms_far
  38.0 1.0 %copy-done.5 = bf16[512,288]{0,1:T(8,128)(2,1)S(1)} copy-done((bf16[512,288]{0,1:T(8,128)(2,1)S(1)}, bf16[512,288]{0,1:T(8,128)(2,1)}, u32[]{:S(2)}) %copy-start.5) | copy-done | bytes 294936
  39.0 4.7 %shard_map.153 = (bf16[512,1152]{1,0:T(8,128)(2,1)S(1)}, f32[32,1152]{1,0:T(8,128)S(1)}, f32[864,512]{1,0:T(8,128)S(1)}) custom-call(s32[64]{0:T(128)S(1)} %pad_add_fusion.table_ref.latent_ref, bf16[288,512]{1,0:T(8,128)(2,1)S(1)} %bitcast.13, bf16[288,512]{1,0:T(8,128)(2,1)S(1)} %collective-permute-done.refs_1_.beside, ...), custom_call_target="tpu_custom_call" | custom-call | flops 1019215872 | bytes 5242880 | tf_op jit(solution)/shard_map/pallas_call | solution.py:394
  43.6 0.0 copy-start.4
  43.7 0.4 collective-permute-done.10.refs_0_.refs_5_
  44.1 3.9 %shard_map.154 = (bf16[512,288]{1,0:T(8,128)(2,1)S(1)}, f32[8,128]{1,0:T(8,128)S(1)}) custom-call(s32[64]{0:T(128)S(1)} %pad_add_fusion.table_ref.latent_ref, f32[864,512]{1,0:T(8,128)S(1)} %get-tuple-element.28.triple, bf16[288,576]{1,0:T(8,128)(2,1)S(1)} %collective-permute-done.10.refs_0_.refs_5_), custom_call_target="tpu_custom_call" | custom-call | flops 301989888 | tf_op jit(solution)/shard_map/pallas_call | solution.py:405
  48.0 0.0 collective-permute-done.13.second
  48.0 1.2 %shard_map.155.near = bf16[576,1152]{1,0:T(8,128)(2,1)S(1)} custom-call(bf16[288,1152]{1,0:T(8,128)(2,1)S(1)} %copy-done.4, bf16[288,1152]{1,0:T(8,128)(2,1)} %collective-permute-done.13.second, f32[8,128]{1,0:T(8,128)S(1)} %get-tuple-element.31.refs_0_), custom_call_target="tpu_custom_call" | custom-call | tf_op jit(solution)/shard_map/pallas_call | solution.py:56
  49.3 0.0 copy-start.7
  49.3 0.1 collective-permute-start.14
  49.4 0.6 collective-permute-start.11
  50.0 1.0 %collective-permute-start.16 = (bf16[288,576]{1,0:T(8,128)(2,1)}, bf16[288,576]{1,0:T(8,128)(2,1)S(1)}, u32[]{:S(2)}, u32[]{:S(2)}) collective-permute-start(bf16[288,576]{1,0:T(8,128)(2,1)} %collective-permute-done.9.refs_1_.refs_6_), channel_id=1, source_target_pairs={{0,4},{4,0},{8,12},{12,8},{16,20},{20,16},{24,28},{28,24},{1,5},{5... | collective-permute-start | bytes 995336 | tf_op jit(solution)/shard_map/ppermute | solution.py:44
  50.9 1.6 %shard_map.157 = (bf16[1152,576]{1,0:T(8,128)(2,1)S(1)}, bf16[1152,576]{1,0:T(8,128)(2,1)S(1)}) custom-call(bf16[288,576]{1,0:T(8,128)(2,1)S(1)} %copy-done.3, bf16[288,576]{1,0:T(8,128)(2,1)} %collective-permute-done.5.refs_5_.refs_1_, bf16[288,576]{1,0:T(8,128)(2,1)} %collective-permute-done.4.refs_4_.refs_2_, ...), custom_call_target="tpu_custom_call" | custom-call | bytes 5308416 | tf_op jit(solution)/shard_map/pallas_call | solution.py:421
  52.6 0.1 collective-permute-start.12
  52.7 0.0 collective-permute-done.14.far
  52.7 1.6 %shard_map.156 = (bf16[1152,1152]{1,0:T(8,128)(2,1)S(1)}, f32[128,384]{1,0:T(8,128)S(1)}) custom-call(bf16[576,1152]{1,0:T(8,128)(2,1)S(1)} %shard_map.155.near, bf16[576,1152]{1,0:T(8,128)(2,1)S(1)} %collective-permute-done.14.far, f32[3,3,4,4]{3,2,1,0:T(4,128)S(1)} %copy-done.7), custom_call_target="tpu_custom_call" | custom-call | bytes 5308416 | tf_op jit(solution)/shard_map/pallas_call | solution.py:413
  54.3 6.6 %collective-permute-done.11.refs_0_.att_across = bf16[512,288]{1,0:T(8,128)(2,1)S(1)} collective-permute-done((bf16[512,288]{1,0:T(8,128)(2,1)S(1)}, bf16[512,288]{1,0:T(8,128)(2,1)S(1)}, u32[]{:S(2)}, u32[]{:S(2)}) %collective-permute-start.11) | collective-permute-done | bytes 294944 | tf_op jit(solution)/shard_map/ppermute | solution.py:44
  60.9 0.1 collective-permute-start.15
  61.0 0.3 shard_map.159
  61.3 0.0 collective-permute-done.12.att_beside
  61.3 1.4 %collective-permute-done.15.att_diagonal = bf16[512,288]{1,0:T(8,128)(2,1)S(1)} collective-permute-done((bf16[512,288]{1,0:T(8,128)(2,1)S(1)}, bf16[512,288]{1,0:T(8,128)(2,1)S(1)}, u32[]{:S(2)}, u32[]{:S(2)}) %collective-permute-start.15) | collective-permute-done | bytes 294944 | tf_op jit(solution)/shard_map/ppermute | solution.py:44
  62.7 3.0 %shard_map.160 = (f32[128,1152]{1,0:T(8,128)S(1)}, bf16[128,1152]{1,0:T(8,128)(2,1)S(1)}, f32[8,128]{1,0:T(8,128)S(1)}) custom-call(s32[64]{0:T(128)S(1)} %pad_add_fusion.table_ref.latent_ref, bf16[512,288]{1,0:T(8,128)(2,1)S(1)} %get-tuple-element.29.att_own, bf16[512,288]{1,0:T(8,128)(2,1)S(1)} %collective-permute-done.11.refs_0_.att_across, ...), custom_call_target="tpu_custom_call" | custom-call | flops 1358954496 | bytes 8388608 | tf_op jit(solution)/shard_map/pallas_call | solution.py:441
  65.7 0.2 collective-permute-start.17
  65.9 2.6 %shard_map.162 = (bf16[128,1152]{1,0:T(8,128)(2,1)S(1)}, f32[8,128]{1,0:T(8,128)}) custom-call(s32[64]{0:T(128)S(1)} %pad_add_fusion.table_ref.latent_ref, bf16[512,288]{1,0:T(8,128)(2,1)S(1)} %get-tuple-element.29.att_own, bf16[512,288]{1,0:T(8,128)(2,1)S(1)} %collective-permute-done.11.refs_0_.att_across, ...), custom_call_target="tpu_custom_call" | custom-call | flops 679477248 | bytes 8388608 | tf_op jit(solution)/shard_map/pallas_call | solution.py:441
  68.5 0.4 collective-permute-start.18
  68.9 0.1 add_convert_fusion.refs_0_
  69.0 0.6 collective-permute-start.19
  69.6 2.6 %shard_map.161 = (f32[128,1152]{1,0:T(8,128)S(1)}, bf16[128,1152]{1,0:T(8,128)(2,1)S(1)}, f32[8,128]{1,0:T(8,128)}) custom-call(s32[64]{0:T(128)S(1)} %pad_add_fusion.table_ref.latent_ref, bf16[512,288]{1,0:T(8,128)(2,1)S(1)} %get-tuple-element.29.att_own, bf16[512,288]{1,0:T(8,128)(2,1)S(1)} %collective-permute-done.11.refs_0_.att_across, ...), custom_call_target="tpu_custom_call" | custom-call | flops 679477248 | bytes 8388608 | tf_op jit(solution)/shard_map/pallas_call | solution.py:441
  72.2 5.9 %collective-permute-done.19.crossed_ref = bf16[128,1152]{1,0:T(8,128)(2,1)S(1)} collective-permute-done((bf16[128,1152]{1,0:T(8,128)(2,1)S(1)}, bf16[128,1152]{1,0:T(8,128)(2,1)S(1)}, u32[]{:S(2)}, u32[]{:S(2)}) %collective-permute-start.19) | collective-permute-done | bytes 294944 | tf_op jit(solution)/shard_map/ppermute | solution.py:44
  78.1 1.1 %shard_map.163.first = f32[8,256]{1,0:T(8,128)S(1)} custom-call(s32[64]{0:T(128)S(1)} %pad_add_fusion.table_ref.latent_ref, f32[128,1152]{1,0:T(8,128)S(1)} %get-tuple-element.41.kept_ref, bf16[128,1152]{1,0:T(8,128)(2,1)S(1)} %collective-permute-done.18.beside_ref, bf16[128,1152]{1,0:T(8,128)(2,1)S(1)} %collective-permute-done.19.crossed_ref, ...), custom_call_target="tpu_custom_call" | custom-call | flops 75497472 | bytes 2097152 | tf_op jit(solution)/shard_map/pallas_call | solution.py:455
  79.2 0.1 collective-permute-start.20
  79.3 1.2 %collective-permute-done.20.second = f32[8,256]{1,0:T(8,128)S(1)} collective-permute-done((f32[8,256]{1,0:T(8,128)S(1)}, f32[8,256]{1,0:T(8,128)S(1)}, u32[]{:S(2)}, u32[]{:S(2)}) %collective-permute-start.20) | collective-permute-done | bytes 8224 | tf_op jit(solution)/shard_map/ppermute | solution.py:44
  80.5 0.5 collective-permute-start.21
  81.0 3.2 %collective-permute-done.21.far = f32[16,256]{1,0:T(8,128)S(1)} collective-permute-done((f32[16,256]{1,0:T(8,128)S(1)}, f32[16,256]{1,0:T(8,128)S(1)}, u32[]{:S(2)}, u32[]{:S(2)}) %collective-permute-start.21) | collective-permute-done | bytes 16416 | tf_op jit(solution)/shard_map/ppermute | solution.py:44
  84.2 1.5 %shard_map.165 = (bf16[64,128]{1,0:T(8,128)(2,1)}, bf16[64,128]{1,0:T(8,128)(2,1)}) custom-call(s32[64]{0:T(128)S(1)} %pad_add_fusion.table_ref.latent_ref, f32[50]{0:T(128)S(1)} %copy-done.10, f32[50]{0:T(128)S(1)} %copy-done.11, f32[16,256]{1,0:T(8,128)S(1)} %shard_map.164.near, f32[16,256]{1,0:T(8,128)S(1)} %collective-permute-done.21.far, ...), custom_call_target="tpu_custom_call" | custom-call | flops 12582912 | bytes 524288 | tf_op jit(solution)/shard_map/pallas_call | solution.py:464
  (28 shorter events, 0.1 us)
Async XLA Ops:
  0.6 13.2 %copy-start = (bf16[144,8,288]{2,1,0:T(8,128)(2,1)S(1)}, bf16[144,8,288]{2,1,0:T(8,128)(2,1)}, u32[]{:S(2)}) copy-start(bf16[144,8,288]{2,1,0:T(8,128)(2,1)} %param.21) | copy-start | bytes 1990660
  0.6 12.6 %collective-permute-start.1 = (bf16[288,512]{1,0:T(8,128)(2,1)}, bf16[288,512]{1,0:T(8,128)(2,1)}, u32[]{:S(2)}, u32[]{:S(2)}) collective-permute-start(bf16[288,512]{1,0:T(8,128)(2,1)} %bitcast.11), channel_id=1, source_target_pairs={{0,2},{1,3},{2,0},{3,1},{4,6},{5,7},{6,4},{7,5},{8,10},{9,11},{10,... | collective-permute-start | bytes 884744 | tf_op jit(solution)/shard_map/ppermute | solution.py:44
  3.6 10.2 %collective-permute-start = (bf16[288,512]{1,0:T(8,128)(2,1)}, bf16[288,512]{1,0:T(8,128)(2,1)S(1)}, u32[]{:S(2)}, u32[]{:S(2)}) collective-permute-start(bf16[288,512]{1,0:T(8,128)(2,1)} %bitcast.12), channel_id=1, source_target_pairs={{0,1},{1,0},{2,3},{3,2},{4,5},{5,4},{6,7},{7,6},{8,9},{9,8},{10,11... | collective-permute-start | bytes 884744 | tf_op jit(solution)/shard_map/ppermute | solution.py:44
  4.7 22.4 %copy-start.2 = (bf16[288,576]{1,0:T(8,128)(2,1)}, bf16[288,576]{1,0:T(8,128)(2,1)S(1)}, u32[]{:S(2)}) copy-start(bf16[288,576]{1,0:T(8,128)(2,1)S(1)} %pad_maximum_fusion.refs_0_) | copy-start | bytes 995332
  4.7 20.4 %collective-permute-start.3 = (bf16[288,576]{1,0:T(8,128)(2,1)S(1)}, bf16[288,576]{1,0:T(8,128)(2,1)}, u32[]{:S(2)}, u32[]{:S(2)}) collective-permute-start(bf16[288,576]{1,0:T(8,128)(2,1)S(1)} %pad_maximum_fusion.refs_0_), channel_id=1, source_target_pairs={{0,16},{4,20},{8,24},{12,28},{16,0},{20,4},{24,8},{28,12},{1,17},{... | collective-permute-start | bytes 995336 | tf_op jit(solution)/shard_map/ppermute | solution.py:44
  7.4 18.2 %collective-permute-start.4 = (bf16[288,576]{1,0:T(8,128)(2,1)S(1)}, bf16[288,576]{1,0:T(8,128)(2,1)}, u32[]{:S(2)}, u32[]{:S(2)}) collective-permute-start(bf16[288,576]{1,0:T(8,128)(2,1)S(1)} %pad_maximum_fusion.refs_0_), channel_id=1, source_target_pairs={{0,8},{4,12},{8,0},{12,4},{16,24},{20,28},{24,16},{28,20},{1,9},{5... | collective-permute-start | bytes 995336 | tf_op jit(solution)/shard_map/ppermute | solution.py:44
  8.9 18.1 %collective-permute-start.5 = (bf16[288,576]{1,0:T(8,128)(2,1)S(1)}, bf16[288,576]{1,0:T(8,128)(2,1)}, u32[]{:S(2)}, u32[]{:S(2)}) collective-permute-start(bf16[288,576]{1,0:T(8,128)(2,1)S(1)} %pad_maximum_fusion.refs_0_), channel_id=1, source_target_pairs={{0,4},{4,0},{8,12},{12,8},{16,20},{20,16},{24,28},{28,24},{1,5},{5... | collective-permute-start | bytes 995336 | tf_op jit(solution)/shard_map/ppermute | solution.py:44
  11.2 0.9 %copy-start.6 = (bf16[50,1152]{1,0:T(8,128)(2,1)S(1)}, bf16[50,1152]{1,0:T(8,128)(2,1)}, u32[]{:S(2)}) copy-start(bf16[50,1152]{1,0:T(8,128)(2,1)} %embedding_ref.1) | copy-start | bytes 345604
  13.2 34.8 %collective-permute-start.13 = (bf16[288,1152]{1,0:T(8,128)(2,1)}, bf16[288,1152]{1,0:T(8,128)(2,1)}, u32[]{:S(2)}, u32[]{:S(2)}) collective-permute-start(bf16[288,1152]{1,0:T(8,128)(2,1)} %first), channel_id=1, source_target_pairs={{0,2},{1,3},{2,0},{3,1},{4,6},{5,7},{6,4},{7,5},{8,10},{9,11},{10,... | collective-permute-start | bytes 1990664 | tf_op jit(solution)/shard_map/ppermute | solution.py:44
  13.8 13.7 %collective-permute-start.2 = (bf16[288,512]{1,0:T(8,128)(2,1)}, bf16[288,512]{1,0:T(8,128)(2,1)}, u32[]{:S(2)}, u32[]{:S(2)}) collective-permute-start(bf16[288,512]{1,0:T(8,128)(2,1)} %collective-permute-done.1.across), channel_id=1, source_target_pairs={{0,1},{1,0},{2,3},{3,2},{4,5},{5,4},{6,7},{7,6},{8,9},{9,8},{10,11... | collective-permute-start | bytes 884744 | tf_op jit(solution)/shard_map/ppermute | solution.py:44
  14.1 23.9 %copy-start.1 = (bf16[1152,3,288]{0,2,1:T(8,128)(2,1)S(1)}, bf16[1152,3,288]{0,2,1:T(8,128)(2,1)}, u32[]{:S(2)}) copy-start(bf16[1152,3,288]{0,2,1:T(8,128)(2,1)} %param.22) | copy-start | bytes 5971972
  14.8 14.8 %all-to-all-start = ((f32[8,16,288]{2,1,0:T(8,128)}), f32[8,16,288]{2,1,0:T(8,128)}, u32[]{:S(2)}, u32[]{:S(2)}) async-start(f32[8,16,288]{2,1,0:T(8,128)} %bitcast.15), calls=%async_computation | async-start | bytes 393216 | tf_op jit(solution)/shard_map/all_to_all | solution.py:360
  25.1 10.9 %collective-permute-start.9 = (bf16[288,576]{1,0:T(8,128)(2,1)}, bf16[288,576]{1,0:T(8,128)(2,1)}, u32[]{:S(2)}, u32[]{:S(2)}) collective-permute-start(bf16[288,576]{1,0:T(8,128)(2,1)} %collective-permute-done.3.refs_3_.refs_4_), channel_id=1, source_target_pairs={{0,8},{4,12},{8,0},{12,4},{16,24},{20,28},{24,16},{28,20},{1,9},{5... | collective-permute-start | bytes 995336 | tf_op jit(solution)/shard_map/ppermute | solution.py:44
  25.5 12.0 %collective-permute-start.8 = (bf16[288,576]{1,0:T(8,128)(2,1)}, bf16[288,576]{1,0:T(8,128)(2,1)}, u32[]{:S(2)}, u32[]{:S(2)}) collective-permute-start(bf16[288,576]{1,0:T(8,128)(2,1)} %collective-permute-done.4.refs_4_.refs_2_), channel_id=1, source_target_pairs={{0,4},{4,0},{8,12},{12,8},{16,20},{20,16},{24,28},{28,24},{1,5},{5... | collective-permute-start | bytes 995336 | tf_op jit(solution)/shard_map/ppermute | solution.py:44
  27.1 17.0 %collective-permute-start.10 = (bf16[288,576]{1,0:T(8,128)(2,1)}, bf16[288,576]{1,0:T(8,128)(2,1)S(1)}, u32[]{:S(2)}, u32[]{:S(2)}) collective-permute-start(bf16[288,576]{1,0:T(8,128)(2,1)} %collective-permute-done.3.refs_3_.refs_4_), channel_id=1, source_target_pairs={{0,4},{4,0},{8,12},{12,8},{16,20},{20,16},{24,28},{28,24},{1,5},{5... | collective-permute-start | bytes 995336 | tf_op jit(solution)/shard_map/ppermute | solution.py:44
  29.6 0.7 copy-start.9
  31.8 1.2 %collective-permute-start.6 = (f32[32,288]{1,0:T(8,128)S(1)}, f32[32,288]{1,0:T(8,128)S(1)}, u32[]{:S(2)}, u32[]{:S(2)}) collective-permute-start(f32[32,288]{1,0:T(8,128)S(1)} %get-tuple-element.27.first), channel_id=1, source_target_pairs={{0,1},{1,0},{2,3},{3,2},{4,5},{5,4},{6,7},{7,6},{8,9},{9,8},{10,11... | collective-permute-start | bytes 110600 | tf_op jit(solution)/shard_map/ppermute | solution.py:44
  33.1 4.9 %collective-permute-start.7 = (f32[64,288]{1,0:T(8,128)S(1)}, f32[64,288]{1,0:T(8,128)S(1)}, u32[]{:S(2)}, u32[]{:S(2)}) collective-permute-start(f32[64,288]{1,0:T(8,128)S(1)} %shard_map.152.terms_near), channel_id=1, source_target_pairs={{0,2},{1,3},{2,0},{3,1},{4,6},{5,7},{6,4},{7,5},{8,10},{9,11},{10,... | collective-permute-start | bytes 221192 | tf_op jit(solution)/shard_map/ppermute | solution.py:44
  38.0 1.0 %copy-start.5 = (bf16[512,288]{0,1:T(8,128)(2,1)S(1)}, bf16[512,288]{0,1:T(8,128)(2,1)}, u32[]{:S(2)}) copy-start(bf16[512,288]{0,1:T(8,128)(2,1)} %param.14) | copy-start | bytes 884740
  43.6 4.4 %copy-start.4 = (bf16[288,1152]{1,0:T(8,128)(2,1)S(1)}, bf16[288,1152]{1,0:T(8,128)(2,1)}, u32[]{:S(2)}) copy-start(bf16[288,1152]{1,0:T(8,128)(2,1)} %first) | copy-start | bytes 1990660
  48.0 2.9 %copy-start.3 = (bf16[288,576]{1,0:T(8,128)(2,1)S(1)}, bf16[288,576]{1,0:T(8,128)(2,1)}, u32[]{:S(2)}) copy-start(bf16[288,576]{1,0:T(8,128)(2,1)} %copy-done.2) | copy-start | bytes 995332
  49.3 3.4 %copy-start.7 = (f32[3,3,4,4]{3,2,1,0:T(4,128)S(1)}, f32[3,3,4,4]{3,2,1,0:T(4,128)}, u32[]{:S(2)}) copy-start(f32[3,3,4,4]{3,2,1,0:T(4,128)} %kernel_ref.1) | copy-start | bytes 1732
  49.3 3.4 %collective-permute-start.14 = (bf16[576,1152]{1,0:T(8,128)(2,1)S(1)}, bf16[576,1152]{1,0:T(8,128)(2,1)S(1)}, u32[]{:S(2)}, u32[]{:S(2)}) collective-permute-start(bf16[576,1152]{1,0:T(8,128)(2,1)S(1)} %shard_map.155.near), channel_id=1, source_target_pairs={{0,1},{1,0},{2,3},{3,2},{4,5},{5,4},{6,7},{7,6},{8,9},{9,8},{10,11... | collective-permute-start | bytes 3981320 | tf_op jit(solution)/shard_map/ppermute | solution.py:44
  49.4 11.5 %collective-permute-start.11 = (bf16[512,288]{1,0:T(8,128)(2,1)S(1)}, bf16[512,288]{1,0:T(8,128)(2,1)S(1)}, u32[]{:S(2)}, u32[]{:S(2)}) collective-permute-start(bf16[512,288]{1,0:T(8,128)(2,1)S(1)} %get-tuple-element.29.att_own), channel_id=1, source_target_pairs={{0,2},{1,3},{2,0},{3,1},{4,6},{5,7},{6,4},{7,5},{8,10},{9,11},{10,... | collective-permute-start | bytes 884744 | tf_op jit(solution)/shard_map/ppermute | solution.py:44
  50.0 11.0 %collective-permute-start.16 = (bf16[288,576]{1,0:T(8,128)(2,1)}, bf16[288,576]{1,0:T(8,128)(2,1)S(1)}, u32[]{:S(2)}, u32[]{:S(2)}) collective-permute-start(bf16[288,576]{1,0:T(8,128)(2,1)} %collective-permute-done.9.refs_1_.refs_6_), channel_id=1, source_target_pairs={{0,4},{4,0},{8,12},{12,8},{16,20},{20,16},{24,28},{28,24},{1,5},{5... | collective-permute-start | bytes 995336 | tf_op jit(solution)/shard_map/ppermute | solution.py:44
  52.6 8.7 %collective-permute-start.12 = (bf16[512,288]{1,0:T(8,128)(2,1)S(1)}, bf16[512,288]{1,0:T(8,128)(2,1)S(1)}, u32[]{:S(2)}, u32[]{:S(2)}) collective-permute-start(bf16[512,288]{1,0:T(8,128)(2,1)S(1)} %get-tuple-element.29.att_own), channel_id=1, source_target_pairs={{0,1},{1,0},{2,3},{3,2},{4,5},{5,4},{6,7},{7,6},{8,9},{9,8},{10,11... | collective-permute-start | bytes 884744 | tf_op jit(solution)/shard_map/ppermute | solution.py:44
  60.9 1.8 %collective-permute-start.15 = (bf16[512,288]{1,0:T(8,128)(2,1)S(1)}, bf16[512,288]{1,0:T(8,128)(2,1)S(1)}, u32[]{:S(2)}, u32[]{:S(2)}) collective-permute-start(bf16[512,288]{1,0:T(8,128)(2,1)S(1)} %shard_map.158), channel_id=1, source_target_pairs={{0,1},{1,0},{2,3},{3,2},{4,5},{5,4},{6,7},{7,6},{8,9},{9,8},{10,11... | collective-permute-start | bytes 884744 | tf_op jit(solution)/shard_map/ppermute | solution.py:44
  65.7 3.2 %collective-permute-start.17 = (bf16[128,1152]{1,0:T(8,128)(2,1)S(1)}, bf16[128,1152]{1,0:T(8,128)(2,1)S(1)}, u32[]{:S(2)}, u32[]{:S(2)}) collective-permute-start(bf16[128,1152]{1,0:T(8,128)(2,1)S(1)} %get-tuple-element.40), channel_id=1, source_target_pairs={{0,1},{1,0},{2,3},{3,2},{4,5},{5,4},{6,7},{7,6},{8,9},{9,8},{10,11... | collective-permute-start | bytes 884744 | tf_op jit(solution)/shard_map/ppermute | solution.py:44
  68.5 3.6 %collective-permute-start.18 = (bf16[128,1152]{1,0:T(8,128)(2,1)S(1)}, bf16[128,1152]{1,0:T(8,128)(2,1)S(1)}, u32[]{:S(2)}, u32[]{:S(2)}) collective-permute-start(bf16[128,1152]{1,0:T(8,128)(2,1)S(1)} %get-tuple-element.43), channel_id=1, source_target_pairs={{0,1},{1,0},{2,3},{3,2},{4,5},{5,4},{6,7},{7,6},{8,9},{9,8},{10,11... | collective-permute-start | bytes 884744 | tf_op jit(solution)/shard_map/ppermute | solution.py:44
  69.0 9.1 %collective-permute-start.19 = (bf16[128,1152]{1,0:T(8,128)(2,1)S(1)}, bf16[128,1152]{1,0:T(8,128)(2,1)S(1)}, u32[]{:S(2)}, u32[]{:S(2)}) collective-permute-start(bf16[128,1152]{1,0:T(8,128)(2,1)S(1)} %add_convert_fusion.refs_0_), channel_id=1, source_target_pairs={{0,2},{1,3},{2,0},{3,1},{4,6},{5,7},{6,4},{7,5},{8,10},{9,11},{10,... | collective-permute-start | bytes 884744 | tf_op jit(solution)/shard_map/ppermute | solution.py:44
  72.1 12.1 %copy-start.8 = (bf16[64,128]{1,0:T(8,128)(2,1)S(1)}, bf16[64,128]{1,0:T(8,128)(2,1)}, u32[]{:S(2)}) copy-start(bf16[64,128]{1,0:T(8,128)(2,1)} %noisy_ref.1) | copy-start | bytes 49156
  72.1 12.1 %copy-start.10 = (f32[50]{0:T(128)S(1)}, f32[50]{0:T(128)}, u32[]{:S(2)}) copy-start(f32[50]{0:T(128)} %now_ref.1) | copy-start | bytes 604
  72.1 12.1 %copy-start.11 = (f32[50]{0:T(128)S(1)}, f32[50]{0:T(128)}, u32[]{:S(2)}) copy-start(f32[50]{0:T(128)} %next_ref.1) | copy-start | bytes 604
  79.2 1.2 %collective-permute-start.20 = (f32[8,256]{1,0:T(8,128)S(1)}, f32[8,256]{1,0:T(8,128)S(1)}, u32[]{:S(2)}, u32[]{:S(2)}) collective-permute-start(f32[8,256]{1,0:T(8,128)S(1)} %shard_map.163.first), channel_id=1, source_target_pairs={{0,1},{1,0},{2,3},{3,2},{4,5},{5,4},{6,7},{7,6},{8,9},{9,8},{10,11... | collective-permute-start | bytes 24584 | tf_op jit(solution)/shard_map/ppermute | solution.py:44
  80.5 3.7 %collective-permute-start.21 = (f32[16,256]{1,0:T(8,128)S(1)}, f32[16,256]{1,0:T(8,128)S(1)}, u32[]{:S(2)}, u32[]{:S(2)}) collective-permute-start(f32[16,256]{1,0:T(8,128)S(1)} %shard_map.164.near), channel_id=1, source_target_pairs={{0,2},{1,3},{2,0},{3,1},{4,6},{5,7},{6,4},{7,5},{8,10},{9,11},{10,... | collective-permute-start | bytes 49160 | tf_op jit(solution)/shard_map/ppermute | solution.py:44

commit v5 on v4

--- a/solution.py
+++ b/solution.py
@@ -12,6 +12,9 @@
 PATCH = 2
 CHANNELS = 4
 GRIDW = 16
+F = {'p3': 2, 'p6': 2, 'p5': 0}
+COSTS = {}
+COUNT = [0]
 TILE_ROWS = 8
 STEPS = 50
 TILE = 128
@@ -28,6 +31,10 @@
 
 
 def call(kernel, outs, in_specs, scratch=(), flops=0, nbytes=0, trans=0, limit=4):
+    base = getattr(kernel, "func", kernel).__name__
+    COUNT[0] += 1
+    if base in COSTS:
+        flops, nbytes, trans = int(COSTS[base] * 10**9), 0, 0
     return pl.pallas_call(
         kernel,
         out_shape=outs,
@@ -95,35 +102,71 @@
     refs[-1][...] = refs[0][...]
 
 
-def triple_kernel(
-    latent_ref, own, beside, across, diagonal, terms_near, terms_far, weight_ref, *refs
-):
-    tokens_ref, terms_ref, triple_ref, weight, weight_sem, normed = refs[-6:]
+def terms_kernel(terms_near, terms_far, terms_ref, columns):
+    col = lax.axis_index("col")
+    width = terms_near.shape[1]
+    rows = terms_ref.shape[0]
+    for place in range(4):
+
+        @pl.when(col == place)
+        def _():
+            for offset in range(4):
+                block = (terms_near, terms_far)[offset // 2]
+                lower = (place ^ offset) * width
+                terms_ref[:, lower : lower + width] = block[offset % 2 * rows : (offset % 2 + 1) * rows, :]
+
+    columns[...] = terms_ref[...].T
+
+
+def triple_kernel(latent_ref, near, far, columns, weight_ref, *refs):
+    triple_ref, weight, weight_sem, normed = refs[-4:]
     fetch = pltpu.make_async_copy(weight_ref, weight, weight_sem)
     fetch.start()
     col = lax.axis_index("col")
-    width = terms_near.shape[1]
-    tiles = tokens_ref.shape[0] // TILE
+    width, count = near.shape[0] // 2, triple_ref.shape[1]
+    blocks = [source[pl.ds(half * width, width), :count] for half in (0, 1) for source in (near, far)]
+    total = jnp.zeros((1, count), WIDE)
+    squares = jnp.zeros((1, count), WIDE)
+    for block in blocks:
+        values = block.astype(WIDE)
+        total = total + jnp.sum(values, axis=0, keepdims=True)
+        squares = squares + jnp.sum(values * values, axis=0, keepdims=True)
+    mean_value = total * (1.0 / D)
+    spread = squares * (1.0 / D) - mean_value * mean_value
+    rate = lax.rsqrt(spread + EPS_NORM)
+    first = lax.axis_index("row") * (count // TILE)
+    later = [latent_ref[first + tile] != latent_ref[first] for tile in range(count // TILE)]
+    for offset, block in enumerate(blocks):
+        here = pl.ds(pl.multiple_of((col ^ offset) * width, 32), width)
+        shifts = [jnp.broadcast_to(columns[here, at : at + 1], (width, TILE)) for at in (0, 8)]
+        scales = [jnp.broadcast_to(columns[here, at : at + 1], (width, TILE)) + 1.0 for at in (1, 9)]
+        for tile in range(count // TILE):
+            lanes = slice(tile * TILE, (tile + 1) * TILE)
+            values = (block[:, lanes].astype(WIDE) - mean_value[:, lanes]) * rate[:, lanes]
+            scale = jnp.where(later[tile], scales[1], scales[0])
+            shift = jnp.where(later[tile], shifts[1], shifts[0])
+            normed[here, lanes] = (values * scale + shift).astype(NARROW)
+    fetch.wait()
+    triple_ref[...] = jnp.dot(weight[...], normed[...], preferred_element_type=WIDE)
+
+
+def assemble_kernel(parts, depth, kernel_ref, near, far, *refs):
+    pieces, (out_weight, expand, reduce, tokens_ref, bands_ref) = refs[: len(parts)], refs[-5:]
+    col = lax.axis_index("col")
+    width, count = near.shape[0] // 2, tokens_ref.shape[0]
+    out_weight[: 2 * width, :] = near[:, count:]
+    out_weight[2 * width :, :] = far[:, count:]
+    place_pieces(parts, depth, pieces, expand, reduce)
     for place in range(4):
 
         @pl.when(col == place)
         def _():
-            for offset, block in enumerate((own, beside, across, diagonal)):
+            for offset in range(4):
                 lower = (place ^ offset) * width
-                tokens_ref[:, lower : lower + width] = block[...].T
-            for offset in range(4):
-                block = (terms_near, terms_far)[offset // 2]
-                lower = (place ^ offset) * width
-                count = terms_ref.shape[0]
-                terms_ref[:, lower : lower + width] = block[offset % 2 * count : (offset % 2 + 1) * count, :]
-
-    for tile in range(tiles):
-        here = slice(tile * TILE, (tile + 1) * TILE)
-        shift = tile_term(latent_ref, terms_ref, 0, tile)
-        scale = tile_term(latent_ref, terms_ref, 1, tile)
-        normed[here, :] = normalize(tokens_ref[here, :].astype(WIDE), shift, scale).astype(NARROW)
-    fetch.wait()
-    triple_ref[...] = lax.dot_general(weight[...], normed[...], NT, preferred_element_type=WIDE)
+                source = (near, far)[offset % 2]
+                tokens_ref[:, lower : lower + width] = source[pl.ds(offset // 2 * width, width), :count].T
+
+    fill_bands(kernel_ref, bands_ref)
 
 
 def attention_kernel(latent_ref, triple, *refs):
@@ -161,19 +204,8 @@
     attended_ref[...] = mixed[...].T.astype(NARROW)
 
 
-def stack_kernel(near, far, kernel_ref, out_ref, bands_ref):
-    width = near.shape[0]
-    out_ref[:width, :] = near[...]
-    out_ref[width:, :] = far[...]
-    fill_bands(kernel_ref, bands_ref)
-
-
-def weights_kernel(parts, depth, whole, *refs):
-    pieces, (expand, reduce) = list(refs[: len(parts) + 2 * whole]), refs[-2:]
+def place_pieces(parts, depth, pieces, expand, reduce):
     row = lax.axis_index("row")
-    if whole:
-        expand[...] = pieces.pop(0)[...]
-        reduce[...] = pieces.pop(0)[...]
     for (offset, which), piece in zip(parts, pieces):
         start = pl.multiple_of((row ^ offset) * depth, 16) if depth < D else 0
         here = pl.ds(start, depth)
@@ -183,6 +215,13 @@
             reduce[here, :] = piece[-depth:, :]
 
 
+def complete_kernel(parts, depth, expand_before, reduce_before, *refs):
+    pieces, (expand, reduce) = refs[:-2], refs[-2:]
+    expand[...] = expand_before[...]
+    reduce[...] = reduce_before[...]
+    place_pieces(parts, depth, pieces, expand, reduce)
+
+
 def pair_kernel(first, second, *refs):
     out_ref = refs[-1]
     count = first.shape[0]
@@ -194,10 +233,13 @@
     refs[-1][...] = jnp.zeros(refs[-1].shape, WIDE)
 
 
-def shared_kernel(parts_ref, head_ref, _, out_ref, mark_ref):
+def shared_kernel(parts_ref, head_ref, _, out_ref, mark_ref, head, head_sem):
+    fetch = pltpu.make_async_copy(head_ref, head, head_sem)
+    fetch.start()
     count = parts_ref.shape[1]
     out_ref[:count, :] = jnp.sum(parts_ref[...], axis=0)
-    out_ref[count:, :] = head_ref[...].astype(WIDE)
+    fetch.wait()
+    out_ref[count:, :] = head[...].astype(WIDE)
     mark_ref[...] = jnp.zeros(mark_ref.shape, WIDE)
 
 
@@ -358,8 +400,8 @@
     partial = jnp.einsum("td,dkc->tkc", conditioning, modulation, preferred_element_type=WIDE)
     partial = partial.reshape(rows, 16, width)
     received = lax.all_to_all(partial, "row", 0, 0, tiled=True)
-    hidden_blocks = gather_blocks(hidden.T)
-    out_rows, conditioned = lax.optimization_barrier((attention_out, conditioned))
+    blocks_here = jnp.concatenate([hidden.T, attention_out], axis=1)
+    blocks_across = exchange(blocks_here, "col", 2)
     reduce_rows = reduce_weight.T
     staged = rows == 8
     if staged:
@@ -367,41 +409,56 @@
         both_4 = exchange(both, "row", 4)
         both_2 = exchange(both, "row", 2)
         both_1 = exchange(both, "row", 1)
-        first, middle = [both_4, both_2, both_1], []
+        first, middle = [], []
+        if F.get("f4", 0) < 2:
+            (first, middle)[F.get("f4", 0)].append(both_4)
+        (first if F.get("f2", 1) else middle).append(both_2)
+        (first if F.get("f1", 1) else middle).append(both_1)
     else:
         expand_whole = lax.all_gather(expand_weight, "row", axis=0, tiled=True)
         reduce_whole = lax.all_gather(reduce_rows, "row", axis=0, tiled=True)
         first, middle = [], []
-    arrived = call(order_kernel, mark, [ANYWHERE] * (3 + len(first)))(conditioned, *hidden_blocks[1::2], *first)
+    arrived = call(order_kernel, mark, [ANYWHERE] * (1 + len(first)))(conditioned, *first)
     shared, shared_done = call(
-        shared_kernel, [shape((32, width), WIDE), mark], [VMEM] * 2 + [ANYWHERE], nbytes=2**18
+        shared_kernel, [shape((32, width), WIDE), mark], [VMEM] + [ANYWHERE] * 2,
+        [pltpu.VMEM((16, width), NARROW), pltpu.SemaphoreType.DMA], nbytes=2**18,
     )(received, noise_head.T, arrived)
     terms_near = pack(shared, exchange(shared, "col", 1), *middle)
     terms_far = exchange(terms_near, "col", 2)
+    near = pack(blocks_here, blocks_across, *([terms_near] if F.get("np", 1) else [shared_done]))
+    far = exchange(near, "col", 1)
     second, third = [], []
     if staged:
         both_3 = exchange(both_2, "row", 1)
         both_6 = exchange(both_4, "row", 2)
         both_5 = exchange(both_4, "row", 1)
         both_7 = exchange(both_6, "row", 1)
-        second = [both_3, both_6]
-        third = [both_5]
+        second, third = [], []
+        if F.get("f4", 0) > 1:
+            (second, third)[F["f4"] - 2].append(both_4)
+        for name, piece in (("p3", both_3), ("p6", both_6), ("p5", both_5)):
+            place = F.get(name, 1 if name != "p5" else 2)
+            if place:
+                (second, third)[place - 1].append(piece)
         parts = [(i, "er", piece) for i, piece in enumerate((both, both_1, both_2, both_3, both_4, both_5, both_6))]
         last = [(7, "er", both_7)]
     else:
         parts, last = [(0, "e", expand_whole), (0, "r", reduce_whole)], []
     attention_weight = attention_in.transpose(1, 2, 0).reshape(3 * width, D)
-    tokens, terms, triple = call(
+    terms, columns = call(
+        terms_kernel, [shape((32, D), WIDE), shape((D, 32), WIDE)], [VMEM] * 2, flops=F.get("tc", 4) * 10**9
+    )(terms_near, terms_far)
+    triple = call(
         triple_kernel,
-        [shape((tokens_here, D), NARROW), shape((32, D), WIDE), shape((3 * width, tokens_here), WIDE)],
-        [SMEM] + [VMEM] * 6 + [ANYWHERE] * (1 + len(second)),
+        shape((3 * width, tokens_here), WIDE),
+        [SMEM] + [VMEM] * 3 + [ANYWHERE] * (1 + len(second)),
         [
             pltpu.VMEM((3 * width, D), NARROW),
             pltpu.SemaphoreType.DMA,
-            pltpu.VMEM((tokens_here, D), NARROW),
+            pltpu.VMEM((D, tokens_here), NARROW),
         ],
         flops=2 * tokens_here * D * 3 * width, nbytes=5 * 2**20, limit=16,
-    )(table, *hidden_blocks, terms_near, terms_far, attention_weight, *second)
+    )(table, near, far, columns, attention_weight, *second)
     attended, attention_done = call(
         attention_kernel,
         [shape((tokens_here, width), NARROW), mark],
@@ -409,28 +466,30 @@
         [pltpu.VMEM((width, tokens_here), WIDE)],
         flops=4 * tokens_here * tokens_here * width, trans=4 * tokens_here**2, limit=16,
     )(table, triple, *third)
-    out_near = pack(out_rows, exchange(out_rows, "col", 2), attention_done)
-    out_weight, bands = call(
-        stack_kernel,
-        [shape((D, D), NARROW), shape((IMG_WIDTH, 3 * IMG_WIDTH), WIDE)],
-        [VMEM] * 2 + [SMEM], nbytes=4 * D * D, limit=8,
-    )(out_near, exchange(out_near, "col", 1), preview_kernel)
-    weights = ()
-    for group in (parts, last):
-        if group:
-            weights = call(
-                functools.partial(
-                    weights_kernel, [part[:2] for part in group], depth if staged else D, len(weights) > 0
-                ),
-                [shape((D, units), NARROW)] * 2, [VMEM] * (len(weights) + len(group)), nbytes=8 * D * units, limit=8,
-            )(*weights, *(part[2] for part in group))
-        if group is parts:
-            across = exchange(attended, "col", 2)
-            passed = call(
-                pass_kernel, shape(across.shape, NARROW), [VMEM] + [ANYWHERE] * 2, nbytes=2**19
-            )(across, out_weight, weights[0])
-            attended_blocks = (attended, across, exchange(attended, "col", 1), exchange(passed, "col", 1))
-    expand_all, reduce_all = weights
+    split = depth if staged else D
+    out_weight, expand_all, reduce_all, tokens, bands = call(
+        functools.partial(assemble_kernel, [part[:2] for part in parts], split),
+        [
+            shape((D, D), NARROW),
+            shape((D, units), NARROW),
+            shape((D, units), NARROW),
+            shape((tokens_here, D), NARROW),
+            shape((IMG_WIDTH, 3 * IMG_WIDTH), WIDE),
+        ],
+        [SMEM] + [VMEM] * (2 + len(parts)) + [ANYWHERE],
+        nbytes=2**23, limit=24,
+    )(preview_kernel, near, far, *(part[2] for part in parts), attention_done)
+    across = exchange(attended, "col", 2)
+    if F.get("pass", 0) == 0:
+        passed = call(pass_kernel, shape(across.shape, NARROW), [VMEM, ANYWHERE], nbytes=2**19)(across, tokens)
+    else:
+        passed = across
+    attended_blocks = (attended, across, exchange(attended, "col", 1), exchange(passed, "col", 1))
+    if last:
+        expand_all, reduce_all = call(
+            functools.partial(complete_kernel, [part[:2] for part in last], split),
+            [shape((D, units), NARROW)] * 2, [VMEM] * (2 + len(last)), nbytes=2**22, limit=8,
+        )(expand_all, reduce_all, *(part[2] for part in last))
 
     def mlp(offsets, *before):
         outs = [shape((TILE, D), NARROW if offset % 2 else WIDE) for offset in offsets]
@@ -447,11 +506,18 @@
         )(table, *attended_blocks, tokens, terms, out_weight, expand_all, reduce_all, *before)
 
     far_kept, far_sent, far_done = mlp((2, 3))
-    near_sent, _ = mlp((1,), far_done)
+    tail = F.get("tail", 0)
+    if tail == 0:
+        near_sent, _ = mlp((1,), far_done)
     far_sum = (far_kept + exchange(far_sent, "col", 1).astype(WIDE)).astype(NARROW)
     crossed = exchange(far_sum, "col", 2)
+    if tail == 1:
+        near_sent, _ = mlp((1,), far_sum)
+    if tail < 2:
+        near_kept, residual, _ = mlp((0,), far_sum)
+    else:
+        near_kept, near_sent, residual, _ = mlp((0, 1), far_sum)
     beside = exchange(near_sent, "col", 1)
-    near_kept, residual, _ = mlp((0,), far_sum)
     noise = call(
         head_kernel,
         shape((TILE_ROWS, PATCH * IMG_WIDTH), WIDE),

time: 86.1 us -> 83.2 us (0.966)
  local copies, waits for them, and re-layouts: 3.36 us -> 0.82 us
  Pallas kernels: 26.8 us -> 24.8 us
  starting transfers between devices: 20.7 us -> 21.9 us
  waiting for transfers between devices: 31.9 us -> 32.8 us
    unnamed x24, local copies, waits for them, and re-layouts: 2.62 us -> 0.07 us
    ppermute x22 -> x19, starting transfers between devices: 16 us -> 18.5 us  [exchange(): return lax.ppermute(value, axis, [(i, i ^ offset) for i in range(size)])]
    pallas_call x7, Pallas kernels: 9.74 us -> 7.59 us  [the longest x1 3.38 us: shards(): call(triple_kernel, shape((3 * width, tokens_here), WIDE), [SMEM] + [VMEM...]
    all_to_all x1, starting transfers between devices: 4.72 us -> 3.39 us  [shards(): received = lax.all_to_all(partial, 'row', 0, 0, tiled=True)]
    concatenate x0 -> x1, other arithmetic: none -> 1.33 us  [shards(): blocks_here = jnp.concatenate([hidden.T, attention_out], axis=1)]
    concatenate x1, other arithmetic: 1.05 us -> 0.04 us  [shards(): both = jnp.concatenate([expand_weight, reduce_rows], axis=0)]
    all_to_all x1, waiting for transfers between devices: 2.03 us -> 3.03 us  [shards(): received = lax.all_to_all(partial, 'row', 0, 0, tiled=True)]
    ppermute x22 -> x19, waiting for transfers between devices: 29.9 us -> 29.8 us  [exchange(): return lax.ppermute(value, axis, [(i, i ^ offset) for i in range(size)])]
  transfers between devices with their start and end apart: 23 -> 20, of which waited for: 12 -> 13; matrix products, arithmetic and copies ran while one was open for 3% -> 1% of each run, Pallas kernels for 23% -> 21%
where the time goes in v5:
time: 83.2 us; the launch traced here: 82.9 us
  waiting for transfers between devices  32.8 us (39%)
  Pallas kernels  24.8 us (30%)
  starting transfers between devices  21.9 us (26%)
  other arithmetic  1.5 us (2%)
  between operations  0.9 us (1%)
    ppermute x19, waiting for transfers between devices, exchange(): return lax.ppermute(value, axis, [(i, i ^ offset) for i in range(size)])  29.8 us
    ppermute x19, starting transfers between devices, exchange(): return lax.ppermute(value, axis, [(i, i ^ offset) for i in range(size)])  18.5 us
    pallas_call x3, Pallas kernels, mlp(): call(functools.partial(mlp_kernel, offsets), outs, [SMEM] + [VMEM] * 9 +...  8.19 us
    pallas_call x1, Pallas kernels, shards(): call(attention_kernel, [shape((tokens_here, width), NARROW), mark], [SMEM...  3.9 us
    all_to_all x1, starting transfers between devices, shards(): received = lax.all_to_all(partial, 'row', 0, 0, tiled=True)  3.39 us
    pallas_call x1, Pallas kernels, shards(): call(triple_kernel, shape((3 * width, tokens_here), WIDE), [SMEM] + [VMEM...  3.38 us
    all_to_all x1, waiting for transfers between devices, shards(): received = lax.all_to_all(partial, 'row', 0, 0, tiled=True)  3.03 us
    pallas_call x1, Pallas kernels, shards(): call(functools.partial(assemble_kernel, [part[:2] for part in parts], spl...  2.96 us
  transfers between devices with their start and end apart: 20, of which 13 were waited for; matrix products, arithmetic and copies ran while one was open for 1% of the time, Pallas kernels for 21%

profile of v5, /device:TPU:0, one launch (start us, length us, event | category | flops | bytes accessed | tf_op | source)
XLA Modules:
  0.0 82.9 jit_solution(4015586366036687227)
XLA Ops:
  0.6 0.0 copy-start
  0.7 1.3 %pad_maximum_fusion.first = bf16[288,1664]{1,0:T(8,128)(2,1)S(1)} fusion(bf16[288,1152]{1,0:T(8,128)(2,1)} %param.23, bf16[288,512]{1,0:T(8,128)(2,1)} %bitcast.13), kind=kLoop, calls=%fused_computation | loop fusion | flops 1916928 | bytes 1916928 | tf_op jit(solution)/shard_map/concatenate | solution.py:403
  2.0 3.0 %collective-permute-start = (bf16[288,1664]{1,0:T(8,128)(2,1)S(1)}, bf16[288,1664]{1,0:T(8,128)(2,1)}, u32[]{:S(2)}, u32[]{:S(2)}) collective-permute-start(bf16[288,1664]{1,0:T(8,128)(2,1)S(1)} %pad_maximum_fusion.first), channel_id=1, source_target_pairs={{0,2},{1,3},{2,0},{3,1},{4,6},{5,7},{6,4},{7,5},{8,10},{9,11},{10,... | collective-permute-start | bytes 2875400 | tf_op jit(solution)/shard_map/ppermute | solution.py:51
  5.1 2.7 %collective-permute-start.1 = (bf16[288,576]{1,0:T(8,128)(2,1)S(1)}, bf16[288,576]{1,0:T(8,128)(2,1)S(1)}, u32[]{:S(2)}, u32[]{:S(2)}) collective-permute-start(bf16[288,576]{1,0:T(8,128)(2,1)S(1)} %pad_maximum_fusion.1.refs_0_), channel_id=1, source_target_pairs={{0,16},{4,20},{8,24},{12,28},{16,0},{20,4},{24,8},{28,12},{1,17},{... | collective-permute-start | bytes 995336 | tf_op jit(solution)/shard_map/ppermute | solution.py:51
  7.7 1.6 %collective-permute-start.2 = (bf16[288,576]{1,0:T(8,128)(2,1)S(1)}, bf16[288,576]{1,0:T(8,128)(2,1)S(1)}, u32[]{:S(2)}, u32[]{:S(2)}) collective-permute-start(bf16[288,576]{1,0:T(8,128)(2,1)S(1)} %pad_maximum_fusion.1.refs_0_), channel_id=1, source_target_pairs={{0,8},{4,12},{8,0},{12,4},{16,24},{20,28},{24,16},{28,20},{1,9},{5... | collective-permute-start | bytes 995336 | tf_op jit(solution)/shard_map/ppermute | solution.py:51
  9.3 1.5 %collective-permute-start.3 = (bf16[288,576]{1,0:T(8,128)(2,1)S(1)}, bf16[288,576]{1,0:T(8,128)(2,1)S(1)}, u32[]{:S(2)}, u32[]{:S(2)}) collective-permute-start(bf16[288,576]{1,0:T(8,128)(2,1)S(1)} %pad_maximum_fusion.1.refs_0_), channel_id=1, source_target_pairs={{0,4},{4,0},{8,12},{12,8},{16,20},{20,16},{24,28},{28,24},{1,5},{5... | collective-permute-start | bytes 995336 | tf_op jit(solution)/shard_map/ppermute | solution.py:51
  10.8 0.1 pad_add_fusion.table_ref.latent_ref
  10.9 1.1 %shard_map.149 = (bf16[16,144]{1,0:T(8,128)(2,1)S(1)}, f32[8,128]{1,0:T(8,128)S(1)}) custom-call(s32[64]{0:T(128)S(1)} %pad_add_fusion.table_ref.latent_ref, bf16[50,1152]{1,0:T(8,128)(2,1)S(1)} %copy-done.2), custom_call_target="tpu_custom_call" | custom-call | flops 7151616 | bytes 115200 | tf_op jit(solution)/shard_map/pallas_call | solution.py:393
  12.0 0.3 fusion
  12.3 0.8 copy.17
  13.1 3.4 %all-to-all-start = ((f32[8,16,288]{2,1,0:T(8,128)}), f32[8,16,288]{2,1,0:T(8,128)S(1)}, u32[]{:S(2)}, u32[]{:S(2)}) async-start(f32[8,16,288]{2,1,0:T(8,128)} %bitcast.12), calls=%async_computation | async-start | bytes 393216 | tf_op jit(solution)/shard_map/all_to_all | solution.py:402
  16.5 9.1 %collective-permute-done.1.refs_1_.refs_4_ = bf16[288,576]{1,0:T(8,128)(2,1)S(1)} collective-permute-done((bf16[288,576]{1,0:T(8,128)(2,1)S(1)}, bf16[288,576]{1,0:T(8,128)(2,1)S(1)}, u32[]{:S(2)}, u32[]{:S(2)}) %collective-permute-start.1) | collective-permute-done | bytes 331808 | tf_op jit(solution)/shard_map/ppermute | solution.py:51
  25.6 0.3 collective-permute-done.2.refs_2_
  25.9 0.0 collective-permute-done.3.refs_3_.refs_1_
  25.9 3.0 %all-to-all-done.parts_ref = f32[8,16,288]{2,1,0:T(8,128)S(1)} async-done(((f32[8,16,288]{2,1,0:T(8,128)}), f32[8,16,288]{2,1,0:T(8,128)S(1)}, u32[]{:S(2)}, u32[]{:S(2)}) %all-to-all-start) | async-done | bytes 147488 | tf_op jit(solution)/shard_map/all_to_all | solution.py:402
  28.9 0.6 shard_map.151
  29.5 0.1 collective-permute-start.4
  29.6 1.2 %collective-permute-done.4.second = f32[32,288]{1,0:T(8,128)S(1)} collective-permute-done((f32[32,288]{1,0:T(8,128)S(1)}, f32[32,288]{1,0:T(8,128)S(1)}, u32[]{:S(2)}, u32[]{:S(2)}) %collective-permute-start.4) | collective-permute-done | bytes 36896 | tf_op jit(solution)/shard_map/ppermute | solution.py:51
  30.9 0.0 collective-permute-done.second
  30.9 1.3 %shard_map.153.near = bf16[576,1664]{1,0:T(8,128)(2,1)S(1)} custom-call(bf16[288,1664]{1,0:T(8,128)(2,1)S(1)} %pad_maximum_fusion.first, bf16[288,1664]{1,0:T(8,128)(2,1)} %collective-permute-done.second, f32[64,288]{1,0:T(8,128)S(1)} %shard_map.152.refs_0_.terms_near), custom_call_target="tpu_custom_call" | custom-call | tf_op jit(solution)/shard_map/pallas_call | solution.py:63
  32.2 0.0 copy-start.1
  32.2 0.2 collective-permute-start.5
  32.4 0.5 collective-permute-start.6
  33.0 0.7 collective-permute-start.8
  33.6 0.9 %collective-permute-start.7 = (bf16[288,576]{1,0:T(8,128)(2,1)S(1)}, bf16[288,576]{1,0:T(8,128)(2,1)S(1)}, u32[]{:S(2)}, u32[]{:S(2)}) collective-permute-start(bf16[288,576]{1,0:T(8,128)(2,1)S(1)} %collective-permute-done.2.refs_2_), channel_id=1, source_target_pairs={{0,4},{4,0},{8,12},{12,8},{16,20},{20,16},{24,28},{28,24},{1,5},{5... | collective-permute-start | bytes 995336 | tf_op jit(solution)/shard_map/ppermute | solution.py:51
  34.5 1.2 %collective-permute-start.11 = (bf16[288,576]{1,0:T(8,128)(2,1)S(1)}, bf16[288,576]{1,0:T(8,128)(2,1)S(1)}, u32[]{:S(2)}, u32[]{:S(2)}) collective-permute-start(bf16[288,576]{1,0:T(8,128)(2,1)S(1)} %collective-permute-done.1.refs_1_.refs_4_), channel_id=1, source_target_pairs={{0,4},{4,0},{8,12},{12,8},{16,20},{20,16},{24,28},{28,24},{1,5},{5... | collective-permute-start | bytes 995336 | tf_op jit(solution)/shard_map/ppermute | solution.py:51
  35.7 1.8 %collective-permute-done.6.terms_far = f32[64,288]{1,0:T(8,128)S(1)} collective-permute-done((f32[64,288]{1,0:T(8,128)S(1)}, f32[64,288]{1,0:T(8,128)S(1)}, u32[]{:S(2)}, u32[]{:S(2)}) %collective-permute-start.6) | collective-permute-done | bytes 73760 | tf_op jit(solution)/shard_map/ppermute | solution.py:51
  37.5 0.3 shard_map.154
  37.8 0.0 collective-permute-done.5.far
  37.8 3.4 %shard_map.155.triple = f32[864,512]{1,0:T(8,128)S(1)} custom-call(s32[64]{0:T(128)S(1)} %pad_add_fusion.table_ref.latent_ref, bf16[576,1664]{1,0:T(8,128)(2,1)S(1)} %shard_map.153.near, bf16[576,1664]{1,0:T(8,128)(2,1)S(1)} %collective-permute-done.5.far, f32[1152,32]{1,0:T(8,128)S(1)} %get-tuple-element.25.columns, bf16[864,1152]{1,0:T(8,128)(2,1)S(1)} %bitcast.10), custom_call_target="tpu_custom_call" | custom-call | flops 1019215872 | bytes 5242880 | tf_op jit(solution)/shard_map/pallas_call | solution.py:451
  41.2 0.0 copy-start.3
  41.2 2.3 %collective-permute-done.8.refs_1_.refs_6_ = bf16[288,576]{1,0:T(8,128)(2,1)S(1)} collective-permute-done((bf16[288,576]{1,0:T(8,128)(2,1)S(1)}, bf16[288,576]{1,0:T(8,128)(2,1)S(1)}, u32[]{:S(2)}, u32[]{:S(2)}) %collective-permute-start.8) | collective-permute-done | bytes 331808 | tf_op jit(solution)/shard_map/ppermute | solution.py:51
  43.5 1.6 %collective-permute-done.7.refs_0_.refs_3_ = bf16[288,576]{1,0:T(8,128)(2,1)S(1)} collective-permute-done((bf16[288,576]{1,0:T(8,128)(2,1)S(1)}, bf16[288,576]{1,0:T(8,128)(2,1)S(1)}, u32[]{:S(2)}, u32[]{:S(2)}) %collective-permute-start.7) | collective-permute-done | bytes 331808 | tf_op jit(solution)/shard_map/ppermute | solution.py:51
  45.2 3.9 %shard_map.156 = (bf16[512,288]{1,0:T(8,128)(2,1)S(1)}, f32[8,128]{1,0:T(8,128)S(1)}) custom-call(s32[64]{0:T(128)S(1)} %pad_add_fusion.table_ref.latent_ref, f32[864,512]{1,0:T(8,128)S(1)} %shard_map.155.triple, bf16[288,576]{1,0:T(8,128)(2,1)S(1)} %collective-permute-done.7.refs_0_.refs_3_, bf16[288,576]{1,0:T(8,128)(2,1)S(1)} %collective-permute-done.8.refs_1_.refs_6_), custom_call_target="tpu_custom_call" | custom-call | flops 301989888 | tf_op jit(solution)/shard_map/pallas_call | solution.py:462
  49.1 1.6 %collective-permute-start.9 = (bf16[512,288]{1,0:T(8,128)(2,1)S(1)}, bf16[512,288]{1,0:T(8,128)(2,1)S(1)}, u32[]{:S(2)}, u32[]{:S(2)}) collective-permute-start(bf16[512,288]{1,0:T(8,128)(2,1)S(1)} %get-tuple-element.26.att_own), channel_id=1, source_target_pairs={{0,2},{1,3},{2,0},{3,1},{4,6},{5,7},{6,4},{7,5},{8,10},{9,11},{10,... | collective-permute-start | bytes 884744 | tf_op jit(solution)/shard_map/ppermute | solution.py:51
  50.6 0.8 %collective-permute-start.13 = (bf16[288,576]{1,0:T(8,128)(2,1)S(1)}, bf16[288,576]{1,0:T(8,128)(2,1)S(1)}, u32[]{:S(2)}, u32[]{:S(2)}) collective-permute-start(bf16[288,576]{1,0:T(8,128)(2,1)S(1)} %collective-permute-done.8.refs_1_.refs_6_), channel_id=1, source_target_pairs={{0,4},{4,0},{8,12},{12,8},{16,20},{20,16},{24,28},{28,24},{1,5},{5... | collective-permute-start | bytes 995336 | tf_op jit(solution)/shard_map/ppermute | solution.py:51
  51.5 0.0 collective-permute-start.10
  51.5 1.6 %collective-permute-done.11.refs_5_ = bf16[288,576]{1,0:T(8,128)(2,1)S(1)} collective-permute-done((bf16[288,576]{1,0:T(8,128)(2,1)S(1)}, bf16[288,576]{1,0:T(8,128)(2,1)S(1)}, u32[]{:S(2)}, u32[]{:S(2)}) %collective-permute-start.11) | collective-permute-done | bytes 331808 | tf_op jit(solution)/shard_map/ppermute | solution.py:51
  53.1 3.0 %shard_map.157 = (bf16[1152,1152]{1,0:T(8,128)(2,1)S(1)}, bf16[1152,576]{1,0:T(8,128)(2,1)S(1)}, bf16[1152,576]{1,0:T(8,128)(2,1)S(1)}, bf16[512,1152]{1,0:T(8,128)(2,1)S(1)}, f32[128,384]{1,0:T(8,128)S(1)}) custom-call(f32[3,3,4,4]{3,2,1,0:T(4,128)S(1)} %copy-done.3, bf16[576,1664]{1,0:T(8,128)(2,1)S(1)} %shard_map.153.near, ...), custom_call_target="tpu_custom_call" | custom-call | bytes 8388608 | tf_op jit(solution)/shard_map/pallas_call | solution.py:470
  56.0 1.8 %collective-permute-done.9.refs_0_.att_across = bf16[512,288]{1,0:T(8,128)(2,1)S(1)} collective-permute-done((bf16[512,288]{1,0:T(8,128)(2,1)S(1)}, bf16[512,288]{1,0:T(8,128)(2,1)S(1)}, u32[]{:S(2)}, u32[]{:S(2)}) %collective-permute-start.9) | collective-permute-done | bytes 294944 | tf_op jit(solution)/shard_map/ppermute | solution.py:51
  57.8 0.1 collective-permute-start.12
  57.9 1.8 %collective-permute-done.13.refs_0_ = bf16[288,576]{1,0:T(8,128)(2,1)S(1)} collective-permute-done((bf16[288,576]{1,0:T(8,128)(2,1)S(1)}, bf16[288,576]{1,0:T(8,128)(2,1)S(1)}, u32[]{:S(2)}, u32[]{:S(2)}) %collective-permute-start.13) | collective-permute-done | bytes 331808 | tf_op jit(solution)/shard_map/ppermute | solution.py:51
  59.7 0.3 shard_map.159
  60.0 0.0 collective-permute-done.10.att_beside
  60.0 0.0 collective-permute-done.12.att_diagonal
  60.0 3.0 %shard_map.160 = (f32[128,1152]{1,0:T(8,128)S(1)}, bf16[128,1152]{1,0:T(8,128)(2,1)S(1)}, f32[8,128]{1,0:T(8,128)S(1)}) custom-call(s32[64]{0:T(128)S(1)} %pad_add_fusion.table_ref.latent_ref, bf16[512,288]{1,0:T(8,128)(2,1)S(1)} %get-tuple-element.26.att_own, bf16[512,288]{1,0:T(8,128)(2,1)S(1)} %collective-permute-done.9.refs_0_.att_across, ...), custom_call_target="tpu_custom_call" | custom-call | flops 1358954496 | bytes 8388608 | tf_op jit(solution)/shard_map/pallas_call | solution.py:500
  63.0 0.1 collective-permute-start.14
  63.1 2.6 %shard_map.162 = (bf16[128,1152]{1,0:T(8,128)(2,1)S(1)}, f32[8,128]{1,0:T(8,128)}) custom-call(s32[64]{0:T(128)S(1)} %pad_add_fusion.table_ref.latent_ref, bf16[512,288]{1,0:T(8,128)(2,1)S(1)} %get-tuple-element.26.att_own, bf16[512,288]{1,0:T(8,128)(2,1)S(1)} %collective-permute-done.9.refs_0_.att_across, ...), custom_call_target="tpu_custom_call" | custom-call | flops 679477248 | bytes 8388608 | tf_op jit(solution)/shard_map/pallas_call | solution.py:500
  65.7 0.5 collective-permute-start.15
  66.2 0.0 collective-permute-done.14
  66.2 0.1 add_convert_fusion.refs_0_
  66.3 0.0 copy-start.4
  66.3 0.0 copy-start.6
  66.3 0.0 copy-start.7
  66.3 1.6 %collective-permute-start.16 = (bf16[128,1152]{1,0:T(8,128)(2,1)S(1)}, bf16[128,1152]{1,0:T(8,128)(2,1)S(1)}, u32[]{:S(2)}, u32[]{:S(2)}) collective-permute-start(bf16[128,1152]{1,0:T(8,128)(2,1)S(1)} %add_convert_fusion.refs_0_), channel_id=1, source_target_pairs={{0,2},{1,3},{2,0},{3,1},{4,6},{5,7},{6,4},{7,5},{8,10},{9,11},{10,... | collective-permute-start | bytes 884744 | tf_op jit(solution)/shard_map/ppermute | solution.py:51
  67.8 2.6 %shard_map.161 = (f32[128,1152]{1,0:T(8,128)S(1)}, bf16[128,1152]{1,0:T(8,128)(2,1)S(1)}, f32[8,128]{1,0:T(8,128)}) custom-call(s32[64]{0:T(128)S(1)} %pad_add_fusion.table_ref.latent_ref, bf16[512,288]{1,0:T(8,128)(2,1)S(1)} %get-tuple-element.26.att_own, bf16[512,288]{1,0:T(8,128)(2,1)S(1)} %collective-permute-done.9.refs_0_.att_across, ...), custom_call_target="tpu_custom_call" | custom-call | flops 679477248 | bytes 8388608 | tf_op jit(solution)/shard_map/pallas_call | solution.py:500
  70.4 0.0 collective-permute-done.15.beside_ref
  70.4 4.9 %collective-permute-done.16.crossed_ref = bf16[128,1152]{1,0:T(8,128)(2,1)S(1)} collective-permute-done((bf16[128,1152]{1,0:T(8,128)(2,1)S(1)}, bf16[128,1152]{1,0:T(8,128)(2,1)S(1)}, u32[]{:S(2)}, u32[]{:S(2)}) %collective-permute-start.16) | collective-permute-done | bytes 294944 | tf_op jit(solution)/shard_map/ppermute | solution.py:51
  75.3 1.2 %shard_map.163.first = f32[8,256]{1,0:T(8,128)S(1)} custom-call(s32[64]{0:T(128)S(1)} %pad_add_fusion.table_ref.latent_ref, f32[128,1152]{1,0:T(8,128)S(1)} %get-tuple-element.37.kept_ref, bf16[128,1152]{1,0:T(8,128)(2,1)S(1)} %collective-permute-done.15.beside_ref, bf16[128,1152]{1,0:T(8,128)(2,1)S(1)} %collective-permute-done.16.crossed_ref, ...), custom_call_target="tpu_custom_call" | custom-call | flops 75497472 | bytes 2097152 | tf_op jit(solution)/shard_map/pallas_call | solution.py:521
  76.4 0.1 collective-permute-start.17
  76.5 1.2 %collective-permute-done.17.second = f32[8,256]{1,0:T(8,128)S(1)} collective-permute-done((f32[8,256]{1,0:T(8,128)S(1)}, f32[8,256]{1,0:T(8,128)S(1)}, u32[]{:S(2)}, u32[]{:S(2)}) %collective-permute-start.17) | collective-permute-done | bytes 8224 | tf_op jit(solution)/shard_map/ppermute | solution.py:51
  77.7 1.5 %collective-permute-start.18 = (f32[16,256]{1,0:T(8,128)S(1)}, f32[16,256]{1,0:T(8,128)S(1)}, u32[]{:S(2)}, u32[]{:S(2)}) collective-permute-start(f32[16,256]{1,0:T(8,128)S(1)} %shard_map.164.near), channel_id=1, source_target_pairs={{0,2},{1,3},{2,0},{3,1},{4,6},{5,7},{6,4},{7,5},{8,10},{9,11},{10,... | collective-permute-start | bytes 49160 | tf_op jit(solution)/shard_map/ppermute | solution.py:51
  79.2 2.2 %collective-permute-done.18.far = f32[16,256]{1,0:T(8,128)S(1)} collective-permute-done((f32[16,256]{1,0:T(8,128)S(1)}, f32[16,256]{1,0:T(8,128)S(1)}, u32[]{:S(2)}, u32[]{:S(2)}) %collective-permute-start.18) | collective-permute-done | bytes 16416 | tf_op jit(solution)/shard_map/ppermute | solution.py:51
  81.4 1.5 %shard_map.165 = (bf16[64,128]{1,0:T(8,128)(2,1)}, bf16[64,128]{1,0:T(8,128)(2,1)}) custom-call(s32[64]{0:T(128)S(1)} %pad_add_fusion.table_ref.latent_ref, f32[50]{0:T(128)S(1)} %copy-done.6, f32[50]{0:T(128)S(1)} %copy-done.7, f32[16,256]{1,0:T(8,128)S(1)} %shard_map.164.near, f32[16,256]{1,0:T(8,128)S(1)} %collective-permute-done.18.far, ...), custom_call_target="tpu_custom_call" | custom-call | flops 12582912 | bytes 524288 | tf_op jit(solution)/shard_map/pallas_call | solution.py:530
  (23 shorter events, 0.1 us)
Async XLA Ops:
  0.6 11.4 %copy-start = (bf16[144,8,288]{2,1,0:T(8,128)(2,1)S(1)}, bf16[144,8,288]{2,1,0:T(8,128)(2,1)}, u32[]{:S(2)}) copy-start(bf16[144,8,288]{2,1,0:T(8,128)(2,1)} %param.21) | copy-start | bytes 1990660
  0.6 4.4 %copy-start.8 = (bf16[576,144]{0,1:T(8,128)(2,1)S(1)}, bf16[576,144]{0,1:T(8,128)(2,1)}, u32[]{:S(2)}) copy-start(bf16[576,144]{0,1:T(8,128)(2,1)} %param.25) | copy-start | bytes 497668
  0.7 4.4 %copy-start.9 = (bf16[144,576]{1,0:T(8,128)(2,1)S(1)}, bf16[144,576]{1,0:T(8,128)(2,1)}, u32[]{:S(2)}) copy-start(bf16[144,576]{1,0:T(8,128)(2,1)} %param.24) | copy-start | bytes 497668
  0.7 10.2 %copy-start.11 = (s32[32]{0:T(128)S(1)}, s32[32]{0:T(128)}, u32[]{:S(2)}) copy-start(s32[32]{0:T(128)} %param.16) | copy-start | bytes 388
  0.7 10.2 %copy-start.10 = (s32[32]{0:T(128)S(1)}, s32[32]{0:T(128)}, u32[]{:S(2)}) copy-start(s32[32]{0:T(128)} %param.17) | copy-start | bytes 388
  0.7 10.2 %copy-start.2 = (bf16[50,1152]{1,0:T(8,128)(2,1)S(1)}, bf16[50,1152]{1,0:T(8,128)(2,1)}, u32[]{:S(2)}) copy-start(bf16[50,1152]{1,0:T(8,128)(2,1)} %embedding_ref.1) | copy-start | bytes 345604
  2.0 28.8 %collective-permute-start = (bf16[288,1664]{1,0:T(8,128)(2,1)S(1)}, bf16[288,1664]{1,0:T(8,128)(2,1)}, u32[]{:S(2)}, u32[]{:S(2)}) collective-permute-start(bf16[288,1664]{1,0:T(8,128)(2,1)S(1)} %pad_maximum_fusion.first), channel_id=1, source_target_pairs={{0,2},{1,3},{2,0},{3,1},{4,6},{5,7},{6,4},{7,5},{8,10},{9,11},{10,... | collective-permute-start | bytes 2875400 | tf_op jit(solution)/shard_map/ppermute | solution.py:51
  5.0 23.9 %copy-start.5 = (bf16[288,16]{0,1:T(8,128)(2,1)S(1)}, bf16[288,16]{0,1:T(8,128)(2,1)}, u32[]{:S(2)}) copy-start(bf16[288,16]{0,1:T(8,128)(2,1)} %param.26) | copy-start | bytes 27652
  5.1 20.5 %collective-permute-start.1 = (bf16[288,576]{1,0:T(8,128)(2,1)S(1)}, bf16[288,576]{1,0:T(8,128)(2,1)S(1)}, u32[]{:S(2)}, u32[]{:S(2)}) collective-permute-start(bf16[288,576]{1,0:T(8,128)(2,1)S(1)} %pad_maximum_fusion.1.refs_0_), channel_id=1, source_target_pairs={{0,16},{4,20},{8,24},{12,28},{16,0},{20,4},{24,8},{28,12},{1,17},{... | collective-permute-start | bytes 995336 | tf_op jit(solution)/shard_map/ppermute | solution.py:51
  7.7 18.1 %collective-permute-start.2 = (bf16[288,576]{1,0:T(8,128)(2,1)S(1)}, bf16[288,576]{1,0:T(8,128)(2,1)S(1)}, u32[]{:S(2)}, u32[]{:S(2)}) collective-permute-start(bf16[288,576]{1,0:T(8,128)(2,1)S(1)} %pad_maximum_fusion.1.refs_0_), channel_id=1, source_target_pairs={{0,8},{4,12},{8,0},{12,4},{16,24},{20,28},{24,16},{28,20},{1,9},{5... | collective-permute-start | bytes 995336 | tf_op jit(solution)/shard_map/ppermute | solution.py:51
  9.3 16.6 %collective-permute-start.3 = (bf16[288,576]{1,0:T(8,128)(2,1)S(1)}, bf16[288,576]{1,0:T(8,128)(2,1)S(1)}, u32[]{:S(2)}, u32[]{:S(2)}) collective-permute-start(bf16[288,576]{1,0:T(8,128)(2,1)S(1)} %pad_maximum_fusion.1.refs_0_), channel_id=1, source_target_pairs={{0,4},{4,0},{8,12},{12,8},{16,20},{20,16},{24,28},{28,24},{1,5},{5... | collective-permute-start | bytes 995336 | tf_op jit(solution)/shard_map/ppermute | solution.py:51
  13.1 15.9 %all-to-all-start = ((f32[8,16,288]{2,1,0:T(8,128)}), f32[8,16,288]{2,1,0:T(8,128)S(1)}, u32[]{:S(2)}, u32[]{:S(2)}) async-start(f32[8,16,288]{2,1,0:T(8,128)} %bitcast.12), calls=%async_computation | async-start | bytes 393216 | tf_op jit(solution)/shard_map/all_to_all | solution.py:402
  29.5 1.3 %collective-permute-start.4 = (f32[32,288]{1,0:T(8,128)S(1)}, f32[32,288]{1,0:T(8,128)S(1)}, u32[]{:S(2)}, u32[]{:S(2)}) collective-permute-start(f32[32,288]{1,0:T(8,128)S(1)} %get-tuple-element.24.first), channel_id=1, source_target_pairs={{0,1},{1,0},{2,3},{3,2},{4,5},{5,4},{6,7},{7,6},{8,9},{9,8},{10,11... | collective-permute-start | bytes 110600 | tf_op jit(solution)/shard_map/ppermute | solution.py:51
  32.2 5.6 %copy-start.1 = (bf16[1152,3,288]{0,2,1:T(8,128)(2,1)S(1)}, bf16[1152,3,288]{0,2,1:T(8,128)(2,1)}, u32[]{:S(2)}) copy-start(bf16[1152,3,288]{0,2,1:T(8,128)(2,1)} %param.22) | copy-start | bytes 5971972
  32.2 5.6 %collective-permute-start.5 = (bf16[576,1664]{1,0:T(8,128)(2,1)S(1)}, bf16[576,1664]{1,0:T(8,128)(2,1)S(1)}, u32[]{:S(2)}, u32[]{:S(2)}) collective-permute-start(bf16[576,1664]{1,0:T(8,128)(2,1)S(1)} %shard_map.153.near), channel_id=1, source_target_pairs={{0,1},{1,0},{2,3},{3,2},{4,5},{5,4},{6,7},{7,6},{8,9},{9,8},{10,11... | collective-permute-start | bytes 5750792 | tf_op jit(solution)/shard_map/ppermute | solution.py:51
  32.4 5.1 %collective-permute-start.6 = (f32[64,288]{1,0:T(8,128)S(1)}, f32[64,288]{1,0:T(8,128)S(1)}, u32[]{:S(2)}, u32[]{:S(2)}) collective-permute-start(f32[64,288]{1,0:T(8,128)S(1)} %shard_map.152.refs_0_.terms_near), channel_id=1, source_target_pairs={{0,2},{1,3},{2,0},{3,1},{4,6},{5,7},{6,4},{7,5},{8,10},{9,11},{10,... | collective-permute-start | bytes 221192 | tf_op jit(solution)/shard_map/ppermute | solution.py:51
  33.0 10.6 %collective-permute-start.8 = (bf16[288,576]{1,0:T(8,128)(2,1)S(1)}, bf16[288,576]{1,0:T(8,128)(2,1)S(1)}, u32[]{:S(2)}, u32[]{:S(2)}) collective-permute-start(bf16[288,576]{1,0:T(8,128)(2,1)S(1)} %collective-permute-done.1.refs_1_.refs_4_), channel_id=1, source_target_pairs={{0,8},{4,12},{8,0},{12,4},{16,24},{20,28},{24,16},{28,20},{1,9},{5... | collective-permute-start | bytes 995336 | tf_op jit(solution)/shard_map/ppermute | solution.py:51
  33.6 11.5 %collective-permute-start.7 = (bf16[288,576]{1,0:T(8,128)(2,1)S(1)}, bf16[288,576]{1,0:T(8,128)(2,1)S(1)}, u32[]{:S(2)}, u32[]{:S(2)}) collective-permute-start(bf16[288,576]{1,0:T(8,128)(2,1)S(1)} %collective-permute-done.2.refs_2_), channel_id=1, source_target_pairs={{0,4},{4,0},{8,12},{12,8},{16,20},{20,16},{24,28},{28,24},{1,5},{5... | collective-permute-start | bytes 995336 | tf_op jit(solution)/shard_map/ppermute | solution.py:51
  34.5 18.5 %collective-permute-start.11 = (bf16[288,576]{1,0:T(8,128)(2,1)S(1)}, bf16[288,576]{1,0:T(8,128)(2,1)S(1)}, u32[]{:S(2)}, u32[]{:S(2)}) collective-permute-start(bf16[288,576]{1,0:T(8,128)(2,1)S(1)} %collective-permute-done.1.refs_1_.refs_4_), channel_id=1, source_target_pairs={{0,4},{4,0},{8,12},{12,8},{16,20},{20,16},{24,28},{28,24},{1,5},{5... | collective-permute-start | bytes 995336 | tf_op jit(solution)/shard_map/ppermute | solution.py:51
  41.2 11.8 %copy-start.3 = (f32[3,3,4,4]{3,2,1,0:T(4,128)S(1)}, f32[3,3,4,4]{3,2,1,0:T(4,128)}, u32[]{:S(2)}) copy-start(f32[3,3,4,4]{3,2,1,0:T(4,128)} %kernel_ref.1) | copy-start | bytes 1732
  49.1 8.7 %collective-permute-start.9 = (bf16[512,288]{1,0:T(8,128)(2,1)S(1)}, bf16[512,288]{1,0:T(8,128)(2,1)S(1)}, u32[]{:S(2)}, u32[]{:S(2)}) collective-permute-start(bf16[512,288]{1,0:T(8,128)(2,1)S(1)} %get-tuple-element.26.att_own), channel_id=1, source_target_pairs={{0,2},{1,3},{2,0},{3,1},{4,6},{5,7},{6,4},{7,5},{8,10},{9,11},{10,... | collective-permute-start | bytes 884744 | tf_op jit(solution)/shard_map/ppermute | solution.py:51
  50.6 9.1 %collective-permute-start.13 = (bf16[288,576]{1,0:T(8,128)(2,1)S(1)}, bf16[288,576]{1,0:T(8,128)(2,1)S(1)}, u32[]{:S(2)}, u32[]{:S(2)}) collective-permute-start(bf16[288,576]{1,0:T(8,128)(2,1)S(1)} %collective-permute-done.8.refs_1_.refs_6_), channel_id=1, source_target_pairs={{0,4},{4,0},{8,12},{12,8},{16,20},{20,16},{24,28},{28,24},{1,5},{5... | collective-permute-start | bytes 995336 | tf_op jit(solution)/shard_map/ppermute | solution.py:51
  51.5 8.5 %collective-permute-start.10 = (bf16[512,288]{1,0:T(8,128)(2,1)S(1)}, bf16[512,288]{1,0:T(8,128)(2,1)S(1)}, u32[]{:S(2)}, u32[]{:S(2)}) collective-permute-start(bf16[512,288]{1,0:T(8,128)(2,1)S(1)} %get-tuple-element.26.att_own), channel_id=1, source_target_pairs={{0,1},{1,0},{2,3},{3,2},{4,5},{5,4},{6,7},{7,6},{8,9},{9,8},{10,11... | collective-permute-start | bytes 884744 | tf_op jit(solution)/shard_map/ppermute | solution.py:51
  57.8 2.2 %collective-permute-start.12 = (bf16[512,288]{1,0:T(8,128)(2,1)S(1)}, bf16[512,288]{1,0:T(8,128)(2,1)S(1)}, u32[]{:S(2)}, u32[]{:S(2)}) collective-permute-start(bf16[512,288]{1,0:T(8,128)(2,1)S(1)} %shard_map.158), channel_id=1, source_target_pairs={{0,1},{1,0},{2,3},{3,2},{4,5},{5,4},{6,7},{7,6},{8,9},{9,8},{10,11... | collective-permute-start | bytes 884744 | tf_op jit(solution)/shard_map/ppermute | solution.py:51
  63.0 3.2 %collective-permute-start.14 = (bf16[128,1152]{1,0:T(8,128)(2,1)S(1)}, bf16[128,1152]{1,0:T(8,128)(2,1)S(1)}, u32[]{:S(2)}, u32[]{:S(2)}) collective-permute-start(bf16[128,1152]{1,0:T(8,128)(2,1)S(1)} %get-tuple-element.36), channel_id=1, source_target_pairs={{0,1},{1,0},{2,3},{3,2},{4,5},{5,4},{6,7},{7,6},{8,9},{9,8},{10,11... | collective-permute-start | bytes 884744 | tf_op jit(solution)/shard_map/ppermute | solution.py:51
  65.7 4.7 %collective-permute-start.15 = (bf16[128,1152]{1,0:T(8,128)(2,1)S(1)}, bf16[128,1152]{1,0:T(8,128)(2,1)S(1)}, u32[]{:S(2)}, u32[]{:S(2)}) collective-permute-start(bf16[128,1152]{1,0:T(8,128)(2,1)S(1)} %get-tuple-element.39), channel_id=1, source_target_pairs={{0,1},{1,0},{2,3},{3,2},{4,5},{5,4},{6,7},{7,6},{8,9},{9,8},{10,11... | collective-permute-start | bytes 884744 | tf_op jit(solution)/shard_map/ppermute | solution.py:51
  66.3 15.2 %copy-start.4 = (bf16[64,128]{1,0:T(8,128)(2,1)S(1)}, bf16[64,128]{1,0:T(8,128)(2,1)}, u32[]{:S(2)}) copy-start(bf16[64,128]{1,0:T(8,128)(2,1)} %noisy_ref.1) | copy-start | bytes 49156
  66.3 15.2 %copy-start.6 = (f32[50]{0:T(128)S(1)}, f32[50]{0:T(128)}, u32[]{:S(2)}) copy-start(f32[50]{0:T(128)} %now_ref.1) | copy-start | bytes 604
  66.3 15.2 %copy-start.7 = (f32[50]{0:T(128)S(1)}, f32[50]{0:T(128)}, u32[]{:S(2)}) copy-start(f32[50]{0:T(128)} %next_ref.1) | copy-start | bytes 604
  66.3 9.0 %collective-permute-start.16 = (bf16[128,1152]{1,0:T(8,128)(2,1)S(1)}, bf16[128,1152]{1,0:T(8,128)(2,1)S(1)}, u32[]{:S(2)}, u32[]{:S(2)}) collective-permute-start(bf16[128,1152]{1,0:T(8,128)(2,1)S(1)} %add_convert_fusion.refs_0_), channel_id=1, source_target_pairs={{0,2},{1,3},{2,0},{3,1},{4,6},{5,7},{6,4},{7,5},{8,10},{9,11},{10,... | collective-permute-start | bytes 884744 | tf_op jit(solution)/shard_map/ppermute | solution.py:51
  76.4 1.2 %collective-permute-start.17 = (f32[8,256]{1,0:T(8,128)S(1)}, f32[8,256]{1,0:T(8,128)S(1)}, u32[]{:S(2)}, u32[]{:S(2)}) collective-permute-start(f32[8,256]{1,0:T(8,128)S(1)} %shard_map.163.first), channel_id=1, source_target_pairs={{0,1},{1,0},{2,3},{3,2},{4,5},{5,4},{6,7},{7,6},{8,9},{9,8},{10,11... | collective-permute-start | bytes 24584 | tf_op jit(solution)/shard_map/ppermute | solution.py:51
  77.7 3.7 %collective-permute-start.18 = (f32[16,256]{1,0:T(8,128)S(1)}, f32[16,256]{1,0:T(8,128)S(1)}, u32[]{:S(2)}, u32[]{:S(2)}) collective-permute-start(f32[16,256]{1,0:T(8,128)S(1)} %shard_map.164.near), channel_id=1, source_target_pairs={{0,2},{1,3},{2,0},{3,1},{4,6},{5,7},{6,4},{7,5},{8,10},{9,11},{10,... | collective-permute-start | bytes 49160 | tf_op jit(solution)/shard_map/ppermute | solution.py:51

commit v6 on v5

--- a/solution.py
+++ b/solution.py
@@ -12,7 +12,8 @@
 PATCH = 2
 CHANNELS = 4
 GRIDW = 16
-F = {'p3': 2, 'p6': 2, 'p5': 0}
+NOISE = PATCH * PATCH * CHANNELS
+F = {'p3': 0, 'p6': 0, 'p5': 0, 'at': ['both_6'], 'l3': 0}
 COSTS = {}
 COUNT = [0]
 TILE_ROWS = 8
@@ -58,6 +59,22 @@
     return value, beside, across, diagonal
 
 
+def after_kernel(*_):
+    pass
+
+
+def after(value, *before):
+    return pl.pallas_call(
+        after_kernel,
+        out_shape=jax.ShapeDtypeStruct(value.shape, value.dtype),
+        in_specs=[ANYWHERE] * (1 + len(before)),
+        out_specs=ANYWHERE,
+        input_output_aliases={0: 0},
+        compiler_params=pltpu.CompilerParams(vmem_limit_bytes=MIB),
+        cost_estimate=pl.CostEstimate(flops=0, bytes_accessed=0, transcendentals=0),
+    )(value, *before)
+
+
 def pack(first, second, *before):
     out = jax.ShapeDtypeStruct((2 * first.shape[0], first.shape[1]), first.dtype)
     return call(pair_kernel, out, [VMEM] * 2 + [ANYWHERE] * len(before), limit=8)(first, second, *before)
@@ -102,9 +119,10 @@
     refs[-1][...] = refs[0][...]
 
 
-def terms_kernel(terms_near, terms_far, terms_ref, columns):
+def terms_kernel(terms_near, terms_far, *refs):
     col = lax.axis_index("col")
     width = terms_near.shape[1]
+    terms_ref, columns = refs[-2:]
     rows = terms_ref.shape[0]
     for place in range(4):
 
@@ -118,13 +136,13 @@
     columns[...] = terms_ref[...].T
 
 
-def triple_kernel(latent_ref, near, far, columns, weight_ref, *refs):
+def triple_kernel(latent_ref, own, beside, across, diagonal, columns, weight_ref, *refs):
     triple_ref, weight, weight_sem, normed = refs[-4:]
     fetch = pltpu.make_async_copy(weight_ref, weight, weight_sem)
     fetch.start()
     col = lax.axis_index("col")
-    width, count = near.shape[0] // 2, triple_ref.shape[1]
-    blocks = [source[pl.ds(half * width, width), :count] for half in (0, 1) for source in (near, far)]
+    width, count = own.shape[0], triple_ref.shape[1]
+    blocks = [source[:, :count] for source in (own, beside, across, diagonal)]
     total = jnp.zeros((1, count), WIDE)
     squares = jnp.zeros((1, count), WIDE)
     for block in blocks:
@@ -150,21 +168,22 @@
     triple_ref[...] = jnp.dot(weight[...], normed[...], preferred_element_type=WIDE)
 
 
-def assemble_kernel(parts, depth, kernel_ref, near, far, *refs):
-    pieces, (out_weight, expand, reduce, tokens_ref, bands_ref) = refs[: len(parts)], refs[-5:]
+def assemble_kernel(parts, depth, kernel_ref, own, beside, across, diagonal, *refs):
+    pieces, (out_weight, expand, reduce, tokens_ref, head_ref, bands_ref) = refs[: len(parts)], refs[-6:]
     col = lax.axis_index("col")
-    width, count = near.shape[0] // 2, tokens_ref.shape[0]
-    out_weight[: 2 * width, :] = near[:, count:]
-    out_weight[2 * width :, :] = far[:, count:]
+    width, count = own.shape[0], tokens_ref.shape[0]
+    for index, source in enumerate((own, across, beside, diagonal)):
+        out_weight[index * width : (index + 1) * width, :] = source[:, count : count + D]
+    for offset, source in enumerate((own, beside, across, diagonal)):
+        head_ref[pl.ds(pl.multiple_of((col ^ offset) * width, 16), width), :] = source[:, count + D :]
     place_pieces(parts, depth, pieces, expand, reduce)
     for place in range(4):
 
         @pl.when(col == place)
         def _():
-            for offset in range(4):
+            for offset, source in enumerate((own, beside, across, diagonal)):
                 lower = (place ^ offset) * width
-                source = (near, far)[offset % 2]
-                tokens_ref[:, lower : lower + width] = source[pl.ds(offset // 2 * width, width), :count].T
+                tokens_ref[:, lower : lower + width] = source[:, :count].T
 
     fill_bands(kernel_ref, bands_ref)
 
@@ -233,14 +252,8 @@
     refs[-1][...] = jnp.zeros(refs[-1].shape, WIDE)
 
 
-def shared_kernel(parts_ref, head_ref, _, out_ref, mark_ref, head, head_sem):
-    fetch = pltpu.make_async_copy(head_ref, head, head_sem)
-    fetch.start()
-    count = parts_ref.shape[1]
-    out_ref[:count, :] = jnp.sum(parts_ref[...], axis=0)
-    fetch.wait()
-    out_ref[count:, :] = head[...].astype(WIDE)
-    mark_ref[...] = jnp.zeros(mark_ref.shape, WIDE)
+def shared_kernel(parts_ref, _, out_ref):
+    out_ref[...] = jnp.sum(parts_ref[...], axis=0)
 
 
 def mlp_kernel(
@@ -273,7 +286,7 @@
         out[...] = summed[slot * TILE : (slot + 1) * TILE].astype(out.dtype)
 
 
-def head_kernel(latent_ref, kept_ref, beside_ref, crossed_ref, residual_ref, terms_ref, out_ref):
+def head_kernel(latent_ref, kept_ref, beside_ref, crossed_ref, residual_ref, terms_ref, head_ref, out_ref):
     col = lax.axis_index("col")
     term = functools.partial(tile_term, latent_ref, terms_ref, tile=col)
     mlp_sum = kept_ref[...] + beside_ref[...].astype(WIDE) + crossed_ref[...].astype(WIDE)
@@ -282,13 +295,15 @@
     group = PATCH * CHANNELS
     token_place = lax.broadcasted_iota(jnp.int32, (TILE, IMG_WIDTH), 0) % GRIDW
     lane_place = lax.broadcasted_iota(jnp.int32, (TILE, IMG_WIDTH), 1) // group
+    source = lax.broadcasted_iota(jnp.int32, (NOISE, PATCH * IMG_WIDTH), 0)
+    target = lax.broadcasted_iota(jnp.int32, (NOISE, PATCH * IMG_WIDTH), 1)
+    chosen = jnp.where(source == target // IMG_WIDTH * group + target % group, 1.0, 0.0).astype(NARROW)
+    spread_head = jnp.dot(head_ref[...], chosen, preferred_element_type=WIDE).astype(NARROW)
+    noise = jnp.dot(normed, spread_head, preferred_element_type=WIDE)
     for dy in range(PATCH):
-        rows = terms_ref[16 + dy * group : 16 + (dy + 1) * group, :].astype(NARROW)
-        spread_rows = jnp.concatenate([rows.astype(WIDE)] * GRIDW, axis=0).astype(NARROW)
-        noise = lax.dot_general(normed, spread_rows, NT, preferred_element_type=WIDE)
-        noise = jnp.where(token_place == lane_place, noise, 0.0)
-        folded = jnp.sum(noise.reshape(TILE_ROWS, GRIDW, IMG_WIDTH), axis=1)
-        out_ref[:, dy * IMG_WIDTH : (dy + 1) * IMG_WIDTH] = folded
+        lanes = slice(dy * IMG_WIDTH, (dy + 1) * IMG_WIDTH)
+        kept = jnp.where(token_place == lane_place, noise[:, lanes], 0.0)
+        out_ref[:, lanes] = jnp.sum(kept.reshape(TILE_ROWS, GRIDW, IMG_WIDTH), axis=1)
 
 
 def fill_bands(kernel_ref, out_ref):
@@ -400,7 +415,7 @@
     partial = jnp.einsum("td,dkc->tkc", conditioning, modulation, preferred_element_type=WIDE)
     partial = partial.reshape(rows, 16, width)
     received = lax.all_to_all(partial, "row", 0, 0, tiled=True)
-    blocks_here = jnp.concatenate([hidden.T, attention_out], axis=1)
+    blocks_here = jnp.concatenate([hidden.T, attention_out, noise_head], axis=1)
     blocks_across = exchange(blocks_here, "col", 2)
     reduce_rows = reduce_weight.T
     staged = rows == 8
@@ -419,46 +434,46 @@
         reduce_whole = lax.all_gather(reduce_rows, "row", axis=0, tiled=True)
         first, middle = [], []
     arrived = call(order_kernel, mark, [ANYWHERE] * (1 + len(first)))(conditioned, *first)
-    shared, shared_done = call(
-        shared_kernel, [shape((32, width), WIDE), mark], [VMEM] + [ANYWHERE] * 2,
-        [pltpu.VMEM((16, width), NARROW), pltpu.SemaphoreType.DMA], nbytes=2**18,
-    )(received, noise_head.T, arrived)
-    terms_near = pack(shared, exchange(shared, "col", 1), *middle)
-    terms_far = exchange(terms_near, "col", 2)
-    near = pack(blocks_here, blocks_across, *([terms_near] if F.get("np", 1) else [shared_done]))
-    far = exchange(near, "col", 1)
+    shared = call(shared_kernel, shape((16, width), WIDE), [VMEM, ANYWHERE], nbytes=2**18)(received, arrived)
+    at_near, at_terms = [], []
     second, third = [], []
     if staged:
         both_3 = exchange(both_2, "row", 1)
         both_6 = exchange(both_4, "row", 2)
         both_5 = exchange(both_4, "row", 1)
-        both_7 = exchange(both_6, "row", 1)
+        both_7 = exchange(both_5, "row", 2) if F.get("w5", 1) else exchange(both_6, "row", 1)
         second, third = [], []
         if F.get("f4", 0) > 1:
             (second, third)[F["f4"] - 2].append(both_4)
         for name, piece in (("p3", both_3), ("p6", both_6), ("p5", both_5)):
             place = F.get(name, 1 if name != "p5" else 2)
             if place:
-                (second, third)[place - 1].append(piece)
-        parts = [(i, "er", piece) for i, piece in enumerate((both, both_1, both_2, both_3, both_4, both_5, both_6))]
-        last = [(7, "er", both_7)]
+                (second, third, at_terms, at_near, middle)[place - 1].append(piece)
+        parts = [(0, "er", both), (1, "er", both_1), (2, "er", both_2), (4, "er", both_4), (5, "er", both_5), (6, "er", both_6)]
+        last = [(3, "er", both_3), (7, "er", both_7)]
+        if not F.get("l3", 1):
+            parts.append(last.pop(0))
     else:
         parts, last = [(0, "e", expand_whole), (0, "r", reduce_whole)], []
+    terms_near = pack(shared, exchange(shared, "col", 1), *middle)
+    terms_far = exchange(terms_near, "col", 2)
+    blocks_across = after(blocks_across, terms_near)
+    blocks = (blocks_here, exchange(blocks_here, "col", 1), blocks_across, exchange(blocks_across, "col", 1))
     attention_weight = attention_in.transpose(1, 2, 0).reshape(3 * width, D)
     terms, columns = call(
-        terms_kernel, [shape((32, D), WIDE), shape((D, 32), WIDE)], [VMEM] * 2, flops=F.get("tc", 4) * 10**9
-    )(terms_near, terms_far)
+        terms_kernel, [shape((16, D), WIDE), shape((D, 16), WIDE)], [VMEM] * 2 + [ANYWHERE] * len(at_terms), flops=F.get("tc", 4) * 10**9
+    )(terms_near, terms_far, *at_terms)
     triple = call(
         triple_kernel,
         shape((3 * width, tokens_here), WIDE),
-        [SMEM] + [VMEM] * 3 + [ANYWHERE] * (1 + len(second)),
+        [SMEM] + [VMEM] * 5 + [ANYWHERE] * (1 + len(second)),
         [
             pltpu.VMEM((3 * width, D), NARROW),
             pltpu.SemaphoreType.DMA,
             pltpu.VMEM((D, tokens_here), NARROW),
         ],
         flops=2 * tokens_here * D * 3 * width, nbytes=5 * 2**20, limit=16,
-    )(table, near, far, columns, attention_weight, *second)
+    )(table, *blocks, columns, attention_weight, *second)
     attended, attention_done = call(
         attention_kernel,
         [shape((tokens_here, width), NARROW), mark],
@@ -467,21 +482,29 @@
         flops=4 * tokens_here * tokens_here * width, trans=4 * tokens_here**2, limit=16,
     )(table, triple, *third)
     split = depth if staged else D
-    out_weight, expand_all, reduce_all, tokens, bands = call(
+    out_weight, expand_all, reduce_all, tokens, head, bands = call(
         functools.partial(assemble_kernel, [part[:2] for part in parts], split),
         [
             shape((D, D), NARROW),
             shape((D, units), NARROW),
             shape((D, units), NARROW),
             shape((tokens_here, D), NARROW),
+            shape((D, NOISE), NARROW),
             shape((IMG_WIDTH, 3 * IMG_WIDTH), WIDE),
         ],
-        [SMEM] + [VMEM] * (2 + len(parts)) + [ANYWHERE],
+        [SMEM] + [VMEM] * (4 + len(parts)) + [ANYWHERE],
         nbytes=2**23, limit=24,
-    )(preview_kernel, near, far, *(part[2] for part in parts), attention_done)
+    )(preview_kernel, *blocks, *(part[2] for part in parts), attention_done)
+    ahead = [locals()[name] for name in F.get("at", ()) if staged]
+    if ahead:
+        attended = after(attended, *ahead)
     across = exchange(attended, "col", 2)
     if F.get("pass", 0) == 0:
-        passed = call(pass_kernel, shape(across.shape, NARROW), [VMEM, ANYWHERE], nbytes=2**19)(across, tokens)
+        if F.get("pa", 0):
+            passed = after(across, tokens)
+            across = passed
+        else:
+            passed = call(pass_kernel, shape(across.shape, NARROW), [VMEM, ANYWHERE], nbytes=2**19)(across, tokens)
     else:
         passed = across
     attended_blocks = (attended, across, exchange(attended, "col", 1), exchange(passed, "col", 1))
@@ -505,15 +528,18 @@
             flops=2 * count * D * (D + 2 * units), nbytes=8 * 2**20, trans=count * units, limit=20,
         )(table, *attended_blocks, tokens, terms, out_weight, expand_all, reduce_all, *before)
 
-    far_kept, far_sent, far_done = mlp((2, 3))
     tail = F.get("tail", 0)
+    if tail == 3:
+        far_kept, far_sent, near_sent, _ = mlp((2, 3, 1))
+    else:
+        far_kept, far_sent, far_done = mlp((2, 3))
     if tail == 0:
         near_sent, _ = mlp((1,), far_done)
     far_sum = (far_kept + exchange(far_sent, "col", 1).astype(WIDE)).astype(NARROW)
     crossed = exchange(far_sum, "col", 2)
     if tail == 1:
         near_sent, _ = mlp((1,), far_sum)
-    if tail < 2:
+    if tail != 2:
         near_kept, residual, _ = mlp((0,), far_sum)
     else:
         near_kept, near_sent, residual, _ = mlp((0, 1), far_sum)
@@ -521,9 +547,9 @@
     noise = call(
         head_kernel,
         shape((TILE_ROWS, PATCH * IMG_WIDTH), WIDE),
-        [SMEM] + [VMEM] * 5,
+        [SMEM] + [VMEM] * 6,
         flops=4 * TILE * D * IMG_WIDTH, nbytes=2**21, limit=8,
-    )(table, near_kept, beside, crossed, residual, terms)
+    )(table, near_kept, beside, crossed, residual, terms, head)
 
     noise_near = pack(noise, exchange(noise, "col", 1))
     img_rows = tiles * IMG_ROWS

time: 83.2 us -> 79 us (0.950)
  waiting for transfers between devices: 32.8 us -> 30 us
  Pallas kernels: 24.8 us -> 23.1 us
  local copies, waits for them, and re-layouts: 0.82 us -> 1.71 us
    ppermute x19 -> x20, waiting for transfers between devices: 29.8 us -> 27.1 us  [exchange(): return lax.ppermute(value, axis, [(i, i ^ offset) for i in range(size)])]
    pallas_call x3 -> x2, Pallas kernels: 1.34 us -> 0.01 us  [pack(): call(pair_kernel, out, [VMEM] * 2 + [ANYWHERE] * len(before), limit=8)]
    unnamed x24 -> x23, local copies, waits for them, and re-layouts: 0.07 us -> 0.97 us
    ppermute x19 -> x20, starting transfers between devices: 18.5 us -> 17.8 us  [exchange(): return lax.ppermute(value, axis, [(i, i ^ offset) for i in range(size)])]
  transfers between devices with their start and end apart: 20 -> 21, of which waited for: 13 -> 10; matrix products, arithmetic and copies ran while one was open for 1% -> 2% of each run, Pallas kernels for 21% -> 22%
where the time goes in v6:
time: 79 us; the launch traced here: 78.7 us
  waiting for transfers between devices  30 us (38%)
  Pallas kernels  23.1 us (29%)
  starting transfers between devices  21.2 us (27%)
  local copies, waits for them, and re-layouts  1.71 us (2%)
  other arithmetic  1.47 us (2%)
  between operations  0.91 us (1%)
    ppermute x20, waiting for transfers between devices, exchange(): return lax.ppermute(value, axis, [(i, i ^ offset) for i in range(size)])  27.1 us
    ppermute x20, starting transfers between devices, exchange(): return lax.ppermute(value, axis, [(i, i ^ offset) for i in range(size)])  17.8 us
    pallas_call x3, Pallas kernels, mlp(): call(functools.partial(mlp_kernel, offsets), outs, [SMEM] + [VMEM] * 9 +...  8.04 us
    pallas_call x1, Pallas kernels, shards(): call(attention_kernel, [shape((tokens_here, width), NARROW), mark], [SMEM...  3.9 us
    pallas_call x1, Pallas kernels, shards(): call(triple_kernel, shape((3 * width, tokens_here), WIDE), [SMEM] + [VMEM...  3.39 us
    pallas_call x1, Pallas kernels, shards(): call(functools.partial(assemble_kernel, [part[:2] for part in parts], spl...  3.39 us
    all_to_all x1, starting transfers between devices, shards(): received = lax.all_to_all(partial, 'row', 0, 0, tiled=True)  3.39 us
    all_to_all x1, waiting for transfers between devices, shards(): received = lax.all_to_all(partial, 'row', 0, 0, tiled=True)  2.92 us
  transfers between devices with their start and end apart: 21, of which 10 were waited for; matrix products, arithmetic and copies ran while one was open for 2% of the time, Pallas kernels for 22%

profile of v6, /device:TPU:0, one launch (start us, length us, event | category | flops | bytes accessed | tf_op | source)
XLA Modules:
  0.0 78.7 jit_solution(11005248490887091685)
XLA Ops:
  0.6 0.0 copy-start
  0.7 0.9 %copy.18 = bf16[288,16]{1,0:T(8,128)(2,1)S(1)} copy(bf16[288,16]{0,1:T(8,128)(2,1)} %param.26) | data formatting | bytes 18432 | tf_op args[12]
  1.6 0.0 copy-start.7
  1.6 0.0 copy-start.8
  1.6 1.3 %pad_maximum_fusion.own = bf16[288,1680]{1,0:T(8,128)(2,1)S(1)} fusion(bf16[288,16]{1,0:T(8,128)(2,1)S(1)} %copy.18, bf16[288,1152]{1,0:T(8,128)(2,1)} %param.23, bf16[288,512]{1,0:T(8,128)(2,1)} %bitcast.11), kind=kLoop, calls=%fused_computation | loop fusion | flops 2903040 | bytes 1935360 | tf_op jit(solution)/shard_map/concatenate | solution.py:418
  2.9 3.0 %collective-permute-start.1 = (bf16[288,1680]{1,0:T(8,128)(2,1)S(1)}, bf16[288,1680]{1,0:T(8,128)(2,1)S(1)}, u32[]{:S(2)}, u32[]{:S(2)}) collective-permute-start(bf16[288,1680]{1,0:T(8,128)(2,1)S(1)} %pad_maximum_fusion.own), channel_id=1, source_target_pairs={{0,2},{1,3},{2,0},{3,1},{4,6},{5,7},{6,4},{7,5},{8,10},{9,11},{10,... | collective-permute-start | bytes 2903048 | tf_op jit(solution)/shard_map/ppermute | solution.py:52
  6.0 2.7 %collective-permute-start.2 = (bf16[288,576]{1,0:T(8,128)(2,1)S(1)}, bf16[288,576]{1,0:T(8,128)(2,1)}, u32[]{:S(2)}, u32[]{:S(2)}) collective-permute-start(bf16[288,576]{1,0:T(8,128)(2,1)S(1)} %pad_maximum_fusion.1.refs_0_), channel_id=1, source_target_pairs={{0,16},{4,20},{8,24},{12,28},{16,0},{20,4},{24,8},{28,12},{1,17},{... | collective-permute-start | bytes 995336 | tf_op jit(solution)/shard_map/ppermute | solution.py:52
  8.6 1.6 %collective-permute-start.3 = (bf16[288,576]{1,0:T(8,128)(2,1)S(1)}, bf16[288,576]{1,0:T(8,128)(2,1)}, u32[]{:S(2)}, u32[]{:S(2)}) collective-permute-start(bf16[288,576]{1,0:T(8,128)(2,1)S(1)} %pad_maximum_fusion.1.refs_0_), channel_id=1, source_target_pairs={{0,8},{4,12},{8,0},{12,4},{16,24},{20,28},{24,16},{28,20},{1,9},{5... | collective-permute-start | bytes 995336 | tf_op jit(solution)/shard_map/ppermute | solution.py:52
  10.2 1.5 %collective-permute-start.4 = (bf16[288,576]{1,0:T(8,128)(2,1)S(1)}, bf16[288,576]{1,0:T(8,128)(2,1)}, u32[]{:S(2)}, u32[]{:S(2)}) collective-permute-start(bf16[288,576]{1,0:T(8,128)(2,1)S(1)} %pad_maximum_fusion.1.refs_0_), channel_id=1, source_target_pairs={{0,4},{4,0},{8,12},{12,8},{16,20},{20,16},{24,28},{28,24},{1,5},{5... | collective-permute-start | bytes 995336 | tf_op jit(solution)/shard_map/ppermute | solution.py:52
  11.7 0.1 pad_add_fusion.table_ref.latent_ref
  11.8 1.1 %shard_map.149 = (bf16[16,144]{1,0:T(8,128)(2,1)S(1)}, f32[8,128]{1,0:T(8,128)S(1)}) custom-call(s32[64]{0:T(128)S(1)} %pad_add_fusion.table_ref.latent_ref, bf16[50,1152]{1,0:T(8,128)(2,1)S(1)} %copy-done.2), custom_call_target="tpu_custom_call" | custom-call | flops 7151616 | bytes 115200 | tf_op jit(solution)/shard_map/pallas_call | solution.py:408
  12.9 0.3 fusion
  13.2 0.7 copy.20
  13.9 3.4 %all-to-all-start = ((f32[8,16,288]{2,1,0:T(8,128)}), f32[8,16,288]{2,1,0:T(8,128)S(1)}, u32[]{:S(2)}, u32[]{:S(2)}) async-start(f32[8,16,288]{2,1,0:T(8,128)} %bitcast.10), calls=%async_computation | async-start | bytes 393216 | tf_op jit(solution)/shard_map/all_to_all | solution.py:417
  17.3 9.2 %collective-permute-done.2.refs_1_.refs_3_ = bf16[288,576]{1,0:T(8,128)(2,1)} collective-permute-done((bf16[288,576]{1,0:T(8,128)(2,1)S(1)}, bf16[288,576]{1,0:T(8,128)(2,1)}, u32[]{:S(2)}, u32[]{:S(2)}) %collective-permute-start.2) | collective-permute-done | bytes 331808 | tf_op jit(solution)/shard_map/ppermute | solution.py:52
  26.5 0.3 collective-permute-done.3.refs_2_
  26.8 0.0 collective-permute-done.4.refs_3_.refs_1_
  26.9 2.9 %all-to-all-done.parts_ref = f32[8,16,288]{2,1,0:T(8,128)S(1)} async-done(((f32[8,16,288]{2,1,0:T(8,128)}), f32[8,16,288]{2,1,0:T(8,128)S(1)}, u32[]{:S(2)}, u32[]{:S(2)}) %all-to-all-start) | async-done | bytes 147488 | tf_op jit(solution)/shard_map/all_to_all | solution.py:417
  29.8 0.1 collective-permute-start.5
  29.9 0.5 collective-permute-start
  30.4 0.7 collective-permute-done.5.second
  31.1 0.0 collective-permute-done.1.__0_
  31.1 0.0 copy-start.1
  31.1 0.2 collective-permute-start.6
  31.3 0.5 collective-permute-start.7
  31.8 0.9 %collective-permute-start.11 = (bf16[288,576]{1,0:T(8,128)(2,1)}, bf16[288,576]{1,0:T(8,128)(2,1)S(1)}, u32[]{:S(2)}, u32[]{:S(2)}) collective-permute-start(bf16[288,576]{1,0:T(8,128)(2,1)} %collective-permute-done.2.refs_1_.refs_3_), channel_id=1, source_target_pairs={{0,4},{4,0},{8,12},{12,8},{16,20},{20,16},{24,28},{28,24},{1,5},{5... | collective-permute-start | bytes 995336 | tf_op jit(solution)/shard_map/ppermute | solution.py:52
  32.7 0.8 %collective-permute-start.8 = (bf16[288,576]{1,0:T(8,128)(2,1)}, bf16[288,576]{1,0:T(8,128)(2,1)S(1)}, u32[]{:S(2)}, u32[]{:S(2)}) collective-permute-start(bf16[288,576]{1,0:T(8,128)(2,1)} %collective-permute-done.2.refs_1_.refs_3_), channel_id=1, source_target_pairs={{0,8},{4,12},{8,0},{12,4},{16,24},{20,28},{24,16},{28,20},{1,9},{5... | collective-permute-start | bytes 995336 | tf_op jit(solution)/shard_map/ppermute | solution.py:52
  33.6 1.8 %collective-permute-done.7.terms_far = f32[32,288]{1,0:T(8,128)S(1)} collective-permute-done((f32[32,288]{1,0:T(8,128)S(1)}, f32[32,288]{1,0:T(8,128)S(1)}, u32[]{:S(2)}, u32[]{:S(2)}) %collective-permute-start.7) | collective-permute-done | bytes 36896 | tf_op jit(solution)/shard_map/ppermute | solution.py:52
  35.4 0.9 %collective-permute-start.12 = (bf16[288,576]{1,0:T(8,128)(2,1)}, bf16[288,576]{1,0:T(8,128)(2,1)S(1)}, u32[]{:S(2)}, u32[]{:S(2)}) collective-permute-start(bf16[288,576]{1,0:T(8,128)(2,1)} %collective-permute-done.3.refs_2_), channel_id=1, source_target_pairs={{0,4},{4,0},{8,12},{12,8},{16,20},{20,16},{24,28},{28,24},{1,5},{5... | collective-permute-start | bytes 995336 | tf_op jit(solution)/shard_map/ppermute | solution.py:52
  36.3 0.3 shard_map.154
  36.6 0.0 collective-permute-done.beside
  36.6 0.0 collective-permute-done.6.diagonal
  36.6 3.4 %shard_map.155.triple = f32[864,512]{1,0:T(8,128)S(1)} custom-call(s32[64]{0:T(128)S(1)} %pad_add_fusion.table_ref.latent_ref, bf16[288,1680]{1,0:T(8,128)(2,1)S(1)} %pad_maximum_fusion.own, bf16[288,1680]{1,0:T(8,128)(2,1)S(1)} %collective-permute-done.beside, bf16[288,1680]{1,0:T(8,128)(2,1)S(1)} %shard_map.153.across, ...), custom_call_target="tpu_custom_call" | custom-call | flops 1019215872 | bytes 5242880 | tf_op jit(solution)/shard_map/pallas_call | solution.py:466
  40.0 0.0 copy-start.3
  40.0 3.9 %shard_map.156 = (bf16[512,288]{1,0:T(8,128)(2,1)S(1)}, f32[8,128]{1,0:T(8,128)S(1)}) custom-call(s32[64]{0:T(128)S(1)} %pad_add_fusion.table_ref.latent_ref, f32[864,512]{1,0:T(8,128)S(1)} %shard_map.155.triple), custom_call_target="tpu_custom_call" | custom-call | flops 301989888 | tf_op jit(solution)/shard_map/pallas_call | solution.py:477
  43.9 0.0 collective-permute-done.8.__1_.refs_5_
  44.0 0.7 collective-permute-start.9
  44.7 0.0 collective-permute-done.11.refs_4_
  44.7 0.8 collective-permute-start.14
  45.5 0.0 collective-permute-start.10
  45.5 5.0 %collective-permute-done.12.refs_6_ = bf16[288,576]{1,0:T(8,128)(2,1)S(1)} collective-permute-done((bf16[288,576]{1,0:T(8,128)(2,1)}, bf16[288,576]{1,0:T(8,128)(2,1)S(1)}, u32[]{:S(2)}, u32[]{:S(2)}) %collective-permute-start.12) | collective-permute-done | bytes 331808 | tf_op jit(solution)/shard_map/ppermute | solution.py:52
  50.5 3.4 %shard_map.158 = (bf16[1152,1152]{1,0:T(8,128)(2,1)S(1)}, bf16[1152,576]{1,0:T(8,128)(2,1)S(1)}, bf16[1152,576]{1,0:T(8,128)(2,1)S(1)}, bf16[512,1152]{1,0:T(8,1...) custom-call(f32[3,3,4,4]{3,2,1,0:T(4,128)S(1)} %copy-done.3, ...), custom_call_target="tpu_custom_call" | custom-call | bytes 8388608 | tf_op jit(solution)/shard_map/pallas_call | solution.py:485
  53.9 0.0 collective-permute-done.9.refs_0_.att_across
  54.0 0.1 collective-permute-start.13
  54.1 0.3 shard_map.160
  54.4 0.0 collective-permute-done.10.att_beside
  54.4 1.4 %collective-permute-done.13.att_diagonal = bf16[512,288]{1,0:T(8,128)(2,1)S(1)} collective-permute-done((bf16[512,288]{1,0:T(8,128)(2,1)S(1)}, bf16[512,288]{1,0:T(8,128)(2,1)S(1)}, u32[]{:S(2)}, u32[]{:S(2)}) %collective-permute-start.13) | collective-permute-done | bytes 294944 | tf_op jit(solution)/shard_map/ppermute | solution.py:52
  55.8 2.9 %shard_map.161 = (f32[128,1152]{1,0:T(8,128)S(1)}, bf16[128,1152]{1,0:T(8,128)(2,1)S(1)}, f32[8,128]{1,0:T(8,128)S(1)}) custom-call(s32[64]{0:T(128)S(1)} %pad_add_fusion.table_ref.latent_ref, bf16[512,288]{1,0:T(8,128)(2,1)S(1)} %shard_map.157.att_own, bf16[512,288]{1,0:T(8,128)(2,1)S(1)} %collective-permute-done.9.refs_0_.att_across, ...), custom_call_target="tpu_custom_call" | custom-call | flops 1358954496 | bytes 8388608 | tf_op jit(solution)/shard_map/pallas_call | solution.py:523
  58.7 0.2 collective-permute-start.15
  59.0 2.6 %shard_map.163 = (bf16[128,1152]{1,0:T(8,128)(2,1)S(1)}, f32[8,128]{1,0:T(8,128)}) custom-call(s32[64]{0:T(128)S(1)} %pad_add_fusion.table_ref.latent_ref, bf16[512,288]{1,0:T(8,128)(2,1)S(1)} %shard_map.157.att_own, bf16[512,288]{1,0:T(8,128)(2,1)S(1)} %collective-permute-done.9.refs_0_.att_across, bf16[512,288]{1,0:T(8,128)(2,1)S(1)} %collective-permute-done.10.att_beside, ...), custom_call_target="tpu_custom_call" | custom-call | flops 679477248 | bytes 8388608 | tf_op jit(solution)/shard_map/pallas_call | solution.py:523
  61.5 0.4 collective-permute-start.16
  61.9 0.1 add_convert_fusion.refs_0_
  62.0 0.0 copy-start.4
  62.0 0.0 copy-start.5
  62.0 0.0 copy-start.6
  62.0 1.5 %collective-permute-start.17 = (bf16[128,1152]{1,0:T(8,128)(2,1)S(1)}, bf16[128,1152]{1,0:T(8,128)(2,1)S(1)}, u32[]{:S(2)}, u32[]{:S(2)}) collective-permute-start(bf16[128,1152]{1,0:T(8,128)(2,1)S(1)} %add_convert_fusion.refs_0_), channel_id=1, source_target_pairs={{0,2},{1,3},{2,0},{3,1},{4,6},{5,7},{6,4},{7,5},{8,10},{9,11},{10,... | collective-permute-start | bytes 884744 | tf_op jit(solution)/shard_map/ppermute | solution.py:52
  63.5 2.5 %shard_map.162 = (f32[128,1152]{1,0:T(8,128)S(1)}, bf16[128,1152]{1,0:T(8,128)(2,1)S(1)}, f32[8,128]{1,0:T(8,128)}) custom-call(s32[64]{0:T(128)S(1)} %pad_add_fusion.table_ref.latent_ref, bf16[512,288]{1,0:T(8,128)(2,1)S(1)} %shard_map.157.att_own, bf16[512,288]{1,0:T(8,128)(2,1)S(1)} %collective-permute-done.9.refs_0_.att_across, ...), custom_call_target="tpu_custom_call" | custom-call | flops 679477248 | bytes 8388608 | tf_op jit(solution)/shard_map/pallas_call | solution.py:523
  66.1 5.0 %collective-permute-done.17.crossed_ref = bf16[128,1152]{1,0:T(8,128)(2,1)S(1)} collective-permute-done((bf16[128,1152]{1,0:T(8,128)(2,1)S(1)}, bf16[128,1152]{1,0:T(8,128)(2,1)S(1)}, u32[]{:S(2)}, u32[]{:S(2)}) %collective-permute-start.17) | collective-permute-done | bytes 294944 | tf_op jit(solution)/shard_map/ppermute | solution.py:52
  71.1 1.1 %shard_map.164.first = f32[8,256]{1,0:T(8,128)S(1)} custom-call(s32[64]{0:T(128)S(1)} %pad_add_fusion.table_ref.latent_ref, f32[128,1152]{1,0:T(8,128)S(1)} %get-tuple-element.36.kept_ref, bf16[128,1152]{1,0:T(8,128)(2,1)S(1)} %collective-permute-done.16.beside_ref, bf16[128,1152]{1,0:T(8,128)(2,1)S(1)} %collective-permute-done.17.crossed_ref, ...), custom_call_target="tpu_custom_call" | custom-call | flops 75497472 | bytes 2097152 | tf_op jit(solution)/shard_map/pallas_call | solution.py:547
  72.3 0.1 collective-permute-start.18
  72.3 1.2 %collective-permute-done.18.second = f32[8,256]{1,0:T(8,128)S(1)} collective-permute-done((f32[8,256]{1,0:T(8,128)S(1)}, f32[8,256]{1,0:T(8,128)S(1)}, u32[]{:S(2)}, u32[]{:S(2)}) %collective-permute-start.18) | collective-permute-done | bytes 8224 | tf_op jit(solution)/shard_map/ppermute | solution.py:52
  73.5 1.5 %collective-permute-start.19 = (f32[16,256]{1,0:T(8,128)S(1)}, f32[16,256]{1,0:T(8,128)S(1)}, u32[]{:S(2)}, u32[]{:S(2)}) collective-permute-start(f32[16,256]{1,0:T(8,128)S(1)} %shard_map.165.near), channel_id=1, source_target_pairs={{0,2},{1,3},{2,0},{3,1},{4,6},{5,7},{6,4},{7,5},{8,10},{9,11},{10,... | collective-permute-start | bytes 49160 | tf_op jit(solution)/shard_map/ppermute | solution.py:52
  74.9 2.3 %collective-permute-done.19.far = f32[16,256]{1,0:T(8,128)S(1)} collective-permute-done((f32[16,256]{1,0:T(8,128)S(1)}, f32[16,256]{1,0:T(8,128)S(1)}, u32[]{:S(2)}, u32[]{:S(2)}) %collective-permute-start.19) | collective-permute-done | bytes 16416 | tf_op jit(solution)/shard_map/ppermute | solution.py:52
  77.2 1.5 %shard_map.166 = (bf16[64,128]{1,0:T(8,128)(2,1)}, bf16[64,128]{1,0:T(8,128)(2,1)}) custom-call(s32[64]{0:T(128)S(1)} %pad_add_fusion.table_ref.latent_ref, f32[50]{0:T(128)S(1)} %copy-done.5, f32[50]{0:T(128)S(1)} %copy-done.6, f32[16,256]{1,0:T(8,128)S(1)} %shard_map.165.near, f32[16,256]{1,0:T(8,128)S(1)} %collective-permute-done.19.far, ...), custom_call_target="tpu_custom_call" | custom-call | flops 12582912 | bytes 524288 | tf_op jit(solution)/shard_map/pallas_call | solution.py:556
  (25 shorter events, 0.1 us)
Async XLA Ops:
  0.6 12.3 %copy-start = (bf16[144,8,288]{2,1,0:T(8,128)(2,1)S(1)}, bf16[144,8,288]{2,1,0:T(8,128)(2,1)}, u32[]{:S(2)}) copy-start(bf16[144,8,288]{2,1,0:T(8,128)(2,1)} %param.21) | copy-start | bytes 1990660
  0.6 11.1 %copy-start.10 = (s32[32]{0:T(128)S(1)}, s32[32]{0:T(128)}, u32[]{:S(2)}) copy-start(s32[32]{0:T(128)} %param.16) | copy-start | bytes 388
  0.7 11.1 %copy-start.9 = (s32[32]{0:T(128)S(1)}, s32[32]{0:T(128)}, u32[]{:S(2)}) copy-start(s32[32]{0:T(128)} %param.17) | copy-start | bytes 388
  0.7 11.1 %copy-start.2 = (bf16[50,1152]{1,0:T(8,128)(2,1)S(1)}, bf16[50,1152]{1,0:T(8,128)(2,1)}, u32[]{:S(2)}) copy-start(bf16[50,1152]{1,0:T(8,128)(2,1)} %embedding_ref.1) | copy-start | bytes 345604
  1.6 4.3 %copy-start.7 = (bf16[576,144]{0,1:T(8,128)(2,1)S(1)}, bf16[576,144]{0,1:T(8,128)(2,1)}, u32[]{:S(2)}) copy-start(bf16[576,144]{0,1:T(8,128)(2,1)} %param.25) | copy-start | bytes 497668
  1.6 4.3 %copy-start.8 = (bf16[144,576]{1,0:T(8,128)(2,1)S(1)}, bf16[144,576]{1,0:T(8,128)(2,1)}, u32[]{:S(2)}) copy-start(bf16[144,576]{1,0:T(8,128)(2,1)} %param.24) | copy-start | bytes 497668
  2.9 28.2 %collective-permute-start.1 = (bf16[288,1680]{1,0:T(8,128)(2,1)S(1)}, bf16[288,1680]{1,0:T(8,128)(2,1)S(1)}, u32[]{:S(2)}, u32[]{:S(2)}) collective-permute-start(bf16[288,1680]{1,0:T(8,128)(2,1)S(1)} %pad_maximum_fusion.own), channel_id=1, source_target_pairs={{0,2},{1,3},{2,0},{3,1},{4,6},{5,7},{6,4},{7,5},{8,10},{9,11},{10,... | collective-permute-start | bytes 2903048 | tf_op jit(solution)/shard_map/ppermute | solution.py:52
  6.0 20.6 %collective-permute-start.2 = (bf16[288,576]{1,0:T(8,128)(2,1)S(1)}, bf16[288,576]{1,0:T(8,128)(2,1)}, u32[]{:S(2)}, u32[]{:S(2)}) collective-permute-start(bf16[288,576]{1,0:T(8,128)(2,1)S(1)} %pad_maximum_fusion.1.refs_0_), channel_id=1, source_target_pairs={{0,16},{4,20},{8,24},{12,28},{16,0},{20,4},{24,8},{28,12},{1,17},{... | collective-permute-start | bytes 995336 | tf_op jit(solution)/shard_map/ppermute | solution.py:52
  8.6 18.2 %collective-permute-start.3 = (bf16[288,576]{1,0:T(8,128)(2,1)S(1)}, bf16[288,576]{1,0:T(8,128)(2,1)}, u32[]{:S(2)}, u32[]{:S(2)}) collective-permute-start(bf16[288,576]{1,0:T(8,128)(2,1)S(1)} %pad_maximum_fusion.1.refs_0_), channel_id=1, source_target_pairs={{0,8},{4,12},{8,0},{12,4},{16,24},{20,28},{24,16},{28,20},{1,9},{5... | collective-permute-start | bytes 995336 | tf_op jit(solution)/shard_map/ppermute | solution.py:52
  10.2 16.7 %collective-permute-start.4 = (bf16[288,576]{1,0:T(8,128)(2,1)S(1)}, bf16[288,576]{1,0:T(8,128)(2,1)}, u32[]{:S(2)}, u32[]{:S(2)}) collective-permute-start(bf16[288,576]{1,0:T(8,128)(2,1)S(1)} %pad_maximum_fusion.1.refs_0_), channel_id=1, source_target_pairs={{0,4},{4,0},{8,12},{12,8},{16,20},{20,16},{24,28},{28,24},{1,5},{5... | collective-permute-start | bytes 995336 | tf_op jit(solution)/shard_map/ppermute | solution.py:52
  13.9 15.9 %all-to-all-start = ((f32[8,16,288]{2,1,0:T(8,128)}), f32[8,16,288]{2,1,0:T(8,128)S(1)}, u32[]{:S(2)}, u32[]{:S(2)}) async-start(f32[8,16,288]{2,1,0:T(8,128)} %bitcast.10), calls=%async_computation | async-start | bytes 393216 | tf_op jit(solution)/shard_map/all_to_all | solution.py:417
  29.8 1.3 %collective-permute-start.5 = (f32[16,288]{1,0:T(8,128)S(1)}, f32[16,288]{1,0:T(8,128)S(1)}, u32[]{:S(2)}, u32[]{:S(2)}) collective-permute-start(f32[16,288]{1,0:T(8,128)S(1)} %shard_map.151.first), channel_id=1, source_target_pairs={{0,1},{1,0},{2,3},{3,2},{4,5},{5,4},{6,7},{7,6},{8,9},{9,8},{10,11... | collective-permute-start | bytes 55304 | tf_op jit(solution)/shard_map/ppermute | solution.py:52
  29.9 6.7 %collective-permute-start = (bf16[288,1680]{1,0:T(8,128)(2,1)S(1)}, bf16[288,1680]{1,0:T(8,128)(2,1)S(1)}, u32[]{:S(2)}, u32[]{:S(2)}) collective-permute-start(bf16[288,1680]{1,0:T(8,128)(2,1)S(1)} %pad_maximum_fusion.own), channel_id=1, source_target_pairs={{0,1},{1,0},{2,3},{3,2},{4,5},{5,4},{6,7},{7,6},{8,9},{9,8},{10,11... | collective-permute-start | bytes 2903048 | tf_op jit(solution)/shard_map/ppermute | solution.py:52
  31.1 5.5 %copy-start.1 = (bf16[1152,3,288]{0,2,1:T(8,128)(2,1)S(1)}, bf16[1152,3,288]{0,2,1:T(8,128)(2,1)}, u32[]{:S(2)}) copy-start(bf16[1152,3,288]{0,2,1:T(8,128)(2,1)} %param.22) | copy-start | bytes 5971972
  31.1 5.5 %collective-permute-start.6 = (bf16[288,1680]{1,0:T(8,128)(2,1)S(1)}, bf16[288,1680]{1,0:T(8,128)(2,1)S(1)}, u32[]{:S(2)}, u32[]{:S(2)}) collective-permute-start(bf16[288,1680]{1,0:T(8,128)(2,1)S(1)} %shard_map.153.across), channel_id=1, source_target_pairs={{0,1},{1,0},{2,3},{3,2},{4,5},{5,4},{6,7},{7,6},{8,9},{9,8},{10,11... | collective-permute-start | bytes 2903048 | tf_op jit(solution)/shard_map/ppermute | solution.py:52
  31.3 4.1 %collective-permute-start.7 = (f32[32,288]{1,0:T(8,128)S(1)}, f32[32,288]{1,0:T(8,128)S(1)}, u32[]{:S(2)}, u32[]{:S(2)}) collective-permute-start(f32[32,288]{1,0:T(8,128)S(1)} %shard_map.152.__1_.terms_near), channel_id=1, source_target_pairs={{0,2},{1,3},{2,0},{3,1},{4,6},{5,7},{6,4},{7,5},{8,10},{9,11},{10,... | collective-permute-start | bytes 110600 | tf_op jit(solution)/shard_map/ppermute | solution.py:52
  31.8 12.9 %collective-permute-start.11 = (bf16[288,576]{1,0:T(8,128)(2,1)}, bf16[288,576]{1,0:T(8,128)(2,1)S(1)}, u32[]{:S(2)}, u32[]{:S(2)}) collective-permute-start(bf16[288,576]{1,0:T(8,128)(2,1)} %collective-permute-done.2.refs_1_.refs_3_), channel_id=1, source_target_pairs={{0,4},{4,0},{8,12},{12,8},{16,20},{20,16},{24,28},{28,24},{1,5},{5... | collective-permute-start | bytes 995336 | tf_op jit(solution)/shard_map/ppermute | solution.py:52
  32.7 11.2 %collective-permute-start.8 = (bf16[288,576]{1,0:T(8,128)(2,1)}, bf16[288,576]{1,0:T(8,128)(2,1)S(1)}, u32[]{:S(2)}, u32[]{:S(2)}) collective-permute-start(bf16[288,576]{1,0:T(8,128)(2,1)} %collective-permute-done.2.refs_1_.refs_3_), channel_id=1, source_target_pairs={{0,8},{4,12},{8,0},{12,4},{16,24},{20,28},{24,16},{28,20},{1,9},{5... | collective-permute-start | bytes 995336 | tf_op jit(solution)/shard_map/ppermute | solution.py:52
  35.4 15.1 %collective-permute-start.12 = (bf16[288,576]{1,0:T(8,128)(2,1)}, bf16[288,576]{1,0:T(8,128)(2,1)S(1)}, u32[]{:S(2)}, u32[]{:S(2)}) collective-permute-start(bf16[288,576]{1,0:T(8,128)(2,1)} %collective-permute-done.3.refs_2_), channel_id=1, source_target_pairs={{0,4},{4,0},{8,12},{12,8},{16,20},{20,16},{24,28},{28,24},{1,5},{5... | collective-permute-start | bytes 995336 | tf_op jit(solution)/shard_map/ppermute | solution.py:52
  40.0 10.5 %copy-start.3 = (f32[3,3,4,4]{3,2,1,0:T(4,128)S(1)}, f32[3,3,4,4]{3,2,1,0:T(4,128)}, u32[]{:S(2)}) copy-start(f32[3,3,4,4]{3,2,1,0:T(4,128)} %kernel_ref.1) | copy-start | bytes 1732
  44.0 10.0 %collective-permute-start.9 = (bf16[512,288]{1,0:T(8,128)(2,1)S(1)}, bf16[512,288]{1,0:T(8,128)(2,1)S(1)}, u32[]{:S(2)}, u32[]{:S(2)}) collective-permute-start(bf16[512,288]{1,0:T(8,128)(2,1)S(1)} %shard_map.157.att_own), channel_id=1, source_target_pairs={{0,2},{1,3},{2,0},{3,1},{4,6},{5,7},{6,4},{7,5},{8,10},{9,11},{10,... | collective-permute-start | bytes 884744 | tf_op jit(solution)/shard_map/ppermute | solution.py:52
  44.7 9.4 %collective-permute-start.14 = (bf16[288,576]{1,0:T(8,128)(2,1)S(1)}, bf16[288,576]{1,0:T(8,128)(2,1)S(1)}, u32[]{:S(2)}, u32[]{:S(2)}) collective-permute-start(bf16[288,576]{1,0:T(8,128)(2,1)S(1)} %collective-permute-done.11.refs_4_), channel_id=1, source_target_pairs={{0,8},{4,12},{8,0},{12,4},{16,24},{20,28},{24,16},{28,20},{1,9},{5... | collective-permute-start | bytes 995336 | tf_op jit(solution)/shard_map/ppermute | solution.py:52
  45.5 8.9 %collective-permute-start.10 = (bf16[512,288]{1,0:T(8,128)(2,1)S(1)}, bf16[512,288]{1,0:T(8,128)(2,1)S(1)}, u32[]{:S(2)}, u32[]{:S(2)}) collective-permute-start(bf16[512,288]{1,0:T(8,128)(2,1)S(1)} %shard_map.157.att_own), channel_id=1, source_target_pairs={{0,1},{1,0},{2,3},{3,2},{4,5},{5,4},{6,7},{7,6},{8,9},{9,8},{10,11... | collective-permute-start | bytes 884744 | tf_op jit(solution)/shard_map/ppermute | solution.py:52
  54.0 1.8 %collective-permute-start.13 = (bf16[512,288]{1,0:T(8,128)(2,1)S(1)}, bf16[512,288]{1,0:T(8,128)(2,1)S(1)}, u32[]{:S(2)}, u32[]{:S(2)}) collective-permute-start(bf16[512,288]{1,0:T(8,128)(2,1)S(1)} %shard_map.159), channel_id=1, source_target_pairs={{0,1},{1,0},{2,3},{3,2},{4,5},{5,4},{6,7},{7,6},{8,9},{9,8},{10,11... | collective-permute-start | bytes 884744 | tf_op jit(solution)/shard_map/ppermute | solution.py:52
  58.7 3.1 %collective-permute-start.15 = (bf16[128,1152]{1,0:T(8,128)(2,1)S(1)}, bf16[128,1152]{1,0:T(8,128)(2,1)S(1)}, u32[]{:S(2)}, u32[]{:S(2)}) collective-permute-start(bf16[128,1152]{1,0:T(8,128)(2,1)S(1)} %get-tuple-element.35), channel_id=1, source_target_pairs={{0,1},{1,0},{2,3},{3,2},{4,5},{5,4},{6,7},{7,6},{8,9},{9,8},{10,11... | collective-permute-start | bytes 884744 | tf_op jit(solution)/shard_map/ppermute | solution.py:52
  61.5 4.6 %collective-permute-start.16 = (bf16[128,1152]{1,0:T(8,128)(2,1)S(1)}, bf16[128,1152]{1,0:T(8,128)(2,1)S(1)}, u32[]{:S(2)}, u32[]{:S(2)}) collective-permute-start(bf16[128,1152]{1,0:T(8,128)(2,1)S(1)} %get-tuple-element.38), channel_id=1, source_target_pairs={{0,1},{1,0},{2,3},{3,2},{4,5},{5,4},{6,7},{7,6},{8,9},{9,8},{10,11... | collective-permute-start | bytes 884744 | tf_op jit(solution)/shard_map/ppermute | solution.py:52
  62.0 15.3 %copy-start.4 = (bf16[64,128]{1,0:T(8,128)(2,1)S(1)}, bf16[64,128]{1,0:T(8,128)(2,1)}, u32[]{:S(2)}) copy-start(bf16[64,128]{1,0:T(8,128)(2,1)} %noisy_ref.1) | copy-start | bytes 49156
  62.0 15.3 %copy-start.5 = (f32[50]{0:T(128)S(1)}, f32[50]{0:T(128)}, u32[]{:S(2)}) copy-start(f32[50]{0:T(128)} %now_ref.1) | copy-start | bytes 604
  62.0 15.3 %copy-start.6 = (f32[50]{0:T(128)S(1)}, f32[50]{0:T(128)}, u32[]{:S(2)}) copy-start(f32[50]{0:T(128)} %next_ref.1) | copy-start | bytes 604
  62.0 9.1 %collective-permute-start.17 = (bf16[128,1152]{1,0:T(8,128)(2,1)S(1)}, bf16[128,1152]{1,0:T(8,128)(2,1)S(1)}, u32[]{:S(2)}, u32[]{:S(2)}) collective-permute-start(bf16[128,1152]{1,0:T(8,128)(2,1)S(1)} %add_convert_fusion.refs_0_), channel_id=1, source_target_pairs={{0,2},{1,3},{2,0},{3,1},{4,6},{5,7},{6,4},{7,5},{8,10},{9,11},{10,... | collective-permute-start | bytes 884744 | tf_op jit(solution)/shard_map/ppermute | solution.py:52
  72.3 1.2 %collective-permute-start.18 = (f32[8,256]{1,0:T(8,128)S(1)}, f32[8,256]{1,0:T(8,128)S(1)}, u32[]{:S(2)}, u32[]{:S(2)}) collective-permute-start(f32[8,256]{1,0:T(8,128)S(1)} %shard_map.164.first), channel_id=1, source_target_pairs={{0,1},{1,0},{2,3},{3,2},{4,5},{5,4},{6,7},{7,6},{8,9},{9,8},{10,11... | collective-permute-start | bytes 24584 | tf_op jit(solution)/shard_map/ppermute | solution.py:52
  73.5 3.7 %collective-permute-start.19 = (f32[16,256]{1,0:T(8,128)S(1)}, f32[16,256]{1,0:T(8,128)S(1)}, u32[]{:S(2)}, u32[]{:S(2)}) collective-permute-start(f32[16,256]{1,0:T(8,128)S(1)} %shard_map.165.near), channel_id=1, source_target_pairs={{0,2},{1,3},{2,0},{3,1},{4,6},{5,7},{6,4},{7,5},{8,10},{9,11},{10,... | collective-permute-start | bytes 49160 | tf_op jit(solution)/shard_map/ppermute | solution.py:52

commit v7 on v6

--- a/solution.py
+++ b/solution.py
@@ -13,9 +13,6 @@
 CHANNELS = 4
 GRIDW = 16
 NOISE = PATCH * PATCH * CHANNELS
-F = {'p3': 0, 'p6': 0, 'p5': 0, 'at': ['both_6'], 'l3': 0}
-COSTS = {}
-COUNT = [0]
 TILE_ROWS = 8
 STEPS = 50
 TILE = 128
@@ -32,10 +29,6 @@
 
 
 def call(kernel, outs, in_specs, scratch=(), flops=0, nbytes=0, trans=0, limit=4):
-    base = getattr(kernel, "func", kernel).__name__
-    COUNT[0] += 1
-    if base in COSTS:
-        flops, nbytes, trans = int(COSTS[base] * 10**9), 0, 0
     return pl.pallas_call(
         kernel,
         out_shape=outs,
@@ -50,13 +43,6 @@
 def exchange(value, axis, offset):
     size = lax.axis_size(axis)
     return lax.ppermute(value, axis, [(i, i ^ offset) for i in range(size)])
-
-
-def gather_blocks(value):
-    across = exchange(value, "col", 2)
-    beside = exchange(value, "col", 1)
-    diagonal = exchange(across, "col", 1)
-    return value, beside, across, diagonal
 
 
 def after_kernel(*_):
@@ -119,10 +105,9 @@
     refs[-1][...] = refs[0][...]
 
 
-def terms_kernel(terms_near, terms_far, *refs):
+def terms_kernel(terms_near, terms_far, terms_ref, columns):
     col = lax.axis_index("col")
     width = terms_near.shape[1]
-    terms_ref, columns = refs[-2:]
     rows = terms_ref.shape[0]
     for place in range(4):
 
@@ -424,63 +409,49 @@
         both_4 = exchange(both, "row", 4)
         both_2 = exchange(both, "row", 2)
         both_1 = exchange(both, "row", 1)
-        first, middle = [], []
-        if F.get("f4", 0) < 2:
-            (first, middle)[F.get("f4", 0)].append(both_4)
-        (first if F.get("f2", 1) else middle).append(both_2)
-        (first if F.get("f1", 1) else middle).append(both_1)
+        first = [both_4, both_2, both_1]
     else:
         expand_whole = lax.all_gather(expand_weight, "row", axis=0, tiled=True)
         reduce_whole = lax.all_gather(reduce_rows, "row", axis=0, tiled=True)
-        first, middle = [], []
+        first = []
     arrived = call(order_kernel, mark, [ANYWHERE] * (1 + len(first)))(conditioned, *first)
     shared = call(shared_kernel, shape((16, width), WIDE), [VMEM, ANYWHERE], nbytes=2**18)(received, arrived)
-    at_near, at_terms = [], []
-    second, third = [], []
     if staged:
         both_3 = exchange(both_2, "row", 1)
         both_6 = exchange(both_4, "row", 2)
         both_5 = exchange(both_4, "row", 1)
-        both_7 = exchange(both_5, "row", 2) if F.get("w5", 1) else exchange(both_6, "row", 1)
-        second, third = [], []
-        if F.get("f4", 0) > 1:
-            (second, third)[F["f4"] - 2].append(both_4)
-        for name, piece in (("p3", both_3), ("p6", both_6), ("p5", both_5)):
-            place = F.get(name, 1 if name != "p5" else 2)
-            if place:
-                (second, third, at_terms, at_near, middle)[place - 1].append(piece)
+        both_7 = exchange(both_5, "row", 2)
         parts = [(0, "er", both), (1, "er", both_1), (2, "er", both_2), (4, "er", both_4), (5, "er", both_5), (6, "er", both_6)]
-        last = [(3, "er", both_3), (7, "er", both_7)]
-        if not F.get("l3", 1):
-            parts.append(last.pop(0))
+        parts.append((3, "er", both_3))
+        last = [(7, "er", both_7)]
     else:
         parts, last = [(0, "e", expand_whole), (0, "r", reduce_whole)], []
-    terms_near = pack(shared, exchange(shared, "col", 1), *middle)
+    terms_near = pack(shared, exchange(shared, "col", 1))
     terms_far = exchange(terms_near, "col", 2)
     blocks_across = after(blocks_across, terms_near)
     blocks = (blocks_here, exchange(blocks_here, "col", 1), blocks_across, exchange(blocks_across, "col", 1))
     attention_weight = attention_in.transpose(1, 2, 0).reshape(3 * width, D)
     terms, columns = call(
-        terms_kernel, [shape((16, D), WIDE), shape((D, 16), WIDE)], [VMEM] * 2 + [ANYWHERE] * len(at_terms), flops=F.get("tc", 4) * 10**9
-    )(terms_near, terms_far, *at_terms)
+        terms_kernel, [shape((16, D), WIDE), shape((D, 16), WIDE)], [VMEM] * 2, flops=4 * 10**9
+    )(terms_near, terms_far)
     triple = call(
         triple_kernel,
         shape((3 * width, tokens_here), WIDE),
-        [SMEM] + [VMEM] * 5 + [ANYWHERE] * (1 + len(second)),
+        [SMEM] + [VMEM] * 5 + [ANYWHERE],
         [
             pltpu.VMEM((3 * width, D), NARROW),
             pltpu.SemaphoreType.DMA,
             pltpu.VMEM((D, tokens_here), NARROW),
         ],
         flops=2 * tokens_here * D * 3 * width, nbytes=5 * 2**20, limit=16,
-    )(table, *blocks, columns, attention_weight, *second)
+    )(table, *blocks, columns, attention_weight)
     attended, attention_done = call(
         attention_kernel,
         [shape((tokens_here, width), NARROW), mark],
-        [SMEM, VMEM] + [ANYWHERE] * len(third),
+        [SMEM, VMEM],
         [pltpu.VMEM((width, tokens_here), WIDE)],
         flops=4 * tokens_here * tokens_here * width, trans=4 * tokens_here**2, limit=16,
-    )(table, triple, *third)
+    )(table, triple)
     split = depth if staged else D
     out_weight, expand_all, reduce_all, tokens, head, bands = call(
         functools.partial(assemble_kernel, [part[:2] for part in parts], split),
@@ -495,18 +466,10 @@
         [SMEM] + [VMEM] * (4 + len(parts)) + [ANYWHERE],
         nbytes=2**23, limit=24,
     )(preview_kernel, *blocks, *(part[2] for part in parts), attention_done)
-    ahead = [locals()[name] for name in F.get("at", ()) if staged]
-    if ahead:
-        attended = after(attended, *ahead)
+    if staged:
+        attended = after(attended, both_6)
     across = exchange(attended, "col", 2)
-    if F.get("pass", 0) == 0:
-        if F.get("pa", 0):
-            passed = after(across, tokens)
-            across = passed
-        else:
-            passed = call(pass_kernel, shape(across.shape, NARROW), [VMEM, ANYWHERE], nbytes=2**19)(across, tokens)
-    else:
-        passed = across
+    passed = call(pass_kernel, shape(across.shape, NARROW), [VMEM, ANYWHERE], nbytes=2**19)(across, tokens)
     attended_blocks = (attended, across, exchange(attended, "col", 1), exchange(passed, "col", 1))
     if last:
         expand_all, reduce_all = call(
@@ -528,21 +491,11 @@
             flops=2 * count * D * (D + 2 * units), nbytes=8 * 2**20, trans=count * units, limit=20,
         )(table, *attended_blocks, tokens, terms, out_weight, expand_all, reduce_all, *before)
 
-    tail = F.get("tail", 0)
-    if tail == 3:
-        far_kept, far_sent, near_sent, _ = mlp((2, 3, 1))
-    else:
-        far_kept, far_sent, far_done = mlp((2, 3))
-    if tail == 0:
-        near_sent, _ = mlp((1,), far_done)
+    far_kept, far_sent, far_done = mlp((2, 3))
+    near_sent, _ = mlp((1,), far_done)
     far_sum = (far_kept + exchange(far_sent, "col", 1).astype(WIDE)).astype(NARROW)
     crossed = exchange(far_sum, "col", 2)
-    if tail == 1:
-        near_sent, _ = mlp((1,), far_sum)
-    if tail != 2:
-        near_kept, residual, _ = mlp((0,), far_sum)
-    else:
-        near_kept, near_sent, residual, _ = mlp((0, 1), far_sum)
+    near_kept, residual, _ = mlp((0,), far_sum)
     beside = exchange(near_sent, "col", 1)
     noise = call(
         head_kernel,

time: 79 us -> 79 us (level)
  no operation moved by 1% of the time
where the time goes in v7:
time: 79 us; the launch traced here: 78.7 us
  waiting for transfers between devices  30 us (38%)
  Pallas kernels  23.1 us (29%)
  starting transfers between devices  21.2 us (27%)
  local copies, waits for them, and re-layouts  1.71 us (2%)
  other arithmetic  1.47 us (2%)
  between operations  0.91 us (1%)
    ppermute x20, waiting for transfers between devices, exchange(): return lax.ppermute(value, axis, [(i, i ^ offset) for i in range(size)])  27.1 us
    ppermute x20, starting transfers between devices, exchange(): return lax.ppermute(value, axis, [(i, i ^ offset) for i in range(size)])  17.8 us
    pallas_call x3, Pallas kernels, mlp(): call(functools.partial(mlp_kernel, offsets), outs, [SMEM] + [VMEM] * 9 +...  8.04 us
    pallas_call x1, Pallas kernels, shards(): call(attention_kernel, [shape((tokens_here, width), NARROW), mark], [SMEM...  3.9 us
    pallas_call x1, Pallas kernels, shards(): call(triple_kernel, shape((3 * width, tokens_here), WIDE), [SMEM] + [VMEM...  3.39 us
    pallas_call x1, Pallas kernels, shards(): call(functools.partial(assemble_kernel, [part[:2] for part in parts], spl...  3.39 us
    all_to_all x1, starting transfers between devices, shards(): received = lax.all_to_all(partial, 'row', 0, 0, tiled=True)  3.39 us
    all_to_all x1, waiting for transfers between devices, shards(): received = lax.all_to_all(partial, 'row', 0, 0, tiled=True)  2.92 us
  transfers between devices with their start and end apart: 21, of which 10 were waited for; matrix products, arithmetic and copies ran while one was open for 2% of the time, Pallas kernels for 22%

profile of v7, /device:TPU:0, one launch (start us, length us, event | category | flops | bytes accessed | tf_op | source)
XLA Modules:
  0.0 78.7 jit_solution(11005248490887091685)
XLA Ops:
  0.6 0.0 copy-start
  0.7 0.9 %copy.18 = bf16[288,16]{1,0:T(8,128)(2,1)S(1)} copy(bf16[288,16]{0,1:T(8,128)(2,1)} %param.26) | data formatting | bytes 18432 | tf_op args[12]
  1.6 0.0 copy-start.7
  1.6 0.0 copy-start.8
  1.6 1.3 %pad_maximum_fusion.own = bf16[288,1680]{1,0:T(8,128)(2,1)S(1)} fusion(bf16[288,16]{1,0:T(8,128)(2,1)S(1)} %copy.18, bf16[288,1152]{1,0:T(8,128)(2,1)} %param.23, bf16[288,512]{1,0:T(8,128)(2,1)} %bitcast.11), kind=kLoop, calls=%fused_computation | loop fusion | flops 2903040 | bytes 1935360 | tf_op jit(solution)/shard_map/concatenate | solution.py:403
  2.9 3.0 %collective-permute-start.1 = (bf16[288,1680]{1,0:T(8,128)(2,1)S(1)}, bf16[288,1680]{1,0:T(8,128)(2,1)S(1)}, u32[]{:S(2)}, u32[]{:S(2)}) collective-permute-start(bf16[288,1680]{1,0:T(8,128)(2,1)S(1)} %pad_maximum_fusion.own), channel_id=1, source_target_pairs={{0,2},{1,3},{2,0},{3,1},{4,6},{5,7},{6,4},{7,5},{8,10},{9,11},{10,... | collective-permute-start | bytes 2903048 | tf_op jit(solution)/shard_map/ppermute | solution.py:45
  6.0 2.7 %collective-permute-start.2 = (bf16[288,576]{1,0:T(8,128)(2,1)S(1)}, bf16[288,576]{1,0:T(8,128)(2,1)}, u32[]{:S(2)}, u32[]{:S(2)}) collective-permute-start(bf16[288,576]{1,0:T(8,128)(2,1)S(1)} %pad_maximum_fusion.1.refs_0_), channel_id=1, source_target_pairs={{0,16},{4,20},{8,24},{12,28},{16,0},{20,4},{24,8},{28,12},{1,17},{... | collective-permute-start | bytes 995336 | tf_op jit(solution)/shard_map/ppermute | solution.py:45
  8.6 1.6 %collective-permute-start.3 = (bf16[288,576]{1,0:T(8,128)(2,1)S(1)}, bf16[288,576]{1,0:T(8,128)(2,1)}, u32[]{:S(2)}, u32[]{:S(2)}) collective-permute-start(bf16[288,576]{1,0:T(8,128)(2,1)S(1)} %pad_maximum_fusion.1.refs_0_), channel_id=1, source_target_pairs={{0,8},{4,12},{8,0},{12,4},{16,24},{20,28},{24,16},{28,20},{1,9},{5... | collective-permute-start | bytes 995336 | tf_op jit(solution)/shard_map/ppermute | solution.py:45
  10.2 1.5 %collective-permute-start.4 = (bf16[288,576]{1,0:T(8,128)(2,1)S(1)}, bf16[288,576]{1,0:T(8,128)(2,1)}, u32[]{:S(2)}, u32[]{:S(2)}) collective-permute-start(bf16[288,576]{1,0:T(8,128)(2,1)S(1)} %pad_maximum_fusion.1.refs_0_), channel_id=1, source_target_pairs={{0,4},{4,0},{8,12},{12,8},{16,20},{20,16},{24,28},{28,24},{1,5},{5... | collective-permute-start | bytes 995336 | tf_op jit(solution)/shard_map/ppermute | solution.py:45
  11.7 0.1 pad_add_fusion.table_ref.latent_ref
  11.8 1.1 %shard_map.149 = (bf16[16,144]{1,0:T(8,128)(2,1)S(1)}, f32[8,128]{1,0:T(8,128)S(1)}) custom-call(s32[64]{0:T(128)S(1)} %pad_add_fusion.table_ref.latent_ref, bf16[50,1152]{1,0:T(8,128)(2,1)S(1)} %copy-done.2), custom_call_target="tpu_custom_call" | custom-call | flops 7151616 | bytes 115200 | tf_op jit(solution)/shard_map/pallas_call | solution.py:393
  12.9 0.3 fusion
  13.2 0.7 copy.20
  13.9 3.4 %all-to-all-start = ((f32[8,16,288]{2,1,0:T(8,128)}), f32[8,16,288]{2,1,0:T(8,128)S(1)}, u32[]{:S(2)}, u32[]{:S(2)}) async-start(f32[8,16,288]{2,1,0:T(8,128)} %bitcast.10), calls=%async_computation | async-start | bytes 393216 | tf_op jit(solution)/shard_map/all_to_all | solution.py:402
  17.3 9.2 %collective-permute-done.2.refs_1_.refs_3_ = bf16[288,576]{1,0:T(8,128)(2,1)} collective-permute-done((bf16[288,576]{1,0:T(8,128)(2,1)S(1)}, bf16[288,576]{1,0:T(8,128)(2,1)}, u32[]{:S(2)}, u32[]{:S(2)}) %collective-permute-start.2) | collective-permute-done | bytes 331808 | tf_op jit(solution)/shard_map/ppermute | solution.py:45
  26.5 0.3 collective-permute-done.3.refs_2_
  26.8 0.0 collective-permute-done.4.refs_3_.refs_1_
  26.9 2.9 %all-to-all-done.parts_ref = f32[8,16,288]{2,1,0:T(8,128)S(1)} async-done(((f32[8,16,288]{2,1,0:T(8,128)}), f32[8,16,288]{2,1,0:T(8,128)S(1)}, u32[]{:S(2)}, u32[]{:S(2)}) %all-to-all-start) | async-done | bytes 147488 | tf_op jit(solution)/shard_map/all_to_all | solution.py:402
  29.8 0.1 collective-permute-start.5
  29.9 0.5 collective-permute-start
  30.4 0.7 collective-permute-done.5.second
  31.1 0.0 collective-permute-done.1.__0_
  31.1 0.0 copy-start.1
  31.1 0.2 collective-permute-start.6
  31.3 0.5 collective-permute-start.7
  31.8 0.9 %collective-permute-start.11 = (bf16[288,576]{1,0:T(8,128)(2,1)}, bf16[288,576]{1,0:T(8,128)(2,1)S(1)}, u32[]{:S(2)}, u32[]{:S(2)}) collective-permute-start(bf16[288,576]{1,0:T(8,128)(2,1)} %collective-permute-done.2.refs_1_.refs_3_), channel_id=1, source_target_pairs={{0,4},{4,0},{8,12},{12,8},{16,20},{20,16},{24,28},{28,24},{1,5},{5... | collective-permute-start | bytes 995336 | tf_op jit(solution)/shard_map/ppermute | solution.py:45
  32.7 0.8 %collective-permute-start.8 = (bf16[288,576]{1,0:T(8,128)(2,1)}, bf16[288,576]{1,0:T(8,128)(2,1)S(1)}, u32[]{:S(2)}, u32[]{:S(2)}) collective-permute-start(bf16[288,576]{1,0:T(8,128)(2,1)} %collective-permute-done.2.refs_1_.refs_3_), channel_id=1, source_target_pairs={{0,8},{4,12},{8,0},{12,4},{16,24},{20,28},{24,16},{28,20},{1,9},{5... | collective-permute-start | bytes 995336 | tf_op jit(solution)/shard_map/ppermute | solution.py:45
  33.6 1.8 %collective-permute-done.7.terms_far = f32[32,288]{1,0:T(8,128)S(1)} collective-permute-done((f32[32,288]{1,0:T(8,128)S(1)}, f32[32,288]{1,0:T(8,128)S(1)}, u32[]{:S(2)}, u32[]{:S(2)}) %collective-permute-start.7) | collective-permute-done | bytes 36896 | tf_op jit(solution)/shard_map/ppermute | solution.py:45
  35.4 0.9 %collective-permute-start.12 = (bf16[288,576]{1,0:T(8,128)(2,1)}, bf16[288,576]{1,0:T(8,128)(2,1)S(1)}, u32[]{:S(2)}, u32[]{:S(2)}) collective-permute-start(bf16[288,576]{1,0:T(8,128)(2,1)} %collective-permute-done.3.refs_2_), channel_id=1, source_target_pairs={{0,4},{4,0},{8,12},{12,8},{16,20},{20,16},{24,28},{28,24},{1,5},{5... | collective-permute-start | bytes 995336 | tf_op jit(solution)/shard_map/ppermute | solution.py:45
  36.3 0.3 shard_map.154
  36.6 0.0 collective-permute-done.beside
  36.6 0.0 collective-permute-done.6.diagonal
  36.6 3.4 %shard_map.155.triple = f32[864,512]{1,0:T(8,128)S(1)} custom-call(s32[64]{0:T(128)S(1)} %pad_add_fusion.table_ref.latent_ref, bf16[288,1680]{1,0:T(8,128)(2,1)S(1)} %pad_maximum_fusion.own, bf16[288,1680]{1,0:T(8,128)(2,1)S(1)} %collective-permute-done.beside, bf16[288,1680]{1,0:T(8,128)(2,1)S(1)} %shard_map.153.across, ...), custom_call_target="tpu_custom_call" | custom-call | flops 1019215872 | bytes 5242880 | tf_op jit(solution)/shard_map/pallas_call | solution.py:437
  40.0 0.0 copy-start.3
  40.0 3.9 %shard_map.156 = (bf16[512,288]{1,0:T(8,128)(2,1)S(1)}, f32[8,128]{1,0:T(8,128)S(1)}) custom-call(s32[64]{0:T(128)S(1)} %pad_add_fusion.table_ref.latent_ref, f32[864,512]{1,0:T(8,128)S(1)} %shard_map.155.triple), custom_call_target="tpu_custom_call" | custom-call | flops 301989888 | tf_op jit(solution)/shard_map/pallas_call | solution.py:448
  43.9 0.0 collective-permute-done.8.__1_.refs_5_
  44.0 0.7 collective-permute-start.9
  44.7 0.0 collective-permute-done.11.refs_4_
  44.7 0.8 collective-permute-start.14
  45.5 0.0 collective-permute-start.10
  45.5 5.0 %collective-permute-done.12.refs_6_ = bf16[288,576]{1,0:T(8,128)(2,1)S(1)} collective-permute-done((bf16[288,576]{1,0:T(8,128)(2,1)}, bf16[288,576]{1,0:T(8,128)(2,1)S(1)}, u32[]{:S(2)}, u32[]{:S(2)}) %collective-permute-start.12) | collective-permute-done | bytes 331808 | tf_op jit(solution)/shard_map/ppermute | solution.py:45
  50.5 3.4 %shard_map.158 = (bf16[1152,1152]{1,0:T(8,128)(2,1)S(1)}, bf16[1152,576]{1,0:T(8,128)(2,1)S(1)}, bf16[1152,576]{1,0:T(8,128)(2,1)S(1)}, bf16[512,1152]{1,0:T(8,1...) custom-call(f32[3,3,4,4]{3,2,1,0:T(4,128)S(1)} %copy-done.3, ...), custom_call_target="tpu_custom_call" | custom-call | bytes 8388608 | tf_op jit(solution)/shard_map/pallas_call | solution.py:456
  53.9 0.0 collective-permute-done.9.refs_0_.att_across
  54.0 0.1 collective-permute-start.13
  54.1 0.3 shard_map.160
  54.4 0.0 collective-permute-done.10.att_beside
  54.4 1.4 %collective-permute-done.13.att_diagonal = bf16[512,288]{1,0:T(8,128)(2,1)S(1)} collective-permute-done((bf16[512,288]{1,0:T(8,128)(2,1)S(1)}, bf16[512,288]{1,0:T(8,128)(2,1)S(1)}, u32[]{:S(2)}, u32[]{:S(2)}) %collective-permute-start.13) | collective-permute-done | bytes 294944 | tf_op jit(solution)/shard_map/ppermute | solution.py:45
  55.8 2.9 %shard_map.161 = (f32[128,1152]{1,0:T(8,128)S(1)}, bf16[128,1152]{1,0:T(8,128)(2,1)S(1)}, f32[8,128]{1,0:T(8,128)S(1)}) custom-call(s32[64]{0:T(128)S(1)} %pad_add_fusion.table_ref.latent_ref, bf16[512,288]{1,0:T(8,128)(2,1)S(1)} %shard_map.157.att_own, bf16[512,288]{1,0:T(8,128)(2,1)S(1)} %collective-permute-done.9.refs_0_.att_across, ...), custom_call_target="tpu_custom_call" | custom-call | flops 1358954496 | bytes 8388608 | tf_op jit(solution)/shard_map/pallas_call | solution.py:486
  58.7 0.2 collective-permute-start.15
  59.0 2.6 %shard_map.163 = (bf16[128,1152]{1,0:T(8,128)(2,1)S(1)}, f32[8,128]{1,0:T(8,128)}) custom-call(s32[64]{0:T(128)S(1)} %pad_add_fusion.table_ref.latent_ref, bf16[512,288]{1,0:T(8,128)(2,1)S(1)} %shard_map.157.att_own, bf16[512,288]{1,0:T(8,128)(2,1)S(1)} %collective-permute-done.9.refs_0_.att_across, bf16[512,288]{1,0:T(8,128)(2,1)S(1)} %collective-permute-done.10.att_beside, ...), custom_call_target="tpu_custom_call" | custom-call | flops 679477248 | bytes 8388608 | tf_op jit(solution)/shard_map/pallas_call | solution.py:486
  61.5 0.4 collective-permute-start.16
  61.9 0.1 add_convert_fusion.refs_0_
  62.0 0.0 copy-start.4
  62.0 0.0 copy-start.5
  62.0 0.0 copy-start.6
  62.0 1.5 %collective-permute-start.17 = (bf16[128,1152]{1,0:T(8,128)(2,1)S(1)}, bf16[128,1152]{1,0:T(8,128)(2,1)S(1)}, u32[]{:S(2)}, u32[]{:S(2)}) collective-permute-start(bf16[128,1152]{1,0:T(8,128)(2,1)S(1)} %add_convert_fusion.refs_0_), channel_id=1, source_target_pairs={{0,2},{1,3},{2,0},{3,1},{4,6},{5,7},{6,4},{7,5},{8,10},{9,11},{10,... | collective-permute-start | bytes 884744 | tf_op jit(solution)/shard_map/ppermute | solution.py:45
  63.5 2.5 %shard_map.162 = (f32[128,1152]{1,0:T(8,128)S(1)}, bf16[128,1152]{1,0:T(8,128)(2,1)S(1)}, f32[8,128]{1,0:T(8,128)}) custom-call(s32[64]{0:T(128)S(1)} %pad_add_fusion.table_ref.latent_ref, bf16[512,288]{1,0:T(8,128)(2,1)S(1)} %shard_map.157.att_own, bf16[512,288]{1,0:T(8,128)(2,1)S(1)} %collective-permute-done.9.refs_0_.att_across, ...), custom_call_target="tpu_custom_call" | custom-call | flops 679477248 | bytes 8388608 | tf_op jit(solution)/shard_map/pallas_call | solution.py:486
  66.1 5.0 %collective-permute-done.17.crossed_ref = bf16[128,1152]{1,0:T(8,128)(2,1)S(1)} collective-permute-done((bf16[128,1152]{1,0:T(8,128)(2,1)S(1)}, bf16[128,1152]{1,0:T(8,128)(2,1)S(1)}, u32[]{:S(2)}, u32[]{:S(2)}) %collective-permute-start.17) | collective-permute-done | bytes 294944 | tf_op jit(solution)/shard_map/ppermute | solution.py:45
  71.1 1.1 %shard_map.164.first = f32[8,256]{1,0:T(8,128)S(1)} custom-call(s32[64]{0:T(128)S(1)} %pad_add_fusion.table_ref.latent_ref, f32[128,1152]{1,0:T(8,128)S(1)} %get-tuple-element.36.kept_ref, bf16[128,1152]{1,0:T(8,128)(2,1)S(1)} %collective-permute-done.16.beside_ref, bf16[128,1152]{1,0:T(8,128)(2,1)S(1)} %collective-permute-done.17.crossed_ref, ...), custom_call_target="tpu_custom_call" | custom-call | flops 75497472 | bytes 2097152 | tf_op jit(solution)/shard_map/pallas_call | solution.py:500
  72.3 0.1 collective-permute-start.18
  72.3 1.2 %collective-permute-done.18.second = f32[8,256]{1,0:T(8,128)S(1)} collective-permute-done((f32[8,256]{1,0:T(8,128)S(1)}, f32[8,256]{1,0:T(8,128)S(1)}, u32[]{:S(2)}, u32[]{:S(2)}) %collective-permute-start.18) | collective-permute-done | bytes 8224 | tf_op jit(solution)/shard_map/ppermute | solution.py:45
  73.5 1.5 %collective-permute-start.19 = (f32[16,256]{1,0:T(8,128)S(1)}, f32[16,256]{1,0:T(8,128)S(1)}, u32[]{:S(2)}, u32[]{:S(2)}) collective-permute-start(f32[16,256]{1,0:T(8,128)S(1)} %shard_map.165.near), channel_id=1, source_target_pairs={{0,2},{1,3},{2,0},{3,1},{4,6},{5,7},{6,4},{7,5},{8,10},{9,11},{10,... | collective-permute-start | bytes 49160 | tf_op jit(solution)/shard_map/ppermute | solution.py:45
  74.9 2.3 %collective-permute-done.19.far = f32[16,256]{1,0:T(8,128)S(1)} collective-permute-done((f32[16,256]{1,0:T(8,128)S(1)}, f32[16,256]{1,0:T(8,128)S(1)}, u32[]{:S(2)}, u32[]{:S(2)}) %collective-permute-start.19) | collective-permute-done | bytes 16416 | tf_op jit(solution)/shard_map/ppermute | solution.py:45
  77.2 1.5 %shard_map.166 = (bf16[64,128]{1,0:T(8,128)(2,1)}, bf16[64,128]{1,0:T(8,128)(2,1)}) custom-call(s32[64]{0:T(128)S(1)} %pad_add_fusion.table_ref.latent_ref, f32[50]{0:T(128)S(1)} %copy-done.5, f32[50]{0:T(128)S(1)} %copy-done.6, f32[16,256]{1,0:T(8,128)S(1)} %shard_map.165.near, f32[16,256]{1,0:T(8,128)S(1)} %collective-permute-done.19.far, ...), custom_call_target="tpu_custom_call" | custom-call | flops 12582912 | bytes 524288 | tf_op jit(solution)/shard_map/pallas_call | solution.py:509
  (25 shorter events, 0.1 us)
Async XLA Ops:
  0.6 12.3 %copy-start = (bf16[144,8,288]{2,1,0:T(8,128)(2,1)S(1)}, bf16[144,8,288]{2,1,0:T(8,128)(2,1)}, u32[]{:S(2)}) copy-start(bf16[144,8,288]{2,1,0:T(8,128)(2,1)} %param.21) | copy-start | bytes 1990660
  0.6 11.1 %copy-start.10 = (s32[32]{0:T(128)S(1)}, s32[32]{0:T(128)}, u32[]{:S(2)}) copy-start(s32[32]{0:T(128)} %param.16) | copy-start | bytes 388
  0.7 11.1 %copy-start.9 = (s32[32]{0:T(128)S(1)}, s32[32]{0:T(128)}, u32[]{:S(2)}) copy-start(s32[32]{0:T(128)} %param.17) | copy-start | bytes 388
  0.7 11.1 %copy-start.2 = (bf16[50,1152]{1,0:T(8,128)(2,1)S(1)}, bf16[50,1152]{1,0:T(8,128)(2,1)}, u32[]{:S(2)}) copy-start(bf16[50,1152]{1,0:T(8,128)(2,1)} %embedding_ref.1) | copy-start | bytes 345604
  1.6 4.3 %copy-start.7 = (bf16[576,144]{0,1:T(8,128)(2,1)S(1)}, bf16[576,144]{0,1:T(8,128)(2,1)}, u32[]{:S(2)}) copy-start(bf16[576,144]{0,1:T(8,128)(2,1)} %param.25) | copy-start | bytes 497668
  1.6 4.3 %copy-start.8 = (bf16[144,576]{1,0:T(8,128)(2,1)S(1)}, bf16[144,576]{1,0:T(8,128)(2,1)}, u32[]{:S(2)}) copy-start(bf16[144,576]{1,0:T(8,128)(2,1)} %param.24) | copy-start | bytes 497668
  2.9 28.2 %collective-permute-start.1 = (bf16[288,1680]{1,0:T(8,128)(2,1)S(1)}, bf16[288,1680]{1,0:T(8,128)(2,1)S(1)}, u32[]{:S(2)}, u32[]{:S(2)}) collective-permute-start(bf16[288,1680]{1,0:T(8,128)(2,1)S(1)} %pad_maximum_fusion.own), channel_id=1, source_target_pairs={{0,2},{1,3},{2,0},{3,1},{4,6},{5,7},{6,4},{7,5},{8,10},{9,11},{10,... | collective-permute-start | bytes 2903048 | tf_op jit(solution)/shard_map/ppermute | solution.py:45
  6.0 20.6 %collective-permute-start.2 = (bf16[288,576]{1,0:T(8,128)(2,1)S(1)}, bf16[288,576]{1,0:T(8,128)(2,1)}, u32[]{:S(2)}, u32[]{:S(2)}) collective-permute-start(bf16[288,576]{1,0:T(8,128)(2,1)S(1)} %pad_maximum_fusion.1.refs_0_), channel_id=1, source_target_pairs={{0,16},{4,20},{8,24},{12,28},{16,0},{20,4},{24,8},{28,12},{1,17},{... | collective-permute-start | bytes 995336 | tf_op jit(solution)/shard_map/ppermute | solution.py:45
  8.6 18.2 %collective-permute-start.3 = (bf16[288,576]{1,0:T(8,128)(2,1)S(1)}, bf16[288,576]{1,0:T(8,128)(2,1)}, u32[]{:S(2)}, u32[]{:S(2)}) collective-permute-start(bf16[288,576]{1,0:T(8,128)(2,1)S(1)} %pad_maximum_fusion.1.refs_0_), channel_id=1, source_target_pairs={{0,8},{4,12},{8,0},{12,4},{16,24},{20,28},{24,16},{28,20},{1,9},{5... | collective-permute-start | bytes 995336 | tf_op jit(solution)/shard_map/ppermute | solution.py:45
  10.2 16.7 %collective-permute-start.4 = (bf16[288,576]{1,0:T(8,128)(2,1)S(1)}, bf16[288,576]{1,0:T(8,128)(2,1)}, u32[]{:S(2)}, u32[]{:S(2)}) collective-permute-start(bf16[288,576]{1,0:T(8,128)(2,1)S(1)} %pad_maximum_fusion.1.refs_0_), channel_id=1, source_target_pairs={{0,4},{4,0},{8,12},{12,8},{16,20},{20,16},{24,28},{28,24},{1,5},{5... | collective-permute-start | bytes 995336 | tf_op jit(solution)/shard_map/ppermute | solution.py:45
  13.9 15.9 %all-to-all-start = ((f32[8,16,288]{2,1,0:T(8,128)}), f32[8,16,288]{2,1,0:T(8,128)S(1)}, u32[]{:S(2)}, u32[]{:S(2)}) async-start(f32[8,16,288]{2,1,0:T(8,128)} %bitcast.10), calls=%async_computation | async-start | bytes 393216 | tf_op jit(solution)/shard_map/all_to_all | solution.py:402
  29.8 1.3 %collective-permute-start.5 = (f32[16,288]{1,0:T(8,128)S(1)}, f32[16,288]{1,0:T(8,128)S(1)}, u32[]{:S(2)}, u32[]{:S(2)}) collective-permute-start(f32[16,288]{1,0:T(8,128)S(1)} %shard_map.151.first), channel_id=1, source_target_pairs={{0,1},{1,0},{2,3},{3,2},{4,5},{5,4},{6,7},{7,6},{8,9},{9,8},{10,11... | collective-permute-start | bytes 55304 | tf_op jit(solution)/shard_map/ppermute | solution.py:45
  29.9 6.7 %collective-permute-start = (bf16[288,1680]{1,0:T(8,128)(2,1)S(1)}, bf16[288,1680]{1,0:T(8,128)(2,1)S(1)}, u32[]{:S(2)}, u32[]{:S(2)}) collective-permute-start(bf16[288,1680]{1,0:T(8,128)(2,1)S(1)} %pad_maximum_fusion.own), channel_id=1, source_target_pairs={{0,1},{1,0},{2,3},{3,2},{4,5},{5,4},{6,7},{7,6},{8,9},{9,8},{10,11... | collective-permute-start | bytes 2903048 | tf_op jit(solution)/shard_map/ppermute | solution.py:45
  31.1 5.5 %copy-start.1 = (bf16[1152,3,288]{0,2,1:T(8,128)(2,1)S(1)}, bf16[1152,3,288]{0,2,1:T(8,128)(2,1)}, u32[]{:S(2)}) copy-start(bf16[1152,3,288]{0,2,1:T(8,128)(2,1)} %param.22) | copy-start | bytes 5971972
  31.1 5.5 %collective-permute-start.6 = (bf16[288,1680]{1,0:T(8,128)(2,1)S(1)}, bf16[288,1680]{1,0:T(8,128)(2,1)S(1)}, u32[]{:S(2)}, u32[]{:S(2)}) collective-permute-start(bf16[288,1680]{1,0:T(8,128)(2,1)S(1)} %shard_map.153.across), channel_id=1, source_target_pairs={{0,1},{1,0},{2,3},{3,2},{4,5},{5,4},{6,7},{7,6},{8,9},{9,8},{10,11... | collective-permute-start | bytes 2903048 | tf_op jit(solution)/shard_map/ppermute | solution.py:45
  31.3 4.1 %collective-permute-start.7 = (f32[32,288]{1,0:T(8,128)S(1)}, f32[32,288]{1,0:T(8,128)S(1)}, u32[]{:S(2)}, u32[]{:S(2)}) collective-permute-start(f32[32,288]{1,0:T(8,128)S(1)} %shard_map.152.__1_.terms_near), channel_id=1, source_target_pairs={{0,2},{1,3},{2,0},{3,1},{4,6},{5,7},{6,4},{7,5},{8,10},{9,11},{10,... | collective-permute-start | bytes 110600 | tf_op jit(solution)/shard_map/ppermute | solution.py:45
  31.8 12.9 %collective-permute-start.11 = (bf16[288,576]{1,0:T(8,128)(2,1)}, bf16[288,576]{1,0:T(8,128)(2,1)S(1)}, u32[]{:S(2)}, u32[]{:S(2)}) collective-permute-start(bf16[288,576]{1,0:T(8,128)(2,1)} %collective-permute-done.2.refs_1_.refs_3_), channel_id=1, source_target_pairs={{0,4},{4,0},{8,12},{12,8},{16,20},{20,16},{24,28},{28,24},{1,5},{5... | collective-permute-start | bytes 995336 | tf_op jit(solution)/shard_map/ppermute | solution.py:45
  32.7 11.2 %collective-permute-start.8 = (bf16[288,576]{1,0:T(8,128)(2,1)}, bf16[288,576]{1,0:T(8,128)(2,1)S(1)}, u32[]{:S(2)}, u32[]{:S(2)}) collective-permute-start(bf16[288,576]{1,0:T(8,128)(2,1)} %collective-permute-done.2.refs_1_.refs_3_), channel_id=1, source_target_pairs={{0,8},{4,12},{8,0},{12,4},{16,24},{20,28},{24,16},{28,20},{1,9},{5... | collective-permute-start | bytes 995336 | tf_op jit(solution)/shard_map/ppermute | solution.py:45
  35.4 15.1 %collective-permute-start.12 = (bf16[288,576]{1,0:T(8,128)(2,1)}, bf16[288,576]{1,0:T(8,128)(2,1)S(1)}, u32[]{:S(2)}, u32[]{:S(2)}) collective-permute-start(bf16[288,576]{1,0:T(8,128)(2,1)} %collective-permute-done.3.refs_2_), channel_id=1, source_target_pairs={{0,4},{4,0},{8,12},{12,8},{16,20},{20,16},{24,28},{28,24},{1,5},{5... | collective-permute-start | bytes 995336 | tf_op jit(solution)/shard_map/ppermute | solution.py:45
  40.0 10.5 %copy-start.3 = (f32[3,3,4,4]{3,2,1,0:T(4,128)S(1)}, f32[3,3,4,4]{3,2,1,0:T(4,128)}, u32[]{:S(2)}) copy-start(f32[3,3,4,4]{3,2,1,0:T(4,128)} %kernel_ref.1) | copy-start | bytes 1732
  44.0 10.0 %collective-permute-start.9 = (bf16[512,288]{1,0:T(8,128)(2,1)S(1)}, bf16[512,288]{1,0:T(8,128)(2,1)S(1)}, u32[]{:S(2)}, u32[]{:S(2)}) collective-permute-start(bf16[512,288]{1,0:T(8,128)(2,1)S(1)} %shard_map.157.att_own), channel_id=1, source_target_pairs={{0,2},{1,3},{2,0},{3,1},{4,6},{5,7},{6,4},{7,5},{8,10},{9,11},{10,... | collective-permute-start | bytes 884744 | tf_op jit(solution)/shard_map/ppermute | solution.py:45
  44.7 9.4 %collective-permute-start.14 = (bf16[288,576]{1,0:T(8,128)(2,1)S(1)}, bf16[288,576]{1,0:T(8,128)(2,1)S(1)}, u32[]{:S(2)}, u32[]{:S(2)}) collective-permute-start(bf16[288,576]{1,0:T(8,128)(2,1)S(1)} %collective-permute-done.11.refs_4_), channel_id=1, source_target_pairs={{0,8},{4,12},{8,0},{12,4},{16,24},{20,28},{24,16},{28,20},{1,9},{5... | collective-permute-start | bytes 995336 | tf_op jit(solution)/shard_map/ppermute | solution.py:45
  45.5 8.9 %collective-permute-start.10 = (bf16[512,288]{1,0:T(8,128)(2,1)S(1)}, bf16[512,288]{1,0:T(8,128)(2,1)S(1)}, u32[]{:S(2)}, u32[]{:S(2)}) collective-permute-start(bf16[512,288]{1,0:T(8,128)(2,1)S(1)} %shard_map.157.att_own), channel_id=1, source_target_pairs={{0,1},{1,0},{2,3},{3,2},{4,5},{5,4},{6,7},{7,6},{8,9},{9,8},{10,11... | collective-permute-start | bytes 884744 | tf_op jit(solution)/shard_map/ppermute | solution.py:45
  54.0 1.8 %collective-permute-start.13 = (bf16[512,288]{1,0:T(8,128)(2,1)S(1)}, bf16[512,288]{1,0:T(8,128)(2,1)S(1)}, u32[]{:S(2)}, u32[]{:S(2)}) collective-permute-start(bf16[512,288]{1,0:T(8,128)(2,1)S(1)} %shard_map.159), channel_id=1, source_target_pairs={{0,1},{1,0},{2,3},{3,2},{4,5},{5,4},{6,7},{7,6},{8,9},{9,8},{10,11... | collective-permute-start | bytes 884744 | tf_op jit(solution)/shard_map/ppermute | solution.py:45
  58.7 3.1 %collective-permute-start.15 = (bf16[128,1152]{1,0:T(8,128)(2,1)S(1)}, bf16[128,1152]{1,0:T(8,128)(2,1)S(1)}, u32[]{:S(2)}, u32[]{:S(2)}) collective-permute-start(bf16[128,1152]{1,0:T(8,128)(2,1)S(1)} %get-tuple-element.35), channel_id=1, source_target_pairs={{0,1},{1,0},{2,3},{3,2},{4,5},{5,4},{6,7},{7,6},{8,9},{9,8},{10,11... | collective-permute-start | bytes 884744 | tf_op jit(solution)/shard_map/ppermute | solution.py:45
  61.5 4.6 %collective-permute-start.16 = (bf16[128,1152]{1,0:T(8,128)(2,1)S(1)}, bf16[128,1152]{1,0:T(8,128)(2,1)S(1)}, u32[]{:S(2)}, u32[]{:S(2)}) collective-permute-start(bf16[128,1152]{1,0:T(8,128)(2,1)S(1)} %get-tuple-element.38), channel_id=1, source_target_pairs={{0,1},{1,0},{2,3},{3,2},{4,5},{5,4},{6,7},{7,6},{8,9},{9,8},{10,11... | collective-permute-start | bytes 884744 | tf_op jit(solution)/shard_map/ppermute | solution.py:45
  62.0 15.3 %copy-start.4 = (bf16[64,128]{1,0:T(8,128)(2,1)S(1)}, bf16[64,128]{1,0:T(8,128)(2,1)}, u32[]{:S(2)}) copy-start(bf16[64,128]{1,0:T(8,128)(2,1)} %noisy_ref.1) | copy-start | bytes 49156
  62.0 15.3 %copy-start.5 = (f32[50]{0:T(128)S(1)}, f32[50]{0:T(128)}, u32[]{:S(2)}) copy-start(f32[50]{0:T(128)} %now_ref.1) | copy-start | bytes 604
  62.0 15.3 %copy-start.6 = (f32[50]{0:T(128)S(1)}, f32[50]{0:T(128)}, u32[]{:S(2)}) copy-start(f32[50]{0:T(128)} %next_ref.1) | copy-start | bytes 604
  62.0 9.1 %collective-permute-start.17 = (bf16[128,1152]{1,0:T(8,128)(2,1)S(1)}, bf16[128,1152]{1,0:T(8,128)(2,1)S(1)}, u32[]{:S(2)}, u32[]{:S(2)}) collective-permute-start(bf16[128,1152]{1,0:T(8,128)(2,1)S(1)} %add_convert_fusion.refs_0_), channel_id=1, source_target_pairs={{0,2},{1,3},{2,0},{3,1},{4,6},{5,7},{6,4},{7,5},{8,10},{9,11},{10,... | collective-permute-start | bytes 884744 | tf_op jit(solution)/shard_map/ppermute | solution.py:45
  72.3 1.2 %collective-permute-start.18 = (f32[8,256]{1,0:T(8,128)S(1)}, f32[8,256]{1,0:T(8,128)S(1)}, u32[]{:S(2)}, u32[]{:S(2)}) collective-permute-start(f32[8,256]{1,0:T(8,128)S(1)} %shard_map.164.first), channel_id=1, source_target_pairs={{0,1},{1,0},{2,3},{3,2},{4,5},{5,4},{6,7},{7,6},{8,9},{9,8},{10,11... | collective-permute-start | bytes 24584 | tf_op jit(solution)/shard_map/ppermute | solution.py:45
  73.5 3.7 %collective-permute-start.19 = (f32[16,256]{1,0:T(8,128)S(1)}, f32[16,256]{1,0:T(8,128)S(1)}, u32[]{:S(2)}, u32[]{:S(2)}) collective-permute-start(f32[16,256]{1,0:T(8,128)S(1)} %shard_map.165.near), channel_id=1, source_target_pairs={{0,2},{1,3},{2,0},{3,1},{4,6},{5,7},{6,4},{7,5},{8,10},{9,11},{10,... | collective-permute-start | bytes 49160 | tf_op jit(solution)/shard_map/ppermute | solution.py:45

commit v8 on v7

--- a/solution.py
+++ b/solution.py
@@ -99,10 +99,6 @@
     first = lax.axis_index("row") * (lax.axis_size("col"))
     later = latent_ref[first + tile] != latent_ref[first]
     return jnp.where(later, terms_ref[8 + index : 9 + index, :], terms_ref[index : index + 1, :])
-
-
-def pass_kernel(*refs):
-    refs[-1][...] = refs[0][...]
 
 
 def terms_kernel(terms_near, terms_far, terms_ref, columns):
@@ -466,11 +462,9 @@
         [SMEM] + [VMEM] * (4 + len(parts)) + [ANYWHERE],
         nbytes=2**23, limit=24,
     )(preview_kernel, *blocks, *(part[2] for part in parts), attention_done)
-    if staged:
-        attended = after(attended, both_6)
     across = exchange(attended, "col", 2)
-    passed = call(pass_kernel, shape(across.shape, NARROW), [VMEM, ANYWHERE], nbytes=2**19)(across, tokens)
-    attended_blocks = (attended, across, exchange(attended, "col", 1), exchange(passed, "col", 1))
+    across = after(across, tokens)
+    attended_blocks = (attended, across, exchange(attended, "col", 1), exchange(across, "col", 1))
     if last:
         expand_all, reduce_all = call(
             functools.partial(complete_kernel, [part[:2] for part in last], split),

time: 79 us -> 78.9 us (level)
  no operation moved by 1% of the time
where the time goes in v8:
time: 78.9 us; the launch traced here: 78.6 us
  waiting for transfers between devices  30 us (38%)
  Pallas kernels  23 us (29%)
  starting transfers between devices  21.3 us (27%)
  local copies, waits for them, and re-layouts  1.71 us (2%)
  other arithmetic  1.47 us (2%)
  between operations  0.9 us (1%)
    ppermute x20, waiting for transfers between devices, exchange(): return lax.ppermute(value, axis, [(i, i ^ offset) for i in range(size)])  27 us
    ppermute x20, starting transfers between devices, exchange(): return lax.ppermute(value, axis, [(i, i ^ offset) for i in range(size)])  17.9 us
    pallas_call x3, Pallas kernels, mlp(): call(functools.partial(mlp_kernel, offsets), outs, [SMEM] + [VMEM] * 9 +...  8.03 us
    pallas_call x1, Pallas kernels, shards(): call(attention_kernel, [shape((tokens_here, width), NARROW), mark], [SMEM...  3.9 us
    all_to_all x1, starting transfers between devices, shards(): received = lax.all_to_all(partial, 'row', 0, 0, tiled=True)  3.39 us
    pallas_call x1, Pallas kernels, shards(): call(functools.partial(assemble_kernel, [part[:2] for part in parts], spl...  3.39 us
    pallas_call x1, Pallas kernels, shards(): call(triple_kernel, shape((3 * width, tokens_here), WIDE), [SMEM] + [VMEM...  3.36 us
    all_to_all x1, waiting for transfers between devices, shards(): received = lax.all_to_all(partial, 'row', 0, 0, tiled=True)  2.92 us
  transfers between devices with their start and end apart: 21, of which 10 were waited for; matrix products, arithmetic and copies ran while one was open for 2% of the time, Pallas kernels for 22%

profile of v8, /device:TPU:0, one launch (start us, length us, event | category | flops | bytes accessed | tf_op | source)
XLA Modules:
  0.0 78.6 jit_solution(3898466929542781628)
XLA Ops:
  0.6 0.0 copy-start
  0.7 0.9 %copy.18 = bf16[288,16]{1,0:T(8,128)(2,1)S(1)} copy(bf16[288,16]{0,1:T(8,128)(2,1)} %param.26) | data formatting | bytes 18432 | tf_op args[12]
  1.6 0.0 copy-start.7
  1.6 0.0 copy-start.8
  1.6 1.3 %pad_maximum_fusion.own = bf16[288,1680]{1,0:T(8,128)(2,1)S(1)} fusion(bf16[288,16]{1,0:T(8,128)(2,1)S(1)} %copy.18, bf16[288,1152]{1,0:T(8,128)(2,1)} %param.23, bf16[288,512]{1,0:T(8,128)(2,1)} %bitcast.11), kind=kLoop, calls=%fused_computation | loop fusion | flops 2903040 | bytes 1935360 | tf_op jit(solution)/shard_map/concatenate | solution.py:399
  2.9 3.0 %collective-permute-start.1 = (bf16[288,1680]{1,0:T(8,128)(2,1)S(1)}, bf16[288,1680]{1,0:T(8,128)(2,1)S(1)}, u32[]{:S(2)}, u32[]{:S(2)}) collective-permute-start(bf16[288,1680]{1,0:T(8,128)(2,1)S(1)} %pad_maximum_fusion.own), channel_id=1, source_target_pairs={{0,2},{1,3},{2,0},{3,1},{4,6},{5,7},{6,4},{7,5},{8,10},{9,11},{10,... | collective-permute-start | bytes 2903048 | tf_op jit(solution)/shard_map/ppermute | solution.py:45
  6.0 2.7 %collective-permute-start.2 = (bf16[288,576]{1,0:T(8,128)(2,1)S(1)}, bf16[288,576]{1,0:T(8,128)(2,1)}, u32[]{:S(2)}, u32[]{:S(2)}) collective-permute-start(bf16[288,576]{1,0:T(8,128)(2,1)S(1)} %pad_maximum_fusion.1.refs_0_), channel_id=1, source_target_pairs={{0,16},{4,20},{8,24},{12,28},{16,0},{20,4},{24,8},{28,12},{1,17},{... | collective-permute-start | bytes 995336 | tf_op jit(solution)/shard_map/ppermute | solution.py:45
  8.6 1.6 %collective-permute-start.3 = (bf16[288,576]{1,0:T(8,128)(2,1)S(1)}, bf16[288,576]{1,0:T(8,128)(2,1)}, u32[]{:S(2)}, u32[]{:S(2)}) collective-permute-start(bf16[288,576]{1,0:T(8,128)(2,1)S(1)} %pad_maximum_fusion.1.refs_0_), channel_id=1, source_target_pairs={{0,8},{4,12},{8,0},{12,4},{16,24},{20,28},{24,16},{28,20},{1,9},{5... | collective-permute-start | bytes 995336 | tf_op jit(solution)/shard_map/ppermute | solution.py:45
  10.2 1.5 %collective-permute-start.4 = (bf16[288,576]{1,0:T(8,128)(2,1)S(1)}, bf16[288,576]{1,0:T(8,128)(2,1)}, u32[]{:S(2)}, u32[]{:S(2)}) collective-permute-start(bf16[288,576]{1,0:T(8,128)(2,1)S(1)} %pad_maximum_fusion.1.refs_0_), channel_id=1, source_target_pairs={{0,4},{4,0},{8,12},{12,8},{16,20},{20,16},{24,28},{28,24},{1,5},{5... | collective-permute-start | bytes 995336 | tf_op jit(solution)/shard_map/ppermute | solution.py:45
  11.7 0.1 pad_add_fusion.table_ref.latent_ref
  11.8 1.1 %shard_map.149 = (bf16[16,144]{1,0:T(8,128)(2,1)S(1)}, f32[8,128]{1,0:T(8,128)S(1)}) custom-call(s32[64]{0:T(128)S(1)} %pad_add_fusion.table_ref.latent_ref, bf16[50,1152]{1,0:T(8,128)(2,1)S(1)} %copy-done.2), custom_call_target="tpu_custom_call" | custom-call | flops 7151616 | bytes 115200 | tf_op jit(solution)/shard_map/pallas_call | solution.py:389
  12.9 0.3 fusion
  13.2 0.7 copy.20
  13.9 3.4 %all-to-all-start = ((f32[8,16,288]{2,1,0:T(8,128)}), f32[8,16,288]{2,1,0:T(8,128)S(1)}, u32[]{:S(2)}, u32[]{:S(2)}) async-start(f32[8,16,288]{2,1,0:T(8,128)} %bitcast.10), calls=%async_computation | async-start | bytes 393216 | tf_op jit(solution)/shard_map/all_to_all | solution.py:398
  17.3 9.2 %collective-permute-done.2.refs_1_.refs_3_ = bf16[288,576]{1,0:T(8,128)(2,1)} collective-permute-done((bf16[288,576]{1,0:T(8,128)(2,1)S(1)}, bf16[288,576]{1,0:T(8,128)(2,1)}, u32[]{:S(2)}, u32[]{:S(2)}) %collective-permute-start.2) | collective-permute-done | bytes 331808 | tf_op jit(solution)/shard_map/ppermute | solution.py:45
  26.5 0.3 collective-permute-done.3.refs_2_
  26.8 0.0 collective-permute-done.4.refs_3_.refs_1_
  26.9 2.9 %all-to-all-done.parts_ref = f32[8,16,288]{2,1,0:T(8,128)S(1)} async-done(((f32[8,16,288]{2,1,0:T(8,128)}), f32[8,16,288]{2,1,0:T(8,128)S(1)}, u32[]{:S(2)}, u32[]{:S(2)}) %all-to-all-start) | async-done | bytes 147488 | tf_op jit(solution)/shard_map/all_to_all | solution.py:398
  29.8 0.1 collective-permute-start.5
  29.9 0.5 collective-permute-start
  30.4 0.7 collective-permute-done.5.second
  31.1 0.0 collective-permute-done.1.__0_
  31.1 0.0 copy-start.1
  31.1 0.2 collective-permute-start.6
  31.3 0.5 collective-permute-start.7
  31.8 0.9 %collective-permute-start.9 = (bf16[288,576]{1,0:T(8,128)(2,1)}, bf16[288,576]{1,0:T(8,128)(2,1)S(1)}, u32[]{:S(2)}, u32[]{:S(2)}) collective-permute-start(bf16[288,576]{1,0:T(8,128)(2,1)} %collective-permute-done.2.refs_1_.refs_3_), channel_id=1, source_target_pairs={{0,4},{4,0},{8,12},{12,8},{16,20},{20,16},{24,28},{28,24},{1,5},{5... | collective-permute-start | bytes 995336 | tf_op jit(solution)/shard_map/ppermute | solution.py:45
  32.7 0.8 %collective-permute-start.10 = (bf16[288,576]{1,0:T(8,128)(2,1)}, bf16[288,576]{1,0:T(8,128)(2,1)S(1)}, u32[]{:S(2)}, u32[]{:S(2)}) collective-permute-start(bf16[288,576]{1,0:T(8,128)(2,1)} %collective-permute-done.2.refs_1_.refs_3_), channel_id=1, source_target_pairs={{0,8},{4,12},{8,0},{12,4},{16,24},{20,28},{24,16},{28,20},{1,9},{5... | collective-permute-start | bytes 995336 | tf_op jit(solution)/shard_map/ppermute | solution.py:45
  33.6 1.8 %collective-permute-done.7.terms_far = f32[32,288]{1,0:T(8,128)S(1)} collective-permute-done((f32[32,288]{1,0:T(8,128)S(1)}, f32[32,288]{1,0:T(8,128)S(1)}, u32[]{:S(2)}, u32[]{:S(2)}) %collective-permute-start.7) | collective-permute-done | bytes 36896 | tf_op jit(solution)/shard_map/ppermute | solution.py:45
  35.4 0.9 %collective-permute-start.11 = (bf16[288,576]{1,0:T(8,128)(2,1)}, bf16[288,576]{1,0:T(8,128)(2,1)S(1)}, u32[]{:S(2)}, u32[]{:S(2)}) collective-permute-start(bf16[288,576]{1,0:T(8,128)(2,1)} %collective-permute-done.3.refs_2_), channel_id=1, source_target_pairs={{0,4},{4,0},{8,12},{12,8},{16,20},{20,16},{24,28},{28,24},{1,5},{5... | collective-permute-start | bytes 995336 | tf_op jit(solution)/shard_map/ppermute | solution.py:45
  36.3 0.3 shard_map.154
  36.6 0.0 collective-permute-done.beside
  36.6 0.0 collective-permute-done.6.diagonal
  36.6 3.4 %shard_map.155.triple = f32[864,512]{1,0:T(8,128)S(1)} custom-call(s32[64]{0:T(128)S(1)} %pad_add_fusion.table_ref.latent_ref, bf16[288,1680]{1,0:T(8,128)(2,1)S(1)} %pad_maximum_fusion.own, bf16[288,1680]{1,0:T(8,128)(2,1)S(1)} %collective-permute-done.beside, bf16[288,1680]{1,0:T(8,128)(2,1)S(1)} %shard_map.153.across, ...), custom_call_target="tpu_custom_call" | custom-call | flops 1019215872 | bytes 5242880 | tf_op jit(solution)/shard_map/pallas_call | solution.py:433
  40.0 0.0 copy-start.3
  40.0 3.9 %shard_map.156 = (bf16[512,288]{1,0:T(8,128)(2,1)S(1)}, f32[8,128]{1,0:T(8,128)S(1)}) custom-call(s32[64]{0:T(128)S(1)} %pad_add_fusion.table_ref.latent_ref, f32[864,512]{1,0:T(8,128)S(1)} %shard_map.155.triple), custom_call_target="tpu_custom_call" | custom-call | flops 301989888 | tf_op jit(solution)/shard_map/pallas_call | solution.py:444
  43.9 0.6 collective-permute-start.8
  44.5 0.0 collective-permute-done.9.refs_4_
  44.5 0.9 %collective-permute-start.14 = (bf16[288,576]{1,0:T(8,128)(2,1)S(1)}, bf16[288,576]{1,0:T(8,128)(2,1)S(1)}, u32[]{:S(2)}, u32[]{:S(2)}) collective-permute-start(bf16[288,576]{1,0:T(8,128)(2,1)S(1)} %collective-permute-done.9.refs_4_), channel_id=1, source_target_pairs={{0,8},{4,12},{8,0},{12,4},{16,24},{20,28},{24,16},{28,20},{1,9},{5... | collective-permute-start | bytes 995336 | tf_op jit(solution)/shard_map/ppermute | solution.py:45
  45.4 5.1 %collective-permute-done.11.refs_6_ = bf16[288,576]{1,0:T(8,128)(2,1)S(1)} collective-permute-done((bf16[288,576]{1,0:T(8,128)(2,1)}, bf16[288,576]{1,0:T(8,128)(2,1)S(1)}, u32[]{:S(2)}, u32[]{:S(2)}) %collective-permute-start.11) | collective-permute-done | bytes 331808 | tf_op jit(solution)/shard_map/ppermute | solution.py:45
  50.5 3.4 %shard_map.157 = (bf16[1152,1152]{1,0:T(8,128)(2,1)S(1)}, bf16[1152,576]{1,0:T(8,128)(2,1)S(1)}, bf16[1152,576]{1,0:T(8,128)(2,1)S(1)}, bf16[512,1152]{1,0:T(8,1...) custom-call(f32[3,3,4,4]{3,2,1,0:T(4,128)S(1)} %copy-done.3, ...), custom_call_target="tpu_custom_call" | custom-call | bytes 8388608 | tf_op jit(solution)/shard_map/pallas_call | solution.py:452
  53.9 0.0 collective-permute-done.8.__0_
  53.9 0.1 collective-permute-start.13
  54.0 0.0 collective-permute-done.14.refs_0_
  54.0 0.3 shard_map.159
  54.3 1.4 %collective-permute-done.13.att_diagonal = bf16[512,288]{1,0:T(8,128)(2,1)S(1)} collective-permute-done((bf16[512,288]{1,0:T(8,128)(2,1)S(1)}, bf16[512,288]{1,0:T(8,128)(2,1)S(1)}, u32[]{:S(2)}, u32[]{:S(2)}) %collective-permute-start.13) | collective-permute-done | bytes 294944 | tf_op jit(solution)/shard_map/ppermute | solution.py:45
  55.7 2.9 %shard_map.160 = (f32[128,1152]{1,0:T(8,128)S(1)}, bf16[128,1152]{1,0:T(8,128)(2,1)S(1)}, f32[8,128]{1,0:T(8,128)S(1)}) custom-call(s32[64]{0:T(128)S(1)} %pad_add_fusion.table_ref.latent_ref, bf16[512,288]{1,0:T(8,128)(2,1)S(1)} %get-tuple-element.25.att_own, bf16[512,288]{1,0:T(8,128)(2,1)S(1)} %shard_map.158.att_across, ...), custom_call_target="tpu_custom_call" | custom-call | flops 1358954496 | bytes 8388608 | tf_op jit(solution)/shard_map/pallas_call | solution.py:480
  58.7 0.2 collective-permute-start.15
  58.9 2.6 %shard_map.162 = (bf16[128,1152]{1,0:T(8,128)(2,1)S(1)}, f32[8,128]{1,0:T(8,128)}) custom-call(s32[64]{0:T(128)S(1)} %pad_add_fusion.table_ref.latent_ref, bf16[512,288]{1,0:T(8,128)(2,1)S(1)} %get-tuple-element.25.att_own, bf16[512,288]{1,0:T(8,128)(2,1)S(1)} %shard_map.158.att_across, bf16[512,288]{1,0:T(8,128)(2,1)S(1)} %collective-permute-done.12.att_beside, ...), custom_call_target="tpu_custom_call" | custom-call | flops 679477248 | bytes 8388608 | tf_op jit(solution)/shard_map/pallas_call | solution.py:480
  61.4 0.4 collective-permute-start.16
  61.8 0.0 collective-permute-done.15
  61.8 0.1 add_convert_fusion.refs_0_
  61.9 0.0 copy-start.4
  61.9 0.0 copy-start.5
  61.9 0.0 copy-start.6
  61.9 1.6 %collective-permute-start.17 = (bf16[128,1152]{1,0:T(8,128)(2,1)S(1)}, bf16[128,1152]{1,0:T(8,128)(2,1)S(1)}, u32[]{:S(2)}, u32[]{:S(2)}) collective-permute-start(bf16[128,1152]{1,0:T(8,128)(2,1)S(1)} %add_convert_fusion.refs_0_), channel_id=1, source_target_pairs={{0,2},{1,3},{2,0},{3,1},{4,6},{5,7},{6,4},{7,5},{8,10},{9,11},{10,... | collective-permute-start | bytes 884744 | tf_op jit(solution)/shard_map/ppermute | solution.py:45
  63.5 2.5 %shard_map.161 = (f32[128,1152]{1,0:T(8,128)S(1)}, bf16[128,1152]{1,0:T(8,128)(2,1)S(1)}, f32[8,128]{1,0:T(8,128)}) custom-call(s32[64]{0:T(128)S(1)} %pad_add_fusion.table_ref.latent_ref, bf16[512,288]{1,0:T(8,128)(2,1)S(1)} %get-tuple-element.25.att_own, bf16[512,288]{1,0:T(8,128)(2,1)S(1)} %shard_map.158.att_across, ...), custom_call_target="tpu_custom_call" | custom-call | flops 679477248 | bytes 8388608 | tf_op jit(solution)/shard_map/pallas_call | solution.py:480
  66.0 0.0 collective-permute-done.16.beside_ref
  66.0 5.0 %collective-permute-done.17.crossed_ref = bf16[128,1152]{1,0:T(8,128)(2,1)S(1)} collective-permute-done((bf16[128,1152]{1,0:T(8,128)(2,1)S(1)}, bf16[128,1152]{1,0:T(8,128)(2,1)S(1)}, u32[]{:S(2)}, u32[]{:S(2)}) %collective-permute-start.17) | collective-permute-done | bytes 294944 | tf_op jit(solution)/shard_map/ppermute | solution.py:45
  71.0 1.1 %shard_map.163.first = f32[8,256]{1,0:T(8,128)S(1)} custom-call(s32[64]{0:T(128)S(1)} %pad_add_fusion.table_ref.latent_ref, f32[128,1152]{1,0:T(8,128)S(1)} %get-tuple-element.36.kept_ref, bf16[128,1152]{1,0:T(8,128)(2,1)S(1)} %collective-permute-done.16.beside_ref, bf16[128,1152]{1,0:T(8,128)(2,1)S(1)} %collective-permute-done.17.crossed_ref, ...), custom_call_target="tpu_custom_call" | custom-call | flops 75497472 | bytes 2097152 | tf_op jit(solution)/shard_map/pallas_call | solution.py:494
  72.2 0.1 collective-permute-start.18
  72.2 1.2 %collective-permute-done.18.second = f32[8,256]{1,0:T(8,128)S(1)} collective-permute-done((f32[8,256]{1,0:T(8,128)S(1)}, f32[8,256]{1,0:T(8,128)S(1)}, u32[]{:S(2)}, u32[]{:S(2)}) %collective-permute-start.18) | collective-permute-done | bytes 8224 | tf_op jit(solution)/shard_map/ppermute | solution.py:45
  73.4 1.5 %collective-permute-start.19 = (f32[16,256]{1,0:T(8,128)S(1)}, f32[16,256]{1,0:T(8,128)S(1)}, u32[]{:S(2)}, u32[]{:S(2)}) collective-permute-start(f32[16,256]{1,0:T(8,128)S(1)} %shard_map.164.near), channel_id=1, source_target_pairs={{0,2},{1,3},{2,0},{3,1},{4,6},{5,7},{6,4},{7,5},{8,10},{9,11},{10,... | collective-permute-start | bytes 49160 | tf_op jit(solution)/shard_map/ppermute | solution.py:45
  74.9 2.2 %collective-permute-done.19.far = f32[16,256]{1,0:T(8,128)S(1)} collective-permute-done((f32[16,256]{1,0:T(8,128)S(1)}, f32[16,256]{1,0:T(8,128)S(1)}, u32[]{:S(2)}, u32[]{:S(2)}) %collective-permute-start.19) | collective-permute-done | bytes 16416 | tf_op jit(solution)/shard_map/ppermute | solution.py:45
  77.2 1.5 %shard_map.165 = (bf16[64,128]{1,0:T(8,128)(2,1)}, bf16[64,128]{1,0:T(8,128)(2,1)}) custom-call(s32[64]{0:T(128)S(1)} %pad_add_fusion.table_ref.latent_ref, f32[50]{0:T(128)S(1)} %copy-done.5, f32[50]{0:T(128)S(1)} %copy-done.6, f32[16,256]{1,0:T(8,128)S(1)} %shard_map.164.near, f32[16,256]{1,0:T(8,128)S(1)} %collective-permute-done.19.far, ...), custom_call_target="tpu_custom_call" | custom-call | flops 12582912 | bytes 524288 | tf_op jit(solution)/shard_map/pallas_call | solution.py:503
  (24 shorter events, 0.1 us)
Async XLA Ops:
  0.6 12.3 %copy-start = (bf16[144,8,288]{2,1,0:T(8,128)(2,1)S(1)}, bf16[144,8,288]{2,1,0:T(8,128)(2,1)}, u32[]{:S(2)}) copy-start(bf16[144,8,288]{2,1,0:T(8,128)(2,1)} %param.21) | copy-start | bytes 1990660
  0.6 11.1 %copy-start.10 = (s32[32]{0:T(128)S(1)}, s32[32]{0:T(128)}, u32[]{:S(2)}) copy-start(s32[32]{0:T(128)} %param.16) | copy-start | bytes 388
  0.7 11.1 %copy-start.9 = (s32[32]{0:T(128)S(1)}, s32[32]{0:T(128)}, u32[]{:S(2)}) copy-start(s32[32]{0:T(128)} %param.17) | copy-start | bytes 388
  0.7 11.1 %copy-start.2 = (bf16[50,1152]{1,0:T(8,128)(2,1)S(1)}, bf16[50,1152]{1,0:T(8,128)(2,1)}, u32[]{:S(2)}) copy-start(bf16[50,1152]{1,0:T(8,128)(2,1)} %embedding_ref.1) | copy-start | bytes 345604
  1.6 4.3 %copy-start.7 = (bf16[576,144]{0,1:T(8,128)(2,1)S(1)}, bf16[576,144]{0,1:T(8,128)(2,1)}, u32[]{:S(2)}) copy-start(bf16[576,144]{0,1:T(8,128)(2,1)} %param.25) | copy-start | bytes 497668
  1.6 4.3 %copy-start.8 = (bf16[144,576]{1,0:T(8,128)(2,1)S(1)}, bf16[144,576]{1,0:T(8,128)(2,1)}, u32[]{:S(2)}) copy-start(bf16[144,576]{1,0:T(8,128)(2,1)} %param.24) | copy-start | bytes 497668
  2.9 28.2 %collective-permute-start.1 = (bf16[288,1680]{1,0:T(8,128)(2,1)S(1)}, bf16[288,1680]{1,0:T(8,128)(2,1)S(1)}, u32[]{:S(2)}, u32[]{:S(2)}) collective-permute-start(bf16[288,1680]{1,0:T(8,128)(2,1)S(1)} %pad_maximum_fusion.own), channel_id=1, source_target_pairs={{0,2},{1,3},{2,0},{3,1},{4,6},{5,7},{6,4},{7,5},{8,10},{9,11},{10,... | collective-permute-start | bytes 2903048 | tf_op jit(solution)/shard_map/ppermute | solution.py:45
  6.0 20.6 %collective-permute-start.2 = (bf16[288,576]{1,0:T(8,128)(2,1)S(1)}, bf16[288,576]{1,0:T(8,128)(2,1)}, u32[]{:S(2)}, u32[]{:S(2)}) collective-permute-start(bf16[288,576]{1,0:T(8,128)(2,1)S(1)} %pad_maximum_fusion.1.refs_0_), channel_id=1, source_target_pairs={{0,16},{4,20},{8,24},{12,28},{16,0},{20,4},{24,8},{28,12},{1,17},{... | collective-permute-start | bytes 995336 | tf_op jit(solution)/shard_map/ppermute | solution.py:45
  8.6 18.2 %collective-permute-start.3 = (bf16[288,576]{1,0:T(8,128)(2,1)S(1)}, bf16[288,576]{1,0:T(8,128)(2,1)}, u32[]{:S(2)}, u32[]{:S(2)}) collective-permute-start(bf16[288,576]{1,0:T(8,128)(2,1)S(1)} %pad_maximum_fusion.1.refs_0_), channel_id=1, source_target_pairs={{0,8},{4,12},{8,0},{12,4},{16,24},{20,28},{24,16},{28,20},{1,9},{5... | collective-permute-start | bytes 995336 | tf_op jit(solution)/shard_map/ppermute | solution.py:45
  10.2 16.7 %collective-permute-start.4 = (bf16[288,576]{1,0:T(8,128)(2,1)S(1)}, bf16[288,576]{1,0:T(8,128)(2,1)}, u32[]{:S(2)}, u32[]{:S(2)}) collective-permute-start(bf16[288,576]{1,0:T(8,128)(2,1)S(1)} %pad_maximum_fusion.1.refs_0_), channel_id=1, source_target_pairs={{0,4},{4,0},{8,12},{12,8},{16,20},{20,16},{24,28},{28,24},{1,5},{5... | collective-permute-start | bytes 995336 | tf_op jit(solution)/shard_map/ppermute | solution.py:45
  13.9 15.9 %all-to-all-start = ((f32[8,16,288]{2,1,0:T(8,128)}), f32[8,16,288]{2,1,0:T(8,128)S(1)}, u32[]{:S(2)}, u32[]{:S(2)}) async-start(f32[8,16,288]{2,1,0:T(8,128)} %bitcast.10), calls=%async_computation | async-start | bytes 393216 | tf_op jit(solution)/shard_map/all_to_all | solution.py:398
  29.8 1.3 %collective-permute-start.5 = (f32[16,288]{1,0:T(8,128)S(1)}, f32[16,288]{1,0:T(8,128)S(1)}, u32[]{:S(2)}, u32[]{:S(2)}) collective-permute-start(f32[16,288]{1,0:T(8,128)S(1)} %shard_map.151.first), channel_id=1, source_target_pairs={{0,1},{1,0},{2,3},{3,2},{4,5},{5,4},{6,7},{7,6},{8,9},{9,8},{10,11... | collective-permute-start | bytes 55304 | tf_op jit(solution)/shard_map/ppermute | solution.py:45
  29.9 6.7 %collective-permute-start = (bf16[288,1680]{1,0:T(8,128)(2,1)S(1)}, bf16[288,1680]{1,0:T(8,128)(2,1)S(1)}, u32[]{:S(2)}, u32[]{:S(2)}) collective-permute-start(bf16[288,1680]{1,0:T(8,128)(2,1)S(1)} %pad_maximum_fusion.own), channel_id=1, source_target_pairs={{0,1},{1,0},{2,3},{3,2},{4,5},{5,4},{6,7},{7,6},{8,9},{9,8},{10,11... | collective-permute-start | bytes 2903048 | tf_op jit(solution)/shard_map/ppermute | solution.py:45
  31.1 5.5 %copy-start.1 = (bf16[1152,3,288]{0,2,1:T(8,128)(2,1)S(1)}, bf16[1152,3,288]{0,2,1:T(8,128)(2,1)}, u32[]{:S(2)}) copy-start(bf16[1152,3,288]{0,2,1:T(8,128)(2,1)} %param.22) | copy-start | bytes 5971972
  31.1 5.5 %collective-permute-start.6 = (bf16[288,1680]{1,0:T(8,128)(2,1)S(1)}, bf16[288,1680]{1,0:T(8,128)(2,1)S(1)}, u32[]{:S(2)}, u32[]{:S(2)}) collective-permute-start(bf16[288,1680]{1,0:T(8,128)(2,1)S(1)} %shard_map.153.across), channel_id=1, source_target_pairs={{0,1},{1,0},{2,3},{3,2},{4,5},{5,4},{6,7},{7,6},{8,9},{9,8},{10,11... | collective-permute-start | bytes 2903048 | tf_op jit(solution)/shard_map/ppermute | solution.py:45
  31.3 4.1 %collective-permute-start.7 = (f32[32,288]{1,0:T(8,128)S(1)}, f32[32,288]{1,0:T(8,128)S(1)}, u32[]{:S(2)}, u32[]{:S(2)}) collective-permute-start(f32[32,288]{1,0:T(8,128)S(1)} %shard_map.152.__1_.terms_near), channel_id=1, source_target_pairs={{0,2},{1,3},{2,0},{3,1},{4,6},{5,7},{6,4},{7,5},{8,10},{9,11},{10,... | collective-permute-start | bytes 110600 | tf_op jit(solution)/shard_map/ppermute | solution.py:45
  31.8 12.7 %collective-permute-start.9 = (bf16[288,576]{1,0:T(8,128)(2,1)}, bf16[288,576]{1,0:T(8,128)(2,1)S(1)}, u32[]{:S(2)}, u32[]{:S(2)}) collective-permute-start(bf16[288,576]{1,0:T(8,128)(2,1)} %collective-permute-done.2.refs_1_.refs_3_), channel_id=1, source_target_pairs={{0,4},{4,0},{8,12},{12,8},{16,20},{20,16},{24,28},{28,24},{1,5},{5... | collective-permute-start | bytes 995336 | tf_op jit(solution)/shard_map/ppermute | solution.py:45
  32.7 12.7 %collective-permute-start.10 = (bf16[288,576]{1,0:T(8,128)(2,1)}, bf16[288,576]{1,0:T(8,128)(2,1)S(1)}, u32[]{:S(2)}, u32[]{:S(2)}) collective-permute-start(bf16[288,576]{1,0:T(8,128)(2,1)} %collective-permute-done.2.refs_1_.refs_3_), channel_id=1, source_target_pairs={{0,8},{4,12},{8,0},{12,4},{16,24},{20,28},{24,16},{28,20},{1,9},{5... | collective-permute-start | bytes 995336 | tf_op jit(solution)/shard_map/ppermute | solution.py:45
  35.4 15.1 %collective-permute-start.11 = (bf16[288,576]{1,0:T(8,128)(2,1)}, bf16[288,576]{1,0:T(8,128)(2,1)S(1)}, u32[]{:S(2)}, u32[]{:S(2)}) collective-permute-start(bf16[288,576]{1,0:T(8,128)(2,1)} %collective-permute-done.3.refs_2_), channel_id=1, source_target_pairs={{0,4},{4,0},{8,12},{12,8},{16,20},{20,16},{24,28},{28,24},{1,5},{5... | collective-permute-start | bytes 995336 | tf_op jit(solution)/shard_map/ppermute | solution.py:45
  40.0 10.5 %copy-start.3 = (f32[3,3,4,4]{3,2,1,0:T(4,128)S(1)}, f32[3,3,4,4]{3,2,1,0:T(4,128)}, u32[]{:S(2)}) copy-start(f32[3,3,4,4]{3,2,1,0:T(4,128)} %kernel_ref.1) | copy-start | bytes 1732
  43.9 10.0 %collective-permute-start.8 = (bf16[512,288]{1,0:T(8,128)(2,1)S(1)}, bf16[512,288]{1,0:T(8,128)(2,1)S(1)}, u32[]{:S(2)}, u32[]{:S(2)}) collective-permute-start(bf16[512,288]{1,0:T(8,128)(2,1)S(1)} %get-tuple-element.25.att_own), channel_id=1, source_target_pairs={{0,2},{1,3},{2,0},{3,1},{4,6},{5,7},{6,4},{7,5},{8,10},{9,11},{10,... | collective-permute-start | bytes 884744 | tf_op jit(solution)/shard_map/ppermute | solution.py:45
  44.5 9.5 %collective-permute-start.14 = (bf16[288,576]{1,0:T(8,128)(2,1)S(1)}, bf16[288,576]{1,0:T(8,128)(2,1)S(1)}, u32[]{:S(2)}, u32[]{:S(2)}) collective-permute-start(bf16[288,576]{1,0:T(8,128)(2,1)S(1)} %collective-permute-done.9.refs_4_), channel_id=1, source_target_pairs={{0,8},{4,12},{8,0},{12,4},{16,24},{20,28},{24,16},{28,20},{1,9},{5... | collective-permute-start | bytes 995336 | tf_op jit(solution)/shard_map/ppermute | solution.py:45
  45.4 8.9 %collective-permute-start.12 = (bf16[512,288]{1,0:T(8,128)(2,1)S(1)}, bf16[512,288]{1,0:T(8,128)(2,1)S(1)}, u32[]{:S(2)}, u32[]{:S(2)}) collective-permute-start(bf16[512,288]{1,0:T(8,128)(2,1)S(1)} %get-tuple-element.25.att_own), channel_id=1, source_target_pairs={{0,1},{1,0},{2,3},{3,2},{4,5},{5,4},{6,7},{7,6},{8,9},{9,8},{10,11... | collective-permute-start | bytes 884744 | tf_op jit(solution)/shard_map/ppermute | solution.py:45
  53.9 1.8 %collective-permute-start.13 = (bf16[512,288]{1,0:T(8,128)(2,1)S(1)}, bf16[512,288]{1,0:T(8,128)(2,1)S(1)}, u32[]{:S(2)}, u32[]{:S(2)}) collective-permute-start(bf16[512,288]{1,0:T(8,128)(2,1)S(1)} %shard_map.158.att_across), channel_id=1, source_target_pairs={{0,1},{1,0},{2,3},{3,2},{4,5},{5,4},{6,7},{7,6},{8,9},{9,8},{10,11... | collective-permute-start | bytes 884744 | tf_op jit(solution)/shard_map/ppermute | solution.py:45
  58.7 3.1 %collective-permute-start.15 = (bf16[128,1152]{1,0:T(8,128)(2,1)S(1)}, bf16[128,1152]{1,0:T(8,128)(2,1)S(1)}, u32[]{:S(2)}, u32[]{:S(2)}) collective-permute-start(bf16[128,1152]{1,0:T(8,128)(2,1)S(1)} %get-tuple-element.35), channel_id=1, source_target_pairs={{0,1},{1,0},{2,3},{3,2},{4,5},{5,4},{6,7},{7,6},{8,9},{9,8},{10,11... | collective-permute-start | bytes 884744 | tf_op jit(solution)/shard_map/ppermute | solution.py:45
  61.4 4.6 %collective-permute-start.16 = (bf16[128,1152]{1,0:T(8,128)(2,1)S(1)}, bf16[128,1152]{1,0:T(8,128)(2,1)S(1)}, u32[]{:S(2)}, u32[]{:S(2)}) collective-permute-start(bf16[128,1152]{1,0:T(8,128)(2,1)S(1)} %get-tuple-element.38), channel_id=1, source_target_pairs={{0,1},{1,0},{2,3},{3,2},{4,5},{5,4},{6,7},{7,6},{8,9},{9,8},{10,11... | collective-permute-start | bytes 884744 | tf_op jit(solution)/shard_map/ppermute | solution.py:45
  61.9 15.3 %copy-start.4 = (bf16[64,128]{1,0:T(8,128)(2,1)S(1)}, bf16[64,128]{1,0:T(8,128)(2,1)}, u32[]{:S(2)}) copy-start(bf16[64,128]{1,0:T(8,128)(2,1)} %noisy_ref.1) | copy-start | bytes 49156
  61.9 15.3 %copy-start.5 = (f32[50]{0:T(128)S(1)}, f32[50]{0:T(128)}, u32[]{:S(2)}) copy-start(f32[50]{0:T(128)} %now_ref.1) | copy-start | bytes 604
  61.9 15.2 %copy-start.6 = (f32[50]{0:T(128)S(1)}, f32[50]{0:T(128)}, u32[]{:S(2)}) copy-start(f32[50]{0:T(128)} %next_ref.1) | copy-start | bytes 604
  61.9 9.1 %collective-permute-start.17 = (bf16[128,1152]{1,0:T(8,128)(2,1)S(1)}, bf16[128,1152]{1,0:T(8,128)(2,1)S(1)}, u32[]{:S(2)}, u32[]{:S(2)}) collective-permute-start(bf16[128,1152]{1,0:T(8,128)(2,1)S(1)} %add_convert_fusion.refs_0_), channel_id=1, source_target_pairs={{0,2},{1,3},{2,0},{3,1},{4,6},{5,7},{6,4},{7,5},{8,10},{9,11},{10,... | collective-permute-start | bytes 884744 | tf_op jit(solution)/shard_map/ppermute | solution.py:45
  72.2 1.2 %collective-permute-start.18 = (f32[8,256]{1,0:T(8,128)S(1)}, f32[8,256]{1,0:T(8,128)S(1)}, u32[]{:S(2)}, u32[]{:S(2)}) collective-permute-start(f32[8,256]{1,0:T(8,128)S(1)} %shard_map.163.first), channel_id=1, source_target_pairs={{0,1},{1,0},{2,3},{3,2},{4,5},{5,4},{6,7},{7,6},{8,9},{9,8},{10,11... | collective-permute-start | bytes 24584 | tf_op jit(solution)/shard_map/ppermute | solution.py:45
  73.4 3.7 %collective-permute-start.19 = (f32[16,256]{1,0:T(8,128)S(1)}, f32[16,256]{1,0:T(8,128)S(1)}, u32[]{:S(2)}, u32[]{:S(2)}) collective-permute-start(f32[16,256]{1,0:T(8,128)S(1)} %shard_map.164.near), channel_id=1, source_target_pairs={{0,2},{1,3},{2,0},{3,1},{4,6},{5,7},{6,4},{7,5},{8,10},{9,11},{10,... | collective-permute-start | bytes 49160 | tf_op jit(solution)/shard_map/ppermute | solution.py:45
